TPU v7x, 32 devices: a whole 2x2x4 slice. The times are simulated.
32 devices in a mesh: section: 2 (over core), dp: 16 (over z, y, x).
Axes of the slice: x: 2, y: 2, z: 4, core: 2. Of those that a mesh axis runs over, the one named last changes fastest.
Arguments:
- input_rows: bfloat16 [49152, 512], P('dp'), may hold values from -6 to 6
- conditioning: bfloat16 [49152, 512], P('dp'), may hold values from -6 to 6
- prompt: bfloat16 [48, 4, 32, 512], P('dp'), may hold values from -6 to 6
- buckets: int32 [48], P('dp'), may hold values from 0 to 2, as said below
- item_len: int32 [48, 4], P('dp'), may hold values from 0 to 1024, as said below
- step_index: int32 [48, 4], P('dp'), may hold values from 0 to 999
- output_gradient: bfloat16 [49152, 512], P('dp'), may hold values from -6 to 6
- grad_skip: bfloat16 [49152, 512], P('dp'), may hold values from -6 to 6
- step_w: bfloat16 [512, 512], replicated, may hold values from -0.25 to 0.25
- conv_w: bfloat16 [3, 512, 1024], replicated, may hold values from -0.15625 to 0.15625
- cond_w: bfloat16 [512, 1024], replicated, may hold values from -0.25 to 0.25
- conv_b: float32 [1024], replicated, may hold values from -2 to 2
- res_w: bfloat16 [512, 1024], replicated, may hold values from -0.25 to 0.25
- res_b: float32 [1024], replicated, may hold values from -2 to 2
- query_w: bfloat16 [512, 512], replicated, may hold values from -0.25 to 0.25
- key_w: bfloat16 [512, 512], replicated, may hold values from -0.25 to 0.25
- value_w: bfloat16 [512, 512], replicated, may hold values from -0.25 to 0.25
- out_w: bfloat16 [512, 1024], replicated, may hold values from -0.75 to 0.75
- out_b: float32 [1024], replicated, may hold values from -2 to 2
Outputs:
- block_out: bfloat16 [49152, 512], P('dp', 'section')
- skip_out: bfloat16 [49152, 512], P('dp', 'section')
- in_grad: bfloat16 [49152, 512], P('dp', 'section')
- step_w_grad: float32 [512, 512], replicated
- conv_w_grad: float32 [3, 512, 1024], replicated
- cond_w_grad: float32 [512, 1024], replicated
- conv_b_grad: float32 [1024], replicated
- res_w_grad: float32 [512, 1024], replicated
- res_b_grad: float32 [1024], replicated
- query_w_grad: float32 [512, 512], replicated
- key_w_grad: float32 [512, 512], replicated
- value_w_grad: float32 [512, 512], replicated
- out_w_grad: float32 [512, 1024], replicated
- out_b_grad: float32 [1024], replicated
- norm_levels: float32 [3], replicated
Inputs may be any that keep to these rules, and one draw needn't show every extreme that they name: micro-batch j holds 2**buckets[j] item slots of 1024 / 2**buckets[j] frames each; micro-batch 0 has bucket 0. `item_len`: slot s of micro-batch j is used for s < 2**buckets[j], with between half of the slot's frames and all of them valid; unused slots hold 0; slot 0 of micro-batch 0 has 1024 valid frames.
All inputs are finite; a program needn't handle non-finite values.
Results may differ from a plain program's by a relative error of at most 0.014.
Values may be sent and summed in bfloat16 or wider, within the bound.
No kernel may reach another device: no remote copies, remote signals or barrier semaphores. Data moves between devices by JAX's collectives and lax.ppermute only.
A program may use at most 192 MiB of HBM per device.

v0:
```python
import math

import jax
import jax.numpy as jnp
from jax import lax
from jax.sharding import PartitionSpec as P

HEADS = 8
DILATION_SIZE = 2
MICRO = 3


ISQ2 = 0.7071067811865476
HIGH = lax.Precision.HIGHEST


def as_sent(shard):

    def short(part):
        return part.astype(jnp.bfloat16) if part.dtype == jnp.float32 else part

    return jax.tree.map(short, shard)


def from_behind(block, axis, distance):
    devices = range(lax.axis_size(axis))
    route = [(i - distance, i) for i in devices if i - distance in devices]
    return lax.ppermute(block, axis, route)


def partner(shard, axis, bit):
    return lax.ppermute(shard, axis, [(i, i ^ 1 << bit) for i in range(lax.axis_size(axis))])


def layout(bucket, lengths, frames):
    slots = lengths.shape[0]
    place = jnp.arange(frames, dtype=jnp.int32)
    span = jnp.int32(frames) // jnp.left_shift(jnp.int32(1), bucket)
    segment = place // span
    inside = place - segment * span
    onehot = (segment[:, None] == jnp.arange(slots, dtype=jnp.int32)[None, :]).astype(jnp.float32)
    limit = jnp.sum(onehot * lengths.astype(jnp.float32)[None, :], axis=1)
    valid = (inside.astype(jnp.float32) < limit).astype(jnp.float32)
    return (segment, onehot, valid)


def embed(steps, width):
    half = width // 2
    freqs = jnp.exp(-math.log(10000.0) * jnp.arange(half, dtype=jnp.float32) / half)
    angles = steps.astype(jnp.float32)[:, None] * freqs[None, :]
    return jnp.concatenate([jnp.sin(angles), jnp.cos(angles)], axis=1)


def neighbour_ok(segment, start_offset):
    frames = segment.shape[0]
    place = jnp.arange(frames, dtype=jnp.int32)
    moved = jnp.roll(segment, -start_offset)
    return (moved == segment) & (place + start_offset >= 0) & (place + start_offset < frames)


def tap_stack(field, segment):
    pieces = []
    for start_offset in (-DILATION_SIZE, 0, DILATION_SIZE):
        inside = neighbour_ok(segment, start_offset)
        pieces.append(
            jnp.where(
                inside[:, None], jnp.roll(field, -start_offset, axis=0), jnp.zeros_like(field)
            )
        )
    return jnp.concatenate(pieces, axis=1)


def tap_return(grads, segment, width):
    total = jnp.zeros((grads.shape[0], width), jnp.float32)
    for item_number, start_offset in enumerate((-DILATION_SIZE, 0, DILATION_SIZE)):
        inside = neighbour_ok(segment, start_offset)
        piece = grads[:, item_number * width : (item_number + 1) * width]
        total = total + jnp.roll(jnp.where(inside[:, None], piece, 0.0), start_offset, axis=0)
    return total


def outer(left, right):
    return jnp.einsum("fi,fo->io", left, right, preferred_element_type=jnp.float32)


def conv_pass(weights, rows, cond_rows, segment, onehot, valid, embedding):
    step_w, conv_w, cond_w, conv_b, res_w, res_b = weights
    width = rows.shape[1]
    step_proj = jnp.dot(embedding.astype(jnp.bfloat16), step_w, preferred_element_type=jnp.float32)
    mixed = (rows.astype(jnp.float32) + jnp.dot(onehot, step_proj, precision=HIGH)) * valid[:, None]
    stacked = tap_stack(mixed.astype(jnp.bfloat16), segment)
    pre_gate = (
        jnp.dot(stacked, conv_w.reshape(-1, 2 * width), preferred_element_type=jnp.float32)
        + jnp.dot(cond_rows, cond_w, preferred_element_type=jnp.float32)
        + conv_b
    )
    gate_low = (jnp.tanh(pre_gate[:, :width]) * jax.nn.sigmoid(pre_gate[:, width:])).astype(
        jnp.bfloat16
    )
    branch = jnp.dot(gate_low, res_w, preferred_element_type=jnp.float32) + res_b
    hidden = (mixed + branch[:, :width]) * valid[:, None] * ISQ2
    return (stacked, pre_gate, gate_low, branch, hidden)


def film_pass(weights, sent, prompt_rows, segment):
    query_w, key_w, value_w, out_w, out_b = weights
    width = sent.shape[1]
    head_size = width // HEADS
    keys_in = prompt_rows.reshape(-1, width)
    keys = jnp.dot(keys_in, key_w, preferred_element_type=jnp.float32).astype(jnp.bfloat16)
    values = jnp.dot(keys_in, value_w, preferred_element_type=jnp.float32).astype(jnp.bfloat16)
    queries = jnp.dot(sent, query_w, preferred_element_type=jnp.float32).astype(jnp.bfloat16)
    owner = jnp.arange(keys.shape[0], dtype=jnp.int32) // prompt_rows.shape[1]
    allowed = segment[:, None] == owner[None, :]
    scores = jnp.einsum(
        "fhc,khc->fhk",
        queries.reshape(-1, HEADS, head_size),
        keys.reshape(-1, HEADS, head_size),
        preferred_element_type=jnp.float32,
    ) * head_size ** (-0.5)
    scores = jnp.where(allowed[:, None, :], scores, -1e30)
    peak = jnp.max(scores, axis=-1, keepdims=True)
    expo = jnp.exp(scores - peak)
    probs = expo / jnp.sum(expo, axis=-1, keepdims=True)
    probs_low = probs.astype(jnp.bfloat16)
    attended = (
        jnp.einsum(
            "fhk,khc->fhc",
            probs_low,
            values.reshape(-1, HEADS, head_size),
            preferred_element_type=jnp.float32,
        )
        .reshape(-1, width)
        .astype(jnp.bfloat16)
    )
    film = jnp.dot(attended, out_w, preferred_element_type=jnp.float32) + out_b
    return (keys_in, keys, values, queries, probs, probs_low, attended, film)


def film_back(weights, sent, prompt_rows, segment, valid, grad_rows):
    query_w, key_w, value_w, out_w, out_b = weights
    width = sent.shape[1]
    head_size = width // HEADS
    factor = head_size ** (-0.5)
    keys_in, keys, values, queries, probs, probs_low, attended, film = film_pass(
        weights, sent, prompt_rows, segment
    )
    sent_full = sent.astype(jnp.float32)
    grad_y = grad_rows.astype(jnp.float32) * valid[:, None]
    d_film = jnp.concatenate([grad_y * sent_full, grad_y], axis=1).astype(jnp.bfloat16)
    g_out_b = jnp.sum(d_film.astype(jnp.float32), axis=0)
    g_out_w = outer(attended, d_film)
    d_att = (
        jnp.dot(d_film, out_w.T, preferred_element_type=jnp.float32)
        .astype(jnp.bfloat16)
        .reshape(-1, HEADS, head_size)
    )
    d_probs = jnp.einsum(
        "fhc,khc->fhk",
        d_att,
        values.reshape(-1, HEADS, head_size),
        preferred_element_type=jnp.float32,
    )
    d_values = (
        jnp.einsum("fhk,fhc->khc", probs_low, d_att, preferred_element_type=jnp.float32)
        .reshape(-1, width)
        .astype(jnp.bfloat16)
    )
    d_scores = (probs * (d_probs - jnp.sum(probs * d_probs, axis=-1, keepdims=True))).astype(
        jnp.bfloat16
    )
    d_queries = (
        (
            jnp.einsum(
                "fhk,khc->fhc",
                d_scores,
                keys.reshape(-1, HEADS, head_size),
                preferred_element_type=jnp.float32,
            )
            * factor
        )
        .reshape(-1, width)
        .astype(jnp.bfloat16)
    )
    d_keys = (
        (
            jnp.einsum(
                "fhk,fhc->khc",
                d_scores,
                queries.reshape(-1, HEADS, head_size),
                preferred_element_type=jnp.float32,
            )
            * factor
        )
        .reshape(-1, width)
        .astype(jnp.bfloat16)
    )
    query_weight_gradient = outer(sent, d_queries)
    g_key_w = outer(keys_in, d_keys)
    g_value_w = outer(keys_in, d_values)
    d_sent = grad_y * (1.0 + film[:, :width]) + jnp.dot(
        d_queries, query_w.T, preferred_element_type=jnp.float32
    )
    return (
        d_sent.astype(jnp.bfloat16),
        (query_weight_gradient, g_key_w, g_value_w, g_out_w, g_out_b),
    )


def conv_back(weights, rows, cond_rows, segment, onehot, valid, embedding, d_sent, skip_rows):
    step_w, conv_w, cond_w, conv_b, res_w, res_b = weights
    width = rows.shape[1]
    stacked, pre_gate, gate_low, branch, hidden = conv_pass(
        weights, rows, cond_rows, segment, onehot, valid, embedding
    )
    d_res = d_sent.astype(jnp.float32) * valid[:, None] * ISQ2
    d_branch = jnp.concatenate(
        [d_res, skip_rows.astype(jnp.float32) * valid[:, None]], axis=1
    ).astype(jnp.bfloat16)
    g_res_b = jnp.sum(d_branch.astype(jnp.float32), axis=0)
    g_res_w = outer(gate_low, d_branch)
    d_gate = jnp.dot(d_branch, res_w.T, preferred_element_type=jnp.float32)
    tanh_part = jnp.tanh(pre_gate[:, :width])
    sig_part = jax.nn.sigmoid(pre_gate[:, width:])
    d_pre = jnp.concatenate(
        [
            d_gate * sig_part * (1.0 - tanh_part * tanh_part),
            d_gate * tanh_part * sig_part * (1.0 - sig_part),
        ],
        axis=1,
    ).astype(jnp.bfloat16)
    g_conv_b = jnp.sum(d_pre.astype(jnp.float32), axis=0)
    g_conv_w = outer(stacked, d_pre).reshape(conv_w.shape)
    g_cond_w = outer(cond_rows, d_pre)
    d_stack = jnp.dot(d_pre, conv_w.reshape(-1, 2 * width).T, preferred_element_type=jnp.float32)
    d_mixed = (d_res + tap_return(d_stack, segment, width)) * valid[:, None]
    low_embed = embedding.astype(jnp.bfloat16).astype(jnp.float32)
    g_step_w = jnp.dot(low_embed.T, jnp.dot(onehot.T, d_mixed, precision=HIGH), precision=HIGH)
    return (d_mixed, (g_step_w, g_conv_w, g_cond_w, g_conv_b, g_res_w, g_res_b))


def on_device(
    input_rows,
    conditioning,
    prompt,
    buckets,
    item_len,
    step_index,
    output_gradient,
    grad_skip,
    step_w,
    conv_w,
    cond_w,
    conv_b,
    res_w,
    res_b,
    query_w,
    key_w,
    value_w,
    out_w,
    out_b,
):
    section = lax.axis_index("section")
    width = input_rows.shape[1]
    frames = input_rows.shape[0] // MICRO
    conv_weights = (step_w, conv_w, cond_w, conv_b, res_w, res_b)
    film_weights = (query_w, key_w, value_w, out_w, out_b)

    def rows_of(array, index):
        return array[index * frames : (index + 1) * frames]

    blank_low = jnp.zeros((frames, width), jnp.bfloat16)
    blank_full = jnp.zeros((frames, width), jnp.float32)
    blank_stats = jnp.zeros((4,), jnp.float32)
    nothing = jnp.zeros((), jnp.float32)
    incoming = blank_low
    arrived = []
    block_rows = []
    stats = blank_stats
    for tick in range(MICRO + 1):
        conv_index = min(tick, MICRO - 1)
        film_index = max(tick - 1, 0)
        hidden_in = incoming

        def conv_forward():
            segment, onehot, valid = layout(buckets[conv_index], item_len[conv_index], frames)
            embedding = embed(step_index[conv_index], width)
            stacked, pre_gate, gate_low, branch, hidden = conv_pass(
                conv_weights,
                rows_of(input_rows, conv_index),
                rows_of(conditioning, conv_index),
                segment,
                onehot,
                valid,
                embedding,
            )
            res_part = branch[:, :width]
            sums = jnp.stack(
                [
                    jnp.sum(valid[:, None] * hidden * hidden),
                    jnp.sum(valid[:, None] * res_part * res_part),
                    jnp.sum(valid),
                    nothing,
                ]
            )
            return (hidden.astype(jnp.bfloat16), branch[:, width:] * valid[:, None], sums)

        def film_forward():
            segment, onehot, valid = layout(buckets[film_index], item_len[film_index], frames)
            film = film_pass(film_weights, hidden_in, prompt[film_index], segment)[-1]
            sent_full = hidden_in.astype(jnp.float32)
            scale = film[:, :width]
            shift = film[:, width:]
            output = (sent_full * (1.0 + scale) + shift) * valid[:, None]
            change = sent_full * scale + shift
            sums = jnp.stack([nothing, nothing, nothing, jnp.sum(valid[:, None] * change * change)])
            return (blank_low, output, sums)

        def spare_forward():
            return (blank_low, blank_full, blank_stats)

        chosen = jnp.where(section == 0, 0 if tick < MICRO else 2, 1 if tick >= 1 else 2)
        outgoing, rows, sums = lax.switch(chosen, (conv_forward, film_forward, spare_forward))
        stats = stats + sums
        block_rows.append(rows)
        if tick < MICRO:
            incoming = jax.tree.map(
                lambda part, own: part.astype(own.dtype),
                from_behind(as_sent(outgoing), "section", 1),
                outgoing,
            )
            arrived.append(incoming)
    accum = tuple((jnp.zeros(weight.shape, jnp.float32) for weight in conv_weights + film_weights))
    returning = blank_low
    grad_rows = []
    for tick in range(MICRO + 1):
        film_index = min(tick, MICRO - 1)
        conv_index = max(tick - 1, 0)
        grad_in = returning
        acc_now = accum

        def conv_backward():
            segment, onehot, valid = layout(buckets[conv_index], item_len[conv_index], frames)
            embedding = embed(step_index[conv_index], width)
            d_mixed, grads = conv_back(
                conv_weights,
                rows_of(input_rows, conv_index),
                rows_of(conditioning, conv_index),
                segment,
                onehot,
                valid,
                embedding,
                grad_in,
                rows_of(grad_skip, conv_index),
            )
            return (
                blank_low,
                d_mixed,
                tuple(jax.tree.map(jnp.add, acc_now[:6], grads)) + acc_now[6:],
            )

        def film_backward():
            segment, onehot, valid = layout(buckets[film_index], item_len[film_index], frames)
            d_sent, grads = film_back(
                film_weights,
                arrived[film_index],
                prompt[film_index],
                segment,
                valid,
                rows_of(output_gradient, film_index),
            )
            return (
                d_sent,
                blank_full,
                acc_now[:6] + tuple(jax.tree.map(jnp.add, acc_now[6:], grads)),
            )

        def reserve_backward():
            return (blank_low, blank_full, acc_now)

        chosen = jnp.where(section == 0, 0 if tick >= 1 else 2, 1 if tick < MICRO else 2)
        outgoing, rows, accum = lax.switch(chosen, (conv_backward, film_backward, reserve_backward))
        grad_rows.append(rows)
        if tick < MICRO:
            returning = jax.tree.map(
                lambda part, own: part.astype(own.dtype),
                from_behind(as_sent(outgoing), "section", -1),
                outgoing,
            )
    g_step, g_conv, g_cond, g_convb, g_res, g_resb, g_query, g_key, g_value, g_out, g_outb = accum
    (
        g_step,
        g_conv,
        g_cond,
        g_convb,
        g_res,
        g_resb,
        g_query,
        g_key,
        g_value,
        g_out,
        g_outb,
        stats,
    ) = lax.psum(
        (
            g_step,
            g_conv,
            g_cond,
            g_convb,
            g_res,
            g_resb,
            g_query,
            g_key,
            g_value,
            g_out,
            g_outb,
            stats,
        ),
        ("section", "dp"),
    )
    levels = jnp.sqrt(jnp.stack([stats[0], stats[1], stats[3]]) / (stats[2] * width))
    half = width // 2
    skip_full = jnp.concatenate(block_rows[:MICRO], axis=0)
    out_full = jnp.concatenate(block_rows[1:], axis=0)
    in_full = jnp.concatenate(grad_rows[1:], axis=0)
    upper_skip = skip_full[:, half:].astype(jnp.bfloat16)
    first_half = jnp.where(
        section == 0,
        in_full[:, half:].astype(jnp.bfloat16),
        out_full[:, :half].astype(jnp.bfloat16),
    )
    second_half = jnp.where(section == 0, upper_skip, jnp.zeros_like(upper_skip))
    got_first, got_second = partner((first_half, second_half), "section", 0)
    block_out = jnp.where(section == 0, got_first, out_full[:, half:].astype(jnp.bfloat16))
    in_grad = jnp.where(section == 0, in_full[:, :half].astype(jnp.bfloat16), got_first)
    skip_out = jnp.where(section == 0, skip_full[:, :half].astype(jnp.bfloat16), got_second)
    return (
        block_out,
        skip_out,
        in_grad,
        g_step,
        g_conv,
        g_cond,
        g_convb,
        g_res,
        g_resb,
        g_query,
        g_key,
        g_value,
        g_out,
        g_outb,
        levels,
    )


def solution(mesh):
    return jax.shard_map(
        on_device,
        mesh=mesh,
        in_specs=(
            P("dp", None),
            P("dp", None),
            P("dp", None, None, None),
            P("dp"),
            P("dp", None),
            P("dp", None),
            P("dp", None),
            P("dp", None),
            P(),
            P(),
            P(),
            P(),
            P(),
            P(),
            P(),
            P(),
            P(),
            P(),
            P(),
        ),
        out_specs=(
            P("dp", "section"),
            P("dp", "section"),
            P("dp", "section"),
            P(),
            P(),
            P(),
            P(),
            P(),
            P(),
            P(),
            P(),
            P(),
            P(),
            P(),
            P(),
        ),
        check_vma=False,
    )
```

profile of v0, /device:TPU:0, one launch (start us, length us, event | category | flops | bytes accessed | tf_op | source)
XLA Modules:
  0.0 690.4 jit_solution(3902014286912071175)
XLA Ops:
  7.2 27.9 %conditional.8 = (bf16[1024,512]{1,0:T(8,128)(2,1)}, bf16[1024,512]{1,0:T(8,128)(2,1)S(1)}, f32[4]{0:T(128)S(1)}) conditional(s32[]{:T(128)} %clamp.16, (bf16[3072,512]{1,0:T(8,128)(2,1)}, s32[3]{0:T(128)}, s32[3,4]{1,0:T(4,128)}, bf16[512,512]{1,0:T(8,128)(2,1)}, s32[3,4]{1,0:T(4,128)}, ...), branch_computations={%region_0.5_spmd, %region_5.10_spmd, %region_10.11_spmd} | conditional | flops 5425406976 | bytes 74071464 | solution.py:323
  39.9 32.1 %conditional.10 = (bf16[1024,512]{1,0:T(8,128)(2,1)}, bf16[1024,512]{1,0:T(8,128)(2,1)}, f32[4]{0:T(128)S(1)}) conditional(s32[]{:T(128)} %clamp.6, (bf16[3072,512]{1,0:T(8,128)(2,1)}, s32[3]{0:T(128)}, s32[3,4]{1,0:T(4,128)}, bf16[512,512]{1,0:T(8,128)(2,1)}, s32[3,4]{1,0:T(4,128)}, ...), branch_computations={%region_22.27_spmd, %region_27.32_spmd, %region_32.33_spmd} | conditional | flops 5425406976 | bytes 74071480 | solution.py:323
  74.4 25.3 %conditional.9 = (bf16[1024,512]{1,0:T(8,128)(2,1)}, f32[512,512]{1,0:T(8,128)S(1)}, f32[3,512,1024]{2,1,0:T(8,128)}, f32[512,1024]{0,1:T(8,128)}, f32[1024]{0:T...) conditional(s32[]{:T(128)} %clamp.7, (s32[3,4]{1,0:T(4,128)}, ...), branch_computations={%region_11.15_spmd, %region_15.21_spmd, %region_21.22_spmd} | conditional | flops 14087700480 | bytes 192188288 | solution.py:382
  88.7 3.5 broadcast_in_dim.447
  101.0 30.2 %conditional.12 = (bf16[1024,512]{1,0:T(8,128)(2,1)}, bf16[1024,512]{1,0:T(8,128)(2,1)}, f32[4]{0:T(128)S(1)}) conditional(s32[]{:T(128)} %clamp.6, (bf16[3072,512]{1,0:T(8,128)(2,1)}, s32[3]{0:T(128)}, s32[3,4]{1,0:T(4,128)}, bf16[512,512]{1,0:T(8,128)(2,1)}, s32[3,4]{1,0:T(4,128)}, ...), branch_computations={%region_44.49_spmd, %region_49.54_spmd, %region_54.55_spmd} | conditional | flops 5425406976 | bytes 74071480 | solution.py:323
  131.2 25.5 %collective-permute-start.4 = (bf16[1024,512]{1,0:T(8,128)(2,1)}, bf16[1024,512]{1,0:T(8,128)(2,1)S(1)}, u32[]{:S(2)}, u32[]{:S(2)}) collective-permute-start(bf16[1024,512]{1,0:T(8,128)(2,1)} %get-tuple-element.895), channel_id=1, source_target_pairs={{0,16},{1,17},{2,18},{3,19},{4,20},{5,21},{6,22},{7,23},{8,24},{9,... | collective-permute-start | bytes 3145736 | tf_op jit(solution)/shard_map/ppermute | solution.py:28
  156.8 58.2 %conditional.11 = (bf16[1024,512]{1,0:T(8,128)(2,1)}, f32[1024,512]{1,0:T(8,128)S(1)}, f32[512,512]{1,0:T(8,128)S(1)}, f32[3,512,1024]{2,1,0:T(8,128)}, f32[512,...) conditional(s32[]{:T(128)} %clamp.6, ...), branch_computations={%region_33.37_spmd, %region_37.43_spmd, %region_43.44_spmd} | conditional | flops 14106314752 | bytes 207921152 | solution.py:382
  164.8 3.6 fusion.184
  174.6 3.6 fusion.183
  178.2 7.0 %add.769 = f32[3,512,1024]{2,1,0:T(8,128)} add(f32[3,512,1024]{2,1,0:T(8,128)} %get-tuple-element.601, f32[3,512,1024]{2,1,0:T(8,128)S(1)} %bitcast.613) | non-fusion elementwise | flops 1572864 | bytes 18874368 | tf_op jit(solution)/shard_map/cond/branch_0_fun/add | solution.py:359
  185.1 4.9 bitcast_add_fusion
  199.8 4.4 convolution_add_fusion.4
  216.4 21.3 %collective-permute-done.3 = bf16[1024,512]{1,0:T(8,128)(2,1)S(1)} collective-permute-done((bf16[1024,512]{1,0:T(8,128)(2,1)}, bf16[1024,512]{1,0:T(8,128)(2,1)S(1)}, u32[]{:S(2)}, u32[]{:S(2)}) %collective-permute-start.3) | collective-permute-done | bytes 1048608 | tf_op jit(solution)/shard_map/ppermute | solution.py:28
  237.7 59.8 %conditional.13 = (bf16[1024,512]{1,0:T(8,128)(2,1)}, f32[1024,512]{1,0:T(8,128)S(1)}, f32[512,512]{1,0:T(8,128)S(1)}, f32[3,512,1024]{2,1,0:T(8,128)}, f32[512,...) conditional(s32[]{:T(128)} %clamp.6, ...), branch_computations={%region_55.59_spmd, %region_59.65_spmd, %region_65.66_spmd} | conditional | flops 14106314752 | bytes 214617792 | solution.py:382
  247.9 3.7 fusion.299
  257.5 3.6 fusion.298
  261.1 7.0 %add.813 = f32[3,512,1024]{2,1,0:T(8,128)} add(f32[3,512,1024]{2,1,0:T(8,128)} %get-tuple-element.676, f32[3,512,1024]{2,1,0:T(8,128)S(1)} %bitcast.614) | non-fusion elementwise | flops 1572864 | bytes 18874368 | tf_op jit(solution)/shard_map/cond/branch_0_fun/add | solution.py:359
  268.1 4.9 bitcast_add_fusion.1
  273.4 3.5 fusion.325
  282.4 4.4 convolution_add_fusion.9
  298.7 16.5 %collective-permute-done.5 = bf16[1024,512]{1,0:T(8,128)(2,1)S(1)} collective-permute-done((bf16[1024,512]{1,0:T(8,128)(2,1)}, bf16[1024,512]{1,0:T(8,128)(2,1)S(1)}, u32[]{:S(2)}, u32[]{:S(2)}) %collective-permute-start.5) | collective-permute-done | bytes 1048608 | tf_op jit(solution)/shard_map/ppermute | solution.py:28
  315.2 59.1 %conditional.14 = (f32[1024,512]{1,0:T(8,128)}, f32[512,512]{1,0:T(8,128)S(1)}, f32[3,512,1024]{2,1,0:T(8,128)}, f32[512,1024]{0,1:T(8,128)}, f32[1024]{0:T(1024...) conditional(s32[]{:T(128)} %clamp.16, ...), branch_computations={%region_66.70_spmd, %region_70.76_spmd, %region_76.77_spmd} | conditional | flops 14106314752 | bytes 212520640 | solution.py:382
  325.6 3.7 fusion.363
  335.0 3.6 fusion.362
  338.6 7.0 %add.840 = f32[3,512,1024]{2,1,0:T(8,128)} add(f32[3,512,1024]{2,1,0:T(8,128)} %get-tuple-element.731, f32[3,512,1024]{2,1,0:T(8,128)S(1)} %bitcast.615) | non-fusion elementwise | flops 1572864 | bytes 18874368 | tf_op jit(solution)/shard_map/cond/branch_0_fun/add | solution.py:359
  345.6 4.9 bitcast_add_fusion.2
  362.5 4.4 convolution_add_fusion.12
  374.3 3.7 copy.224
  394.5 44.9 %all-reduce.1 = (f32[1024]{0:T(1024)}, f32[1024]{0:T(1024)}, f32[1024]{0:T(1024)}, f32[4]{0:T(128)S(1)}) all-reduce(f32[1024]{0:T(1024)S(1)} %get-tuple-element.917, f32[1024]{0:T(1024)S(1)} %get-tuple-element.919, f32[1024]{0:T(1024)S(1)} %get-tuple-element.924, ...), channel_id=1, replica_groups=mesh['section'=2,'dp'=16] {'section','dp'}, use_global_device_ids=true, to_apply=%region_91.92 | all-reduce | flops 3076 | bytes 24608 | tf_op jit(solution)/shard_map/psum | solution.py:404
  444.4 3.9 slice_select_fusion.12
  448.2 217.3 %all-reduce.5.cloned.1.call-done = (f32[512,512]{1,0:T(8,128)}, f32[3,512,1024]{2,1,0:T(8,128)}, f32[512,1024]{1,0:T(8,128)}, f32[512,1024]{1,0:T(8,128)}, f32[5...) async-done(((f32[512,512]{1,0:T(8,128)}, f32[3,512,1024]{2,1,0:T(8,128)}, f32[512,1024]{1,0:T(8,128)}, f32[512,1024]{1,0:T(8,128)}, ...) | async-done | bytes 16777232 | tf_op jit(solution)/shard_map/psum | solution.py:404
  667.8 6.8 copy.441
  (378 shorter events, 189.9 us)
Async XLA Ops:
  7.2 658.3 %all-reduce.5.cloned.1.call-start = ((), (), s32[]{:S(2)}) async-start(), calls=%async_computation | async-start | bytes 33554432 | tf_op jit(solution)/shard_map/psum | solution.py:404
  36.2 3.8 copy-start.155
  36.2 3.8 collective-permute-start
  72.1 28.9 %collective-permute-start.2 = (bf16[1024,512]{1,0:T(8,128)(2,1)}, bf16[1024,512]{1,0:T(8,128)(2,1)}, u32[]{:S(2)}, u32[]{:S(2)}) collective-permute-start(bf16[1024,512]{1,0:T(8,128)(2,1)} %get-tuple-element.881), channel_id=1, source_target_pairs={{0,16},{1,17},{2,18},{3,19},{4,20},{5,21},{6,22},{7,23},{8,24},{9,... | collective-permute-start | bytes 3145736 | tf_op jit(solution)/shard_map/ppermute | solution.py:28
  99.7 57.1 %collective-permute-start.1 = (bf16[1024,512]{1,0:T(8,128)(2,1)}, bf16[1024,512]{1,0:T(8,128)(2,1)}, u32[]{:S(2)}, u32[]{:S(2)}) collective-permute-start(bf16[1024,512]{1,0:T(8,128)(2,1)} %get-tuple-element.869), channel_id=1, source_target_pairs={{16,0},{17,1},{18,2},{19,3},{20,4},{21,5},{22,6},{23,7},{24,8},{25... | collective-permute-start | bytes 3145736 | tf_op jit(solution)/shard_map/ppermute | solution.py:28
  131.2 25.6 %copy-start.159 = (f32[4]{0:T(128)}, f32[4]{0:T(128)S(1)}, u32[]{:S(2)}) copy-start(f32[4]{0:T(128)S(1)} %get-tuple-element.927) | copy-start | bytes 52
  131.2 85.1 %collective-permute-start.4 = (bf16[1024,512]{1,0:T(8,128)(2,1)}, bf16[1024,512]{1,0:T(8,128)(2,1)S(1)}, u32[]{:S(2)}, u32[]{:S(2)}) collective-permute-start(bf16[1024,512]{1,0:T(8,128)(2,1)} %get-tuple-element.895), channel_id=1, source_target_pairs={{0,16},{1,17},{2,18},{3,19},{4,20},{5,21},{6,22},{7,23},{8,24},{9,... | collective-permute-start | bytes 3145736 | tf_op jit(solution)/shard_map/ppermute | solution.py:28
  164.8 3.7 copy-start.129
  185.1 4.9 copy-start.112
  185.1 5.0 copy-start.114
  185.1 5.3 copy-start.166
  215.0 22.6 %copy-start.44 = (f32[1024,512]{1,0:T(8,128)}, f32[1024,512]{1,0:T(8,128)S(1)}, u32[]{:S(2)}) copy-start(f32[1024,512]{1,0:T(8,128)S(1)} %get-tuple-element.882) | copy-start | bytes 6291460
  215.0 22.6 %collective-permute-start.3 = (bf16[1024,512]{1,0:T(8,128)(2,1)}, bf16[1024,512]{1,0:T(8,128)(2,1)S(1)}, u32[]{:S(2)}, u32[]{:S(2)}) collective-permute-start(bf16[1024,512]{1,0:T(8,128)(2,1)} %get-tuple-element.883), channel_id=1, source_target_pairs={{16,0},{17,1},{18,2},{19,3},{20,4},{21,5},{22,6},{23,7},{24,8},{25... | collective-permute-start | bytes 3145736 | tf_op jit(solution)/shard_map/ppermute | solution.py:28
  247.9 3.7 copy-start.39
  247.9 3.7 copy-start.130
  268.1 4.9 copy-start.116
  268.1 4.9 copy-start.118
  268.1 5.3 copy-start.168
  297.4 17.8 %copy-start.46 = (f32[1024,512]{1,0:T(8,128)}, f32[1024,512]{1,0:T(8,128)S(1)}, u32[]{:S(2)}) copy-start(f32[1024,512]{1,0:T(8,128)S(1)} %get-tuple-element.896) | copy-start | bytes 6291460
  297.4 17.8 %collective-permute-start.5 = (bf16[1024,512]{1,0:T(8,128)(2,1)}, bf16[1024,512]{1,0:T(8,128)(2,1)S(1)}, u32[]{:S(2)}, u32[]{:S(2)}) collective-permute-start(bf16[1024,512]{1,0:T(8,128)(2,1)} %get-tuple-element.897), channel_id=1, source_target_pairs={{16,0},{17,1},{18,2},{19,3},{20,4},{21,5},{22,6},{23,7},{24,8},{25... | collective-permute-start | bytes 3145736 | tf_op jit(solution)/shard_map/ppermute | solution.py:28
  325.6 3.7 copy-start.40
  325.6 3.7 copy-start.131
  345.6 4.9 copy-start.120
  345.6 4.9 copy-start.122
  345.6 5.3 copy-start.170
  374.3 3.7 copy-start.25
  374.3 3.7 copy-start.32
  383.8 4.7 copy-start.47
  387.1 5.2 copy-start.48
  388.4 53.5 %collective-permute-start.7 = (bf16[3072,256]{1,0:T(8,128)(2,1)}, bf16[3072,256]{1,0:T(8,128)(2,1)}, u32[]{:S(2)}, u32[]{:S(2)}) collective-permute-start(bf16[3072,256]{1,0:T(8,128)(2,1)} %slice_select_fusion.13), channel_id=1, source_target_pairs={{0,16},{16,0},{1,17},{17,1},{2,18},{18,2},{3,19},{19,3},{4,20},{20... | collective-permute-start | bytes 4718600 | tf_op jit(solution)/shard_map/ppermute | solution.py:32
  394.5 48.7 %collective-permute-start.6 = (bf16[3072,256]{1,0:T(8,128)(2,1)}, bf16[3072,256]{1,0:T(8,128)(2,1)}, u32[]{:S(2)}, u32[]{:S(2)}) collective-permute-start(bf16[3072,256]{1,0:T(8,128)(2,1)} %slice_select_fusion.16), channel_id=1, source_target_pairs={{0,16},{16,0},{1,17},{17,1},{2,18},{18,2},{3,19},{19,3},{4,20},{20... | collective-permute-start | bytes 4718600 | tf_op jit(solution)/shard_map/ppermute | solution.py:32
  667.8 6.8 copy-start.99
  (60 other events, 139.7 us)
Sparse Core Ops, SparseCore 0:
  378.2 287.2 all-reduce.4
where the time goes:
time: 699 us; the launch traced here: 690 us
  waiting for transfers between devices  257 us (37%)
  matrix products  123 us (18%)
  other arithmetic  85.4 us (12%)
  loops' own time  70.9 us (10%)
  local copies, waits for them, and re-layouts  59.8 us (9%)
  blocking collectives  44.9 us (6%)
  starting transfers between devices  33.1 us (5%)
  between operations  15.4 us (2%)
    psum x1, waiting for transfers between devices, on_device(): lax.psum((g_step, g_conv, g_cond, g_convb, g_res, g_resb, g_query, g_key,...  217 us
    psum x1, blocking collectives, on_device(): lax.psum((g_step, g_conv, g_cond, g_convb, g_res, g_resb, g_query, g_key,...  44.9 us
    another operation x4, loops' own time, on_device(): lax.switch(chosen, (conv_backward, film_backward, reserve_backward))  42.9 us
    ppermute x6, waiting for transfers between devices, from_behind(): return lax.ppermute(block, axis, route)  40.2 us
    dot_general x9, matrix products, outer(): jnp.einsum('fi,fo->io', left, right, preferred_element_type=jnp.float32)  38.9 us
    ppermute x6, starting transfers between devices, from_behind(): return lax.ppermute(block, axis, route)  33 us
    another operation x4, loops' own time, on_device(): lax.switch(chosen, (conv_forward, film_forward, spare_forward))  28 us
    unnamed x72, local copies, waits for them, and re-layouts  25.1 us
  transfers between devices with their start and end apart: 9, of which 4 were waited for; matrix products, arithmetic and copies ran while one was open for 14% of the time, Pallas kernels for 0%

commit v1 on v0

v1 whole, which is shorter than its diff:
```python
import functools
import math

import jax
import jax.numpy as jnp
from jax import lax
from jax.experimental import pallas as pl
from jax.experimental.pallas import tpu as pltpu
from jax.sharding import PartitionSpec as P

HEADS = 8
SHIFT = 2
EDGE = 16
ISQ2 = 0.7071067811865476
F32 = jnp.float32
BF16 = jnp.bfloat16
VMEM = 56 * 1024 * 1024
KB_VMEM = 48 * 1024 * 1024
KC_VMEM = 48 * 1024 * 1024


def nn(a, b):
    return lax.dot_general(a, b, (((1,), (0,)), ((), ())), preferred_element_type=F32)


def nt(a, b):
    return lax.dot_general(a, b, (((1,), (1,)), ((), ())), preferred_element_type=F32)


def tn(a, b):
    return lax.dot_general(a, b, (((0,), (0,)), ((), ())), preferred_element_type=F32)


def rows_iota(rows, cols):
    return lax.broadcasted_iota(jnp.int32, (rows, cols), 0)


def col_sums(x):
    rows, cols = x.shape
    return jnp.sum(x.reshape(rows // 8, 8, cols), axis=0)


def plan(g, tile, slots, buckets, item_len):
    mb = g // slots
    q = g - mb * slots
    span = slots >> buckets[mb]
    slot = q // span
    off = q - slot * span
    lim = item_len[mb, slot] - off * tile
    return mb, slot, lim, off > 0, off < span - 1


def forward_kernel(
    cfg,
    sec_ref,
    buckets,
    item_len,
    steps,
    prev_ref,
    rows_ref,
    next_ref,
    cond_ref,
    gout_ref,
    gskip_ref,
    prompt_ref,
    mask_ref,
    step_w,
    conv_w,
    cond_w,
    conv_b,
    res_w,
    res_b,
    query_w,
    key_w,
    value_w,
    out_w,
    out_b,
    o_stack,
    o_dpre,
    o_dsent,
    o_block_keep,
    o_block_give,
    o_skip_keep,
    o_skip_give,
    o_keep,
    o_give,
    o_vec,
    o_emb,
    proj,
    keys,
    values,
    d_keys,
    d_values,
    g_out,
    g_res,
    g_query,
    sums,
    stats,
    count,
):
    tile, slots, nq, subs, tiles, mb_own, micro = cfg
    t = pl.program_id(0)
    section = sec_ref[0]
    size = subs * tile
    width = rows_ref.shape[1]
    half = width // 2
    head = width // HEADS
    mb0 = section * (micro - mb_own)
    items = mb_own * slots
    keep_left = section == 0

    @pl.when(t == 0)
    def _():
        row = rows_iota(items, half)
        when = jnp.zeros((items, half), F32)
        for i in range(items):
            s = steps[mb0 + i // slots, i % slots].astype(F32)
            when = jnp.where(row == i, s, when)
        lane = lax.broadcasted_iota(jnp.int32, (items, half), 1).astype(F32)
        angle = when * jnp.exp(lane * F32(-math.log(10000.0) / half))
        emb = jnp.concatenate([jnp.sin(angle), jnp.cos(angle)], axis=1)
        o_emb[...] = emb
        proj[...] = nn(emb.astype(BF16), step_w[...])
        here = prompt_ref[pl.ds(pl.multiple_of(mb0 * slots * nq, 16), items * nq), :]
        factor = head ** (-0.5)
        keys[...] = (nn(here, key_w[...]).astype(BF16) * BF16(factor)).astype(BF16)
        values[...] = nn(here, value_w[...]).astype(BF16)
        d_keys[...] = jnp.zeros_like(d_keys)
        d_values[...] = jnp.zeros_like(d_values)
        g_out[...] = jnp.zeros_like(g_out)
        g_res[...] = jnp.zeros_like(g_res)
        g_query[...] = jnp.zeros_like(g_query)
        sums[...] = jnp.zeros_like(sums)
        stats[...] = jnp.zeros_like(stats)
        count[0] = 0

    ext = jnp.concatenate([prev_ref[...], rows_ref[...], next_ref[...]], axis=0)
    place = rows_iota(tile + 2 * EDGE, width)
    spread = tile + 2 * EDGE
    mixed, behind, ahead, at = [], [], [], []
    limit = jnp.zeros((size, width), jnp.int32)
    row = rows_iota(size, width)
    for k in range(subs):
        mb, slot, lim, prev_in, next_in = plan(
            section * tiles + t * subs + k, tile, slots, buckets, item_len
        )
        item = (mb - mb0) * slots + slot
        at.append(pl.multiple_of(item * nq, nq))
        lo = jnp.where(prev_in, 0, EDGE)
        hi = jnp.where(next_in, tile + 2 * EDGE, tile + EDGE)
        hi = jnp.minimum(hi, lim + EDGE)
        part = ext[k * tile : k * tile + spread].astype(F32) + proj[pl.ds(item, 1), :]
        part = jnp.where((place >= lo) & (place < hi), part, 0.0)
        mixed.append(part[EDGE : EDGE + tile])
        behind.append(pltpu.roll(part, SHIFT, 0)[EDGE : EDGE + tile].astype(BF16))
        ahead.append(pltpu.roll(part, spread - SHIFT, 0)[EDGE : EDGE + tile].astype(BF16))
        limit = jnp.where(row >= k * tile, lim + k * tile, limit)
        count[0] += jnp.clip(lim, 0, tile)
    mixed = jnp.concatenate(mixed, axis=0)
    valid = row < limit
    stacked = jnp.concatenate(
        [jnp.concatenate(behind, axis=0), mixed.astype(BF16), jnp.concatenate(ahead, axis=0)],
        axis=1,
    )
    o_stack[...] = stacked
    pre = nn(stacked, conv_w[...]) + nn(cond_ref[...], cond_w[...]) + conv_b[...]
    a = jnp.tanh(pre[:, :width])
    s = 0.5 * jnp.tanh(0.5 * pre[:, width:]) + 0.5
    both = a * s
    gate = both.astype(BF16)
    slope_a = s - both * a
    slope_s = both - both * s
    branch = nn(gate, res_w[...]) + res_b[...]
    res_part = jnp.where(valid, branch[:, :width], 0.0)
    skip = jnp.where(valid, branch[:, width:], 0.0).astype(BF16)
    o_skip_keep[...] = jnp.where(keep_left, skip[:, :half], skip[:, half:])
    o_skip_give[...] = jnp.where(keep_left, skip[:, half:], skip[:, :half])
    hidden = (mixed + res_part) * ISQ2
    sent = hidden.astype(BF16)
    sent_f = sent.astype(F32)
    stats[0] += col_sums(hidden * hidden)
    stats[1] += col_sums(res_part * res_part)

    query = nn(sent, query_w[...]).astype(BF16)
    mask = mask_ref[...]
    probs, probs_low, key_bd, value_bd, attended = [], [], [], [], []
    for k in range(subs):
        key_bd.append(jnp.concatenate([keys[pl.ds(at[k], nq), :]] * HEADS, axis=0) * mask)
        value_bd.append(jnp.concatenate([values[pl.ds(at[k], nq), :]] * HEADS, axis=0) * mask)
        scores = nt(key_bd[k], query[k * tile : (k + 1) * tile]).reshape(HEADS, nq, tile)
        expo = jnp.exp(scores - jnp.max(scores, axis=1, keepdims=True))
        probs.append(expo * (1.0 / jnp.sum(expo, axis=1, keepdims=True)))
        probs_low.append(probs[k].astype(BF16).reshape(HEADS * nq, tile))
        attended.append(tn(probs_low[k], value_bd[k]).astype(BF16))
    attended = jnp.concatenate(attended, axis=0)
    film = nn(attended, out_w[...]) + out_b[...]
    scale = film[:, :width]
    change = jnp.where(valid, sent_f * scale + film[:, width:], 0.0)
    block = (sent_f + change).astype(BF16)
    o_block_keep[...] = jnp.where(keep_left, block[:, :half], block[:, half:])
    o_block_give[...] = jnp.where(keep_left, block[:, half:], block[:, :half])
    stats[2] += col_sums(change * change)

    gy = jnp.where(valid, gout_ref[...].astype(F32), 0.0)
    d_film = jnp.concatenate([(gy * sent_f).astype(BF16), gy.astype(BF16)], axis=1)
    sums[2] += col_sums(d_film.astype(F32))
    g_out[...] += tn(attended, d_film)
    d_att = nt(d_film, out_w[...]).astype(BF16)
    low_lane = lax.broadcasted_iota(jnp.int32, (nq, 2 * head), 1) < head

    def own_heads(x):
        pieces = []
        for p in range(HEADS // 2):
            at_row, at_lane = 2 * p * nq, 2 * p * head
            first = x[at_row : at_row + nq, at_lane : at_lane + 2 * head]
            second = x[at_row + nq : at_row + 2 * nq, at_lane : at_lane + 2 * head]
            pieces.append(jnp.where(low_lane, first, second))
        return jnp.concatenate(pieces, axis=1)

    d_query = []
    for k in range(subs):
        here = slice(k * tile, (k + 1) * tile)
        d_probs = nt(value_bd[k], d_att[here]).reshape(HEADS, nq, tile)
        weighted = probs[k] * d_probs
        inner = jnp.sum(weighted, axis=1, keepdims=True)
        d_scores = (weighted - probs[k] * inner).astype(BF16).reshape(HEADS * nq, tile)
        d_values[pl.ds(at[k], nq), :] += own_heads(nn(probs_low[k], d_att[here]))
        d_keys[pl.ds(at[k], nq), :] += own_heads(nn(d_scores, query[here]))
        d_query.append(tn(d_scores, key_bd[k]).astype(BF16))
    d_query = jnp.concatenate(d_query, axis=0)
    g_query[...] += tn(sent, d_query)
    d_sent = (gy * (1.0 + scale) + nt(d_query, query_w[...])).astype(BF16)
    o_dsent[...] = d_sent

    d_res = jnp.where(valid, d_sent.astype(F32) * ISQ2, 0.0).astype(BF16)
    gs = jnp.where(valid, gskip_ref[...].astype(F32), 0.0).astype(BF16)
    d_branch = jnp.concatenate([d_res, gs], axis=1)
    sums[1] += col_sums(d_branch.astype(F32))
    g_res[...] += tn(gate, d_branch)
    d_gate = nt(d_branch, res_w[...])
    d_pre = jnp.concatenate(
        [(d_gate * slope_a).astype(BF16), (d_gate * slope_s).astype(BF16)], axis=1
    )
    sums[0] += col_sums(d_pre.astype(F32))
    o_dpre[...] = d_pre

    @pl.when(t == tiles // subs - 1)
    def _():
        here = prompt_ref[pl.ds(pl.multiple_of(mb0 * slots * nq, 16), items * nq), :]
        factor = head ** (-0.5)
        mine = pl.multiple_of(section * half, half)
        theirs = pl.multiple_of(half - section * half, half)

        def put(i, ref, left):
            o_keep[i] = ref[pl.ds(mine, half), pl.ds(left, width)].astype(BF16)
            o_give[i] = ref[pl.ds(theirs, half), pl.ds(left, width)].astype(BF16)

        put(0, g_out, 0)
        put(1, g_out, width)
        put(2, g_res, 0)
        put(3, g_res, width)
        put(4, g_query, 0)
        g_query[...] = tn(here, (d_keys[...] * factor).astype(BF16))
        put(5, g_query, 0)
        g_query[...] = tn(here, d_values[...].astype(BF16))
        put(6, g_query, 0)
        for i in range(3):
            line = jnp.sum(sums[i], axis=0, keepdims=True)
            o_vec[2 * i : 2 * i + 1, :] = line[:, :width]
            o_vec[2 * i + 1 : 2 * i + 2, :] = line[:, width:]
        for i in range(3):
            o_vec[6 + i : 7 + i, :] = jnp.sum(stats[i], axis=0, keepdims=True)
        lane = lax.broadcasted_iota(jnp.int32, (16 - 9, width), 1)
        digits = (count[0] >> (3 * jnp.minimum(lane, 8))) & 7
        o_vec[9:16, :] = jnp.where(lane < 8, digits, 0).astype(F32)


def weight_kernel(cfg, sec_ref, stack_ref, cond_ref, dpre_ref, o_keep, o_give, acc):
    taps = cfg
    i = pl.program_id(0)
    section = sec_ref[0]
    width = acc.shape[0]
    half = width // 2

    @pl.when(i < taps)
    def _():
        acc[...] = tn(stack_ref[...], dpre_ref[...])

    @pl.when(i == taps)
    def _():
        acc[...] = tn(cond_ref[...], dpre_ref[...])

    mine = pl.multiple_of(section * half, half)
    theirs = pl.multiple_of(half - section * half, half)
    for side in range(2):
        o_keep[side] = acc[pl.ds(mine, half), pl.ds(side * width, width)].astype(BF16)
        o_give[side] = acc[pl.ds(theirs, half), pl.ds(side * width, width)].astype(BF16)


def back_kernel(
    cfg,
    sec_ref,
    buckets,
    item_len,
    prev_ref,
    dpre_ref,
    next_ref,
    other_ref,
    dsent_ref,
    conv_w,
    emb_ref,
    vec_ref,
    after_ref,
    o_keep,
    o_give,
    o_rows,
    d_step,
):
    tile, slots, subs, tiles, mb_own, micro = cfg
    t = pl.program_id(0)
    section = sec_ref[0]
    size = subs * tile
    width = dsent_ref.shape[1]
    half = width // 2
    mb0 = section * (micro - mb_own)

    @pl.when(t == 0)
    def _():
        d_step[...] = jnp.zeros_like(d_step)

    steps = tiles // subs
    before = jnp.where(t == 0, other_ref[EDGE:, :], prev_ref[...])
    after = jnp.where(t == steps - 1, other_ref[:EDGE, :], next_ref[...])
    ext = jnp.concatenate([before, dpre_ref[...], after], axis=0)
    spread = tile + 2 * EDGE
    place = rows_iota(spread, 2 * width)
    ahead, behind, item = [], [], []
    limit = jnp.zeros((size, width), jnp.int32)
    row = rows_iota(size, width)
    for k in range(subs):
        mb, slot, lim, prev_in, next_in = plan(
            section * tiles + t * subs + k, tile, slots, buckets, item_len
        )
        item.append((mb - mb0) * slots + slot)
        lo = jnp.where(prev_in, 0, EDGE)
        hi = jnp.where(next_in, spread, tile + EDGE)
        part = ext[k * tile : k * tile + spread].astype(F32)
        part = jnp.where((place >= lo) & (place < hi), part, 0.0)
        ahead.append(pltpu.roll(part, spread - SHIFT, 0)[EDGE : EDGE + tile].astype(BF16))
        behind.append(pltpu.roll(part, SHIFT, 0)[EDGE : EDGE + tile].astype(BF16))
        limit = jnp.where(row >= k * tile, lim + k * tile, limit)
    d_in = nt(jnp.concatenate(ahead, axis=0), conv_w[:width, :])
    d_in += nt(dpre_ref[...], conv_w[width : 2 * width, :])
    d_in += nt(jnp.concatenate(behind, axis=0), conv_w[2 * width :, :])
    d_mixed = jnp.where(row < limit, dsent_ref[...].astype(F32) * ISQ2 + d_in, 0.0)
    for k in range(subs):
        line = jnp.sum(col_sums(d_mixed[k * tile : (k + 1) * tile]), axis=0, keepdims=True)
        d_step[pl.ds(item[k], 1), :] += line
    low = d_mixed.astype(BF16)
    o_keep[...] = jnp.where(section == 0, low[:, :half], low[:, half:])
    o_give[...] = jnp.where(section == 0, low[:, half:], low[:, :half])

    @pl.when(t == steps - 1)
    def _():
        both = jnp.concatenate([emb_ref[...], d_step[...], vec_ref[...]], axis=0)
        o_rows[...] = both.astype(BF16)


SMALL = pl.CostEstimate(flops=1024, bytes_accessed=1024, transcendentals=0)
LARGE = pl.CostEstimate(flops=1 << 36, bytes_accessed=1024, transcendentals=0)
ANYWHERE = pl.BlockSpec(memory_space=pl.ANY)
PARAMS = pltpu.CompilerParams(vmem_limit_bytes=VMEM)


IN_VMEM = pl.BlockSpec(memory_space=pltpu.VMEM)
IN_SMEM = pl.BlockSpec(memory_space=pltpu.SMEM)
IN_HBM = pl.BlockSpec(memory_space=pltpu.HBM)


def struct(rows, width, dtype=BF16):
    return jax.ShapeDtypeStruct((rows, width), dtype)


def total(a, b):
    return (a.astype(F32) + b.astype(F32)).astype(BF16)


def at_bit(bit, rows):
    return pl.ds(pl.multiple_of(bit * rows, 16), rows)


def split_body(bit, held, got, keep, give):
    rows = keep.shape[0]
    keep[...] = total(held[at_bit(bit, rows), :], got[at_bit(bit, rows), :])
    give[...] = total(held[at_bit(1 - bit, rows), :], got[at_bit(1 - bit, rows), :])


def add_body(bit, held, got, out):
    out[...] = total(held[...], got[...])


def merge_body(bit, cur, got, out):
    rows = cur.shape[0]
    out[at_bit(bit, rows), :] = cur[...]
    out[at_bit(1 - bit, rows), :] = got[...]


def gather_body(bit, cur, got, out):
    rows = cur.shape[0] - EDGE
    out[at_bit(bit, rows), :] = cur[:rows, :]
    out[at_bit(1 - bit, rows), :] = got[:rows, :]
    out[2 * rows :, :] = total(cur[rows:, :], got[rows:, :])


def pair_kernel(bodies, outs, *refs):
    n = len(bodies)
    bits, arrays, results = refs[:n], refs[n : 3 * n], refs[3 * n + 1 :]
    for i, body in enumerate(bodies):
        count = outs[i]
        body(bits[i][0], arrays[2 * i], arrays[2 * i + 1], *results[:count])
        results = results[count:]


def pair_call(works, after, cost):
    outs = [len(w[4]) for w in works]
    shapes = [x for w in works for x in w[4]]
    return pl.pallas_call(
        functools.partial(pair_kernel, [w[0] for w in works], outs),
        in_specs=[IN_SMEM] * len(works) + [IN_VMEM] * (2 * len(works)) + [ANYWHERE],
        out_specs=[IN_VMEM] * len(shapes),
        out_shape=shapes,
        compiler_params=pltpu.CompilerParams(vmem_limit_bytes=24 * 1024 * 1024),
        cost_estimate=cost,
        name=works[0][0].__name__,
    )(*[w[1] for w in works], *[x for w in works for x in w[2:4]], after)


def then_kernel(x_ref, after_ref, out_ref):
    pass


def then(x, after):
    return pl.pallas_call(
        then_kernel,
        in_specs=[ANYWHERE, ANYWHERE],
        out_specs=ANYWHERE,
        out_shape=jax.ShapeDtypeStruct(x.shape, x.dtype),
        input_output_aliases={0: 0},
        cost_estimate=SMALL,
        name="then",
    )(x, after)


def join_kernel(count, sec_ref, *refs):
    section = sec_ref[0]
    arrays, outs = refs[: 2 * count], refs[2 * count + 1 : 3 * count + 1]
    mark, sems = refs[-2:]
    mark[...] = jnp.zeros_like(mark)
    copies = []
    for i in range(count):
        rows = arrays[2 * i].shape[0]
        for j, place in enumerate((section, 1 - section)):
            copies.append(
                pltpu.make_async_copy(
                    arrays[2 * i + j], outs[i].at[at_bit(place, rows), :], sems.at[2 * i + j]
                )
            )
    for copy in copies:
        copy.start()
    for copy in copies:
        copy.wait()


def join(sec, after, *pairs):
    rows, width = pairs[0][0].shape
    count = len(pairs)
    return pl.pallas_call(
        functools.partial(join_kernel, count),
        in_specs=[IN_SMEM] + [IN_VMEM] * (2 * count) + [ANYWHERE],
        out_specs=[IN_HBM] * count + [IN_VMEM],
        out_shape=[struct(2 * rows, width)] * count + [struct(8, 128, F32)],
        scratch_shapes=[pltpu.SemaphoreType.DMA((2 * count,))],
        compiler_params=pltpu.CompilerParams(vmem_limit_bytes=16 * 1024 * 1024),
        cost_estimate=SMALL,
        name="join",
    )(sec, *[x for pair in pairs for x in pair], after)


def swap(x):
    return lax.ppermute(x, "section", [(0, 1), (1, 0)])


class Sum:
    def __init__(self, orders):
        self.chips = lax.axis_size("dp")
        self.section = lax.axis_index("section")
        self.chip = lax.axis_index("dp")
        self.orders = orders
        self.levels = len(orders[0])

    def bit_of(self, step, section):
        where = jnp.where(section == 0, self.orders[0][step], self.orders[1][step])
        return ((self.chip >> where) & 1).astype(jnp.int32)

    def bit(self, step):
        return self.bit_of(step, self.section).reshape(1)

    def send(self, x, step):
        chips = self.chips
        route = [
            (s * chips + d, s * chips + (d ^ (1 << self.orders[s][step])))
            for s in range(2)
            for d in range(chips)
        ]
        return lax.ppermute(x, ("section", "dp"), route)

    def runs(self):
        mine, theirs = self.section, 1 - self.section
        own, other = self.bit_of(0, mine), self.bit_of(0, theirs)
        return jnp.stack(
            [2 * mine + own, 2 * mine + 1 - own, 2 * theirs + other, 2 * theirs + 1 - other]
        ).astype(jnp.int32)


class Batch:
    def __init__(self, sums, keep, give):
        self.sums = sums
        self.held = keep
        self.got = swap(give)
        self.step = 0

    def turn(self, after, more=(), cost=LARGE):
        sums, last = self.sums, self.sums.levels - 1
        at = self.step
        self.step += 1
        rows, width = self.held.shape
        if at < last:
            work = (split_body, sums.bit(at), self.held, self.got, [struct(rows // 2, width)] * 2)
            self.held, give, *rest = pair_call([work, *more], after, cost)
            self.got = sums.send(give, at)
        elif at <= last + 1:
            work = (add_body, sums.bit(0), self.held, self.got, [struct(rows, width)])
            self.held, *rest = pair_call([work, *more], after, cost)
            self.got = sums.send(self.held, at if at == last else last - 1)
        else:
            back = 2 * last + 1 - at
            work = (merge_body, sums.bit(back), self.held, self.got, [struct(2 * rows, width)])
            self.held, *rest = pair_call([work, *more], after, cost)
            self.got = sums.send(self.held, back - 1)
        return (self.held, *rest)

    @property
    def turns(self):
        return 2 * self.sums.levels - 1

    def spread(self, kinds, first):
        runs = self.sums.runs()
        *outs, done = place(runs, (0, 2), (self.held, swap(self.held)), kinds, first)
        self.got = then(self.got, done)
        return place(runs, (1, 3), (self.got, swap(self.got)), kinds, done, outs)


def place_kernel(which, spots, runs, p0, p1, after_ref, *refs):
    count = len(set(spot[0] for spot in spots if spot is not None))
    outs, (mark, buf, sems) = refs[-3 - count : -3], refs[-3:]
    mark[...] = jnp.zeros_like(mark)
    rows = buf.shape[1]
    per_run = p0.shape[0] // rows
    for wait in (False, True):
        for run in range(4):
            mine, theirs = runs[which[0]] == run, runs[which[1]] == run
            base = run * per_run

            @pl.when(mine | theirs)
            def _(run=run, mine=mine):
                slot = jnp.where(mine, 0, 1)
                for w in range(run * per_run, (run + 1) * per_run):
                    spot = spots[w]
                    if spot is None:
                        continue
                    j = w - base
                    k, row, col = spot
                    copy = pltpu.make_async_copy(
                        buf.at[slot * per_run + j],
                        outs[k].at[pl.ds(row, rows), pl.ds(col, buf.shape[2])],
                        sems.at[slot * per_run + j],
                    )
                    if wait:
                        copy.wait()
                    else:
                        part = slice(j * rows, (j + 1) * rows)
                        value = jnp.where(mine, p0[part, :], p1[part, :])
                        buf[slot * per_run + j] = value.astype(F32)
                        copy.start()


def place(runs, which, pieces, kinds, after, outs=()):
    length, width = pieces[0].shape
    quarter = width // 4
    per_run = length // quarter
    spots, shapes = [None] * (4 * per_run), []
    first = 0
    for k, count in enumerate(kinds):
        across = min(count, 2)
        for i in range(count):
            for section in range(2):
                for u in range(2):
                    w = section * 2 * per_run + 2 * (first + i) + u
                    row = (i // across) * width + (2 * section + u) * quarter
                    spots[w] = (k, row, (i % across) * width)
        shapes.append(struct(width * max(count // 2, 1), across * width, F32))
        first += count
    return pl.pallas_call(
        functools.partial(place_kernel, which, spots),
        in_specs=[IN_SMEM] + [IN_VMEM] * 2 + [ANYWHERE] + [IN_HBM] * len(outs),
        out_specs=[IN_HBM] * len(kinds) + [IN_VMEM],
        out_shape=shapes + [struct(8, 128, F32)],
        input_output_aliases={4 + k: k for k in range(len(outs))},
        scratch_shapes=[
            pltpu.VMEM((2 * per_run, quarter, width), F32),
            pltpu.SemaphoreType.DMA((2 * per_run,)),
        ],
        compiler_params=pltpu.CompilerParams(vmem_limit_bytes=24 * 1024 * 1024),
        cost_estimate=SMALL,
        name="place",
    )(runs, *pieces, after, *outs)


def step_kernel(group, rows_ref, after_ref, out_ref, mark):
    mark[...] = jnp.zeros_like(mark)
    width = rows_ref.shape[1]
    rows = rows_ref[: rows_ref.shape[0] - EDGE, :].astype(F32).reshape(-1, 2 * group, width)
    emb = rows[:, :group].reshape(-1, width).astype(BF16)
    out_ref[...] = tn(emb, rows[:, group:].reshape(-1, width).astype(BF16))


def padded(x, rows):
    return x if x.shape[0] == rows else jnp.pad(x, ((0, rows - x.shape[0]), (0, 0)))


def on_device(
    input_rows,
    conditioning,
    prompt,
    buckets,
    item_len,
    step_index,
    output_gradient,
    grad_skip,
    step_w,
    conv_w,
    cond_w,
    conv_b,
    res_w,
    res_b,
    query_w,
    key_w,
    value_w,
    out_w,
    out_b,
):
    section = lax.axis_index("section")
    sec = section.astype(jnp.int32).reshape(1)
    total, width = input_rows.shape
    micro, slots = item_len.shape
    nq = prompt.shape[2]
    frames = total // micro
    tile = frames // slots
    own = total // 2
    tiles = own // tile
    subs = 2
    size = subs * tile
    grid = tiles // subs
    mb_own = -(-own // frames)
    items = mb_own * slots
    half = width // 2
    taps = conv_w.shape[0]
    per = size // EDGE
    last = total // EDGE - 1
    wide = 2 * width
    conv_flat = conv_w.reshape(taps * width, wide)
    flat_prompt = prompt.reshape(-1, width)
    head = width // HEADS
    mask = (
        jnp.arange(HEADS * nq)[:, None] // nq == jnp.arange(width)[None, :] // head
    ).astype(BF16)

    def whole(x):
        n = x.ndim
        return pl.BlockSpec(x.shape, lambda t, *_: (0,) * n, pipeline_mode=pl.Buffered(1))

    smem = pl.BlockSpec(memory_space=pltpu.SMEM)

    def chip_tile(cols):
        return pl.BlockSpec((size, cols), lambda t, s, *_: (s[0] * grid + t, 0))

    def own_tile(cols):
        return pl.BlockSpec((size, cols), lambda t, *_: (t, 0))

    def const(shape):
        return pl.BlockSpec(shape, lambda t, *_: (0,) * len(shape))

    prev_chip = pl.BlockSpec(
        (EDGE, width), lambda t, s, *_: (jnp.maximum((s[0] * grid + t) * per - 1, 0), 0)
    )
    next_chip = pl.BlockSpec(
        (EDGE, width), lambda t, s, *_: (jnp.minimum((s[0] * grid + t + 1) * per, last), 0)
    )
    vectors = [x.reshape(1, -1) for x in (conv_b, res_b, out_b)]
    weights = [
        step_w,
        conv_flat,
        cond_w,
        vectors[0],
        res_w,
        vectors[1],
        query_w,
        key_w,
        value_w,
        out_w,
        vectors[2],
    ]

    def shape(*dims, dtype=BF16):
        return jax.ShapeDtypeStruct(dims, dtype)

    macs = own * width * width * 25
    (
        stack,
        d_pre,
        d_sent,
        block_keep,
        block_give,
        skip_keep,
        skip_give,
        keep_a,
        give_a,
        vec,
        emb,
    ) = pl.pallas_call(
        functools.partial(forward_kernel, (tile, slots, nq, subs, tiles, mb_own, micro)),
        grid_spec=pltpu.PrefetchScalarGridSpec(
            num_scalar_prefetch=1,
            grid=(grid,),
            in_specs=[smem, smem, smem, prev_chip, chip_tile(width), next_chip]
            + [chip_tile(width)] * 3
            + [whole(flat_prompt), whole(mask)]
            + [whole(w) for w in weights],
            out_specs=[own_tile(taps * width), own_tile(wide), own_tile(width)]
            + [own_tile(half)] * 4
            + [const((7, half, width)), const((7, half, width)), const((16, width))]
            + [const((items, width))],
            scratch_shapes=[
                pltpu.VMEM((items, width), F32),
                pltpu.VMEM((items * nq, width), BF16),
                pltpu.VMEM((items * nq, width), BF16),
                pltpu.VMEM((items * nq, width), F32),
                pltpu.VMEM((items * nq, width), F32),
                pltpu.VMEM((width, wide), F32),
                pltpu.VMEM((width, wide), F32),
                pltpu.VMEM((width, width), F32),
                pltpu.VMEM((3, 8, wide), F32),
                pltpu.VMEM((3, 8, width), F32),
                pltpu.SMEM((1,), jnp.int32),
            ],
        ),
        out_shape=[
            shape(own, taps * width),
            shape(own, wide),
            shape(own, width),
            shape(own, half),
            shape(own, half),
            shape(own, half),
            shape(own, half),
            shape(7, half, width),
            shape(7, half, width),
            shape(16, width, dtype=F32),
            shape(items, width, dtype=F32),
        ],
        compiler_params=pltpu.CompilerParams(vmem_limit_bytes=VMEM),
        cost_estimate=LARGE,
        name="forward",
    )(
        sec,
        buckets,
        item_len,
        step_index,
        input_rows,
        input_rows,
        input_rows,
        conditioning,
        output_gradient,
        grad_skip,
        flat_prompt,
        mask,
        *weights,
    )

    edge = swap(jnp.concatenate([d_pre[:EDGE], d_pre[own - EDGE :]], axis=0))

    bits = list(range(lax.axis_size("dp").bit_length() - 1))
    other = [bits[1], bits[0]] + bits[2:]
    if len(other) > 3:
        other[-2], other[-1] = other[-1], other[-2]
    sums = Sum((bits, other))
    unit = 16 * lax.axis_size("dp") // 2

    film_blocks = 7
    rows_a = -(-film_blocks * half // unit) * unit
    batch_a = Batch(
        sums,
        padded(keep_a.reshape(-1, width), rows_a),
        padded(give_a.reshape(-1, width), rows_a),
    )
    conv_blocks = 2 * (taps + 1)
    pair = pl.BlockSpec((2, half, width), lambda i, *_: (i, 0, 0))
    keep_b, give_b = pl.pallas_call(
        functools.partial(weight_kernel, taps),
        grid_spec=pltpu.PrefetchScalarGridSpec(
            num_scalar_prefetch=1,
            grid=(taps + 1,),
            in_specs=[
                pl.BlockSpec((own, width), lambda i, s: (0, jnp.minimum(i, taps - 1))),
                pl.BlockSpec(
                    (own, width), lambda i, s: (s[0], 0), pipeline_mode=pl.Buffered(1)
                ),
                whole(d_pre),
            ],
            out_specs=[pair, pair],
            scratch_shapes=[pltpu.VMEM((width, wide), F32)],
        ),
        out_shape=[shape(conv_blocks, half, width)] * 2,
        compiler_params=pltpu.CompilerParams(vmem_limit_bytes=KB_VMEM),
        cost_estimate=LARGE,
        name="weights",
    )(sec, stack, conditioning, d_pre)

    rows_b = -(-conv_blocks * half // unit) * unit
    batch_b = Batch(
        sums,
        padded(keep_b.reshape(-1, width), rows_b),
        padded(give_b.reshape(-1, width), rows_b),
    )
    (after,) = batch_a.turn(keep_b)
    (after,) = batch_b.turn(after)

    rows_last = own // EDGE - 1
    in_keep, in_give, rows_now = pl.pallas_call(
        functools.partial(back_kernel, (tile, slots, subs, tiles, mb_own, micro)),
        grid_spec=pltpu.PrefetchScalarGridSpec(
            num_scalar_prefetch=1,
            grid=(grid,),
            in_specs=[
                smem,
                smem,
                pl.BlockSpec((EDGE, wide), lambda t, *_: (jnp.maximum(t * per - 1, 0), 0)),
                own_tile(wide),
                pl.BlockSpec(
                    (EDGE, wide), lambda t, *_: (jnp.minimum((t + 1) * per, rows_last), 0)
                ),
                whole(edge),
                own_tile(width),
                whole(conv_flat),
                whole(emb),
                whole(vec),
                ANYWHERE,
            ],
            out_specs=[own_tile(half), own_tile(half), const((2 * items + EDGE, width))],
            scratch_shapes=[pltpu.VMEM((items, width), F32)],
        ),
        out_shape=[shape(own, half), shape(own, half), shape(2 * items + EDGE, width)],
        compiler_params=pltpu.CompilerParams(vmem_limit_bytes=KC_VMEM),
        cost_estimate=LARGE,
        name="back",
    )(
        sec,
        buckets,
        item_len,
        d_pre,
        d_pre,
        d_pre,
        edge,
        d_sent,
        conv_flat,
        emb,
        vec,
        after,
    )

    block_got, skip_got, in_got = swap(block_give), swap(skip_give), swap(in_give)
    gathers = sums.levels + 1
    rows_got, rows_bit = swap(rows_now), sec

    block_out, skip_out, after = join(
        sec, rows_now, (block_keep, block_got), (skip_keep, skip_got)
    )
    done = 0
    for name in "ab" * (batch_a.turns - 1):
        if name == "b" and done < gathers:
            n = 2 * rows_now.shape[0] - EDGE
            work = (gather_body, rows_bit, rows_now, rows_got, [struct(n, width)])
            after, rows_now = batch_b.turn(after, [work])
            if done < sums.levels:
                route = [(d, d ^ (1 << done)) for d in range(sums.chips)]
                rows_got = lax.ppermute(rows_now, "dp", route)
                rows_bit = ((sums.chip >> done) & 1).astype(jnp.int32).reshape(1)
            done += 1
        else:
            cost = LARGE if done else SMALL
            (after,) = (batch_a if name == "a" else batch_b).turn(after, cost=cost)

    in_grad, mark = join(sec, after, (in_keep, in_got))
    g_step, mark = pl.pallas_call(
        functools.partial(step_kernel, items),
        in_specs=[IN_VMEM, ANYWHERE],
        out_specs=[IN_VMEM, IN_VMEM],
        out_shape=[struct(width, width, F32), struct(8, 128, F32)],
        compiler_params=pltpu.CompilerParams(vmem_limit_bytes=24 * 1024 * 1024),
        cost_estimate=SMALL,
        name="step_grad",
    )(rows_now, mark)
    g_out, g_res, g_query, g_key, g_value, mark = batch_a.spread((2, 2, 1, 1, 1), mark)
    g_conv, g_cond, mark = batch_b.spread((2 * taps, 2), mark)
    vec = rows_now[rows_now.shape[0] - EDGE :].astype(F32)
    g_conv = g_conv.reshape(conv_w.shape)
    g_convb, g_resb, g_outb = (vec[2 * i : 2 * i + 2].reshape(wide) for i in range(3))
    sizes = jnp.sum(vec[6:9], axis=1)
    frames_valid = sum(vec[9, i] * (1 << 3 * i) for i in range(8))
    levels = jnp.sqrt(sizes / (frames_valid * width))
    return (
        block_out,
        skip_out,
        in_grad,
        g_step,
        g_conv,
        g_cond,
        g_convb,
        g_res,
        g_resb,
        g_query,
        g_key,
        g_value,
        g_out,
        g_outb,
        levels,
    )


def solution(mesh):
    rows = P("dp", None)
    split = P("dp", "section")
    return jax.shard_map(
        on_device,
        mesh=mesh,
        in_specs=(rows, rows, P("dp", None, None, None), P("dp"), rows, rows, rows, rows)
        + (P(),) * 11,
        out_specs=(split,) * 3 + (P(),) * 12,
        check_vma=False,
    )
```

time: 699 us -> 193 us (0.28); the launches traced: 690 us -> 193 us
  waiting for transfers between devices: 257 us -> 50.6 us
  matrix products: 123 us -> 0 us
  Pallas kernels: 0 us -> 84.3 us
  other arithmetic: 85.4 us -> 2.19 us
  loops' own time: 70.9 us -> 0 us
  blocking collectives: 44.9 us -> 0 us
  local copies, waits for them, and re-layouts: 59.8 us -> 17.4 us
  between operations: 15.4 us -> 6.21 us
    psum x1 -> x0, waiting for transfers between devices: 217 us -> none  [on_device(): lax.psum((g_step, g_conv, g_cond, g_convb, g_res, g_resb, g_query, g_key,...]
    dot_general x48 -> x0, matrix products: 123 us -> none  [the longest x9 38.9 us: outer(): jnp.einsum('fi,fo->io', left, right, preferred_element_type=jnp.float32)]
    pallas_call x0 -> x26, Pallas kernels: none -> 84.3 us  [the longest x1 37.1 us: on_device(): pl.pallas_call(functools.partial(forward_kernel, (tile, slots, nq, subs,...]
    another operation x8 -> x0, loops' own time: 70.9 us -> none  [the longest x4 42.9 us: on_device(): lax.switch(chosen, (conv_backward, film_backward, reserve_backward))]
    psum x1 -> x0, blocking collectives: 44.9 us -> none  [on_device(): lax.psum((g_step, g_conv, g_cond, g_convb, g_res, g_resb, g_query, g_key,...]
    add x10 -> x0, other arithmetic: 20.9 us -> none  [the longest x9 20.9 us: conv_backward(): jax.tree.map(jnp.add, acc_now[:6], grads)]
    another operation x14 -> x1, other arithmetic: 17.6 us -> 0.08 us  [runs(): jnp.stack([2 * mine + own, 2 * mine + 1 - own, 2 * theirs + other, 2 * th...]
    select_n x23 -> x2, other arithmetic: 17.2 us -> 0.01 us  [the longest x1 0.01 us: on_device(): jnp.arange(HEADS * nq)[:, None] // nq == jnp.arange(width)[None, :] // head]
  transfers between devices with their start and end apart: 9 -> 29, of which waited for: 4 -> 9; matrix products, arithmetic and copies ran while one was open for 14% -> 2% of each run, Pallas kernels for 0% -> 23%
where the time goes in v1:
time: 193 us
  Pallas kernels  84.3 us (44%)
  waiting for transfers between devices  50.6 us (26%)
  starting transfers between devices  31.8 us (16%)
  local copies, waits for them, and re-layouts  17.4 us (9%)
  between operations  6.21 us (3%)
  other arithmetic  2.19 us (1%)
    pallas_call x1, Pallas kernels, on_device(): pl.pallas_call(functools.partial(forward_kernel, (tile, slots, nq, subs,...  37.1 us
    ppermute x14, waiting for transfers between devices, send(): return lax.ppermute(x, ('section', 'dp'), route)  34.8 us
    ppermute x14, starting transfers between devices, send(): return lax.ppermute(x, ('section', 'dp'), route)  20.1 us
    unnamed x56, local copies, waits for them, and re-layouts  16 us
    ppermute x4, waiting for transfers between devices, on_device(): rows_got = lax.ppermute(rows_now, 'dp', route)  13.1 us
    pallas_call x4, Pallas kernels, place(): pl.pallas_call(functools.partial(place_kernel, which, spots), in_specs=[I...  12.7 us
    pallas_call x1, Pallas kernels, on_device(): pl.pallas_call(functools.partial(weight_kernel, taps), grid_spec=pltpu.Pr...  11.4 us
    pallas_call x1, Pallas kernels, on_device(): pl.pallas_call(functools.partial(back_kernel, (tile, slots, subs, tiles,...  8.73 us
  transfers between devices with their start and end apart: 29, of which 9 were waited for; matrix products, arithmetic and copies ran while one was open for 2% of the time, Pallas kernels for 23%

profile of v1, /device:TPU:0, one launch (start us, length us, event | category | flops | bytes accessed | tf_op | source)
XLA Modules:
  0.0 192.6 jit_solution(14783184611107253782)
XLA Ops:
  1.5 37.1 %forward.1 = (bf16[1536,1536]{1,0:T(8,128)(2,1)}, bf16[1536,1024]{1,0:T(8,128)(2,1)}, bf16[1536,512]{1,0:T(8,128)(2,1)}, bf16[1536,256]{1,0:T(8,128)(2,1)}, bf16...) custom-call(s32[1]{0:T(128)} %bitcast.sec_ref.refs_1_, ...), custom_call_target="tpu_custom_call" | custom-call | flops 68719476736 | bytes 1024 | tf_op jit(solution)/shard_map/forward/pallas_call | solution.py:740
  41.0 11.4 %weights.1 = (bf16[8,256,512]{2,1,0:T(8,128)(2,1)S(1)}, bf16[8,256,512]{2,1,0:T(8,128)(2,1)}) custom-call(s32[1]{0:T(128)} %bitcast.sec_ref.refs_1_, bf16[1536,1536]{1,0:T(8,128)(2,1)} %get-tuple-element.83.stack_ref, bf16[3072,512]{1,0:T(8,128)(2,1)} %cond_ref.3, bf16[1536,1024]{1,0:T(8,128)(2,1)} %get-tuple-element.79.dpre_ref.prev_ref.next_ref), custom_call_target="tpu_custom_call" | custom-call | flops 68719476736 | bytes 1024 | tf_op jit(solution)/shard_map/weights/pallas_call | solution.py:817
  54.2 1.6 copy-done.19
  58.6 2.5 %collective-permute-start.8 = (bf16[896,512]{1,0:T(8,128)(2,1)}, bf16[896,512]{1,0:T(8,128)(2,1)S(1)}, u32[]{:S(2)}, u32[]{:S(2)}) collective-permute-start(bf16[896,512]{1,0:T(8,128)(2,1)} %get-tuple-element.96), channel_id=1, source_target_pairs={{0,1},{1,0},{2,3},{3,2},{4,5},{5,4},{6,7},{7,6},{8,9},{9,8},{10,11... | collective-permute-start | bytes 2752520 | tf_op jit(solution)/shard_map/ppermute | solution.py:515
  61.1 3.1 %split_body.7 = (bf16[1024,512]{1,0:T(8,128)(2,1)S(1)}, bf16[1024,512]{1,0:T(8,128)(2,1)}) custom-call(s32[1]{0:T(128)} %bitcast.6.refs_0_, bf16[2048,512]{1,0:T(8,128)(2,1)S(1)} %bitcast.32, bf16[2048,512]{1,0:T(8,128)(2,1)} %collective-permute-done.3.refs_2_, bf16[896,512]{1,0:T(8,128)(2,1)S(1)} %get-tuple-element.88.refs_3_.refs_1_), custom_call_target="tpu_custom_call" | custom-call | flops 68719476736 | bytes 1024 | tf_op jit(solution)/shard_map/split_body/pallas_call | solution.py:427
  64.4 8.7 %back.1 = (bf16[1536,256]{1,0:T(8,128)(2,1)S(1)}, bf16[1536,256]{1,0:T(8,128)(2,1)S(1)}, bf16[32,512]{1,0:T(8,128)(2,1)S(1)}) custom-call(s32[1]{0:T(128)} %bitcast.sec_ref.refs_1_, s32[3]{0:T(128)S(1)} %copy-done.17, s32[3,4]{1,0:T(4,128)S(1)} %copy-done.16, bf16[1536,1024]{1,0:T(8,128)(2,1)} %get-tuple-element.79.dpre_ref.prev_ref.next_ref, ...), custom_call_target="tpu_custom_call" | custom-call | flops 68719476736 | bytes 1024 | tf_op jit(solution)/shard_map/back/pallas_call | solution.py:848
  75.5 3.1 %join.2 = (bf16[3072,256]{1,0:T(8,128)(2,1)}, bf16[3072,256]{1,0:T(8,128)(2,1)}, f32[8,128]{1,0:T(8,128)S(1)}) custom-call(s32[1]{0:T(128)} %bitcast.sec_ref.refs_1_, bf16[1536,256]{1,0:T(8,128)(2,1)S(1)} %copy-done.6, bf16[1536,256]{1,0:T(8,128)(2,1)} %collective-permute-done.refs_1_, bf16[1536,256]{1,0:T(8,128)(2,1)S(1)} %copy-done.7, ...), custom_call_target="tpu_custom_call" | custom-call | flops 1024 | bytes 1024 | tf_op jit(solution)/shard_map/join/pallas_call | solution.py:477
  78.8 1.9 collective-permute-start.11
  80.7 5.4 %collective-permute-done.6.refs_3_ = bf16[1024,512]{1,0:T(8,128)(2,1)} collective-permute-done((bf16[1024,512]{1,0:T(8,128)(2,1)}, bf16[1024,512]{1,0:T(8,128)(2,1)}, u32[]{:S(2)}, u32[]{:S(2)}) %collective-permute-start.6) | collective-permute-done | bytes 1048608 | tf_op jit(solution)/shard_map/ppermute | solution.py:515
  87.6 2.5 %collective-permute-start.10 = (bf16[48,512]{1,0:T(8,128)(2,1)S(1)}, bf16[48,512]{1,0:T(8,128)(2,1)S(1)}, u32[]{:S(2)}, u32[]{:S(2)}) collective-permute-start(bf16[48,512]{1,0:T(8,128)(2,1)S(1)} %get-tuple-element.101.refs_4_), channel_id=1, source_target_pairs={{0,1},{1,0},{2,3},{3,2},{4,5},{5,4},{6,7},{7,6},{8,9},{9,8},{10,11... | collective-permute-start | bytes 147464 | tf_op jit(solution)/shard_map/ppermute | solution.py:905
  90.1 1.5 collective-permute-start.9
  91.8 1.6 collective-permute-start.14
  93.4 5.9 %collective-permute-done.9.refs_3_ = bf16[512,512]{1,0:T(8,128)(2,1)S(1)} collective-permute-done((bf16[512,512]{1,0:T(8,128)(2,1)S(1)}, bf16[512,512]{1,0:T(8,128)(2,1)S(1)}, u32[]{:S(2)}, u32[]{:S(2)}) %collective-permute-start.9) | collective-permute-done | bytes 524320 | tf_op jit(solution)/shard_map/ppermute | solution.py:515
  99.5 1.6 collective-permute-start.13
  101.0 1.6 collective-permute-start.12
  102.7 2.6 %collective-permute-start.17 = (bf16[224,512]{1,0:T(8,128)(2,1)S(1)}, bf16[224,512]{1,0:T(8,128)(2,1)S(1)}, u32[]{:S(2)}, u32[]{:S(2)}) collective-permute-start(bf16[224,512]{1,0:T(8,128)(2,1)S(1)} %add_body.4.refs_6_.refs_1_), channel_id=1, source_target_pairs={{0,8},{1,9},{2,10},{3,11},{4,12},{5,13},{6,14},{7,15},{8,0},{9,1},... | collective-permute-start | bytes 688136 | tf_op jit(solution)/shard_map/ppermute | solution.py:515
  105.3 9.1 %collective-permute-done.12.refs_3_ = bf16[256,512]{1,0:T(8,128)(2,1)S(1)} collective-permute-done((bf16[256,512]{1,0:T(8,128)(2,1)S(1)}, bf16[256,512]{1,0:T(8,128)(2,1)S(1)}, u32[]{:S(2)}, u32[]{:S(2)}) %collective-permute-start.12) | collective-permute-done | bytes 262176 | tf_op jit(solution)/shard_map/ppermute | solution.py:515
  114.6 3.2 %collective-permute-start.15 = (bf16[256,512]{1,0:T(8,128)(2,1)S(1)}, bf16[256,512]{1,0:T(8,128)(2,1)S(1)}, u32[]{:S(2)}, u32[]{:S(2)}) collective-permute-start(bf16[256,512]{1,0:T(8,128)(2,1)S(1)} %get-tuple-element.108.refs_3_.refs_2_), channel_id=1, source_target_pairs={{0,8},{1,9},{2,10},{3,11},{4,12},{5,13},{6,14},{7,15},{8,0},{9,1},... | collective-permute-start | bytes 786440 | tf_op jit(solution)/shard_map/ppermute | solution.py:515
  118.0 4.7 %collective-permute-done.16.refs_5_ = bf16[144,512]{1,0:T(8,128)(2,1)S(1)} collective-permute-done((bf16[144,512]{1,0:T(8,128)(2,1)S(1)}, bf16[144,512]{1,0:T(8,128)(2,1)S(1)}, u32[]{:S(2)}, u32[]{:S(2)}) %collective-permute-start.16) | collective-permute-done | bytes 147488 | tf_op jit(solution)/shard_map/ppermute | solution.py:905
  122.7 3.6 %collective-permute-done.15.refs_3_ = bf16[256,512]{1,0:T(8,128)(2,1)S(1)} collective-permute-done((bf16[256,512]{1,0:T(8,128)(2,1)S(1)}, bf16[256,512]{1,0:T(8,128)(2,1)S(1)}, u32[]{:S(2)}, u32[]{:S(2)}) %collective-permute-start.15) | collective-permute-done | bytes 262176 | tf_op jit(solution)/shard_map/ppermute | solution.py:515
  127.1 3.7 %collective-permute-start.19 = (bf16[272,512]{1,0:T(8,128)(2,1)S(1)}, bf16[272,512]{1,0:T(8,128)(2,1)S(1)}, u32[]{:S(2)}, u32[]{:S(2)}) collective-permute-start(bf16[272,512]{1,0:T(8,128)(2,1)S(1)} %get-tuple-element.111.refs_4_), channel_id=1, source_target_pairs={{0,8},{1,9},{2,10},{3,11},{4,12},{5,13},{6,14},{7,15},{8,0},{9,1},... | collective-permute-start | bytes 835592 | tf_op jit(solution)/shard_map/ppermute | solution.py:905
  131.4 2.6 %collective-permute-done.18.refs_3_ = bf16[256,512]{1,0:T(8,128)(2,1)S(1)} collective-permute-done((bf16[256,512]{1,0:T(8,128)(2,1)S(1)}, bf16[256,512]{1,0:T(8,128)(2,1)S(1)}, u32[]{:S(2)}, u32[]{:S(2)}) %collective-permute-start.18) | collective-permute-done | bytes 262176 | tf_op jit(solution)/shard_map/ppermute | solution.py:515
  133.9 8.4 %collective-permute-done.19.refs_5_ = bf16[272,512]{1,0:T(8,128)(2,1)S(1)} collective-permute-done((bf16[272,512]{1,0:T(8,128)(2,1)S(1)}, bf16[272,512]{1,0:T(8,128)(2,1)S(1)}, u32[]{:S(2)}, u32[]{:S(2)}) %collective-permute-start.19) | collective-permute-done | bytes 278560 | tf_op jit(solution)/shard_map/ppermute | solution.py:905
  143.9 1.6 collective-permute-start.26
  146.6 8.2 %collective-permute-done.21.refs_2_ = bf16[512,512]{1,0:T(8,128)(2,1)S(1)} collective-permute-done((bf16[512,512]{1,0:T(8,128)(2,1)S(1)}, bf16[512,512]{1,0:T(8,128)(2,1)S(1)}, u32[]{:S(2)}, u32[]{:S(2)}) %collective-permute-start.21) | collective-permute-done | bytes 524320 | tf_op jit(solution)/shard_map/ppermute | solution.py:515
  155.1 1.9 collective-permute-start.23
  158.2 2.3 %join.3 = (bf16[3072,256]{1,0:T(8,128)(2,1)}, f32[8,128]{1,0:T(8,128)S(1)}) custom-call(s32[1]{0:T(128)} %bitcast.sec_ref.refs_1_, bf16[1536,256]{1,0:T(8,128)(2,1)S(1)} %copy-done.5, bf16[1536,256]{1,0:T(8,128)(2,1)} %collective-permute-done.5.refs_1_, bf16[1024,512]{1,0:T(8,128)(2,1)S(1)} %merge_body.7.refs_2_.p0), custom_call_target="tpu_custom_call" | custom-call | flops 1024 | bytes 1024 | tf_op jit(solution)/shard_map/join/pallas_call | solution.py:477
  161.8 3.4 %place.4 = (f32[512,1024]{1,0:T(8,128)}, f32[512,1024]{1,0:T(8,128)}, f32[512,512]{1,0:T(8,128)}, f32[512,512]{1,0:T(8,128)}, f32[512,512]{1,0:T(8,128)}, /*index=5*/f32[8,128]{1,0:T(8,128)S(1)}) custom-call(s32[4]{0:T(128)S(1)} %pad_add_fusion.runs, bf16[896,512]{1,0:T(8,128)(2,1)} %merge_body.6.refs_3_.p0, bf16[896,512]{1,0:T(8,128)(2,1)} %collective-permute-done.26.p1, ...), custom_call_target="tpu_custom_call" | custom-call | flops 1024 | bytes 1024 | tf_op jit(solution)/shard_map/place/pallas_call | solution.py:613
  166.8 2.7 %collective-permute-done.27.p1 = bf16[896,512]{1,0:T(8,128)(2,1)S(1)} collective-permute-done((bf16[896,512]{1,0:T(8,128)(2,1)}, bf16[896,512]{1,0:T(8,128)(2,1)S(1)}, u32[]{:S(2)}, u32[]{:S(2)}) %collective-permute-start.27) | collective-permute-done | bytes 917536 | tf_op jit(solution)/shard_map/ppermute | solution.py:490
  172.0 2.5 %place.5 = (f32[512,1024]{1,0:T(8,128)}, f32[512,1024]{1,0:T(8,128)}, f32[512,512]{1,0:T(8,128)}, f32[512,512]{1,0:T(8,128)}, f32[512,512]{1,0:T(8,128)}, /*index=5*/f32[8,128]{1,0:T(8,128)S(1)}) custom-call(s32[4]{0:T(128)S(1)} %copy-done.13, ...), custom_call_target="tpu_custom_call", output_to_operand_aliasing={{0}: (4, {}), {1}: (5, {}), {2}: (6, {}), {3}: (7, {}), {4}... | custom-call | flops 1024 | bytes 1024 | tf_op jit(solution)/shard_map/place/pallas_call | solution.py:613
  174.5 3.4 %place.6 = (f32[1536,1024]{1,0:T(8,128)}, f32[512,1024]{1,0:T(8,128)}, f32[8,128]{1,0:T(8,128)S(1)}) custom-call(s32[4]{0:T(128)S(1)} %copy-done.13, bf16[1024,512]{1,0:T(8,128)(2,1)S(1)} %merge_body.7.refs_2_.p0, bf16[1024,512]{1,0:T(8,128)(2,1)} %collective-permute-done.24.p1, f32[8,128]{1,0:T(8,128)S(1)} %get-tuple-element.124.after_ref), custom_call_target="tpu_custom_call" | custom-call | flops 1024 | bytes 1024 | tf_op jit(solution)/shard_map/place/pallas_call | solution.py:613
  189.1 3.3 %place.7 = (f32[1536,1024]{1,0:T(8,128)}, f32[512,1024]{1,0:T(8,128)}, f32[8,128]{1,0:T(8,128)}) custom-call(s32[4]{0:T(128)S(1)} %copy-done.14, bf16[1024,512]{1,0:T(8,128)(2,1)S(1)} %copy-done.1, bf16[1024,512]{1,0:T(8,128)(2,1)S(1)} %collective-permute-done.28.p1, f32[8,128]{1,0:T(8,128)S(1)} %copy-done.9, ...), custom_call_target="tpu_custom_call", output_to_operand_aliasing={{0}: (4, {}), {1}: (5, {})} | custom-call | flops 1024 | bytes 1024 | tf_op jit(solution)/shard_map/place/pallas_call | solution.py:613
  (118 shorter events, 29.5 us)
Async XLA Ops:
  40.0 24.3 %collective-permute-start.2 = (bf16[32,1024]{1,0:T(8,128)(2,1)}, bf16[32,1024]{1,0:T(8,128)(2,1)}, u32[]{:S(2)}, u32[]{:S(2)}) collective-permute-start(bf16[32,1024]{1,0:T(8,128)(2,1)} %pad_maximum_fusion), channel_id=1, source_target_pairs={{0,16},{16,0},{1,17},{17,1},{2,18},{18,2},{3,19},{19,3},{4,20},{20... | collective-permute-start | bytes 196616 | tf_op jit(solution)/shard_map/ppermute | solution.py:490
  40.4 34.8 %collective-permute-start = (bf16[1536,256]{1,0:T(8,128)(2,1)}, bf16[1536,256]{1,0:T(8,128)(2,1)}, u32[]{:S(2)}, u32[]{:S(2)}) collective-permute-start(bf16[1536,256]{1,0:T(8,128)(2,1)} %get-tuple-element.76), channel_id=1, source_target_pairs={{0,16},{16,0},{1,17},{17,1},{2,18},{18,2},{3,19},{19,3},{4,20},{20... | collective-permute-start | bytes 2359304 | tf_op jit(solution)/shard_map/ppermute | solution.py:490
  40.5 34.9 %collective-permute-start.1 = (bf16[1536,256]{1,0:T(8,128)(2,1)}, bf16[1536,256]{1,0:T(8,128)(2,1)}, u32[]{:S(2)}, u32[]{:S(2)}) collective-permute-start(bf16[1536,256]{1,0:T(8,128)(2,1)} %get-tuple-element.78), channel_id=1, source_target_pairs={{0,16},{16,0},{1,17},{17,1},{2,18},{18,2},{3,19},{19,3},{4,20},{20... | collective-permute-start | bytes 2359304 | tf_op jit(solution)/shard_map/ppermute | solution.py:490
  40.9 13.3 %collective-permute-start.4 = (bf16[1792,512]{1,0:T(8,128)(2,1)}, bf16[1792,512]{1,0:T(8,128)(2,1)S(1)}, u32[]{:S(2)}, u32[]{:S(2)}) collective-permute-start(bf16[1792,512]{1,0:T(8,128)(2,1)} %bitcast.40), channel_id=1, source_target_pairs={{0,16},{16,0},{1,17},{17,1},{2,18},{18,2},{3,19},{19,3},{4,20},{20... | collective-permute-start | bytes 5505032 | tf_op jit(solution)/shard_map/ppermute | solution.py:490
  53.8 7.3 %collective-permute-start.3 = (bf16[2048,512]{1,0:T(8,128)(2,1)}, bf16[2048,512]{1,0:T(8,128)(2,1)}, u32[]{:S(2)}, u32[]{:S(2)}) collective-permute-start(bf16[2048,512]{1,0:T(8,128)(2,1)} %bitcast.8), channel_id=1, source_target_pairs={{0,16},{16,0},{1,17},{17,1},{2,18},{18,2},{3,19},{19,3},{4,20},{20... | collective-permute-start | bytes 6291464 | tf_op jit(solution)/shard_map/ppermute | solution.py:490
  58.6 20.0 %collective-permute-start.8 = (bf16[896,512]{1,0:T(8,128)(2,1)}, bf16[896,512]{1,0:T(8,128)(2,1)S(1)}, u32[]{:S(2)}, u32[]{:S(2)}) collective-permute-start(bf16[896,512]{1,0:T(8,128)(2,1)} %get-tuple-element.96), channel_id=1, source_target_pairs={{0,1},{1,0},{2,3},{3,2},{4,5},{5,4},{6,7},{7,6},{8,9},{9,8},{10,11... | collective-permute-start | bytes 2752520 | tf_op jit(solution)/shard_map/ppermute | solution.py:515
  64.2 21.9 %collective-permute-start.6 = (bf16[1024,512]{1,0:T(8,128)(2,1)}, bf16[1024,512]{1,0:T(8,128)(2,1)}, u32[]{:S(2)}, u32[]{:S(2)}) collective-permute-start(bf16[1024,512]{1,0:T(8,128)(2,1)} %get-tuple-element.95), channel_id=1, source_target_pairs={{0,1},{1,0},{2,3},{3,2},{4,5},{5,4},{6,7},{7,6},{8,9},{9,8},{10,11... | collective-permute-start | bytes 3145736 | tf_op jit(solution)/shard_map/ppermute | solution.py:515
  64.4 11.1 %copy-start.6 = (bf16[1536,256]{1,0:T(8,128)(2,1)S(1)}, bf16[1536,256]{1,0:T(8,128)(2,1)}, u32[]{:S(2)}) copy-start(bf16[1536,256]{1,0:T(8,128)(2,1)} %get-tuple-element.75.refs_0_) | copy-start | bytes 2359300
  64.4 11.0 %copy-start.7 = (bf16[1536,256]{1,0:T(8,128)(2,1)S(1)}, bf16[1536,256]{1,0:T(8,128)(2,1)}, u32[]{:S(2)}) copy-start(bf16[1536,256]{1,0:T(8,128)(2,1)} %get-tuple-element.77.refs_2_) | copy-start | bytes 2359300
  74.9 5.8 %collective-permute-start.7 = (bf16[32,512]{1,0:T(8,128)(2,1)S(1)}, bf16[32,512]{1,0:T(8,128)(2,1)S(1)}, u32[]{:S(2)}, u32[]{:S(2)}) collective-permute-start(bf16[32,512]{1,0:T(8,128)(2,1)S(1)} %get-tuple-element.90.refs_4_), channel_id=1, source_target_pairs={{0,16},{16,0},{1,17},{17,1},{2,18},{18,2},{3,19},{19,3},{4,20},{20... | collective-permute-start | bytes 98312 | tf_op jit(solution)/shard_map/ppermute | solution.py:490
  75.2 81.9 %collective-permute-start.5 = (bf16[1536,256]{1,0:T(8,128)(2,1)}, bf16[1536,256]{1,0:T(8,128)(2,1)}, u32[]{:S(2)}, u32[]{:S(2)}) collective-permute-start(bf16[1536,256]{1,0:T(8,128)(2,1)} %copy-done.15), channel_id=1, source_target_pairs={{0,16},{16,0},{1,17},{17,1},{2,18},{18,2},{3,19},{19,3},{4,20},{20... | collective-permute-start | bytes 2359304 | tf_op jit(solution)/shard_map/ppermute | solution.py:490
  78.8 12.8 %collective-permute-start.11 = (bf16[448,512]{1,0:T(8,128)(2,1)S(1)}, bf16[448,512]{1,0:T(8,128)(2,1)S(1)}, u32[]{:S(2)}, u32[]{:S(2)}) collective-permute-start(bf16[448,512]{1,0:T(8,128)(2,1)S(1)} %get-tuple-element.102), channel_id=1, source_target_pairs={{0,2},{1,3},{2,0},{3,1},{4,6},{5,7},{6,4},{7,5},{8,10},{9,11},{10,... | collective-permute-start | bytes 1376264 | tf_op jit(solution)/shard_map/ppermute | solution.py:515
  87.6 5.8 %collective-permute-start.10 = (bf16[48,512]{1,0:T(8,128)(2,1)S(1)}, bf16[48,512]{1,0:T(8,128)(2,1)S(1)}, u32[]{:S(2)}, u32[]{:S(2)}) collective-permute-start(bf16[48,512]{1,0:T(8,128)(2,1)S(1)} %get-tuple-element.101.refs_4_), channel_id=1, source_target_pairs={{0,1},{1,0},{2,3},{3,2},{4,5},{5,4},{6,7},{7,6},{8,9},{9,8},{10,11... | collective-permute-start | bytes 147464 | tf_op jit(solution)/shard_map/ppermute | solution.py:905
  90.1 9.2 %collective-permute-start.9 = (bf16[512,512]{1,0:T(8,128)(2,1)S(1)}, bf16[512,512]{1,0:T(8,128)(2,1)S(1)}, u32[]{:S(2)}, u32[]{:S(2)}) collective-permute-start(bf16[512,512]{1,0:T(8,128)(2,1)S(1)} %get-tuple-element.100), channel_id=1, source_target_pairs={{0,2},{1,3},{2,0},{3,1},{4,6},{5,7},{6,4},{7,5},{8,10},{9,11},{10,... | collective-permute-start | bytes 1572872 | tf_op jit(solution)/shard_map/ppermute | solution.py:515
  91.8 10.8 %collective-permute-start.14 = (bf16[224,512]{1,0:T(8,128)(2,1)S(1)}, bf16[224,512]{1,0:T(8,128)(2,1)S(1)}, u32[]{:S(2)}, u32[]{:S(2)}) collective-permute-start(bf16[224,512]{1,0:T(8,128)(2,1)S(1)} %get-tuple-element.107), channel_id=1, source_target_pairs={{0,4},{1,5},{2,6},{3,7},{4,0},{5,1},{6,2},{7,3},{8,12},{9,13},{10,... | collective-permute-start | bytes 688136 | tf_op jit(solution)/shard_map/ppermute | solution.py:515
  99.5 5.9 %collective-permute-start.13 = (bf16[80,512]{1,0:T(8,128)(2,1)S(1)}, bf16[80,512]{1,0:T(8,128)(2,1)S(1)}, u32[]{:S(2)}, u32[]{:S(2)}) collective-permute-start(bf16[80,512]{1,0:T(8,128)(2,1)S(1)} %get-tuple-element.106.refs_4_), channel_id=1, source_target_pairs={{0,2},{1,3},{2,0},{3,1},{4,6},{5,7},{6,4},{7,5},{8,10},{9,11},{10,... | collective-permute-start | bytes 245768 | tf_op jit(solution)/shard_map/ppermute | solution.py:905
  101.0 13.4 %collective-permute-start.12 = (bf16[256,512]{1,0:T(8,128)(2,1)S(1)}, bf16[256,512]{1,0:T(8,128)(2,1)S(1)}, u32[]{:S(2)}, u32[]{:S(2)}) collective-permute-start(bf16[256,512]{1,0:T(8,128)(2,1)S(1)} %get-tuple-element.105), channel_id=1, source_target_pairs={{0,4},{1,5},{2,6},{3,7},{4,0},{5,1},{6,2},{7,3},{8,12},{9,13},{10,... | collective-permute-start | bytes 786440 | tf_op jit(solution)/shard_map/ppermute | solution.py:515
  102.7 15.1 %collective-permute-start.17 = (bf16[224,512]{1,0:T(8,128)(2,1)S(1)}, bf16[224,512]{1,0:T(8,128)(2,1)S(1)}, u32[]{:S(2)}, u32[]{:S(2)}) collective-permute-start(bf16[224,512]{1,0:T(8,128)(2,1)S(1)} %add_body.4.refs_6_.refs_1_), channel_id=1, source_target_pairs={{0,8},{1,9},{2,10},{3,11},{4,12},{5,13},{6,14},{7,15},{8,0},{9,1},... | collective-permute-start | bytes 688136 | tf_op jit(solution)/shard_map/ppermute | solution.py:515
  114.5 8.2 %collective-permute-start.16 = (bf16[144,512]{1,0:T(8,128)(2,1)S(1)}, bf16[144,512]{1,0:T(8,128)(2,1)S(1)}, u32[]{:S(2)}, u32[]{:S(2)}) collective-permute-start(bf16[144,512]{1,0:T(8,128)(2,1)S(1)} %get-tuple-element.109.refs_4_), channel_id=1, source_target_pairs={{0,4},{1,5},{2,6},{3,7},{4,0},{5,1},{6,2},{7,3},{8,12},{9,13},{10,... | collective-permute-start | bytes 442376 | tf_op jit(solution)/shard_map/ppermute | solution.py:905
  114.6 11.7 %collective-permute-start.15 = (bf16[256,512]{1,0:T(8,128)(2,1)S(1)}, bf16[256,512]{1,0:T(8,128)(2,1)S(1)}, u32[]{:S(2)}, u32[]{:S(2)}) collective-permute-start(bf16[256,512]{1,0:T(8,128)(2,1)S(1)} %get-tuple-element.108.refs_3_.refs_2_), channel_id=1, source_target_pairs={{0,8},{1,9},{2,10},{3,11},{4,12},{5,13},{6,14},{7,15},{8,0},{9,1},... | collective-permute-start | bytes 786440 | tf_op jit(solution)/shard_map/ppermute | solution.py:515
  117.9 13.0 %collective-permute-start.20 = (bf16[224,512]{1,0:T(8,128)(2,1)S(1)}, bf16[224,512]{1,0:T(8,128)(2,1)S(1)}, u32[]{:S(2)}, u32[]{:S(2)}) collective-permute-start(bf16[224,512]{1,0:T(8,128)(2,1)S(1)} %add_body.6.refs_6_.refs_1_), channel_id=1, source_target_pairs={{0,4},{1,5},{2,6},{3,7},{4,0},{5,1},{6,2},{7,3},{8,12},{9,13},{10,... | collective-permute-start | bytes 688136 | tf_op jit(solution)/shard_map/ppermute | solution.py:515
  126.4 7.5 %collective-permute-start.18 = (bf16[256,512]{1,0:T(8,128)(2,1)S(1)}, bf16[256,512]{1,0:T(8,128)(2,1)S(1)}, u32[]{:S(2)}, u32[]{:S(2)}) collective-permute-start(bf16[256,512]{1,0:T(8,128)(2,1)S(1)} %get-tuple-element.110.refs_3_.refs_2_), channel_id=1, source_target_pairs={{0,4},{1,5},{2,6},{3,7},{4,0},{5,1},{6,2},{7,3},{8,12},{9,13},{10,... | collective-permute-start | bytes 786440 | tf_op jit(solution)/shard_map/ppermute | solution.py:515
  127.1 15.2 %collective-permute-start.19 = (bf16[272,512]{1,0:T(8,128)(2,1)S(1)}, bf16[272,512]{1,0:T(8,128)(2,1)S(1)}, u32[]{:S(2)}, u32[]{:S(2)}) collective-permute-start(bf16[272,512]{1,0:T(8,128)(2,1)S(1)} %get-tuple-element.111.refs_4_), channel_id=1, source_target_pairs={{0,8},{1,9},{2,10},{3,11},{4,12},{5,13},{6,14},{7,15},{8,0},{9,1},... | collective-permute-start | bytes 835592 | tf_op jit(solution)/shard_map/ppermute | solution.py:905
  130.8 12.1 %collective-permute-start.22 = (bf16[448,512]{1,0:T(8,128)(2,1)S(1)}, bf16[448,512]{1,0:T(8,128)(2,1)S(1)}, u32[]{:S(2)}, u32[]{:S(2)}) collective-permute-start(bf16[448,512]{1,0:T(8,128)(2,1)S(1)} %merge_body.4.refs_6_.refs_1_), channel_id=1, source_target_pairs={{0,2},{1,3},{2,0},{3,1},{4,6},{5,7},{6,4},{7,5},{8,10},{9,11},{10,... | collective-permute-start | bytes 1376264 | tf_op jit(solution)/shard_map/ppermute | solution.py:515
  142.4 12.5 %collective-permute-start.21 = (bf16[512,512]{1,0:T(8,128)(2,1)S(1)}, bf16[512,512]{1,0:T(8,128)(2,1)S(1)}, u32[]{:S(2)}, u32[]{:S(2)}) collective-permute-start(bf16[512,512]{1,0:T(8,128)(2,1)S(1)} %get-tuple-element.112.refs_3_.refs_1_), channel_id=1, source_target_pairs={{0,2},{1,3},{2,0},{3,1},{4,6},{5,7},{6,4},{7,5},{8,10},{9,11},{10,... | collective-permute-start | bytes 1572872 | tf_op jit(solution)/shard_map/ppermute | solution.py:515
  143.9 17.9 %collective-permute-start.26 = (bf16[896,512]{1,0:T(8,128)(2,1)}, bf16[896,512]{1,0:T(8,128)(2,1)}, u32[]{:S(2)}, u32[]{:S(2)}) collective-permute-start(bf16[896,512]{1,0:T(8,128)(2,1)} %merge_body.6.refs_3_.p0), channel_id=1, source_target_pairs={{0,16},{16,0},{1,17},{17,1},{2,18},{18,2},{3,19},{19,3},{4,20},{20... | collective-permute-start | bytes 2752520 | tf_op jit(solution)/shard_map/ppermute | solution.py:490
  145.5 20.3 %collective-permute-start.25 = (bf16[896,512]{1,0:T(8,128)(2,1)}, bf16[896,512]{1,0:T(8,128)(2,1)S(1)}, u32[]{:S(2)}, u32[]{:S(2)}) collective-permute-start(bf16[896,512]{1,0:T(8,128)(2,1)} %merge_body.6.refs_3_.p0), channel_id=1, source_target_pairs={{0,1},{1,0},{2,3},{3,2},{4,5},{5,4},{6,7},{7,6},{8,9},{9,8},{10,11... | collective-permute-start | bytes 2752520 | tf_op jit(solution)/shard_map/ppermute | solution.py:515
  154.9 19.6 %collective-permute-start.24 = (bf16[1024,512]{1,0:T(8,128)(2,1)S(1)}, bf16[1024,512]{1,0:T(8,128)(2,1)}, u32[]{:S(2)}, u32[]{:S(2)}) collective-permute-start(bf16[1024,512]{1,0:T(8,128)(2,1)S(1)} %merge_body.7.refs_2_.p0), channel_id=1, source_target_pairs={{0,16},{16,0},{1,17},{17,1},{2,18},{18,2},{3,19},{19,3},{4,20},{20... | collective-permute-start | bytes 3145736 | tf_op jit(solution)/shard_map/ppermute | solution.py:490
  155.1 23.4 %collective-permute-start.23 = (bf16[1024,512]{1,0:T(8,128)(2,1)S(1)}, bf16[1024,512]{1,0:T(8,128)(2,1)S(1)}, u32[]{:S(2)}, u32[]{:S(2)}) collective-permute-start(bf16[1024,512]{1,0:T(8,128)(2,1)S(1)} %merge_body.7.refs_2_.p0), channel_id=1, source_target_pairs={{0,1},{1,0},{2,3},{3,2},{4,5},{5,4},{6,7},{7,6},{8,9},{9,8},{10,11... | collective-permute-start | bytes 3145736 | tf_op jit(solution)/shard_map/ppermute | solution.py:515
  166.8 2.7 %collective-permute-start.27 = (bf16[896,512]{1,0:T(8,128)(2,1)}, bf16[896,512]{1,0:T(8,128)(2,1)S(1)}, u32[]{:S(2)}, u32[]{:S(2)}) collective-permute-start(bf16[896,512]{1,0:T(8,128)(2,1)} %then.2.p0), channel_id=1, source_target_pairs={{0,16},{16,0},{1,17},{17,1},{2,18},{18,2},{3,19},{19,3},{4,20},{20... | collective-permute-start | bytes 2752520 | tf_op jit(solution)/shard_map/ppermute | solution.py:490
  174.5 13.4 %copy-start.14 = (s32[4]{0:T(128)S(1)}, s32[4]{0:T(128)}, u32[]{:S(2)}) copy-start(s32[4]{0:T(128)} %copy-done.12) | copy-start | bytes 52
  179.5 8.3 %collective-permute-start.28 = (bf16[1024,512]{1,0:T(8,128)(2,1)}, bf16[1024,512]{1,0:T(8,128)(2,1)S(1)}, u32[]{:S(2)}, u32[]{:S(2)}) collective-permute-start(bf16[1024,512]{1,0:T(8,128)(2,1)} %then.3.p0), channel_id=1, source_target_pairs={{0,16},{16,0},{1,17},{17,1},{2,18},{18,2},{3,19},{19,3},{4,20},{20... | collective-permute-start | bytes 3145736 | tf_op jit(solution)/shard_map/ppermute | solution.py:490
  (23 other events, 67.6 us)

commit v2 on v1

--- a/solution.py
+++ b/solution.py
@@ -61,7 +61,6 @@
     next_ref,
     cond_ref,
     gout_ref,
-    gskip_ref,
     prompt_ref,
     mask_ref,
     step_w,
@@ -76,7 +75,8 @@
     out_w,
     out_b,
     o_stack,
-    o_dpre,
+    o_slope,
+    o_gate,
     o_dsent,
     o_block_keep,
     o_block_give,
@@ -92,11 +92,12 @@
     d_keys,
     d_values,
     g_out,
-    g_res,
     g_query,
     sums,
     stats,
     count,
+    out_t,
+    query_t,
 ):
     tile, slots, nq, subs, tiles, mb_own, micro = cfg
     t = pl.program_id(0)
@@ -128,7 +129,8 @@
         d_keys[...] = jnp.zeros_like(d_keys)
         d_values[...] = jnp.zeros_like(d_values)
         g_out[...] = jnp.zeros_like(g_out)
-        g_res[...] = jnp.zeros_like(g_res)
+        out_t[...] = out_w[...].T
+        query_t[...] = query_w[...].T
         g_query[...] = jnp.zeros_like(g_query)
         sums[...] = jnp.zeros_like(sums)
         stats[...] = jnp.zeros_like(stats)
@@ -168,8 +170,10 @@
     s = 0.5 * jnp.tanh(0.5 * pre[:, width:]) + 0.5
     both = a * s
     gate = both.astype(BF16)
-    slope_a = s - both * a
-    slope_s = both - both * s
+    o_gate[...] = gate
+    o_slope[...] = jnp.concatenate(
+        [(s - both * a).astype(BF16), (both - both * s).astype(BF16)], axis=1
+    )
     branch = nn(gate, res_w[...]) + res_b[...]
     res_part = jnp.where(valid, branch[:, :width], 0.0)
     skip = jnp.where(valid, branch[:, width:], 0.0).astype(BF16)
@@ -203,9 +207,9 @@
 
     gy = jnp.where(valid, gout_ref[...].astype(F32), 0.0)
     d_film = jnp.concatenate([(gy * sent_f).astype(BF16), gy.astype(BF16)], axis=1)
-    sums[2] += col_sums(d_film.astype(F32))
+    sums[...] += col_sums(d_film.astype(F32))
     g_out[...] += tn(attended, d_film)
-    d_att = nt(d_film, out_w[...]).astype(BF16)
+    d_att = nn(d_film, out_t[...]).astype(BF16)
     low_lane = lax.broadcasted_iota(jnp.int32, (nq, 2 * head), 1) < head
 
     def own_heads(x):
@@ -229,20 +233,8 @@
         d_query.append(tn(d_scores, key_bd[k]).astype(BF16))
     d_query = jnp.concatenate(d_query, axis=0)
     g_query[...] += tn(sent, d_query)
-    d_sent = (gy * (1.0 + scale) + nt(d_query, query_w[...])).astype(BF16)
+    d_sent = (gy * (1.0 + scale) + nn(d_query, query_t[...])).astype(BF16)
     o_dsent[...] = d_sent
-
-    d_res = jnp.where(valid, d_sent.astype(F32) * ISQ2, 0.0).astype(BF16)
-    gs = jnp.where(valid, gskip_ref[...].astype(F32), 0.0).astype(BF16)
-    d_branch = jnp.concatenate([d_res, gs], axis=1)
-    sums[1] += col_sums(d_branch.astype(F32))
-    g_res[...] += tn(gate, d_branch)
-    d_gate = nt(d_branch, res_w[...])
-    d_pre = jnp.concatenate(
-        [(d_gate * slope_a).astype(BF16), (d_gate * slope_s).astype(BF16)], axis=1
-    )
-    sums[0] += col_sums(d_pre.astype(F32))
-    o_dpre[...] = d_pre
 
     @pl.when(t == tiles // subs - 1)
     def _():
@@ -257,17 +249,15 @@
 
         put(0, g_out, 0)
         put(1, g_out, width)
-        put(2, g_res, 0)
-        put(3, g_res, width)
+        put(2, g_query, 0)
+        g_query[...] = tn(here, (d_keys[...] * factor).astype(BF16))
+        put(3, g_query, 0)
+        g_query[...] = tn(here, d_values[...].astype(BF16))
         put(4, g_query, 0)
-        g_query[...] = tn(here, (d_keys[...] * factor).astype(BF16))
-        put(5, g_query, 0)
-        g_query[...] = tn(here, d_values[...].astype(BF16))
-        put(6, g_query, 0)
-        for i in range(3):
-            line = jnp.sum(sums[i], axis=0, keepdims=True)
-            o_vec[2 * i : 2 * i + 1, :] = line[:, :width]
-            o_vec[2 * i + 1 : 2 * i + 2, :] = line[:, width:]
+        o_vec[0:4, :] = jnp.zeros((4, width), F32)
+        line = jnp.sum(sums[...], axis=0, keepdims=True)
+        o_vec[4:5, :] = line[:, :width]
+        o_vec[5:6, :] = line[:, width:]
         for i in range(3):
             o_vec[6 + i : 7 + i, :] = jnp.sum(stats[i], axis=0, keepdims=True)
         lane = lax.broadcasted_iota(jnp.int32, (16 - 9, width), 1)
@@ -275,21 +265,83 @@
         o_vec[9:16, :] = jnp.where(lane < 8, digits, 0).astype(F32)
 
 
-def weight_kernel(cfg, sec_ref, stack_ref, cond_ref, dpre_ref, o_keep, o_give, acc):
-    taps = cfg
-    i = pl.program_id(0)
+def branch_kernel(
+    cfg,
+    sec_ref,
+    buckets,
+    item_len,
+    gskip_ref,
+    dsent_ref,
+    slope_ref,
+    gate_ref,
+    res_w,
+    o_dpre,
+    o_edge,
+    o_vec,
+    o_keep,
+    o_give,
+    g_res,
+    res_t,
+    sums,
+):
+    tile, slots, subs, tiles = cfg
+    t = pl.program_id(0)
+    section = sec_ref[0]
+    size = subs * tile
+    width = dsent_ref.shape[1]
+    half = width // 2
+    last = tiles // subs - 1
+
+    @pl.when(t == 0)
+    def _():
+        res_t[...] = res_w[...].T
+        g_res[...] = jnp.zeros_like(g_res)
+        sums[...] = jnp.zeros_like(sums)
+
+    row = rows_iota(size, width)
+    limit = jnp.zeros((size, width), jnp.int32)
+    for k in range(subs):
+        lim = plan(section * tiles + t * subs + k, tile, slots, buckets, item_len)[2]
+        limit = jnp.where(row >= k * tile, lim + k * tile, limit)
+    d_res = (dsent_ref[...].astype(F32) * ISQ2).astype(BF16)
+    gs = jnp.where(row < limit, gskip_ref[...].astype(F32), 0.0).astype(BF16)
+    d_branch = jnp.concatenate([d_res, gs], axis=1)
+    sums[1] += col_sums(d_branch.astype(F32))
+    g_res[...] += tn(gate_ref[...], d_branch)
+    d_gate = nn(d_branch, res_t[...])
+    slope = slope_ref[...].astype(F32)
+    d_pre = jnp.concatenate(
+        [(d_gate * slope[:, :width]).astype(BF16), (d_gate * slope[:, width:]).astype(BF16)],
+        axis=1,
+    )
+    sums[0] += col_sums(d_pre.astype(F32))
+    o_dpre[...] = d_pre
+
+    @pl.when(t == 0)
+    def _():
+        o_edge[:EDGE, :] = d_pre[:EDGE, :]
+
+    @pl.when(t == last)
+    def _():
+        o_edge[EDGE:, :] = d_pre[size - EDGE :, :]
+        mine = pl.multiple_of(section * half, half)
+        theirs = pl.multiple_of(half - section * half, half)
+        for side in range(2):
+            o_keep[side] = g_res[pl.ds(mine, half), pl.ds(side * width, width)].astype(BF16)
+            o_give[side] = g_res[pl.ds(theirs, half), pl.ds(side * width, width)].astype(BF16)
+        for i in range(2):
+            line = jnp.sum(sums[i], axis=0, keepdims=True)
+            o_vec[2 * i : 2 * i + 1, :] = line[:, :width]
+            o_vec[2 * i + 1 : 2 * i + 2, :] = line[:, width:]
+        o_vec[4:16, :] = jnp.zeros((12, width), F32)
+
+
+def weight_kernel(sec_ref, left_ref, dpre_ref, *refs):
+    o_keep, o_give, acc = refs[-3:]
     section = sec_ref[0]
     width = acc.shape[0]
     half = width // 2
-
-    @pl.when(i < taps)
-    def _():
-        acc[...] = tn(stack_ref[...], dpre_ref[...])
-
-    @pl.when(i == taps)
-    def _():
-        acc[...] = tn(cond_ref[...], dpre_ref[...])
-
+    acc[...] = tn(left_ref[...], dpre_ref[...])
     mine = pl.multiple_of(section * half, half)
     theirs = pl.multiple_of(half - section * half, half)
     for side in range(2):
@@ -302,68 +354,77 @@
     sec_ref,
     buckets,
     item_len,
-    prev_ref,
     dpre_ref,
-    next_ref,
     other_ref,
     dsent_ref,
     conv_w,
-    emb_ref,
+    steps,
     vec_ref,
+    vec_more,
     after_ref,
     o_keep,
     o_give,
     o_rows,
+    acc,
     d_step,
 ):
-    tile, slots, subs, tiles, mb_own, micro = cfg
-    t = pl.program_id(0)
+    tile, slots, tiles, micro = cfg
+    tap = pl.program_id(0)
     section = sec_ref[0]
-    size = subs * tile
     width = dsent_ref.shape[1]
     half = width // 2
-    mb0 = section * (micro - mb_own)
-
-    @pl.when(t == 0)
+    plans = [plan(section * tiles + k, tile, slots, buckets, item_len) for k in range(tiles)]
+    spread = tile + 2 * EDGE
+
+    def moved(offset):
+        place = rows_iota(spread, 2 * width)
+        pieces = []
+        for k in range(tiles):
+            lo = jnp.where(plans[k][3], 0, EDGE)
+            hi = jnp.where(plans[k][4], spread, tile + EDGE)
+            before = dpre_ref[k * tile - EDGE : k * tile, :] if k else other_ref[EDGE:, :]
+            here = dpre_ref[k * tile : (k + 1) * tile, :]
+            end = (k + 1) * tile
+            after = dpre_ref[end : end + EDGE, :] if k < tiles - 1 else other_ref[:EDGE, :]
+            part = jnp.concatenate([before, here, after], axis=0).astype(F32)
+            part = jnp.where((place >= lo) & (place < hi), part, 0.0)
+            part = pltpu.roll(part, (spread - offset) % spread, 0)
+            pieces.append(part[EDGE : EDGE + tile].astype(BF16))
+        return jnp.concatenate(pieces, axis=0)
+
+    @pl.when(tap == 0)
     def _():
+        acc[...] = nt(moved(SHIFT), conv_w[...])
+
+    @pl.when(tap == 1)
+    def _():
+        acc[...] += nt(dpre_ref[...], conv_w[...])
+
+    @pl.when(tap == 2)
+    def _():
+        acc[...] += nt(moved(-SHIFT), conv_w[...])
+        items = micro * slots
+        group = d_step.shape[0]
         d_step[...] = jnp.zeros_like(d_step)
-
-    steps = tiles // subs
-    before = jnp.where(t == 0, other_ref[EDGE:, :], prev_ref[...])
-    after = jnp.where(t == steps - 1, other_ref[:EDGE, :], next_ref[...])
-    ext = jnp.concatenate([before, dpre_ref[...], after], axis=0)
-    spread = tile + 2 * EDGE
-    place = rows_iota(spread, 2 * width)
-    ahead, behind, item = [], [], []
-    limit = jnp.zeros((size, width), jnp.int32)
-    row = rows_iota(size, width)
-    for k in range(subs):
-        mb, slot, lim, prev_in, next_in = plan(
-            section * tiles + t * subs + k, tile, slots, buckets, item_len
-        )
-        item.append((mb - mb0) * slots + slot)
-        lo = jnp.where(prev_in, 0, EDGE)
-        hi = jnp.where(next_in, spread, tile + EDGE)
-        part = ext[k * tile : k * tile + spread].astype(F32)
-        part = jnp.where((place >= lo) & (place < hi), part, 0.0)
-        ahead.append(pltpu.roll(part, spread - SHIFT, 0)[EDGE : EDGE + tile].astype(BF16))
-        behind.append(pltpu.roll(part, SHIFT, 0)[EDGE : EDGE + tile].astype(BF16))
-        limit = jnp.where(row >= k * tile, lim + k * tile, limit)
-    d_in = nt(jnp.concatenate(ahead, axis=0), conv_w[:width, :])
-    d_in += nt(dpre_ref[...], conv_w[width : 2 * width, :])
-    d_in += nt(jnp.concatenate(behind, axis=0), conv_w[2 * width :, :])
-    d_mixed = jnp.where(row < limit, dsent_ref[...].astype(F32) * ISQ2 + d_in, 0.0)
-    for k in range(subs):
-        line = jnp.sum(col_sums(d_mixed[k * tile : (k + 1) * tile]), axis=0, keepdims=True)
-        d_step[pl.ds(item[k], 1), :] += line
-    low = d_mixed.astype(BF16)
-    o_keep[...] = jnp.where(section == 0, low[:, :half], low[:, half:])
-    o_give[...] = jnp.where(section == 0, low[:, half:], low[:, :half])
-
-    @pl.when(t == steps - 1)
-    def _():
-        both = jnp.concatenate([emb_ref[...], d_step[...], vec_ref[...]], axis=0)
-        o_rows[...] = both.astype(BF16)
+        for k in range(tiles):
+            mb, slot, lim = plans[k][:3]
+            rows = slice(k * tile, (k + 1) * tile)
+            d_mixed = dsent_ref[rows, :].astype(F32) * ISQ2 + acc[rows, :]
+            d_mixed = jnp.where(rows_iota(tile, width) < lim, d_mixed, 0.0)
+            line = jnp.sum(col_sums(d_mixed), axis=0, keepdims=True)
+            d_step[pl.ds(mb * slots + slot, 1), :] += line
+            low = d_mixed.astype(BF16)
+            o_keep[rows, :] = jnp.where(section == 0, low[:, :half], low[:, half:])
+            o_give[rows, :] = jnp.where(section == 0, low[:, half:], low[:, :half])
+        lane = lax.broadcasted_iota(jnp.int32, (1, width), 1)
+        index = jnp.zeros((1, width), jnp.int32)
+        for i in range(items):
+            index = jnp.where(lane == i, steps[i // slots, i % slots], index)
+        index = jnp.where(section == 0, index, 0)
+        d_step[items : items + 1, :] = (index >> 5).astype(F32)
+        d_step[items + 1 : items + 2, :] = (index & 31).astype(F32)
+        o_rows[:group, :] = d_step[...].astype(BF16)
+        o_rows[group:, :] = (vec_ref[...] + vec_more[...]).astype(BF16)
 
 
 SMALL = pl.CostEstimate(flops=1024, bytes_accessed=1024, transcendentals=0)
@@ -436,16 +497,16 @@
 
 
 def then_kernel(x_ref, after_ref, out_ref):
-    pass
+    out_ref[...] = x_ref[...]
 
 
 def then(x, after):
     return pl.pallas_call(
         then_kernel,
-        in_specs=[ANYWHERE, ANYWHERE],
-        out_specs=ANYWHERE,
+        in_specs=[IN_VMEM, ANYWHERE],
+        out_specs=IN_VMEM,
         out_shape=jax.ShapeDtypeStruct(x.shape, x.dtype),
-        input_output_aliases={0: 0},
+        compiler_params=pltpu.CompilerParams(vmem_limit_bytes=16 * 1024 * 1024),
         cost_estimate=SMALL,
         name="then",
     )(x, after)
@@ -553,15 +614,19 @@
     def turns(self):
         return 2 * self.sums.levels - 1
 
-    def spread(self, kinds, first):
-        runs = self.sums.runs()
-        *outs, done = place(runs, (0, 2), (self.held, swap(self.held)), kinds, first)
-        self.got = then(self.got, done)
-        return place(runs, (1, 3), (self.got, swap(self.got)), kinds, done, outs)
-
-
-def place_kernel(which, spots, runs, p0, p1, after_ref, *refs):
-    count = len(set(spot[0] for spot in spots if spot is not None))
+    def early(self, shapes, spots, after, outs=()):
+        return place(self.sums.runs(), (0, 2), (self.held, swap(self.held)), shapes, spots, after, outs)
+
+    def arrive(self, after):
+        self.got = then(self.got, after)
+        self.last = swap(self.got)
+        return self.got
+
+    def late(self, shapes, spots, after, outs):
+        return place(self.sums.runs(), (1, 3), (self.got, self.last), shapes, spots, after, outs)
+
+
+def place_kernel(which, spots, count, runs, p0, p1, after_ref, *refs):
     outs, (mark, buf, sems) = refs[-3 - count : -3], refs[-3:]
     mark[...] = jnp.zeros_like(mark)
     rows = buf.shape[1]
@@ -594,27 +659,29 @@
                         copy.start()
 
 
-def place(runs, which, pieces, kinds, after, outs=()):
+def spots_of(targets, width):
+    quarter = width // 4
+    spots = []
+    for section in range(2):
+        for k, row, col in targets:
+            for u in range(2):
+                spots.append((k, row + (2 * section + u) * quarter, col))
+    return spots
+
+
+def place(runs, which, pieces, shapes, spots, after, outs=()):
     length, width = pieces[0].shape
     quarter = width // 4
     per_run = length // quarter
-    spots, shapes = [None] * (4 * per_run), []
-    first = 0
-    for k, count in enumerate(kinds):
-        across = min(count, 2)
-        for i in range(count):
-            for section in range(2):
-                for u in range(2):
-                    w = section * 2 * per_run + 2 * (first + i) + u
-                    row = (i // across) * width + (2 * section + u) * quarter
-                    spots[w] = (k, row, (i % across) * width)
-        shapes.append(struct(width * max(count // 2, 1), across * width, F32))
-        first += count
+    half = len(spots) // 2
+    full = [None] * (4 * per_run)
+    full[:half] = spots[:half]
+    full[2 * per_run : 2 * per_run + half] = spots[half:]
     return pl.pallas_call(
-        functools.partial(place_kernel, which, spots),
+        functools.partial(place_kernel, which, full, len(shapes)),
         in_specs=[IN_SMEM] + [IN_VMEM] * 2 + [ANYWHERE] + [IN_HBM] * len(outs),
-        out_specs=[IN_HBM] * len(kinds) + [IN_VMEM],
-        out_shape=shapes + [struct(8, 128, F32)],
+        out_specs=[IN_HBM] * len(shapes) + [IN_VMEM],
+        out_shape=list(shapes) + [struct(8, 128, F32)],
         input_output_aliases={4 + k: k for k in range(len(outs))},
         scratch_shapes=[
             pltpu.VMEM((2 * per_run, quarter, width), F32),
@@ -626,12 +693,24 @@
     )(runs, *pieces, after, *outs)
 
 
-def step_kernel(group, rows_ref, after_ref, out_ref, mark):
+def step_kernel(items, group, rows_ref, after_ref, out_ref, mark):
     mark[...] = jnp.zeros_like(mark)
     width = rows_ref.shape[1]
-    rows = rows_ref[: rows_ref.shape[0] - EDGE, :].astype(F32).reshape(-1, 2 * group, width)
-    emb = rows[:, :group].reshape(-1, width).astype(BF16)
-    out_ref[...] = tn(emb, rows[:, group:].reshape(-1, width).astype(BF16))
+    half = width // 2
+    rows = rows_ref[: rows_ref.shape[0] - EDGE, :].astype(F32).reshape(-1, group, width)
+    lanes = (rows.shape[0], group, 128)
+    index = 32.0 * rows[:, items : items + 1, :128] + rows[:, items + 1 : items + 2, :128]
+    diagonal = lax.broadcasted_iota(jnp.int32, lanes, 1) == lax.broadcasted_iota(
+        jnp.int32, lanes, 2
+    )
+    index = jnp.sum(jnp.where(diagonal, index, 0.0), axis=2, keepdims=True)
+    index = index.reshape(-1, 1)
+    lane = lax.broadcasted_iota(jnp.int32, (index.shape[0], half), 1).astype(F32)
+    angle = index * jnp.exp(lane * F32(-math.log(10000.0) / half))
+    emb = jnp.concatenate([jnp.sin(angle), jnp.cos(angle)], axis=1)
+    used = lax.broadcasted_iota(jnp.int32, rows.shape, 1) < items
+    sums = jnp.where(used, rows, 0.0).reshape(-1, width)
+    out_ref[...] = tn(emb.astype(BF16), sums.astype(BF16))
 
 
 def padded(x, rows):
@@ -724,10 +803,15 @@
     def shape(*dims, dtype=BF16):
         return jax.ShapeDtypeStruct(dims, dtype)
 
-    macs = own * width * width * 25
+    def blocks_of(n):
+        return const((n, half, width)), shape(n, half, width)
+
+    film_blocks = 5
+    film_spec, film_shape = blocks_of(film_blocks)
     (
         stack,
-        d_pre,
+        slope,
+        gate,
         d_sent,
         block_keep,
         block_give,
@@ -736,20 +820,19 @@
         keep_a,
         give_a,
         vec,
-        emb,
+        _,
     ) = pl.pallas_call(
         functools.partial(forward_kernel, (tile, slots, nq, subs, tiles, mb_own, micro)),
         grid_spec=pltpu.PrefetchScalarGridSpec(
             num_scalar_prefetch=1,
             grid=(grid,),
             in_specs=[smem, smem, smem, prev_chip, chip_tile(width), next_chip]
-            + [chip_tile(width)] * 3
+            + [chip_tile(width)] * 2
             + [whole(flat_prompt), whole(mask)]
             + [whole(w) for w in weights],
-            out_specs=[own_tile(taps * width), own_tile(wide), own_tile(width)]
+            out_specs=[own_tile(taps * width), own_tile(wide), own_tile(width), own_tile(width)]
             + [own_tile(half)] * 4
-            + [const((7, half, width)), const((7, half, width)), const((16, width))]
-            + [const((items, width))],
+            + [film_spec, film_spec, const((16, width)), const((items, width))],
             scratch_shapes=[
                 pltpu.VMEM((items, width), F32),
                 pltpu.VMEM((items * nq, width), BF16),
@@ -757,23 +840,25 @@
                 pltpu.VMEM((items * nq, width), F32),
                 pltpu.VMEM((items * nq, width), F32),
                 pltpu.VMEM((width, wide), F32),
-                pltpu.VMEM((width, wide), F32),
                 pltpu.VMEM((width, width), F32),
-                pltpu.VMEM((3, 8, wide), F32),
+                pltpu.VMEM((8, wide), F32),
                 pltpu.VMEM((3, 8, width), F32),
                 pltpu.SMEM((1,), jnp.int32),
+                pltpu.VMEM((wide, width), BF16),
+                pltpu.VMEM((width, width), BF16),
             ],
         ),
         out_shape=[
             shape(own, taps * width),
             shape(own, wide),
             shape(own, width),
+            shape(own, width),
             shape(own, half),
             shape(own, half),
             shape(own, half),
             shape(own, half),
-            shape(7, half, width),
-            shape(7, half, width),
+            film_shape,
+            film_shape,
             shape(16, width, dtype=F32),
             shape(items, width, dtype=F32),
         ],
@@ -790,13 +875,10 @@
         input_rows,
         conditioning,
         output_gradient,
-        grad_skip,
         flat_prompt,
         mask,
         *weights,
     )
-
-    edge = swap(jnp.concatenate([d_pre[:EDGE], d_pre[own - EDGE :]], axis=0))
 
     bits = list(range(lax.axis_size("dp").bit_length() - 1))
     other = [bits[1], bits[0]] + bits[2:]
@@ -805,70 +887,96 @@
     sums = Sum((bits, other))
     unit = 16 * lax.axis_size("dp") // 2
 
-    film_blocks = 7
-    rows_a = -(-film_blocks * half // unit) * unit
-    batch_a = Batch(
-        sums,
-        padded(keep_a.reshape(-1, width), rows_a),
-        padded(give_a.reshape(-1, width), rows_a),
-    )
-    conv_blocks = 2 * (taps + 1)
-    pair = pl.BlockSpec((2, half, width), lambda i, *_: (i, 0, 0))
-    keep_b, give_b = pl.pallas_call(
-        functools.partial(weight_kernel, taps),
-        grid_spec=pltpu.PrefetchScalarGridSpec(
-            num_scalar_prefetch=1,
-            grid=(taps + 1,),
-            in_specs=[
-                pl.BlockSpec((own, width), lambda i, s: (0, jnp.minimum(i, taps - 1))),
-                pl.BlockSpec(
-                    (own, width), lambda i, s: (s[0], 0), pipeline_mode=pl.Buffered(1)
-                ),
-                whole(d_pre),
-            ],
-            out_specs=[pair, pair],
-            scratch_shapes=[pltpu.VMEM((width, wide), F32)],
-        ),
-        out_shape=[shape(conv_blocks, half, width)] * 2,
-        compiler_params=pltpu.CompilerParams(vmem_limit_bytes=KB_VMEM),
-        cost_estimate=LARGE,
-        name="weights",
-    )(sec, stack, conditioning, d_pre)
-
-    rows_b = -(-conv_blocks * half // unit) * unit
-    batch_b = Batch(
-        sums,
-        padded(keep_b.reshape(-1, width), rows_b),
-        padded(give_b.reshape(-1, width), rows_b),
-    )
-    (after,) = batch_a.turn(keep_b)
-    (after,) = batch_b.turn(after)
-
-    rows_last = own // EDGE - 1
-    in_keep, in_give, rows_now = pl.pallas_call(
-        functools.partial(back_kernel, (tile, slots, subs, tiles, mb_own, micro)),
+    def batch(keep, give):
+        rows = keep.shape[0] * half
+        rows = -(-rows // unit) * unit
+        return Batch(
+            sums, padded(keep.reshape(-1, width), rows), padded(give.reshape(-1, width), rows)
+        )
+
+    batch_a = batch(keep_a, give_a)
+    block_got, skip_got = swap(block_give), swap(skip_give)
+
+    side = pl.BlockSpec((2, half, width), lambda t, *_: (0, 0, 0))
+    d_pre, edge, vec_more, keep_c, give_c = pl.pallas_call(
+        functools.partial(branch_kernel, (tile, slots, subs, tiles)),
         grid_spec=pltpu.PrefetchScalarGridSpec(
             num_scalar_prefetch=1,
             grid=(grid,),
+            in_specs=[smem, smem, chip_tile(width), own_tile(width), own_tile(wide)]
+            + [own_tile(width), whole(res_w)],
+            out_specs=[own_tile(wide), const((2 * EDGE, wide)), const((16, width)), side, side],
+            scratch_shapes=[
+                pltpu.VMEM((width, wide), F32),
+                pltpu.VMEM((wide, width), BF16),
+                pltpu.VMEM((2, 8, wide), F32),
+            ],
+        ),
+        out_shape=[
+            shape(own, wide),
+            shape(2 * EDGE, wide),
+            shape(16, width, dtype=F32),
+            shape(4, half, width),
+            shape(4, half, width),
+        ],
+        compiler_params=pltpu.CompilerParams(vmem_limit_bytes=KB_VMEM),
+        cost_estimate=LARGE,
+        name="branch",
+    )(sec, buckets, item_len, grad_skip, d_sent, slope, gate, res_w)
+    other_edge = swap(edge)
+    (after,) = batch_a.turn(vec_more)
+
+    def weight_grads(left, count, index, after, first=0, outs=(), total=0):
+        spec = pl.BlockSpec((2, half, width), lambda i, *_: (first + i, 0, 0))
+        return pl.pallas_call(
+            weight_kernel,
+            grid_spec=pltpu.PrefetchScalarGridSpec(
+                num_scalar_prefetch=1,
+                grid=(count,),
+                in_specs=[pl.BlockSpec((own, width), index), whole(d_pre)]
+                + [ANYWHERE] * (1 + len(outs)),
+                out_specs=[spec, spec],
+                scratch_shapes=[pltpu.VMEM((width, wide), F32)],
+            ),
+            out_shape=[shape(2 * (first + count), half, width)] * 2,
+            input_output_aliases={4 + k: k for k in range(len(outs))},
+            compiler_params=pltpu.CompilerParams(vmem_limit_bytes=KB_VMEM),
+            cost_estimate=LARGE,
+            name="weights",
+        )(sec, left, d_pre, after, *outs)
+
+    keep_b, give_b = weight_grads(stack, taps, lambda i, s: (0, i), after)
+    batch_b = batch(keep_b, give_b)
+    keep_c, give_c = weight_grads(
+        conditioning, 1, lambda i, s: (s[0], 0), keep_b, 1, (keep_c, give_c)
+    )
+    batch_c = batch(keep_c, give_c)
+    (after,) = batch_a.turn(keep_c)
+    (after,) = batch_b.turn(after)
+    (after,) = batch_c.turn(after)
+
+    group = -(-(micro * slots + 2) // 16) * 16
+    in_keep, in_give, rows_now = pl.pallas_call(
+        functools.partial(back_kernel, (tile, slots, tiles, micro)),
+        grid_spec=pltpu.PrefetchScalarGridSpec(
+            num_scalar_prefetch=1,
+            grid=(taps,),
             in_specs=[
                 smem,
                 smem,
-                pl.BlockSpec((EDGE, wide), lambda t, *_: (jnp.maximum(t * per - 1, 0), 0)),
-                own_tile(wide),
-                pl.BlockSpec(
-                    (EDGE, wide), lambda t, *_: (jnp.minimum((t + 1) * per, rows_last), 0)
-                ),
+                whole(d_pre),
                 whole(edge),
-                own_tile(width),
-                whole(conv_flat),
-                whole(emb),
+                whole(d_sent),
+                pl.BlockSpec((width, wide), lambda k, *_: (k, 0)),
+                smem,
                 whole(vec),
+                whole(vec_more),
                 ANYWHERE,
             ],
-            out_specs=[own_tile(half), own_tile(half), const((2 * items + EDGE, width))],
-            scratch_shapes=[pltpu.VMEM((items, width), F32)],
+            out_specs=[const((own, half)), const((own, half)), const((group + EDGE, width))],
+            scratch_shapes=[pltpu.VMEM((own, width), F32), pltpu.VMEM((group, width), F32)],
         ),
-        out_shape=[shape(own, half), shape(own, half), shape(2 * items + EDGE, width)],
+        out_shape=[shape(own, half), shape(own, half), shape(group + EDGE, width)],
         compiler_params=pltpu.CompilerParams(vmem_limit_bytes=KC_VMEM),
         cost_estimate=LARGE,
         name="back",
@@ -877,41 +985,47 @@
         buckets,
         item_len,
         d_pre,
-        d_pre,
-        d_pre,
-        edge,
+        other_edge,
         d_sent,
         conv_flat,
-        emb,
+        step_index,
         vec,
+        vec_more,
         after,
     )
-
-    block_got, skip_got, in_got = swap(block_give), swap(skip_give), swap(in_give)
-    gathers = sums.levels + 1
-    rows_got, rows_bit = swap(rows_now), sec
+    in_got = swap(in_give)
 
     block_out, skip_out, after = join(
         sec, rows_now, (block_keep, block_got), (skip_keep, skip_got)
     )
-    done = 0
-    for name in "ab" * (batch_a.turns - 1):
-        if name == "b" and done < gathers:
-            n = 2 * rows_now.shape[0] - EDGE
-            work = (gather_body, rows_bit, rows_now, rows_got, [struct(n, width)])
-            after, rows_now = batch_b.turn(after, [work])
-            if done < sums.levels:
-                route = [(d, d ^ (1 << done)) for d in range(sums.chips)]
+    rows_got, rows_bit, gathered = swap(rows_now), sec, 0
+    batches = {"a": batch_a, "b": batch_b, "c": batch_c}
+    first = True
+    for name in "ab-c" * (batch_a.turns - 3) + "abcTbc":
+        if name == "T":
+            after = batch_a.arrive(after)
+            continue
+        if name == "-":
+            first = False
+            continue
+        turner = batches[name]
+        if name == "c" and gathered <= sums.levels:
+            n = rows_now.shape[0]
+            work = (add_body, rows_bit, rows_now, rows_got, [struct(n, width)])
+            if gathered:
+                work = (gather_body, rows_bit, rows_now, rows_got, [struct(2 * n - EDGE, width)])
+            after, rows_now = turner.turn(after, [work])
+            if gathered < sums.levels:
+                route = [(d, d ^ (1 << gathered)) for d in range(sums.chips)]
                 rows_got = lax.ppermute(rows_now, "dp", route)
-                rows_bit = ((sums.chip >> done) & 1).astype(jnp.int32).reshape(1)
-            done += 1
+                rows_bit = ((sums.chip >> gathered) & 1).astype(jnp.int32).reshape(1)
+            gathered += 1
         else:
-            cost = LARGE if done else SMALL
-            (after,) = (batch_a if name == "a" else batch_b).turn(after, cost=cost)
+            (after,) = turner.turn(after, cost=SMALL if first else LARGE)
 
     in_grad, mark = join(sec, after, (in_keep, in_got))
     g_step, mark = pl.pallas_call(
-        functools.partial(step_kernel, items),
+        functools.partial(step_kernel, micro * slots, group),
         in_specs=[IN_VMEM, ANYWHERE],
         out_specs=[IN_VMEM, IN_VMEM],
         out_shape=[struct(width, width, F32), struct(8, 128, F32)],
@@ -919,10 +1033,26 @@
         cost_estimate=SMALL,
         name="step_grad",
     )(rows_now, mark)
-    g_out, g_res, g_query, g_key, g_value, mark = batch_a.spread((2, 2, 1, 1, 1), mark)
-    g_conv, g_cond, mark = batch_b.spread((2 * taps, 2), mark)
+
+    def pairs(k, count, base=0):
+        return [(k, base + i * width, col) for i in range(count) for col in (0, width)]
+
+    square, tall = struct(width, width, F32), struct(width, wide, F32)
+    shapes_a = [tall, square, square, square]
+    spots_a = spots_of(pairs(0, 1) + [(k, 0, 0) for k in (1, 2, 3)], width)
+    shapes_b, spots_b = [struct(taps * width, wide, F32)], spots_of(pairs(0, taps), width)
+    shapes_c, spots_c = [tall, tall], spots_of(pairs(0, 1) + pairs(1, 1), width)
+    *outs_a, mark = batch_a.early(shapes_a, spots_a, mark)
+    *outs_a, mark = batch_a.late(shapes_a, spots_a, mark, outs_a)
+    *outs_b, mark = batch_b.early(shapes_b, spots_b, mark)
+    *outs_c, mark = batch_c.early(shapes_c, spots_c, mark)
+    mark = batch_c.arrive(batch_b.arrive(mark))
+    *outs_b, mark = batch_b.late(shapes_b, spots_b, mark, outs_b)
+    *outs_c, mark = batch_c.late(shapes_c, spots_c, mark, outs_c)
+    g_out, g_query, g_key, g_value = outs_a
+    g_conv = outs_b[0].reshape(conv_w.shape)
+    g_res, g_cond = outs_c
     vec = rows_now[rows_now.shape[0] - EDGE :].astype(F32)
-    g_conv = g_conv.reshape(conv_w.shape)
     g_convb, g_resb, g_outb = (vec[2 * i : 2 * i + 2].reshape(wide) for i in range(3))
     sizes = jnp.sum(vec[6:9], axis=1)
     frames_valid = sum(vec[9, i] * (1 << 3 * i) for i in range(8))

time: 193 us -> 176 us (0.912)
  waiting for transfers between devices: 50.6 us -> 18.6 us
  starting transfers between devices: 31.8 us -> 47.8 us
  local copies, waits for them, and re-layouts: 17.4 us -> 6.38 us
  Pallas kernels: 84.3 us -> 95 us
    ppermute x14 -> x21, waiting for transfers between devices: 34.8 us -> 16.2 us  [send(): return lax.ppermute(x, ('section', 'dp'), route)]
    pallas_call x9 -> x14, Pallas kernels: 34.1 us -> 50 us  [the longest x6 15.9 us: place(): pl.pallas_call(functools.partial(place_kernel, which, full, len(shapes)),...]
    ppermute x14 -> x21, starting transfers between devices: 20.1 us -> 34.3 us  [send(): return lax.ppermute(x, ('section', 'dp'), route)]
    ppermute x4, waiting for transfers between devices: 13.1 us -> 2.33 us  [on_device(): rows_got = lax.ppermute(rows_now, 'dp', route)]
    unnamed x56 -> x44, local copies, waits for them, and re-layouts: 16 us -> 5.71 us
    ppermute x11 -> x14, starting transfers between devices: 3.85 us -> 9.01 us  [swap(): return lax.ppermute(x, 'section', [(0, 1), (1, 0)])]
    pallas_call x1, Pallas kernels: 37.1 us -> 32.4 us  [on_device(): pl.pallas_call(functools.partial(forward_kernel, (tile, slots, nq, subs,...]
    ppermute x4, starting transfers between devices: 7.86 us -> 4.41 us  [on_device(): rows_got = lax.ppermute(rows_now, 'dp', route)]
  transfers between devices with their start and end apart: 29 -> 39, of which waited for: 9 -> 10; matrix products, arithmetic and copies ran while one was open for 2% -> 2% of each run, Pallas kernels for 23% -> 34%
where the time goes in v2:
time: 176 us
  Pallas kernels  95 us (54%)
  starting transfers between devices  47.8 us (27%)
  waiting for transfers between devices  18.6 us (11%)
  local copies, waits for them, and re-layouts  6.38 us (4%)
  between operations  6.38 us (4%)
    ppermute x21, starting transfers between devices, send(): return lax.ppermute(x, ('section', 'dp'), route)  34.3 us
    pallas_call x1, Pallas kernels, on_device(): pl.pallas_call(functools.partial(forward_kernel, (tile, slots, nq, subs,...  32.4 us
    ppermute x21, waiting for transfers between devices, send(): return lax.ppermute(x, ('section', 'dp'), route)  16.2 us
    pallas_call x6, Pallas kernels, place(): pl.pallas_call(functools.partial(place_kernel, which, full, len(shapes)),...  15.9 us
    pallas_call x2, Pallas kernels, weight_grads(): pl.pallas_call(weight_kernel, grid_spec=pltpu.PrefetchScalarGridSpec(num_...  12.6 us
    pallas_call x1, Pallas kernels, on_device(): pl.pallas_call(functools.partial(back_kernel, (tile, slots, tiles, micro)...  9.99 us
    ppermute x14, starting transfers between devices, swap(): return lax.ppermute(x, 'section', [(0, 1), (1, 0)])  9.01 us
    pallas_call x1, Pallas kernels, on_device(): pl.pallas_call(functools.partial(branch_kernel, (tile, slots, subs, tiles...  8.1 us
  transfers between devices with their start and end apart: 39, of which 10 were waited for; matrix products, arithmetic and copies ran while one was open for 2% of the time, Pallas kernels for 34%

profile of v2, /device:TPU:0, one launch (start us, length us, event | category | flops | bytes accessed | tf_op | source)
XLA Modules:
  0.0 175.7 jit_solution(14204022885550951913)
XLA Ops:
  1.5 32.4 %forward.1 = (bf16[1536,1536]{1,0:T(8,128)(2,1)}, bf16[1536,1024]{1,0:T(8,128)(2,1)}, bf16[1536,512]{1,0:T(8,128)(2,1)}, bf16[1536,512]{1,0:T(8,128)(2,1)}, bf16...) custom-call(s32[1]{0:T(128)} %bitcast.sec_ref.refs_1_, ...), custom_call_target="tpu_custom_call" | custom-call | flops 68719476736 | bytes 1024 | tf_op jit(solution)/shard_map/forward/pallas_call | solution.py:824
  35.8 8.1 %branch.1 = (bf16[1536,1024]{1,0:T(8,128)(2,1)}, bf16[32,1024]{1,0:T(8,128)(2,1)}, f32[16,512]{1,0:T(8,128)S(1)}, bf16[4,256,512]{2,1,0:T(8,128)(2,1)S(1)}, bf16[4,256,512]{2,1,0:T(8,128)(2,1)S(1)}) custom-call(s32[1]{0:T(128)} %bitcast.sec_ref.refs_1_, s32[3]{0:T(128)S(1)} %copy-done.8, s32[3,4]{1,0:T(4,128)S(1)} %copy-done.5, bf16[3072,512]{1,0:T(8,128)(2,1)} %gskip_ref.1, ...), custom_call_target="tpu_custom_call" | custom-call | flops 68719476736 | bytes 1024 | tf_op jit(solution)/shard_map/branch/pallas_call | solution.py:901
  46.2 3.0 %collective-permute-start.6 = (bf16[640,512]{1,0:T(8,128)(2,1)S(1)}, bf16[640,512]{1,0:T(8,128)(2,1)S(1)}, u32[]{:S(2)}, u32[]{:S(2)}) collective-permute-start(bf16[640,512]{1,0:T(8,128)(2,1)S(1)} %get-tuple-element.111), channel_id=1, source_target_pairs={{0,1},{1,0},{2,3},{3,2},{4,5},{5,4},{6,7},{7,6},{8,9},{9,8},{10,11... | collective-permute-start | bytes 1966088 | tf_op jit(solution)/shard_map/ppermute | solution.py:576
  49.2 8.4 %weights.2 = (bf16[6,256,512]{2,1,0:T(8,128)(2,1)S(1)}, bf16[6,256,512]{2,1,0:T(8,128)(2,1)S(1)}) custom-call(s32[1]{0:T(128)} %bitcast.sec_ref.refs_1_, bf16[1536,1536]{1,0:T(8,128)(2,1)} %get-tuple-element.101.left_ref, bf16[1536,1024]{1,0:T(8,128)(2,1)} %get-tuple-element.97.dpre_ref, bf16[640,512]{1,0:T(8,128)(2,1)S(1)} %get-tuple-element.104.refs_0_.refs_1_), custom_call_target="tpu_custom_call" | custom-call | flops 68719476736 | bytes 1024 | tf_op jit(solution)/shard_map/weights/pallas_call | solution.py:931
  57.6 4.3 %weights.3 = (bf16[4,256,512]{2,1,0:T(8,128)(2,1)S(1)}, bf16[4,256,512]{2,1,0:T(8,128)(2,1)S(1)}) custom-call(s32[1]{0:T(128)} %bitcast.sec_ref.refs_1_, bf16[3072,512]{1,0:T(8,128)(2,1)} %left_ref.1, bf16[1536,1024]{1,0:T(8,128)(2,1)} %get-tuple-element.97.dpre_ref, ...), custom_call_target="tpu_custom_call", output_to_operand_aliasing={{0}: (4, {}), {1}: (5, {})} | custom-call | flops 68719476736 | bytes 1024 | tf_op jit(solution)/shard_map/weights/pallas_call | solution.py:931
  63.3 1.5 collective-permute-start.11
  69.1 10.0 %back.1 = (bf16[1536,256]{1,0:T(8,128)(2,1)S(1)}, bf16[1536,256]{1,0:T(8,128)(2,1)}, bf16[32,512]{1,0:T(8,128)(2,1)S(1)}) custom-call(s32[1]{0:T(128)} %bitcast.sec_ref.refs_1_, s32[3]{0:T(128)S(1)} %copy-done.9, s32[3,4]{1,0:T(4,128)S(1)} %copy-done.6, bf16[1536,1024]{1,0:T(8,128)(2,1)} %get-tuple-element.97.dpre_ref, ...), custom_call_target="tpu_custom_call" | custom-call | flops 68719476736 | bytes 1024 | tf_op jit(solution)/shard_map/back/pallas_call | solution.py:959
  80.3 3.1 %join.2 = (bf16[3072,256]{1,0:T(8,128)(2,1)}, bf16[3072,256]{1,0:T(8,128)(2,1)}, f32[8,128]{1,0:T(8,128)S(1)}) custom-call(s32[1]{0:T(128)} %bitcast.sec_ref.refs_1_, bf16[1536,256]{1,0:T(8,128)(2,1)S(1)} %copy-done, bf16[1536,256]{1,0:T(8,128)(2,1)} %collective-permute-done.refs_1_, bf16[1536,256]{1,0:T(8,128)(2,1)S(1)} %copy-done.1, ...), custom_call_target="tpu_custom_call" | custom-call | flops 1024 | bytes 1024 | tf_op jit(solution)/shard_map/join/pallas_call | solution.py:538
  84.5 1.7 collective-permute-start.15
  89.3 1.6 collective-permute-start.12
  91.7 2.1 %collective-permute-start.19 = (bf16[160,512]{1,0:T(8,128)(2,1)S(1)}, bf16[160,512]{1,0:T(8,128)(2,1)S(1)}, u32[]{:S(2)}, u32[]{:S(2)}) collective-permute-start(bf16[160,512]{1,0:T(8,128)(2,1)S(1)} %add_body.6.refs_3_.refs_1_), channel_id=1, source_target_pairs={{0,8},{1,9},{2,10},{3,11},{4,12},{5,13},{6,14},{7,15},{8,0},{9,1},... | collective-permute-start | bytes 491528 | tf_op jit(solution)/shard_map/ppermute | solution.py:576
  93.7 1.7 collective-permute-done.14.refs_2_
  95.5 1.6 collective-permute-start.18
  98.3 1.6 collective-permute-start.16
  100.6 4.5 %collective-permute-start.23 = (bf16[160,512]{1,0:T(8,128)(2,1)S(1)}, bf16[160,512]{1,0:T(8,128)(2,1)S(1)}, u32[]{:S(2)}, u32[]{:S(2)}) collective-permute-start(bf16[160,512]{1,0:T(8,128)(2,1)S(1)} %add_body.7.refs_3_.refs_1_), channel_id=1, source_target_pairs={{0,4},{1,5},{2,6},{3,7},{4,0},{5,1},{6,2},{7,3},{8,12},{9,13},{10,... | collective-permute-start | bytes 491528 | tf_op jit(solution)/shard_map/ppermute | solution.py:576
  105.1 3.9 %collective-permute-start.22 = (bf16[192,512]{1,0:T(8,128)(2,1)S(1)}, bf16[192,512]{1,0:T(8,128)(2,1)S(1)}, u32[]{:S(2)}, u32[]{:S(2)}) collective-permute-start(bf16[192,512]{1,0:T(8,128)(2,1)S(1)} %add_body.8.refs_6_.refs_1_), channel_id=1, source_target_pairs={{0,8},{1,9},{2,10},{3,11},{4,12},{5,13},{6,14},{7,15},{8,0},{9,1},... | collective-permute-start | bytes 589832 | tf_op jit(solution)/shard_map/ppermute | solution.py:576
  109.3 4.8 %collective-permute-done.23.refs_2_ = bf16[160,512]{1,0:T(8,128)(2,1)S(1)} collective-permute-done((bf16[160,512]{1,0:T(8,128)(2,1)S(1)}, bf16[160,512]{1,0:T(8,128)(2,1)S(1)}, u32[]{:S(2)}, u32[]{:S(2)}) %collective-permute-start.23) | collective-permute-done | bytes 163872 | tf_op jit(solution)/shard_map/ppermute | solution.py:576
  115.4 2.9 %collective-permute-start.26 = (bf16[192,512]{1,0:T(8,128)(2,1)S(1)}, bf16[192,512]{1,0:T(8,128)(2,1)S(1)}, u32[]{:S(2)}, u32[]{:S(2)}) collective-permute-start(bf16[192,512]{1,0:T(8,128)(2,1)S(1)} %add_body.10.refs_6_.refs_1_), channel_id=1, source_target_pairs={{0,4},{1,5},{2,6},{3,7},{4,0},{5,1},{6,2},{7,3},{8,12},{9,13},{10,... | collective-permute-start | bytes 589832 | tf_op jit(solution)/shard_map/ppermute | solution.py:576
  118.4 3.2 %collective-permute-start.25 = (bf16[144,512]{1,0:T(8,128)(2,1)S(1)}, bf16[144,512]{1,0:T(8,128)(2,1)S(1)}, u32[]{:S(2)}, u32[]{:S(2)}) collective-permute-start(bf16[144,512]{1,0:T(8,128)(2,1)S(1)} %get-tuple-element.139.refs_4_), channel_id=1, source_target_pairs={{0,8},{1,9},{2,10},{3,11},{4,12},{5,13},{6,14},{7,15},{8,0},{9,1},... | collective-permute-start | bytes 442376 | tf_op jit(solution)/shard_map/ppermute | solution.py:1020
  124.6 4.8 %collective-permute-done.24.refs_3_ = bf16[128,512]{1,0:T(8,128)(2,1)S(1)} collective-permute-done((bf16[128,512]{1,0:T(8,128)(2,1)S(1)}, bf16[128,512]{1,0:T(8,128)(2,1)S(1)}, u32[]{:S(2)}, u32[]{:S(2)}) %collective-permute-start.24) | collective-permute-done | bytes 131104 | tf_op jit(solution)/shard_map/ppermute | solution.py:576
  129.9 2.3 %collective-permute-done.25.refs_5_ = bf16[144,512]{1,0:T(8,128)(2,1)S(1)} collective-permute-done((bf16[144,512]{1,0:T(8,128)(2,1)S(1)}, bf16[144,512]{1,0:T(8,128)(2,1)S(1)}, u32[]{:S(2)}, u32[]{:S(2)}) %collective-permute-start.25) | collective-permute-done | bytes 147488 | tf_op jit(solution)/shard_map/ppermute | solution.py:1020
  135.3 1.9 %collective-permute-done.29.refs_2_ = bf16[384,512]{1,0:T(8,128)(2,1)S(1)} collective-permute-done((bf16[384,512]{1,0:T(8,128)(2,1)S(1)}, bf16[384,512]{1,0:T(8,128)(2,1)S(1)}, u32[]{:S(2)}, u32[]{:S(2)}) %collective-permute-start.29) | collective-permute-done | bytes 393248 | tf_op jit(solution)/shard_map/ppermute | solution.py:576
  137.2 3.1 %collective-permute-start.33 = (bf16[768,512]{1,0:T(8,128)(2,1)S(1)}, bf16[768,512]{1,0:T(8,128)(2,1)}, u32[]{:S(2)}, u32[]{:S(2)}) collective-permute-start(bf16[768,512]{1,0:T(8,128)(2,1)S(1)} %merge_body.10.refs_3_.p0), channel_id=1, source_target_pairs={{0,16},{16,0},{1,17},{17,1},{2,18},{18,2},{3,19},{19,3},{4,20},{20... | collective-permute-start | bytes 2359304 | tf_op jit(solution)/shard_map/ppermute | solution.py:551
  140.4 2.0 %collective-permute-start.31 = (bf16[768,512]{1,0:T(8,128)(2,1)S(1)}, bf16[768,512]{1,0:T(8,128)(2,1)S(1)}, u32[]{:S(2)}, u32[]{:S(2)}) collective-permute-start(bf16[768,512]{1,0:T(8,128)(2,1)S(1)} %merge_body.10.refs_3_.p0), channel_id=1, source_target_pairs={{0,1},{1,0},{2,3},{3,2},{4,5},{5,4},{6,7},{7,6},{8,9},{9,8},{10,11... | collective-permute-start | bytes 2359304 | tf_op jit(solution)/shard_map/ppermute | solution.py:576
  144.9 2.3 %join.3 = (bf16[3072,256]{1,0:T(8,128)(2,1)}, f32[8,128]{1,0:T(8,128)S(1)}) custom-call(s32[1]{0:T(128)} %bitcast.sec_ref.refs_1_, bf16[1536,256]{1,0:T(8,128)(2,1)S(1)} %get-tuple-element.118.refs_0_, bf16[1536,256]{1,0:T(8,128)(2,1)} %collective-permute-done.7.refs_1_, bf16[512,512]{1,0:T(8,128)(2,1)S(1)} %merge_body.11.refs_2_.p0), custom_call_target="tpu_custom_call" | custom-call | flops 1024 | bytes 1024 | tf_op jit(solution)/shard_map/join/pallas_call | solution.py:538
  147.3 2.3 %step_grad.1 = (f32[512,512]{1,0:T(8,128)}, f32[8,128]{1,0:T(8,128)S(1)}) custom-call(bf16[272,512]{1,0:T(8,128)(2,1)S(1)} %copy-done.3, f32[8,128]{1,0:T(8,128)S(1)} %get-tuple-element.143.after_ref), custom_call_target="tpu_custom_call" | custom-call | flops 1024 | bytes 1024 | tf_op jit(solution)/shard_map/step_grad/pallas_call | solution.py:1027
  149.5 2.9 %place.6 = (f32[512,1024]{1,0:T(8,128)}, f32[512,512]{1,0:T(8,128)}, f32[512,512]{1,0:T(8,128)}, f32[512,512]{1,0:T(8,128)}, f32[8,128]{1,0:T(8,128)S(1)}) custom-call(s32[4]{0:T(128)S(1)} %pad_add_fusion.runs, bf16[640,512]{1,0:T(8,128)(2,1)} %merge_body.7.refs_3_.p0, bf16[640,512]{1,0:T(8,128)(2,1)} %collective-permute-done.35.p1, ...), custom_call_target="tpu_custom_call" | custom-call | flops 1024 | bytes 1024 | tf_op jit(solution)/shard_map/place/pallas_call | solution.py:680
  152.4 2.7 %place.7 = (f32[512,1024]{1,0:T(8,128)}, f32[512,512]{1,0:T(8,128)}, f32[512,512]{1,0:T(8,128)}, f32[512,512]{1,0:T(8,128)}, f32[8,128]{1,0:T(8,128)S(1)}) custom-call(s32[4]{0:T(128)S(1)} %pad_add_fusion.runs, bf16[640,512]{1,0:T(8,128)(2,1)S(1)} %then.3.refs_3_.p0, ...), custom_call_target="tpu_custom_call", output_to_operand_aliasing={{0}: (4, {}), {1}: (5, {}), {2}: (6, {}), {3}: (7, {})} | custom-call | flops 1024 | bytes 1024 | tf_op jit(solution)/shard_map/place/pallas_call | solution.py:680
  155.2 2.9 %place.8 = (f32[1536,1024]{1,0:T(8,128)}, f32[8,128]{1,0:T(8,128)S(1)}) custom-call(s32[4]{0:T(128)S(1)} %pad_add_fusion.runs, bf16[768,512]{1,0:T(8,128)(2,1)S(1)} %merge_body.10.refs_3_.p0, bf16[768,512]{1,0:T(8,128)(2,1)} %collective-permute-done.33.p1, f32[8,128]{1,0:T(8,128)S(1)} %get-tuple-element.151.after_ref), custom_call_target="tpu_custom_call" | custom-call | flops 1024 | bytes 1024 | tf_op jit(solution)/shard_map/place/pallas_call | solution.py:680
  158.1 2.5 %place.9 = (f32[512,1024]{1,0:T(8,128)}, f32[512,1024]{1,0:T(8,128)}, f32[8,128]{1,0:T(8,128)S(1)}) custom-call(s32[4]{0:T(128)S(1)} %pad_add_fusion.runs, bf16[512,512]{1,0:T(8,128)(2,1)S(1)} %merge_body.11.refs_2_.p0, bf16[512,512]{1,0:T(8,128)(2,1)} %collective-permute-done.32.p1, f32[8,128]{1,0:T(8,128)S(1)} %get-tuple-element.152.after_ref), custom_call_target="tpu_custom_call" | custom-call | flops 1024 | bytes 1024 | tf_op jit(solution)/shard_map/place/pallas_call | solution.py:680
  170.6 2.3 %place.10 = (f32[1536,1024]{1,0:T(8,128)}, f32[8,128]{1,0:T(8,128)S(1)}) custom-call(s32[4]{0:T(128)S(1)} %pad_add_fusion.runs, bf16[768,512]{1,0:T(8,128)(2,1)S(1)} %then.4.after_ref.p0, bf16[768,512]{1,0:T(8,128)(2,1)S(1)} %collective-permute-done.36.p1, bf16[512,512]{1,0:T(8,128)(2,1)S(1)} %then.5.after_ref.p0, ...), custom_call_target="tpu_custom_call", output_to_operand_aliasing={{0}: (4, {})} | custom-call | flops 1024 | bytes 1024 | tf_op jit(solution)/shard_map/place/pallas_call | solution.py:680
  172.9 2.6 %place.11 = (f32[512,1024]{1,0:T(8,128)}, f32[512,1024]{1,0:T(8,128)}, f32[8,128]{1,0:T(8,128)}) custom-call(s32[4]{0:T(128)S(1)} %pad_add_fusion.runs, bf16[512,512]{1,0:T(8,128)(2,1)S(1)} %then.5.after_ref.p0, bf16[512,512]{1,0:T(8,128)(2,1)S(1)} %collective-permute-done.38.p1, ...), custom_call_target="tpu_custom_call", output_to_operand_aliasing={{0}: (4, {}), {1}: (5, {})} | custom-call | flops 1024 | bytes 1024 | tf_op jit(solution)/shard_map/place/pallas_call | solution.py:680
  (136 shorter events, 34.4 us)
Async XLA Ops:
  33.9 10.7 %collective-permute-start.3 = (bf16[1280,512]{1,0:T(8,128)(2,1)}, bf16[1280,512]{1,0:T(8,128)(2,1)S(1)}, u32[]{:S(2)}, u32[]{:S(2)}) collective-permute-start(bf16[1280,512]{1,0:T(8,128)(2,1)} %bitcast.45), channel_id=1, source_target_pairs={{0,16},{16,0},{1,17},{17,1},{2,18},{18,2},{3,19},{19,3},{4,20},{20... | collective-permute-start | bytes 3932168 | tf_op jit(solution)/shard_map/ppermute | solution.py:551
  43.9 23.7 %collective-permute-start.2 = (bf16[32,1024]{1,0:T(8,128)(2,1)}, bf16[32,1024]{1,0:T(8,128)(2,1)}, u32[]{:S(2)}, u32[]{:S(2)}) collective-permute-start(bf16[32,1024]{1,0:T(8,128)(2,1)} %get-tuple-element.98), channel_id=1, source_target_pairs={{0,16},{16,0},{1,17},{17,1},{2,18},{18,2},{3,19},{19,3},{4,20},{20... | collective-permute-start | bytes 196616 | tf_op jit(solution)/shard_map/ppermute | solution.py:551
  44.0 35.0 %collective-permute-start = (bf16[1536,256]{1,0:T(8,128)(2,1)}, bf16[1536,256]{1,0:T(8,128)(2,1)}, u32[]{:S(2)}, u32[]{:S(2)}) collective-permute-start(bf16[1536,256]{1,0:T(8,128)(2,1)} %get-tuple-element.91), channel_id=1, source_target_pairs={{0,16},{16,0},{1,17},{17,1},{2,18},{18,2},{3,19},{19,3},{4,20},{20... | collective-permute-start | bytes 2359304 | tf_op jit(solution)/shard_map/ppermute | solution.py:551
  44.5 34.7 %collective-permute-start.1 = (bf16[1536,256]{1,0:T(8,128)(2,1)}, bf16[1536,256]{1,0:T(8,128)(2,1)}, u32[]{:S(2)}, u32[]{:S(2)}) collective-permute-start(bf16[1536,256]{1,0:T(8,128)(2,1)} %get-tuple-element.93), channel_id=1, source_target_pairs={{0,16},{16,0},{1,17},{17,1},{2,18},{18,2},{3,19},{19,3},{4,20},{20... | collective-permute-start | bytes 2359304 | tf_op jit(solution)/shard_map/ppermute | solution.py:551
  46.2 15.7 %collective-permute-start.6 = (bf16[640,512]{1,0:T(8,128)(2,1)S(1)}, bf16[640,512]{1,0:T(8,128)(2,1)S(1)}, u32[]{:S(2)}, u32[]{:S(2)}) collective-permute-start(bf16[640,512]{1,0:T(8,128)(2,1)S(1)} %get-tuple-element.111), channel_id=1, source_target_pairs={{0,1},{1,0},{2,3},{3,2},{4,5},{5,4},{6,7},{7,6},{8,9},{9,8},{10,11... | collective-permute-start | bytes 1966088 | tf_op jit(solution)/shard_map/ppermute | solution.py:576
  63.3 20.1 %collective-permute-start.11 = (bf16[320,512]{1,0:T(8,128)(2,1)}, bf16[320,512]{1,0:T(8,128)(2,1)}, u32[]{:S(2)}, u32[]{:S(2)}) collective-permute-start(bf16[320,512]{1,0:T(8,128)(2,1)} %get-tuple-element.122), channel_id=1, source_target_pairs={{0,2},{1,3},{2,0},{3,1},{4,6},{5,7},{6,4},{7,5},{8,10},{9,11},{10,... | collective-permute-start | bytes 983048 | tf_op jit(solution)/shard_map/ppermute | solution.py:576
  66.0 21.4 %collective-permute-start.10 = (bf16[768,512]{1,0:T(8,128)(2,1)}, bf16[768,512]{1,0:T(8,128)(2,1)S(1)}, u32[]{:S(2)}, u32[]{:S(2)}) collective-permute-start(bf16[768,512]{1,0:T(8,128)(2,1)} %get-tuple-element.121), channel_id=1, source_target_pairs={{0,1},{1,0},{2,3},{3,2},{4,5},{5,4},{6,7},{7,6},{8,9},{9,8},{10,11... | collective-permute-start | bytes 2359304 | tf_op jit(solution)/shard_map/ppermute | solution.py:576
  67.6 20.6 %collective-permute-start.8 = (bf16[512,512]{1,0:T(8,128)(2,1)}, bf16[512,512]{1,0:T(8,128)(2,1)}, u32[]{:S(2)}, u32[]{:S(2)}) collective-permute-start(bf16[512,512]{1,0:T(8,128)(2,1)} %get-tuple-element.120), channel_id=1, source_target_pairs={{0,1},{1,0},{2,3},{3,2},{4,5},{5,4},{6,7},{7,6},{8,9},{9,8},{10,11... | collective-permute-start | bytes 1572872 | tf_op jit(solution)/shard_map/ppermute | solution.py:576
  79.1 9.1 %collective-permute-start.9 = (bf16[32,512]{1,0:T(8,128)(2,1)S(1)}, bf16[32,512]{1,0:T(8,128)(2,1)}, u32[]{:S(2)}, u32[]{:S(2)}) collective-permute-start(bf16[32,512]{1,0:T(8,128)(2,1)S(1)} %get-tuple-element.115.refs_4_), channel_id=1, source_target_pairs={{0,16},{16,0},{1,17},{17,1},{2,18},{18,2},{3,19},{19,3},{4,20},{20... | collective-permute-start | bytes 98312 | tf_op jit(solution)/shard_map/ppermute | solution.py:551
  86.2 56.2 %collective-permute-start.7 = (bf16[1536,256]{1,0:T(8,128)(2,1)}, bf16[1536,256]{1,0:T(8,128)(2,1)}, u32[]{:S(2)}, u32[]{:S(2)}) collective-permute-start(bf16[1536,256]{1,0:T(8,128)(2,1)} %get-tuple-element.119), channel_id=1, source_target_pairs={{0,16},{16,0},{1,17},{17,1},{2,18},{18,2},{3,19},{19,3},{4,20},{20... | collective-permute-start | bytes 2359304 | tf_op jit(solution)/shard_map/ppermute | solution.py:551
  87.6 7.8 %collective-permute-start.14 = (bf16[384,512]{1,0:T(8,128)(2,1)S(1)}, bf16[384,512]{1,0:T(8,128)(2,1)S(1)}, u32[]{:S(2)}, u32[]{:S(2)}) collective-permute-start(bf16[384,512]{1,0:T(8,128)(2,1)S(1)} %get-tuple-element.129), channel_id=1, source_target_pairs={{0,2},{1,3},{2,0},{3,1},{4,6},{5,7},{6,4},{7,5},{8,10},{9,11},{10,... | collective-permute-start | bytes 1179656 | tf_op jit(solution)/shard_map/ppermute | solution.py:576
  89.3 8.9 %collective-permute-start.12 = (bf16[256,512]{1,0:T(8,128)(2,1)S(1)}, bf16[256,512]{1,0:T(8,128)(2,1)S(1)}, u32[]{:S(2)}, u32[]{:S(2)}) collective-permute-start(bf16[256,512]{1,0:T(8,128)(2,1)S(1)} %get-tuple-element.127), channel_id=1, source_target_pairs={{0,2},{1,3},{2,0},{3,1},{4,6},{5,7},{6,4},{7,5},{8,10},{9,11},{10,... | collective-permute-start | bytes 786440 | tf_op jit(solution)/shard_map/ppermute | solution.py:576
  91.7 8.9 %collective-permute-start.19 = (bf16[160,512]{1,0:T(8,128)(2,1)S(1)}, bf16[160,512]{1,0:T(8,128)(2,1)S(1)}, u32[]{:S(2)}, u32[]{:S(2)}) collective-permute-start(bf16[160,512]{1,0:T(8,128)(2,1)S(1)} %add_body.6.refs_3_.refs_1_), channel_id=1, source_target_pairs={{0,8},{1,9},{2,10},{3,11},{4,12},{5,13},{6,14},{7,15},{8,0},{9,1},... | collective-permute-start | bytes 491528 | tf_op jit(solution)/shard_map/ppermute | solution.py:576
  95.5 9.6 %collective-permute-start.18 = (bf16[192,512]{1,0:T(8,128)(2,1)S(1)}, bf16[192,512]{1,0:T(8,128)(2,1)S(1)}, u32[]{:S(2)}, u32[]{:S(2)}) collective-permute-start(bf16[192,512]{1,0:T(8,128)(2,1)S(1)} %get-tuple-element.135), channel_id=1, source_target_pairs={{0,4},{1,5},{2,6},{3,7},{4,0},{5,1},{6,2},{7,3},{8,12},{9,13},{10,... | collective-permute-start | bytes 589832 | tf_op jit(solution)/shard_map/ppermute | solution.py:576
  98.3 10.8 %collective-permute-start.16 = (bf16[128,512]{1,0:T(8,128)(2,1)S(1)}, bf16[128,512]{1,0:T(8,128)(2,1)S(1)}, u32[]{:S(2)}, u32[]{:S(2)}) collective-permute-start(bf16[128,512]{1,0:T(8,128)(2,1)S(1)} %get-tuple-element.133), channel_id=1, source_target_pairs={{0,4},{1,5},{2,6},{3,7},{4,0},{5,1},{6,2},{7,3},{8,12},{9,13},{10,... | collective-permute-start | bytes 393224 | tf_op jit(solution)/shard_map/ppermute | solution.py:576
  99.9 9.1 %collective-permute-start.17 = (bf16[48,512]{1,0:T(8,128)(2,1)S(1)}, bf16[48,512]{1,0:T(8,128)(2,1)S(1)}, u32[]{:S(2)}, u32[]{:S(2)}) collective-permute-start(bf16[48,512]{1,0:T(8,128)(2,1)S(1)} %get-tuple-element.134.refs_4_), channel_id=1, source_target_pairs={{0,2},{1,3},{2,0},{3,1},{4,6},{5,7},{6,4},{7,5},{8,10},{9,11},{10,... | collective-permute-start | bytes 147464 | tf_op jit(solution)/shard_map/ppermute | solution.py:1020
  100.6 13.5 %collective-permute-start.23 = (bf16[160,512]{1,0:T(8,128)(2,1)S(1)}, bf16[160,512]{1,0:T(8,128)(2,1)S(1)}, u32[]{:S(2)}, u32[]{:S(2)}) collective-permute-start(bf16[160,512]{1,0:T(8,128)(2,1)S(1)} %add_body.7.refs_3_.refs_1_), channel_id=1, source_target_pairs={{0,4},{1,5},{2,6},{3,7},{4,0},{5,1},{6,2},{7,3},{8,12},{9,13},{10,... | collective-permute-start | bytes 491528 | tf_op jit(solution)/shard_map/ppermute | solution.py:576
  105.1 10.2 %collective-permute-start.22 = (bf16[192,512]{1,0:T(8,128)(2,1)S(1)}, bf16[192,512]{1,0:T(8,128)(2,1)S(1)}, u32[]{:S(2)}, u32[]{:S(2)}) collective-permute-start(bf16[192,512]{1,0:T(8,128)(2,1)S(1)} %add_body.8.refs_6_.refs_1_), channel_id=1, source_target_pairs={{0,8},{1,9},{2,10},{3,11},{4,12},{5,13},{6,14},{7,15},{8,0},{9,1},... | collective-permute-start | bytes 589832 | tf_op jit(solution)/shard_map/ppermute | solution.py:576
  109.1 9.2 %collective-permute-start.20 = (bf16[128,512]{1,0:T(8,128)(2,1)S(1)}, bf16[128,512]{1,0:T(8,128)(2,1)S(1)}, u32[]{:S(2)}, u32[]{:S(2)}) collective-permute-start(bf16[128,512]{1,0:T(8,128)(2,1)S(1)} %get-tuple-element.136.refs_3_.refs_2_), channel_id=1, source_target_pairs={{0,8},{1,9},{2,10},{3,11},{4,12},{5,13},{6,14},{7,15},{8,0},{9,1},... | collective-permute-start | bytes 393224 | tf_op jit(solution)/shard_map/ppermute | solution.py:576
  109.2 9.1 %collective-permute-start.21 = (bf16[80,512]{1,0:T(8,128)(2,1)S(1)}, bf16[80,512]{1,0:T(8,128)(2,1)S(1)}, u32[]{:S(2)}, u32[]{:S(2)}) collective-permute-start(bf16[80,512]{1,0:T(8,128)(2,1)S(1)} %get-tuple-element.137.refs_4_), channel_id=1, source_target_pairs={{0,4},{1,5},{2,6},{3,7},{4,0},{5,1},{6,2},{7,3},{8,12},{9,13},{10,... | collective-permute-start | bytes 245768 | tf_op jit(solution)/shard_map/ppermute | solution.py:1020
  114.2 8.5 %collective-permute-start.27 = (bf16[320,512]{1,0:T(8,128)(2,1)S(1)}, bf16[320,512]{1,0:T(8,128)(2,1)S(1)}, u32[]{:S(2)}, u32[]{:S(2)}) collective-permute-start(bf16[320,512]{1,0:T(8,128)(2,1)S(1)} %merge_body.6.refs_3_.refs_1_), channel_id=1, source_target_pairs={{0,2},{1,3},{2,0},{3,1},{4,6},{5,7},{6,4},{7,5},{8,10},{9,11},{10,... | collective-permute-start | bytes 983048 | tf_op jit(solution)/shard_map/ppermute | solution.py:576
  115.4 9.2 %collective-permute-start.26 = (bf16[192,512]{1,0:T(8,128)(2,1)S(1)}, bf16[192,512]{1,0:T(8,128)(2,1)S(1)}, u32[]{:S(2)}, u32[]{:S(2)}) collective-permute-start(bf16[192,512]{1,0:T(8,128)(2,1)S(1)} %add_body.10.refs_6_.refs_1_), channel_id=1, source_target_pairs={{0,4},{1,5},{2,6},{3,7},{4,0},{5,1},{6,2},{7,3},{8,12},{9,13},{10,... | collective-permute-start | bytes 589832 | tf_op jit(solution)/shard_map/ppermute | solution.py:576
  118.4 13.9 %collective-permute-start.25 = (bf16[144,512]{1,0:T(8,128)(2,1)S(1)}, bf16[144,512]{1,0:T(8,128)(2,1)S(1)}, u32[]{:S(2)}, u32[]{:S(2)}) collective-permute-start(bf16[144,512]{1,0:T(8,128)(2,1)S(1)} %get-tuple-element.139.refs_4_), channel_id=1, source_target_pairs={{0,8},{1,9},{2,10},{3,11},{4,12},{5,13},{6,14},{7,15},{8,0},{9,1},... | collective-permute-start | bytes 442376 | tf_op jit(solution)/shard_map/ppermute | solution.py:1020
  123.5 10.8 %collective-permute-start.30 = (bf16[640,512]{1,0:T(8,128)(2,1)}, bf16[640,512]{1,0:T(8,128)(2,1)S(1)}, u32[]{:S(2)}, u32[]{:S(2)}) collective-permute-start(bf16[640,512]{1,0:T(8,128)(2,1)} %merge_body.7.refs_3_.p0), channel_id=1, source_target_pairs={{0,1},{1,0},{2,3},{3,2},{4,5},{5,4},{6,7},{7,6},{8,9},{9,8},{10,11... | collective-permute-start | bytes 1966088 | tf_op jit(solution)/shard_map/ppermute | solution.py:576
  124.6 19.0 %collective-permute-start.35 = (bf16[640,512]{1,0:T(8,128)(2,1)}, bf16[640,512]{1,0:T(8,128)(2,1)}, u32[]{:S(2)}, u32[]{:S(2)}) collective-permute-start(bf16[640,512]{1,0:T(8,128)(2,1)} %merge_body.7.refs_3_.p0), channel_id=1, source_target_pairs={{0,16},{16,0},{1,17},{17,1},{2,18},{18,2},{3,19},{19,3},{4,20},{20... | collective-permute-start | bytes 1966088 | tf_op jit(solution)/shard_map/ppermute | solution.py:551
  132.3 8.1 %collective-permute-start.28 = (bf16[256,512]{1,0:T(8,128)(2,1)S(1)}, bf16[256,512]{1,0:T(8,128)(2,1)S(1)}, u32[]{:S(2)}, u32[]{:S(2)}) collective-permute-start(bf16[256,512]{1,0:T(8,128)(2,1)S(1)} %get-tuple-element.140.after_ref.refs_1_), channel_id=1, source_target_pairs={{0,2},{1,3},{2,0},{3,1},{4,6},{5,7},{6,4},{7,5},{8,10},{9,11},{10,... | collective-permute-start | bytes 786440 | tf_op jit(solution)/shard_map/ppermute | solution.py:576
  134.4 18.0 %collective-permute-start.34 = (bf16[640,512]{1,0:T(8,128)(2,1)S(1)}, bf16[640,512]{1,0:T(8,128)(2,1)}, u32[]{:S(2)}, u32[]{:S(2)}) collective-permute-start(bf16[640,512]{1,0:T(8,128)(2,1)S(1)} %then.3.refs_3_.p0), channel_id=1, source_target_pairs={{0,16},{16,0},{1,17},{17,1},{2,18},{18,2},{3,19},{19,3},{4,20},{20... | collective-permute-start | bytes 1966088 | tf_op jit(solution)/shard_map/ppermute | solution.py:551
  137.2 17.9 %collective-permute-start.33 = (bf16[768,512]{1,0:T(8,128)(2,1)S(1)}, bf16[768,512]{1,0:T(8,128)(2,1)}, u32[]{:S(2)}, u32[]{:S(2)}) collective-permute-start(bf16[768,512]{1,0:T(8,128)(2,1)S(1)} %merge_body.10.refs_3_.p0), channel_id=1, source_target_pairs={{0,16},{16,0},{1,17},{17,1},{2,18},{18,2},{3,19},{19,3},{4,20},{20... | collective-permute-start | bytes 2359304 | tf_op jit(solution)/shard_map/ppermute | solution.py:551
  140.4 20.2 %collective-permute-start.31 = (bf16[768,512]{1,0:T(8,128)(2,1)S(1)}, bf16[768,512]{1,0:T(8,128)(2,1)S(1)}, u32[]{:S(2)}, u32[]{:S(2)}) collective-permute-start(bf16[768,512]{1,0:T(8,128)(2,1)S(1)} %merge_body.10.refs_3_.p0), channel_id=1, source_target_pairs={{0,1},{1,0},{2,3},{3,2},{4,5},{5,4},{6,7},{7,6},{8,9},{9,8},{10,11... | collective-permute-start | bytes 2359304 | tf_op jit(solution)/shard_map/ppermute | solution.py:576
  142.4 15.7 %collective-permute-start.32 = (bf16[512,512]{1,0:T(8,128)(2,1)S(1)}, bf16[512,512]{1,0:T(8,128)(2,1)}, u32[]{:S(2)}, u32[]{:S(2)}) collective-permute-start(bf16[512,512]{1,0:T(8,128)(2,1)S(1)} %merge_body.11.refs_2_.p0), channel_id=1, source_target_pairs={{0,16},{16,0},{1,17},{17,1},{2,18},{18,2},{3,19},{19,3},{4,20},{20... | collective-permute-start | bytes 1572872 | tf_op jit(solution)/shard_map/ppermute | solution.py:551
  143.7 22.8 %collective-permute-start.37 = (bf16[512,512]{1,0:T(8,128)(2,1)S(1)}, bf16[512,512]{1,0:T(8,128)(2,1)}, u32[]{:S(2)}, u32[]{:S(2)}) collective-permute-start(bf16[512,512]{1,0:T(8,128)(2,1)S(1)} %merge_body.11.refs_2_.p0), channel_id=1, source_target_pairs={{0,1},{1,0},{2,3},{3,2},{4,5},{5,4},{6,7},{7,6},{8,9},{9,8},{10,11... | collective-permute-start | bytes 1572872 | tf_op jit(solution)/shard_map/ppermute | solution.py:576
  160.6 9.9 %collective-permute-start.36 = (bf16[768,512]{1,0:T(8,128)(2,1)S(1)}, bf16[768,512]{1,0:T(8,128)(2,1)S(1)}, u32[]{:S(2)}, u32[]{:S(2)}) collective-permute-start(bf16[768,512]{1,0:T(8,128)(2,1)S(1)} %then.4.after_ref.p0), channel_id=1, source_target_pairs={{0,16},{16,0},{1,17},{17,1},{2,18},{18,2},{3,19},{19,3},{4,20},{20... | collective-permute-start | bytes 2359304 | tf_op jit(solution)/shard_map/ppermute | solution.py:551
  (27 other events, 201.7 us)

commit v3 on v1

--- a/solution.py
+++ b/solution.py
@@ -63,7 +63,6 @@
     gout_ref,
     gskip_ref,
     prompt_ref,
-    mask_ref,
     step_w,
     conv_w,
     cond_w,
@@ -77,6 +76,7 @@
     out_b,
     o_stack,
     o_dpre,
+    o_edge,
     o_dsent,
     o_block_keep,
     o_block_give,
@@ -84,19 +84,25 @@
     o_skip_give,
     o_keep,
     o_give,
+    o_keep_c,
+    o_give_c,
     o_vec,
-    o_emb,
     proj,
     keys,
     values,
     d_keys,
     d_values,
     g_out,
-    g_res,
     g_query,
     sums,
     stats,
     count,
+    out_t,
+    query_t,
+    res_t,
+    g_res,
+    g_cond,
+    own_head,
 ):
     tile, slots, nq, subs, tiles, mb_own, micro = cfg
     t = pl.program_id(0)
@@ -119,7 +125,6 @@
         lane = lax.broadcasted_iota(jnp.int32, (items, half), 1).astype(F32)
         angle = when * jnp.exp(lane * F32(-math.log(10000.0) / half))
         emb = jnp.concatenate([jnp.sin(angle), jnp.cos(angle)], axis=1)
-        o_emb[...] = emb
         proj[...] = nn(emb.astype(BF16), step_w[...])
         here = prompt_ref[pl.ds(pl.multiple_of(mb0 * slots * nq, 16), items * nq), :]
         factor = head ** (-0.5)
@@ -128,18 +133,29 @@
         d_keys[...] = jnp.zeros_like(d_keys)
         d_values[...] = jnp.zeros_like(d_values)
         g_out[...] = jnp.zeros_like(g_out)
+        out_t[...] = out_w[...].T
+        query_t[...] = query_w[...].T
+        res_t[...] = res_w[...].T
         g_res[...] = jnp.zeros_like(g_res)
+        g_cond[...] = jnp.zeros_like(g_cond)
+        at_row = rows_iota(HEADS * nq, width) // nq
+        at_lane = lax.broadcasted_iota(jnp.int32, (HEADS * nq, width), 1) // head
+        own_head[...] = jnp.where(at_row == at_lane, 1.0, 0.0).astype(BF16)
         g_query[...] = jnp.zeros_like(g_query)
         sums[...] = jnp.zeros_like(sums)
         stats[...] = jnp.zeros_like(stats)
         count[0] = 0
 
     ext = jnp.concatenate([prev_ref[...], rows_ref[...], next_ref[...]], axis=0)
-    place = rows_iota(tile + 2 * EDGE, width)
     spread = tile + 2 * EDGE
+    place = rows_iota(spread, 128)
+
+    def lanes(mask):
+        return jnp.concatenate([mask] * (width // 128), axis=1)
+
     mixed, behind, ahead, at = [], [], [], []
-    limit = jnp.zeros((size, width), jnp.int32)
-    row = rows_iota(size, width)
+    valid = []
+    row = rows_iota(tile, 128)
     for k in range(subs):
         mb, slot, lim, prev_in, next_in = plan(
             section * tiles + t * subs + k, tile, slots, buckets, item_len
@@ -150,14 +166,14 @@
         hi = jnp.where(next_in, tile + 2 * EDGE, tile + EDGE)
         hi = jnp.minimum(hi, lim + EDGE)
         part = ext[k * tile : k * tile + spread].astype(F32) + proj[pl.ds(item, 1), :]
-        part = jnp.where((place >= lo) & (place < hi), part, 0.0)
+        part = part * lanes(jnp.where((place >= lo) & (place < hi), 1.0, 0.0))
         mixed.append(part[EDGE : EDGE + tile])
         behind.append(pltpu.roll(part, SHIFT, 0)[EDGE : EDGE + tile].astype(BF16))
         ahead.append(pltpu.roll(part, spread - SHIFT, 0)[EDGE : EDGE + tile].astype(BF16))
-        limit = jnp.where(row >= k * tile, lim + k * tile, limit)
+        valid.append(jnp.where(row < lim, 1.0, 0.0))
         count[0] += jnp.clip(lim, 0, tile)
     mixed = jnp.concatenate(mixed, axis=0)
-    valid = row < limit
+    valid = lanes(jnp.concatenate(valid, axis=0))
     stacked = jnp.concatenate(
         [jnp.concatenate(behind, axis=0), mixed.astype(BF16), jnp.concatenate(ahead, axis=0)],
         axis=1,
@@ -171,8 +187,8 @@
     slope_a = s - both * a
     slope_s = both - both * s
     branch = nn(gate, res_w[...]) + res_b[...]
-    res_part = jnp.where(valid, branch[:, :width], 0.0)
-    skip = jnp.where(valid, branch[:, width:], 0.0).astype(BF16)
+    res_part = branch[:, :width] * valid
+    skip = (branch[:, width:] * valid).astype(BF16)
     o_skip_keep[...] = jnp.where(keep_left, skip[:, :half], skip[:, half:])
     o_skip_give[...] = jnp.where(keep_left, skip[:, half:], skip[:, :half])
     hidden = (mixed + res_part) * ISQ2
@@ -182,7 +198,7 @@
     stats[1] += col_sums(res_part * res_part)
 
     query = nn(sent, query_w[...]).astype(BF16)
-    mask = mask_ref[...]
+    mask = own_head[...]
     probs, probs_low, key_bd, value_bd, attended = [], [], [], [], []
     for k in range(subs):
         key_bd.append(jnp.concatenate([keys[pl.ds(at[k], nq), :]] * HEADS, axis=0) * mask)
@@ -195,17 +211,17 @@
     attended = jnp.concatenate(attended, axis=0)
     film = nn(attended, out_w[...]) + out_b[...]
     scale = film[:, :width]
-    change = jnp.where(valid, sent_f * scale + film[:, width:], 0.0)
+    change = (sent_f * scale + film[:, width:]) * valid
     block = (sent_f + change).astype(BF16)
     o_block_keep[...] = jnp.where(keep_left, block[:, :half], block[:, half:])
     o_block_give[...] = jnp.where(keep_left, block[:, half:], block[:, :half])
     stats[2] += col_sums(change * change)
 
-    gy = jnp.where(valid, gout_ref[...].astype(F32), 0.0)
+    gy = gout_ref[...].astype(F32) * valid
     d_film = jnp.concatenate([(gy * sent_f).astype(BF16), gy.astype(BF16)], axis=1)
     sums[2] += col_sums(d_film.astype(F32))
     g_out[...] += tn(attended, d_film)
-    d_att = nt(d_film, out_w[...]).astype(BF16)
+    d_att = nn(d_film, out_t[...]).astype(BF16)
     low_lane = lax.broadcasted_iota(jnp.int32, (nq, 2 * head), 1) < head
 
     def own_heads(x):
@@ -229,20 +245,25 @@
         d_query.append(tn(d_scores, key_bd[k]).astype(BF16))
     d_query = jnp.concatenate(d_query, axis=0)
     g_query[...] += tn(sent, d_query)
-    d_sent = (gy * (1.0 + scale) + nt(d_query, query_w[...])).astype(BF16)
+    d_sent = (gy * (1.0 + scale) + nn(d_query, query_t[...])).astype(BF16)
     o_dsent[...] = d_sent
 
-    d_res = jnp.where(valid, d_sent.astype(F32) * ISQ2, 0.0).astype(BF16)
-    gs = jnp.where(valid, gskip_ref[...].astype(F32), 0.0).astype(BF16)
+    d_res = (d_sent.astype(F32) * ISQ2).astype(BF16)
+    gs = (gskip_ref[...].astype(F32) * valid).astype(BF16)
     d_branch = jnp.concatenate([d_res, gs], axis=1)
     sums[1] += col_sums(d_branch.astype(F32))
     g_res[...] += tn(gate, d_branch)
-    d_gate = nt(d_branch, res_w[...])
+    d_gate = nn(d_branch, res_t[...])
     d_pre = jnp.concatenate(
         [(d_gate * slope_a).astype(BF16), (d_gate * slope_s).astype(BF16)], axis=1
     )
     sums[0] += col_sums(d_pre.astype(F32))
     o_dpre[...] = d_pre
+    g_cond[...] += tn(cond_ref[...], d_pre)
+
+    @pl.when(t == 0)
+    def _():
+        o_edge[:EDGE, :] = d_pre[:EDGE, :]
 
     @pl.when(t == tiles // subs - 1)
     def _():
@@ -251,19 +272,23 @@
         mine = pl.multiple_of(section * half, half)
         theirs = pl.multiple_of(half - section * half, half)
 
-        def put(i, ref, left):
-            o_keep[i] = ref[pl.ds(mine, half), pl.ds(left, width)].astype(BF16)
-            o_give[i] = ref[pl.ds(theirs, half), pl.ds(left, width)].astype(BF16)
+        o_edge[EDGE:, :] = d_pre[size - EDGE :, :]
+
+        def put(i, ref, left, keep=o_keep, give=o_give):
+            keep[i] = ref[pl.ds(mine, half), pl.ds(left, width)].astype(BF16)
+            give[i] = ref[pl.ds(theirs, half), pl.ds(left, width)].astype(BF16)
 
         put(0, g_out, 0)
         put(1, g_out, width)
-        put(2, g_res, 0)
-        put(3, g_res, width)
+        put(2, g_query, 0)
+        g_query[...] = tn(here, (d_keys[...] * factor).astype(BF16))
+        put(3, g_query, 0)
+        g_query[...] = tn(here, d_values[...].astype(BF16))
         put(4, g_query, 0)
-        g_query[...] = tn(here, (d_keys[...] * factor).astype(BF16))
-        put(5, g_query, 0)
-        g_query[...] = tn(here, d_values[...].astype(BF16))
-        put(6, g_query, 0)
+        put(0, g_res, 0, o_keep_c, o_give_c)
+        put(1, g_res, width, o_keep_c, o_give_c)
+        put(2, g_cond, 0, o_keep_c, o_give_c)
+        put(3, g_cond, width, o_keep_c, o_give_c)
         for i in range(3):
             line = jnp.sum(sums[i], axis=0, keepdims=True)
             o_vec[2 * i : 2 * i + 1, :] = line[:, :width]
@@ -275,21 +300,12 @@
         o_vec[9:16, :] = jnp.where(lane < 8, digits, 0).astype(F32)
 
 
-def weight_kernel(cfg, sec_ref, stack_ref, cond_ref, dpre_ref, o_keep, o_give, acc):
-    taps = cfg
-    i = pl.program_id(0)
+def weight_kernel(sec_ref, left_ref, dpre_ref, *refs):
+    o_keep, o_give, acc = refs[-3:]
     section = sec_ref[0]
     width = acc.shape[0]
     half = width // 2
-
-    @pl.when(i < taps)
-    def _():
-        acc[...] = tn(stack_ref[...], dpre_ref[...])
-
-    @pl.when(i == taps)
-    def _():
-        acc[...] = tn(cond_ref[...], dpre_ref[...])
-
+    acc[...] = tn(left_ref[...], dpre_ref[...])
     mine = pl.multiple_of(section * half, half)
     theirs = pl.multiple_of(half - section * half, half)
     for side in range(2):
@@ -308,7 +324,7 @@
     other_ref,
     dsent_ref,
     conv_w,
-    emb_ref,
+    steps,
     vec_ref,
     after_ref,
     o_keep,
@@ -316,43 +332,42 @@
     o_rows,
     d_step,
 ):
-    tile, slots, subs, tiles, mb_own, micro = cfg
+    tile, slots, subs, tiles, micro = cfg
     t = pl.program_id(0)
     section = sec_ref[0]
-    size = subs * tile
     width = dsent_ref.shape[1]
     half = width // 2
-    mb0 = section * (micro - mb_own)
+    count = tiles // subs
 
     @pl.when(t == 0)
     def _():
         d_step[...] = jnp.zeros_like(d_step)
 
-    steps = tiles // subs
     before = jnp.where(t == 0, other_ref[EDGE:, :], prev_ref[...])
-    after = jnp.where(t == steps - 1, other_ref[:EDGE, :], next_ref[...])
+    after = jnp.where(t == count - 1, other_ref[:EDGE, :], next_ref[...])
     ext = jnp.concatenate([before, dpre_ref[...], after], axis=0)
     spread = tile + 2 * EDGE
-    place = rows_iota(spread, 2 * width)
-    ahead, behind, item = [], [], []
-    limit = jnp.zeros((size, width), jnp.int32)
-    row = rows_iota(size, width)
+    place = rows_iota(spread, 128)
+    row = rows_iota(tile, 128)
+    ahead, behind, valid, item = [], [], [], []
     for k in range(subs):
         mb, slot, lim, prev_in, next_in = plan(
             section * tiles + t * subs + k, tile, slots, buckets, item_len
         )
-        item.append((mb - mb0) * slots + slot)
+        item.append(mb * slots + slot)
         lo = jnp.where(prev_in, 0, EDGE)
         hi = jnp.where(next_in, spread, tile + EDGE)
+        here = jnp.where((place >= lo) & (place < hi), 1.0, 0.0)
         part = ext[k * tile : k * tile + spread].astype(F32)
-        part = jnp.where((place >= lo) & (place < hi), part, 0.0)
+        part = part * jnp.concatenate([here] * (2 * width // 128), axis=1)
         ahead.append(pltpu.roll(part, spread - SHIFT, 0)[EDGE : EDGE + tile].astype(BF16))
         behind.append(pltpu.roll(part, SHIFT, 0)[EDGE : EDGE + tile].astype(BF16))
-        limit = jnp.where(row >= k * tile, lim + k * tile, limit)
+        valid.append(jnp.where(row < lim, 1.0, 0.0))
+    valid = jnp.concatenate([jnp.concatenate(valid, axis=0)] * (width // 128), axis=1)
     d_in = nt(jnp.concatenate(ahead, axis=0), conv_w[:width, :])
     d_in += nt(dpre_ref[...], conv_w[width : 2 * width, :])
     d_in += nt(jnp.concatenate(behind, axis=0), conv_w[2 * width :, :])
-    d_mixed = jnp.where(row < limit, dsent_ref[...].astype(F32) * ISQ2 + d_in, 0.0)
+    d_mixed = (dsent_ref[...].astype(F32) * ISQ2 + d_in) * valid
     for k in range(subs):
         line = jnp.sum(col_sums(d_mixed[k * tile : (k + 1) * tile]), axis=0, keepdims=True)
         d_step[pl.ds(item[k], 1), :] += line
@@ -360,10 +375,19 @@
     o_keep[...] = jnp.where(section == 0, low[:, :half], low[:, half:])
     o_give[...] = jnp.where(section == 0, low[:, half:], low[:, :half])
 
-    @pl.when(t == steps - 1)
+    @pl.when(t == count - 1)
     def _():
-        both = jnp.concatenate([emb_ref[...], d_step[...], vec_ref[...]], axis=0)
-        o_rows[...] = both.astype(BF16)
+        items = micro * slots
+        group = d_step.shape[0]
+        lane = lax.broadcasted_iota(jnp.int32, (1, width), 1)
+        index = jnp.zeros((1, width), jnp.int32)
+        for i in range(items):
+            index = jnp.where(lane == i, steps[i // slots, i % slots], index)
+        index = jnp.where(section == 0, index, 0)
+        d_step[items : items + 1, :] = (index >> 5).astype(F32)
+        d_step[items + 1 : items + 2, :] = (index & 31).astype(F32)
+        o_rows[:group, :] = d_step[...].astype(BF16)
+        o_rows[group:, :] = vec_ref[...].astype(BF16)
 
 
 SMALL = pl.CostEstimate(flops=1024, bytes_accessed=1024, transcendentals=0)
@@ -436,16 +460,16 @@
 
 
 def then_kernel(x_ref, after_ref, out_ref):
-    pass
+    out_ref[...] = x_ref[...]
 
 
 def then(x, after):
     return pl.pallas_call(
         then_kernel,
-        in_specs=[ANYWHERE, ANYWHERE],
-        out_specs=ANYWHERE,
+        in_specs=[IN_VMEM, ANYWHERE],
+        out_specs=IN_VMEM,
         out_shape=jax.ShapeDtypeStruct(x.shape, x.dtype),
-        input_output_aliases={0: 0},
+        compiler_params=pltpu.CompilerParams(vmem_limit_bytes=16 * 1024 * 1024),
         cost_estimate=SMALL,
         name="then",
     )(x, after)
@@ -530,20 +554,21 @@
         self.step = 0
 
     def turn(self, after, more=(), cost=LARGE):
-        sums, last = self.sums, self.sums.levels - 1
+        sums = self.sums
+        halved = sums.levels - 2
         at = self.step
         self.step += 1
         rows, width = self.held.shape
-        if at < last:
+        if at < halved:
             work = (split_body, sums.bit(at), self.held, self.got, [struct(rows // 2, width)] * 2)
             self.held, give, *rest = pair_call([work, *more], after, cost)
             self.got = sums.send(give, at)
-        elif at <= last + 1:
+        elif at <= halved + 2:
             work = (add_body, sums.bit(0), self.held, self.got, [struct(rows, width)])
             self.held, *rest = pair_call([work, *more], after, cost)
-            self.got = sums.send(self.held, at if at == last else last - 1)
+            self.got = sums.send(self.held, at if at < halved + 2 else halved - 1)
         else:
-            back = 2 * last + 1 - at
+            back = 2 * halved + 2 - at
             work = (merge_body, sums.bit(back), self.held, self.got, [struct(2 * rows, width)])
             self.held, *rest = pair_call([work, *more], after, cost)
             self.got = sums.send(self.held, back - 1)
@@ -551,17 +576,21 @@
 
     @property
     def turns(self):
-        return 2 * self.sums.levels - 1
-
-    def spread(self, kinds, first):
-        runs = self.sums.runs()
-        *outs, done = place(runs, (0, 2), (self.held, swap(self.held)), kinds, first)
-        self.got = then(self.got, done)
-        return place(runs, (1, 3), (self.got, swap(self.got)), kinds, done, outs)
-
-
-def place_kernel(which, spots, runs, p0, p1, after_ref, *refs):
-    count = len(set(spot[0] for spot in spots if spot is not None))
+        return 2 * self.sums.levels - 2
+
+    def early(self, shapes, spots, after, outs=()):
+        return place(self.sums.runs(), (0, 2), (self.held, swap(self.held)), shapes, spots, after, outs)
+
+    def arrive(self, after):
+        self.got = then(self.got, after)
+        self.last = swap(self.got)
+        return self.got
+
+    def late(self, shapes, spots, after, outs):
+        return place(self.sums.runs(), (1, 3), (self.got, self.last), shapes, spots, after, outs)
+
+
+def place_kernel(which, spots, count, runs, p0, p1, after_ref, *refs):
     outs, (mark, buf, sems) = refs[-3 - count : -3], refs[-3:]
     mark[...] = jnp.zeros_like(mark)
     rows = buf.shape[1]
@@ -594,27 +623,29 @@
                         copy.start()
 
 
-def place(runs, which, pieces, kinds, after, outs=()):
+def spots_of(targets, width):
+    quarter = width // 4
+    spots = []
+    for section in range(2):
+        for k, row, col in targets:
+            for u in range(2):
+                spots.append((k, row + (2 * section + u) * quarter, col))
+    return spots
+
+
+def place(runs, which, pieces, shapes, spots, after, outs=()):
     length, width = pieces[0].shape
     quarter = width // 4
     per_run = length // quarter
-    spots, shapes = [None] * (4 * per_run), []
-    first = 0
-    for k, count in enumerate(kinds):
-        across = min(count, 2)
-        for i in range(count):
-            for section in range(2):
-                for u in range(2):
-                    w = section * 2 * per_run + 2 * (first + i) + u
-                    row = (i // across) * width + (2 * section + u) * quarter
-                    spots[w] = (k, row, (i % across) * width)
-        shapes.append(struct(width * max(count // 2, 1), across * width, F32))
-        first += count
+    half = len(spots) // 2
+    full = [None] * (4 * per_run)
+    full[:half] = spots[:half]
+    full[2 * per_run : 2 * per_run + half] = spots[half:]
     return pl.pallas_call(
-        functools.partial(place_kernel, which, spots),
+        functools.partial(place_kernel, which, full, len(shapes)),
         in_specs=[IN_SMEM] + [IN_VMEM] * 2 + [ANYWHERE] + [IN_HBM] * len(outs),
-        out_specs=[IN_HBM] * len(kinds) + [IN_VMEM],
-        out_shape=shapes + [struct(8, 128, F32)],
+        out_specs=[IN_HBM] * len(shapes) + [IN_VMEM],
+        out_shape=list(shapes) + [struct(8, 128, F32)],
         input_output_aliases={4 + k: k for k in range(len(outs))},
         scratch_shapes=[
             pltpu.VMEM((2 * per_run, quarter, width), F32),
@@ -626,12 +657,33 @@
     )(runs, *pieces, after, *outs)
 
 
-def step_kernel(group, rows_ref, after_ref, out_ref, mark):
+def step_kernel(items, group, rows_ref, after_ref, out_ref, o_low, o_res, o_out, o_levels, mark):
     mark[...] = jnp.zeros_like(mark)
     width = rows_ref.shape[1]
-    rows = rows_ref[: rows_ref.shape[0] - EDGE, :].astype(F32).reshape(-1, 2 * group, width)
-    emb = rows[:, :group].reshape(-1, width).astype(BF16)
-    out_ref[...] = tn(emb, rows[:, group:].reshape(-1, width).astype(BF16))
+    half = width // 2
+    rows = rows_ref[: rows_ref.shape[0] - EDGE, :].astype(F32).reshape(-1, group, width)
+    lanes = (rows.shape[0], group, 128)
+    index = 32.0 * rows[:, items : items + 1, :128] + rows[:, items + 1 : items + 2, :128]
+    diagonal = lax.broadcasted_iota(jnp.int32, lanes, 1) == lax.broadcasted_iota(
+        jnp.int32, lanes, 2
+    )
+    index = jnp.sum(jnp.where(diagonal, index, 0.0), axis=2, keepdims=True)
+    index = index.reshape(-1, 1)
+    lane = lax.broadcasted_iota(jnp.int32, (index.shape[0], half), 1).astype(F32)
+    angle = index * jnp.exp(lane * F32(-math.log(10000.0) / half))
+    emb = jnp.concatenate([jnp.sin(angle), jnp.cos(angle)], axis=1)
+    used = lax.broadcasted_iota(jnp.int32, rows.shape, 1) < items
+    sums = jnp.where(used, rows, 0.0).reshape(-1, width)
+    out_ref[...] = tn(emb.astype(BF16), sums.astype(BF16))
+    vec = rows_ref[rows_ref.shape[0] - EDGE :, :].astype(F32)
+    for i, out in enumerate((o_low, o_res, o_out)):
+        out[:, :width] = vec[2 * i : 2 * i + 1, :]
+        out[:, width:] = vec[2 * i + 1 : 2 * i + 2, :]
+    digit = lax.broadcasted_iota(jnp.int32, (1, width), 1)
+    weight = jnp.where(digit < 8, 1 << (3 * jnp.minimum(digit, 8)), 0).astype(F32)
+    frames = jnp.sum(vec[9:10, :] * weight, axis=1, keepdims=True) * width
+    sizes = jnp.sum(vec[6:9, :], axis=1, keepdims=True)
+    o_levels[...] = jnp.broadcast_to(jnp.sqrt(sizes / frames), o_levels.shape)
 
 
 def padded(x, rows):
@@ -680,10 +732,6 @@
     wide = 2 * width
     conv_flat = conv_w.reshape(taps * width, wide)
     flat_prompt = prompt.reshape(-1, width)
-    head = width // HEADS
-    mask = (
-        jnp.arange(HEADS * nq)[:, None] // nq == jnp.arange(width)[None, :] // head
-    ).astype(BF16)
 
     def whole(x):
         n = x.ndim
@@ -724,10 +772,15 @@
     def shape(*dims, dtype=BF16):
         return jax.ShapeDtypeStruct(dims, dtype)
 
-    macs = own * width * width * 25
+    def blocks_of(n):
+        return const((n, half, width)), shape(n, half, width)
+
+    film_spec, film_shape = blocks_of(5)
+    side_spec, side_shape = blocks_of(4)
     (
         stack,
         d_pre,
+        edge,
         d_sent,
         block_keep,
         block_give,
@@ -735,8 +788,9 @@
         skip_give,
         keep_a,
         give_a,
+        keep_c,
+        give_c,
         vec,
-        emb,
     ) = pl.pallas_call(
         functools.partial(forward_kernel, (tile, slots, nq, subs, tiles, mb_own, micro)),
         grid_spec=pltpu.PrefetchScalarGridSpec(
@@ -744,12 +798,12 @@
             grid=(grid,),
             in_specs=[smem, smem, smem, prev_chip, chip_tile(width), next_chip]
             + [chip_tile(width)] * 3
-            + [whole(flat_prompt), whole(mask)]
+            + [whole(flat_prompt)]
             + [whole(w) for w in weights],
-            out_specs=[own_tile(taps * width), own_tile(wide), own_tile(width)]
+            out_specs=[own_tile(taps * width), own_tile(wide), const((2 * EDGE, wide))]
+            + [own_tile(width)]
             + [own_tile(half)] * 4
-            + [const((7, half, width)), const((7, half, width)), const((16, width))]
-            + [const((items, width))],
+            + [film_spec, film_spec, side_spec, side_spec, const((16, width))],
             scratch_shapes=[
                 pltpu.VMEM((items, width), F32),
                 pltpu.VMEM((items * nq, width), BF16),
@@ -757,25 +811,32 @@
                 pltpu.VMEM((items * nq, width), F32),
                 pltpu.VMEM((items * nq, width), F32),
                 pltpu.VMEM((width, wide), F32),
-                pltpu.VMEM((width, wide), F32),
                 pltpu.VMEM((width, width), F32),
                 pltpu.VMEM((3, 8, wide), F32),
                 pltpu.VMEM((3, 8, width), F32),
                 pltpu.SMEM((1,), jnp.int32),
+                pltpu.VMEM((wide, width), BF16),
+                pltpu.VMEM((width, width), BF16),
+                pltpu.VMEM((wide, width), BF16),
+                pltpu.VMEM((width, wide), F32),
+                pltpu.VMEM((width, wide), F32),
+                pltpu.VMEM((HEADS * nq, width), BF16),
             ],
         ),
         out_shape=[
             shape(own, taps * width),
             shape(own, wide),
+            shape(2 * EDGE, wide),
             shape(own, width),
             shape(own, half),
             shape(own, half),
             shape(own, half),
             shape(own, half),
-            shape(7, half, width),
-            shape(7, half, width),
+            film_shape,
+            film_shape,
+            side_shape,
+            side_shape,
             shape(16, width, dtype=F32),
-            shape(items, width, dtype=F32),
         ],
         compiler_params=pltpu.CompilerParams(vmem_limit_bytes=VMEM),
         cost_estimate=LARGE,
@@ -792,61 +853,49 @@
         output_gradient,
         grad_skip,
         flat_prompt,
-        mask,
         *weights,
     )
-
-    edge = swap(jnp.concatenate([d_pre[:EDGE], d_pre[own - EDGE :]], axis=0))
 
     bits = list(range(lax.axis_size("dp").bit_length() - 1))
     other = [bits[1], bits[0]] + bits[2:]
     if len(other) > 3:
         other[-2], other[-1] = other[-1], other[-2]
     sums = Sum((bits, other))
-    unit = 16 * lax.axis_size("dp") // 2
-
-    film_blocks = 7
-    rows_a = -(-film_blocks * half // unit) * unit
-    batch_a = Batch(
-        sums,
-        padded(keep_a.reshape(-1, width), rows_a),
-        padded(give_a.reshape(-1, width), rows_a),
-    )
-    conv_blocks = 2 * (taps + 1)
-    pair = pl.BlockSpec((2, half, width), lambda i, *_: (i, 0, 0))
+    unit = 16 * lax.axis_size("dp") // 4
+
+    def batch(keep, give):
+        rows = keep.shape[0] * half
+        rows = -(-rows // unit) * unit
+        return Batch(
+            sums, padded(keep.reshape(-1, width), rows), padded(give.reshape(-1, width), rows)
+        )
+
+    batch_a, batch_c = batch(keep_a, give_a), batch(keep_c, give_c)
+    block_got, skip_got, other_edge = swap(block_give), swap(skip_give), swap(edge)
+    spec = pl.BlockSpec((2, half, width), lambda i, *_: (i, 0, 0))
     keep_b, give_b = pl.pallas_call(
-        functools.partial(weight_kernel, taps),
+        weight_kernel,
         grid_spec=pltpu.PrefetchScalarGridSpec(
             num_scalar_prefetch=1,
-            grid=(taps + 1,),
-            in_specs=[
-                pl.BlockSpec((own, width), lambda i, s: (0, jnp.minimum(i, taps - 1))),
-                pl.BlockSpec(
-                    (own, width), lambda i, s: (s[0], 0), pipeline_mode=pl.Buffered(1)
-                ),
-                whole(d_pre),
-            ],
-            out_specs=[pair, pair],
+            grid=(taps,),
+            in_specs=[pl.BlockSpec((own, width), lambda i, *_: (0, i)), whole(d_pre)],
+            out_specs=[spec, spec],
             scratch_shapes=[pltpu.VMEM((width, wide), F32)],
         ),
-        out_shape=[shape(conv_blocks, half, width)] * 2,
+        out_shape=[shape(2 * taps, half, width)] * 2,
         compiler_params=pltpu.CompilerParams(vmem_limit_bytes=KB_VMEM),
         cost_estimate=LARGE,
         name="weights",
-    )(sec, stack, conditioning, d_pre)
-
-    rows_b = -(-conv_blocks * half // unit) * unit
-    batch_b = Batch(
-        sums,
-        padded(keep_b.reshape(-1, width), rows_b),
-        padded(give_b.reshape(-1, width), rows_b),
-    )
+    )(sec, stack, d_pre)
+    batch_b = batch(keep_b, give_b)
     (after,) = batch_a.turn(keep_b)
+    (after,) = batch_c.turn(after)
     (after,) = batch_b.turn(after)
 
+    group = -(-(micro * slots + 2) // 16) * 16
     rows_last = own // EDGE - 1
     in_keep, in_give, rows_now = pl.pallas_call(
-        functools.partial(back_kernel, (tile, slots, subs, tiles, mb_own, micro)),
+        functools.partial(back_kernel, (tile, slots, subs, tiles, micro)),
         grid_spec=pltpu.PrefetchScalarGridSpec(
             num_scalar_prefetch=1,
             grid=(grid,),
@@ -858,17 +907,17 @@
                 pl.BlockSpec(
                     (EDGE, wide), lambda t, *_: (jnp.minimum((t + 1) * per, rows_last), 0)
                 ),
-                whole(edge),
+                whole(other_edge),
                 own_tile(width),
                 whole(conv_flat),
-                whole(emb),
+                smem,
                 whole(vec),
                 ANYWHERE,
             ],
-            out_specs=[own_tile(half), own_tile(half), const((2 * items + EDGE, width))],
-            scratch_shapes=[pltpu.VMEM((items, width), F32)],
+            out_specs=[own_tile(half), own_tile(half), const((group + EDGE, width))],
+            scratch_shapes=[pltpu.VMEM((group, width), F32)],
         ),
-        out_shape=[shape(own, half), shape(own, half), shape(2 * items + EDGE, width)],
+        out_shape=[shape(own, half), shape(own, half), shape(group + EDGE, width)],
         compiler_params=pltpu.CompilerParams(vmem_limit_bytes=KC_VMEM),
         cost_estimate=LARGE,
         name="back",
@@ -879,54 +928,73 @@
         d_pre,
         d_pre,
         d_pre,
-        edge,
+        other_edge,
         d_sent,
         conv_flat,
-        emb,
+        step_index,
         vec,
         after,
     )
-
-    block_got, skip_got, in_got = swap(block_give), swap(skip_give), swap(in_give)
-    gathers = sums.levels + 1
-    rows_got, rows_bit = swap(rows_now), sec
+    in_got = swap(in_give)
 
     block_out, skip_out, after = join(
         sec, rows_now, (block_keep, block_got), (skip_keep, skip_got)
     )
-    done = 0
-    for name in "ab" * (batch_a.turns - 1):
-        if name == "b" and done < gathers:
-            n = 2 * rows_now.shape[0] - EDGE
-            work = (gather_body, rows_bit, rows_now, rows_got, [struct(n, width)])
-            after, rows_now = batch_b.turn(after, [work])
-            if done < sums.levels:
-                route = [(d, d ^ (1 << done)) for d in range(sums.chips)]
+    rows_got, rows_bit, gathered = swap(rows_now), sec, 0
+    batches = {"a": batch_a, "b": batch_b, "c": batch_c}
+    first = True
+    for name in "ac-b" * (batch_a.turns - 1):
+        if name == "-":
+            first = False
+            continue
+        turner = batches[name]
+        if name == "b" and gathered <= sums.levels:
+            n = rows_now.shape[0]
+            work = (add_body, rows_bit, rows_now, rows_got, [struct(n, width)])
+            if gathered:
+                work = (gather_body, rows_bit, rows_now, rows_got, [struct(2 * n - EDGE, width)])
+            after, rows_now = turner.turn(after, [work])
+            if gathered < sums.levels:
+                route = [(d, d ^ (1 << gathered)) for d in range(sums.chips)]
                 rows_got = lax.ppermute(rows_now, "dp", route)
-                rows_bit = ((sums.chip >> done) & 1).astype(jnp.int32).reshape(1)
-            done += 1
+                rows_bit = ((sums.chip >> gathered) & 1).astype(jnp.int32).reshape(1)
+            gathered += 1
         else:
-            cost = LARGE if done else SMALL
-            (after,) = (batch_a if name == "a" else batch_b).turn(after, cost=cost)
-
-    in_grad, mark = join(sec, after, (in_keep, in_got))
-    g_step, mark = pl.pallas_call(
-        functools.partial(step_kernel, items),
+            (after,) = turner.turn(after, cost=SMALL if first else LARGE)
+
+    line = struct(1, wide, F32)
+    g_step, g_convb, g_resb, g_outb, levels, mark = pl.pallas_call(
+        functools.partial(step_kernel, micro * slots, group),
         in_specs=[IN_VMEM, ANYWHERE],
-        out_specs=[IN_VMEM, IN_VMEM],
-        out_shape=[struct(width, width, F32), struct(8, 128, F32)],
+        out_specs=[IN_VMEM] * 6,
+        out_shape=[struct(width, width, F32), line, line, line]
+        + [struct(3, 128, F32), struct(8, 128, F32)],
         compiler_params=pltpu.CompilerParams(vmem_limit_bytes=24 * 1024 * 1024),
-        cost_estimate=SMALL,
+        cost_estimate=LARGE,
         name="step_grad",
-    )(rows_now, mark)
-    g_out, g_res, g_query, g_key, g_value, mark = batch_a.spread((2, 2, 1, 1, 1), mark)
-    g_conv, g_cond, mark = batch_b.spread((2 * taps, 2), mark)
-    vec = rows_now[rows_now.shape[0] - EDGE :].astype(F32)
-    g_conv = g_conv.reshape(conv_w.shape)
-    g_convb, g_resb, g_outb = (vec[2 * i : 2 * i + 2].reshape(wide) for i in range(3))
-    sizes = jnp.sum(vec[6:9], axis=1)
-    frames_valid = sum(vec[9, i] * (1 << 3 * i) for i in range(8))
-    levels = jnp.sqrt(sizes / (frames_valid * width))
+    )(rows_now, after)
+    in_grad, mark = join(sec, mark, (in_keep, in_got))
+
+    def pairs(k, count, base=0):
+        return [(k, base + i * width, col) for i in range(count) for col in (0, width)]
+
+    square, tall = struct(width, width, F32), struct(width, wide, F32)
+    shapes_a = [tall, square, square, square]
+    spots_a = spots_of(pairs(0, 1) + [(k, 0, 0) for k in (1, 2, 3)], width)
+    shapes_b, spots_b = [struct(taps * width, wide, F32)], spots_of(pairs(0, taps), width)
+    shapes_c, spots_c = [tall, tall], spots_of(pairs(0, 1) + pairs(1, 1), width)
+    *outs_a, mark = batch_a.early(shapes_a, spots_a, mark)
+    *outs_c, mark = batch_c.early(shapes_c, spots_c, mark)
+    *outs_b, mark = batch_b.early(shapes_b, spots_b, mark)
+    mark = batch_b.arrive(batch_c.arrive(batch_a.arrive(mark)))
+    *outs_a, mark = batch_a.late(shapes_a, spots_a, mark, outs_a)
+    *outs_c, mark = batch_c.late(shapes_c, spots_c, mark, outs_c)
+    *outs_b, mark = batch_b.late(shapes_b, spots_b, mark, outs_b)
+    g_out, g_query, g_key, g_value = outs_a
+    g_conv = outs_b[0].reshape(conv_w.shape)
+    g_res, g_cond = outs_c
+    g_convb, g_resb, g_outb = (x.reshape(wide) for x in (g_convb, g_resb, g_outb))
+    levels = levels[:, 0]
     return (
         block_out,
         skip_out,

time: 193 us -> 179 us (0.927)
  waiting for transfers between devices: 50.6 us -> 38.1 us
  starting transfers between devices: 31.8 us -> 42 us
  local copies, waits for them, and re-layouts: 17.4 us -> 7.79 us
  Pallas kernels: 84.3 us -> 89.9 us
  between operations: 6.21 us -> 1.12 us
  other arithmetic: 2.19 us -> 0.08 us
    ppermute x14 -> x18, starting transfers between devices: 20.1 us -> 32.9 us  [send(): return lax.ppermute(x, ('section', 'dp'), route)]
    ppermute x14 -> x18, waiting for transfers between devices: 34.8 us -> 24.7 us  [send(): return lax.ppermute(x, ('section', 'dp'), route)]
    unnamed x56 -> x34, local copies, waits for them, and re-layouts: 16 us -> 7.16 us
    pallas_call x14 -> x18, Pallas kernels: 7.7 us -> 10.1 us  [pair_call(): pl.pallas_call(functools.partial(pair_kernel, [w[0] for w in works], outs...]
    ppermute x4, starting transfers between devices: 7.86 us -> 5.85 us  [on_device(): rows_got = lax.ppermute(rows_now, 'dp', route)]
    pallas_call x8 -> x11, Pallas kernels: 25.4 us -> 26.5 us  [the longest x6 14 us: place(): pl.pallas_call(functools.partial(place_kernel, which, full, len(shapes)),...]
  transfers between devices with their start and end apart: 29 -> 36, of which waited for: 9 -> 10; matrix products, arithmetic and copies ran while one was open for 2% -> 0% of each run, Pallas kernels for 23% -> 27%
where the time goes in v3:
time: 179 us
  Pallas kernels  89.9 us (50%)
  starting transfers between devices  42 us (23%)
  waiting for transfers between devices  38.1 us (21%)
  local copies, waits for them, and re-layouts  7.79 us (4%)
    pallas_call x1, Pallas kernels, on_device(): pl.pallas_call(functools.partial(forward_kernel, (tile, slots, nq, subs,...  38.8 us
    ppermute x18, starting transfers between devices, send(): return lax.ppermute(x, ('section', 'dp'), route)  32.9 us
    ppermute x18, waiting for transfers between devices, send(): return lax.ppermute(x, ('section', 'dp'), route)  24.7 us
    pallas_call x6, Pallas kernels, place(): pl.pallas_call(functools.partial(place_kernel, which, full, len(shapes)),...  14 us
    ppermute x4, waiting for transfers between devices, on_device(): rows_got = lax.ppermute(rows_now, 'dp', route)  11.3 us
    pallas_call x18, Pallas kernels, pair_call(): pl.pallas_call(functools.partial(pair_kernel, [w[0] for w in works], outs...  10.1 us
    pallas_call x1, Pallas kernels, on_device(): pl.pallas_call(functools.partial(back_kernel, (tile, slots, subs, tiles,...  9.21 us
    pallas_call x1, Pallas kernels, on_device(): pl.pallas_call(weight_kernel, grid_spec=pltpu.PrefetchScalarGridSpec(num_...  8.97 us
  transfers between devices with their start and end apart: 36, of which 10 were waited for; matrix products, arithmetic and copies ran while one was open for 0% of the time, Pallas kernels for 27%

profile of v3, /device:TPU:0, one launch (start us, length us, event | category | flops | bytes accessed | tf_op | source)
XLA Modules:
  0.0 179.0 jit_solution(13940817487612789010)
XLA Ops:
  0.7 38.8 %forward.1 = (bf16[1536,1536]{1,0:T(8,128)(2,1)}, bf16[1536,1024]{1,0:T(8,128)(2,1)}, bf16[32,1024]{1,0:T(8,128)(2,1)}, bf16[1536,512]{1,0:T(8,128)(2,1)}, bf16[...) custom-call(s32[1]{0:T(128)} %bitcast.sec_ref.refs_1_, ...), custom_call_target="tpu_custom_call" | custom-call | flops 68719476736 | bytes 1024 | tf_op jit(solution)/shard_map/forward/pallas_call | solution.py:794
  40.0 9.0 %weights.1 = (bf16[6,256,512]{2,1,0:T(8,128)(2,1)S(1)}, bf16[6,256,512]{2,1,0:T(8,128)(2,1)}) custom-call(s32[1]{0:T(128)} %bitcast.sec_ref.refs_1_, bf16[1536,1536]{1,0:T(8,128)(2,1)} %get-tuple-element.92.left_ref, bf16[1536,1024]{1,0:T(8,128)(2,1)} %get-tuple-element.88.dpre_ref.prev_ref.next_ref), custom_call_target="tpu_custom_call" | custom-call | flops 68719476736 | bytes 1024 | tf_op jit(solution)/shard_map/weights/pallas_call | solution.py:876
  57.4 2.9 %collective-permute-start.10 = (bf16[640,512]{1,0:T(8,128)(2,1)}, bf16[640,512]{1,0:T(8,128)(2,1)}, u32[]{:S(2)}, u32[]{:S(2)}) collective-permute-start(bf16[640,512]{1,0:T(8,128)(2,1)} %get-tuple-element.109), channel_id=1, source_target_pairs={{0,1},{1,0},{2,3},{3,2},{4,5},{5,4},{6,7},{7,6},{8,9},{9,8},{10,11... | collective-permute-start | bytes 1966088 | tf_op jit(solution)/shard_map/ppermute | solution.py:539
  60.3 2.3 %split_body.7 = (bf16[512,512]{1,0:T(8,128)(2,1)S(1)}, bf16[512,512]{1,0:T(8,128)(2,1)}) custom-call(s32[1]{0:T(128)} %bitcast.6.refs_0_, bf16[1024,512]{1,0:T(8,128)(2,1)S(1)} %bitcast.28, bf16[1024,512]{1,0:T(8,128)(2,1)} %collective-permute-done.4.refs_2_, bf16[640,512]{1,0:T(8,128)(2,1)S(1)} %get-tuple-element.99.refs_3_.refs_1_), custom_call_target="tpu_custom_call" | custom-call | flops 68719476736 | bytes 1024 | tf_op jit(solution)/shard_map/split_body/pallas_call | solution.py:451
  64.1 1.7 collective-permute-start.7
  65.9 9.2 %back.1 = (bf16[1536,256]{1,0:T(8,128)(2,1)S(1)}, bf16[1536,256]{1,0:T(8,128)(2,1)S(1)}, bf16[32,512]{1,0:T(8,128)(2,1)}) custom-call(s32[1]{0:T(128)} %bitcast.sec_ref.refs_1_, s32[3]{0:T(128)S(1)} %copy-done.7, s32[3,4]{1,0:T(4,128)S(1)} %copy-done.5, bf16[1536,1024]{1,0:T(8,128)(2,1)} %get-tuple-element.88.dpre_ref.prev_ref.next_ref, ...), custom_call_target="tpu_custom_call" | custom-call | flops 68719476736 | bytes 1024 | tf_op jit(solution)/shard_map/back/pallas_call | solution.py:897
  76.6 3.1 %join.2 = (bf16[3072,256]{1,0:T(8,128)(2,1)}, bf16[3072,256]{1,0:T(8,128)(2,1)}, f32[8,128]{1,0:T(8,128)S(1)}) custom-call(s32[1]{0:T(128)} %bitcast.sec_ref.refs_1_, bf16[1536,256]{1,0:T(8,128)(2,1)S(1)} %copy-done, bf16[1536,256]{1,0:T(8,128)(2,1)} %collective-permute-done.refs_1_, bf16[1536,256]{1,0:T(8,128)(2,1)S(1)} %copy-done.1, ...), custom_call_target="tpu_custom_call" | custom-call | flops 1024 | bytes 1024 | tf_op jit(solution)/shard_map/join/pallas_call | solution.py:501
  87.2 1.7 collective-permute-start.12
  89.0 1.6 collective-permute-start.18
  91.0 1.6 collective-permute-start.17
  92.6 2.5 %collective-permute-done.11.refs_3_ = bf16[384,512]{1,0:T(8,128)(2,1)S(1)} collective-permute-done((bf16[384,512]{1,0:T(8,128)(2,1)S(1)}, bf16[384,512]{1,0:T(8,128)(2,1)S(1)}, u32[]{:S(2)}, u32[]{:S(2)}) %collective-permute-start.11) | collective-permute-done | bytes 393248 | tf_op jit(solution)/shard_map/ppermute | solution.py:539
  95.2 1.6 collective-permute-start.15
  98.9 3.6 %collective-permute-start.22 = (bf16[320,512]{1,0:T(8,128)(2,1)S(1)}, bf16[320,512]{1,0:T(8,128)(2,1)S(1)}, u32[]{:S(2)}, u32[]{:S(2)}) collective-permute-start(bf16[320,512]{1,0:T(8,128)(2,1)S(1)} %add_body.12.refs_3_.refs_1_), channel_id=1, source_target_pairs={{0,8},{1,9},{2,10},{3,11},{4,12},{5,13},{6,14},{7,15},{8,0},{9,1},... | collective-permute-start | bytes 983048 | tf_op jit(solution)/shard_map/ppermute | solution.py:539
  102.5 2.0 %collective-permute-done.17.refs_2_ = bf16[256,512]{1,0:T(8,128)(2,1)S(1)} collective-permute-done((bf16[256,512]{1,0:T(8,128)(2,1)S(1)}, bf16[256,512]{1,0:T(8,128)(2,1)S(1)}, u32[]{:S(2)}, u32[]{:S(2)}) %collective-permute-start.17) | collective-permute-done | bytes 262176 | tf_op jit(solution)/shard_map/ppermute | solution.py:539
  104.5 5.2 %collective-permute-start.21 = (bf16[256,512]{1,0:T(8,128)(2,1)S(1)}, bf16[256,512]{1,0:T(8,128)(2,1)S(1)}, u32[]{:S(2)}, u32[]{:S(2)}) collective-permute-start(bf16[256,512]{1,0:T(8,128)(2,1)S(1)} %add_body.13.refs_6_.refs_1_), channel_id=1, source_target_pairs={{0,8},{1,9},{2,10},{3,11},{4,12},{5,13},{6,14},{7,15},{8,0},{9,1},... | collective-permute-start | bytes 786440 | tf_op jit(solution)/shard_map/ppermute | solution.py:539
  109.7 13.8 %collective-permute-done.15.refs_3_ = bf16[384,512]{1,0:T(8,128)(2,1)S(1)} collective-permute-done((bf16[384,512]{1,0:T(8,128)(2,1)S(1)}, bf16[384,512]{1,0:T(8,128)(2,1)S(1)}, u32[]{:S(2)}, u32[]{:S(2)}) %collective-permute-start.15) | collective-permute-done | bytes 393248 | tf_op jit(solution)/shard_map/ppermute | solution.py:539
  123.6 4.0 %collective-permute-start.19 = (bf16[384,512]{1,0:T(8,128)(2,1)S(1)}, bf16[384,512]{1,0:T(8,128)(2,1)S(1)}, u32[]{:S(2)}, u32[]{:S(2)}) collective-permute-start(bf16[384,512]{1,0:T(8,128)(2,1)S(1)} %get-tuple-element.120.refs_3_.refs_2_), channel_id=1, source_target_pairs={{0,8},{1,9},{2,10},{3,11},{4,12},{5,13},{6,14},{7,15},{8,0},{9,1},... | collective-permute-start | bytes 1179656 | tf_op jit(solution)/shard_map/ppermute | solution.py:539
  127.6 2.5 %collective-permute-start.20 = (bf16[80,512]{1,0:T(8,128)(2,1)S(1)}, bf16[80,512]{1,0:T(8,128)(2,1)S(1)}, u32[]{:S(2)}, u32[]{:S(2)}) collective-permute-start(bf16[80,512]{1,0:T(8,128)(2,1)S(1)} %get-tuple-element.121.refs_4_), channel_id=1, source_target_pairs={{0,4},{1,5},{2,6},{3,7},{4,0},{5,1},{6,2},{7,3},{8,12},{9,13},{10,... | collective-permute-start | bytes 245768 | tf_op jit(solution)/shard_map/ppermute | solution.py:959
  132.4 1.7 collective-permute-done.20.refs_5_
  134.1 3.5 %collective-permute-done.19.refs_3_ = bf16[384,512]{1,0:T(8,128)(2,1)S(1)} collective-permute-done((bf16[384,512]{1,0:T(8,128)(2,1)S(1)}, bf16[384,512]{1,0:T(8,128)(2,1)S(1)}, u32[]{:S(2)}, u32[]{:S(2)}) %collective-permute-start.19) | collective-permute-done | bytes 393248 | tf_op jit(solution)/shard_map/ppermute | solution.py:539
  139.4 1.6 collective-permute-start.29
  141.2 9.6 %collective-permute-done.24.refs_5_ = bf16[144,512]{1,0:T(8,128)(2,1)S(1)} collective-permute-done((bf16[144,512]{1,0:T(8,128)(2,1)S(1)}, bf16[144,512]{1,0:T(8,128)(2,1)S(1)}, u32[]{:S(2)}, u32[]{:S(2)}) %collective-permute-start.24) | collective-permute-done | bytes 147488 | tf_op jit(solution)/shard_map/ppermute | solution.py:959
  153.4 2.3 %step_grad.1 = (f32[512,512]{1,0:T(8,128)}, f32[1,1024]{1,0:T(1,128)}, f32[1,1024]{1,0:T(1,128)}, f32[1,1024]{1,0:T(1,128)}, f32[3,128]{1,0:T(4,128)S(1)}, /*index=5*/f32[8,128]{1,0:T(8,128)S(1)}) custom-call(bf16[272,512]{1,0:T(8,128)(2,1)S(1)} %get-tuple-element.124.rows_ref, bf16[768,512]{1,0:T(8,128)(2,1)S(1)} %get-tuple-element.125.after_ref.p0), custom_call_target="tpu_custom_call" | custom-call | flops 68719476736 | bytes 1024 | tf_op jit(solution)/shard_map/step_grad/pallas_call | solution.py:966
  155.6 2.3 %join.3 = (bf16[3072,256]{1,0:T(8,128)(2,1)}, f32[8,128]{1,0:T(8,128)S(1)}) custom-call(s32[1]{0:T(128)} %bitcast.sec_ref.refs_1_, bf16[1536,256]{1,0:T(8,128)(2,1)S(1)} %get-tuple-element.105.refs_0_, bf16[1536,256]{1,0:T(8,128)(2,1)} %collective-permute-done.6.refs_1_, f32[8,128]{1,0:T(8,128)S(1)} %get-tuple-element.126.refs_2_), custom_call_target="tpu_custom_call" | custom-call | flops 1024 | bytes 1024 | tf_op jit(solution)/shard_map/join/pallas_call | solution.py:501
  157.9 2.7 %place.6 = (f32[512,1024]{1,0:T(8,128)}, f32[512,512]{1,0:T(8,128)}, f32[512,512]{1,0:T(8,128)}, f32[512,512]{1,0:T(8,128)}, f32[8,128]{1,0:T(8,128)S(1)}) custom-call(s32[4]{0:T(128)S(1)} %pad_add_fusion.runs, bf16[640,512]{1,0:T(8,128)(2,1)} %merge_body.3.refs_3_.p0, bf16[640,512]{1,0:T(8,128)(2,1)S(1)} %collective-permute-done.32.p1, ...), custom_call_target="tpu_custom_call" | custom-call | flops 1024 | bytes 1024 | tf_op jit(solution)/shard_map/place/pallas_call | solution.py:644
  160.6 2.0 %place.7 = (f32[512,1024]{1,0:T(8,128)}, f32[512,1024]{1,0:T(8,128)}, f32[8,128]{1,0:T(8,128)S(1)}) custom-call(s32[4]{0:T(128)S(1)} %pad_add_fusion.runs, bf16[512,512]{1,0:T(8,128)(2,1)S(1)} %merge_body.4.refs_6_.p0, bf16[512,512]{1,0:T(8,128)(2,1)S(1)} %collective-permute-done.31.p1, f32[8,128]{1,0:T(8,128)S(1)} %get-tuple-element.130.after_ref), custom_call_target="tpu_custom_call" | custom-call | flops 1024 | bytes 1024 | tf_op jit(solution)/shard_map/place/pallas_call | solution.py:644
  162.6 2.3 %place.8 = (f32[1536,1024]{1,0:T(8,128)}, f32[8,128]{1,0:T(8,128)S(1)}) custom-call(s32[4]{0:T(128)S(1)} %pad_add_fusion.runs, bf16[768,512]{1,0:T(8,128)(2,1)S(1)} %get-tuple-element.125.after_ref.p0, bf16[768,512]{1,0:T(8,128)(2,1)S(1)} %collective-permute-done.30.p1, f32[8,128]{1,0:T(8,128)S(1)} %get-tuple-element.131.after_ref), custom_call_target="tpu_custom_call" | custom-call | flops 1024 | bytes 1024 | tf_op jit(solution)/shard_map/place/pallas_call | solution.py:644
  166.2 2.2 %collective-permute-done.27.x_ref = bf16[768,512]{1,0:T(8,128)(2,1)S(1)} collective-permute-done((bf16[768,512]{1,0:T(8,128)(2,1)S(1)}, bf16[768,512]{1,0:T(8,128)(2,1)S(1)}, u32[]{:S(2)}, u32[]{:S(2)}) %collective-permute-start.27) | collective-permute-done | bytes 786464 | tf_op jit(solution)/shard_map/ppermute | solution.py:539
  169.7 2.0 %collective-permute-done.35.p1 = bf16[640,512]{1,0:T(8,128)(2,1)S(1)} collective-permute-done((bf16[640,512]{1,0:T(8,128)(2,1)S(1)}, bf16[640,512]{1,0:T(8,128)(2,1)S(1)}, u32[]{:S(2)}, u32[]{:S(2)}) %collective-permute-start.35) | collective-permute-done | bytes 655392 | tf_op jit(solution)/shard_map/ppermute | solution.py:514
  171.7 2.1 %place.9 = (f32[512,1024]{1,0:T(8,128)}, f32[512,512]{1,0:T(8,128)}, f32[512,512]{1,0:T(8,128)}, f32[512,512]{1,0:T(8,128)}, f32[8,128]{1,0:T(8,128)S(1)}) custom-call(s32[4]{0:T(128)S(1)} %pad_add_fusion.runs, bf16[640,512]{1,0:T(8,128)(2,1)S(1)} %then.3.after_ref.p0, ...), custom_call_target="tpu_custom_call", output_to_operand_aliasing={{0}: (4, {}), {1}: (5, {}), {2}: (6, {}), {3}: (7, {})} | custom-call | flops 1024 | bytes 1024 | tf_op jit(solution)/shard_map/place/pallas_call | solution.py:644
  173.9 2.0 %place.10 = (f32[512,1024]{1,0:T(8,128)}, f32[512,1024]{1,0:T(8,128)}, f32[8,128]{1,0:T(8,128)S(1)}) custom-call(s32[4]{0:T(128)S(1)} %pad_add_fusion.runs, bf16[512,512]{1,0:T(8,128)(2,1)S(1)} %then.4.after_ref.p0, bf16[512,512]{1,0:T(8,128)(2,1)S(1)} %collective-permute-done.34.p1, ...), custom_call_target="tpu_custom_call", output_to_operand_aliasing={{0}: (4, {}), {1}: (5, {})} | custom-call | flops 1024 | bytes 1024 | tf_op jit(solution)/shard_map/place/pallas_call | solution.py:644
  175.9 2.9 %place.11 = (f32[1536,1024]{1,0:T(8,128)}, f32[8,128]{1,0:T(8,128)}) custom-call(s32[4]{0:T(128)S(1)} %pad_add_fusion.runs, bf16[768,512]{1,0:T(8,128)(2,1)S(1)} %then.5.after_ref.p0, bf16[768,512]{1,0:T(8,128)(2,1)S(1)} %collective-permute-done.33.p1, f32[8,128]{1,0:T(8,128)S(1)} %get-tuple-element.140.after_ref, ...), custom_call_target="tpu_custom_call", output_to_operand_aliasing={{0}: (4, {})} | custom-call | flops 1024 | bytes 1024 | tf_op jit(solution)/shard_map/place/pallas_call | solution.py:644
  (109 shorter events, 31.6 us)
Async XLA Ops:
  39.4 11.7 %collective-permute-start.5 = (bf16[1280,512]{1,0:T(8,128)(2,1)}, bf16[1280,512]{1,0:T(8,128)(2,1)S(1)}, u32[]{:S(2)}, u32[]{:S(2)}) collective-permute-start(bf16[1280,512]{1,0:T(8,128)(2,1)} %bitcast.32), channel_id=1, source_target_pairs={{0,16},{16,0},{1,17},{17,1},{2,18},{18,2},{3,19},{19,3},{4,20},{20... | collective-permute-start | bytes 3932168 | tf_op jit(solution)/shard_map/ppermute | solution.py:514
  40.0 17.4 %collective-permute-start.4 = (bf16[1024,512]{1,0:T(8,128)(2,1)}, bf16[1024,512]{1,0:T(8,128)(2,1)}, u32[]{:S(2)}, u32[]{:S(2)}) collective-permute-start(bf16[1024,512]{1,0:T(8,128)(2,1)} %bitcast.33), channel_id=1, source_target_pairs={{0,16},{16,0},{1,17},{17,1},{2,18},{18,2},{3,19},{19,3},{4,20},{20... | collective-permute-start | bytes 3145736 | tf_op jit(solution)/shard_map/ppermute | solution.py:514
  50.2 12.4 %collective-permute-start.3 = (bf16[1536,512]{1,0:T(8,128)(2,1)}, bf16[1536,512]{1,0:T(8,128)(2,1)S(1)}, u32[]{:S(2)}, u32[]{:S(2)}) collective-permute-start(bf16[1536,512]{1,0:T(8,128)(2,1)} %bitcast.8), channel_id=1, source_target_pairs={{0,16},{16,0},{1,17},{17,1},{2,18},{18,2},{3,19},{19,3},{4,20},{20... | collective-permute-start | bytes 4718600 | tf_op jit(solution)/shard_map/ppermute | solution.py:514
  50.6 13.5 %collective-permute-start.2 = (bf16[32,1024]{1,0:T(8,128)(2,1)}, bf16[32,1024]{1,0:T(8,128)(2,1)}, u32[]{:S(2)}, u32[]{:S(2)}) collective-permute-start(bf16[32,1024]{1,0:T(8,128)(2,1)} %get-tuple-element.89), channel_id=1, source_target_pairs={{0,16},{16,0},{1,17},{17,1},{2,18},{18,2},{3,19},{19,3},{4,20},{20... | collective-permute-start | bytes 196616 | tf_op jit(solution)/shard_map/ppermute | solution.py:514
  50.7 25.3 %collective-permute-start = (bf16[1536,256]{1,0:T(8,128)(2,1)}, bf16[1536,256]{1,0:T(8,128)(2,1)}, u32[]{:S(2)}, u32[]{:S(2)}) collective-permute-start(bf16[1536,256]{1,0:T(8,128)(2,1)} %get-tuple-element.85), channel_id=1, source_target_pairs={{0,16},{16,0},{1,17},{17,1},{2,18},{18,2},{3,19},{19,3},{4,20},{20... | collective-permute-start | bytes 2359304 | tf_op jit(solution)/shard_map/ppermute | solution.py:514
  52.2 23.9 %collective-permute-start.1 = (bf16[1536,256]{1,0:T(8,128)(2,1)}, bf16[1536,256]{1,0:T(8,128)(2,1)}, u32[]{:S(2)}, u32[]{:S(2)}) collective-permute-start(bf16[1536,256]{1,0:T(8,128)(2,1)} %get-tuple-element.87), channel_id=1, source_target_pairs={{0,16},{16,0},{1,17},{17,1},{2,18},{18,2},{3,19},{19,3},{4,20},{20... | collective-permute-start | bytes 2359304 | tf_op jit(solution)/shard_map/ppermute | solution.py:514
  57.4 22.3 %collective-permute-start.10 = (bf16[640,512]{1,0:T(8,128)(2,1)}, bf16[640,512]{1,0:T(8,128)(2,1)}, u32[]{:S(2)}, u32[]{:S(2)}) collective-permute-start(bf16[640,512]{1,0:T(8,128)(2,1)} %get-tuple-element.109), channel_id=1, source_target_pairs={{0,1},{1,0},{2,3},{3,2},{4,5},{5,4},{6,7},{7,6},{8,9},{9,8},{10,11... | collective-permute-start | bytes 1966088 | tf_op jit(solution)/shard_map/ppermute | solution.py:539
  62.6 20.0 %collective-permute-start.9 = (bf16[512,512]{1,0:T(8,128)(2,1)}, bf16[512,512]{1,0:T(8,128)(2,1)}, u32[]{:S(2)}, u32[]{:S(2)}) collective-permute-start(bf16[512,512]{1,0:T(8,128)(2,1)} %get-tuple-element.108), channel_id=1, source_target_pairs={{0,1},{1,0},{2,3},{3,2},{4,5},{5,4},{6,7},{7,6},{8,9},{9,8},{10,11... | collective-permute-start | bytes 1572872 | tf_op jit(solution)/shard_map/ppermute | solution.py:539
  64.1 20.2 %collective-permute-start.7 = (bf16[768,512]{1,0:T(8,128)(2,1)}, bf16[768,512]{1,0:T(8,128)(2,1)}, u32[]{:S(2)}, u32[]{:S(2)}) collective-permute-start(bf16[768,512]{1,0:T(8,128)(2,1)} %get-tuple-element.107), channel_id=1, source_target_pairs={{0,1},{1,0},{2,3},{3,2},{4,5},{5,4},{6,7},{7,6},{8,9},{9,8},{10,11... | collective-permute-start | bytes 2359304 | tf_op jit(solution)/shard_map/ppermute | solution.py:539
  75.9 8.4 %collective-permute-start.8 = (bf16[32,512]{1,0:T(8,128)(2,1)}, bf16[32,512]{1,0:T(8,128)(2,1)}, u32[]{:S(2)}, u32[]{:S(2)}) collective-permute-start(bf16[32,512]{1,0:T(8,128)(2,1)} %get-tuple-element.102.refs_4_), channel_id=1, source_target_pairs={{0,16},{16,0},{1,17},{17,1},{2,18},{18,2},{3,19},{19,3},{4,20},{20... | collective-permute-start | bytes 98312 | tf_op jit(solution)/shard_map/ppermute | solution.py:514
  76.0 75.4 %collective-permute-start.6 = (bf16[1536,256]{1,0:T(8,128)(2,1)}, bf16[1536,256]{1,0:T(8,128)(2,1)}, u32[]{:S(2)}, u32[]{:S(2)}) collective-permute-start(bf16[1536,256]{1,0:T(8,128)(2,1)} %copy-done.4), channel_id=1, source_target_pairs={{0,16},{16,0},{1,17},{17,1},{2,18},{18,2},{3,19},{19,3},{4,20},{20... | collective-permute-start | bytes 2359304 | tf_op jit(solution)/shard_map/ppermute | solution.py:514
  81.0 8.0 %collective-permute-start.14 = (bf16[320,512]{1,0:T(8,128)(2,1)S(1)}, bf16[320,512]{1,0:T(8,128)(2,1)S(1)}, u32[]{:S(2)}, u32[]{:S(2)}) collective-permute-start(bf16[320,512]{1,0:T(8,128)(2,1)S(1)} %get-tuple-element.117), channel_id=1, source_target_pairs={{0,2},{1,3},{2,0},{3,1},{4,6},{5,7},{6,4},{7,5},{8,10},{9,11},{10,... | collective-permute-start | bytes 983048 | tf_op jit(solution)/shard_map/ppermute | solution.py:539
  83.7 7.2 %collective-permute-start.13 = (bf16[256,512]{1,0:T(8,128)(2,1)S(1)}, bf16[256,512]{1,0:T(8,128)(2,1)S(1)}, u32[]{:S(2)}, u32[]{:S(2)}) collective-permute-start(bf16[256,512]{1,0:T(8,128)(2,1)S(1)} %get-tuple-element.116), channel_id=1, source_target_pairs={{0,2},{1,3},{2,0},{3,1},{4,6},{5,7},{6,4},{7,5},{8,10},{9,11},{10,... | collective-permute-start | bytes 786440 | tf_op jit(solution)/shard_map/ppermute | solution.py:539
  85.7 9.5 %collective-permute-start.11 = (bf16[384,512]{1,0:T(8,128)(2,1)S(1)}, bf16[384,512]{1,0:T(8,128)(2,1)S(1)}, u32[]{:S(2)}, u32[]{:S(2)}) collective-permute-start(bf16[384,512]{1,0:T(8,128)(2,1)S(1)} %get-tuple-element.114), channel_id=1, source_target_pairs={{0,2},{1,3},{2,0},{3,1},{4,6},{5,7},{6,4},{7,5},{8,10},{9,11},{10,... | collective-permute-start | bytes 1179656 | tf_op jit(solution)/shard_map/ppermute | solution.py:539
  89.0 9.8 %collective-permute-start.18 = (bf16[320,512]{1,0:T(8,128)(2,1)S(1)}, bf16[320,512]{1,0:T(8,128)(2,1)S(1)}, u32[]{:S(2)}, u32[]{:S(2)}) collective-permute-start(bf16[320,512]{1,0:T(8,128)(2,1)S(1)} %add_body.9.refs_3_.refs_1_), channel_id=1, source_target_pairs={{0,4},{1,5},{2,6},{3,7},{4,0},{5,1},{6,2},{7,3},{8,12},{9,13},{10,... | collective-permute-start | bytes 983048 | tf_op jit(solution)/shard_map/ppermute | solution.py:539
  91.0 13.5 %collective-permute-start.17 = (bf16[256,512]{1,0:T(8,128)(2,1)S(1)}, bf16[256,512]{1,0:T(8,128)(2,1)S(1)}, u32[]{:S(2)}, u32[]{:S(2)}) collective-permute-start(bf16[256,512]{1,0:T(8,128)(2,1)S(1)} %add_body.10.refs_6_.refs_1_), channel_id=1, source_target_pairs={{0,4},{1,5},{2,6},{3,7},{4,0},{5,1},{6,2},{7,3},{8,12},{9,13},{10,... | collective-permute-start | bytes 786440 | tf_op jit(solution)/shard_map/ppermute | solution.py:539
  95.2 28.3 %collective-permute-start.15 = (bf16[384,512]{1,0:T(8,128)(2,1)S(1)}, bf16[384,512]{1,0:T(8,128)(2,1)S(1)}, u32[]{:S(2)}, u32[]{:S(2)}) collective-permute-start(bf16[384,512]{1,0:T(8,128)(2,1)S(1)} %get-tuple-element.118.refs_3_.refs_2_), channel_id=1, source_target_pairs={{0,4},{1,5},{2,6},{3,7},{4,0},{5,1},{6,2},{7,3},{8,12},{9,13},{10,... | collective-permute-start | bytes 1179656 | tf_op jit(solution)/shard_map/ppermute | solution.py:539
  96.9 12.8 %collective-permute-start.16 = (bf16[48,512]{1,0:T(8,128)(2,1)S(1)}, bf16[48,512]{1,0:T(8,128)(2,1)S(1)}, u32[]{:S(2)}, u32[]{:S(2)}) collective-permute-start(bf16[48,512]{1,0:T(8,128)(2,1)S(1)} %get-tuple-element.119.refs_4_), channel_id=1, source_target_pairs={{0,2},{1,3},{2,0},{3,1},{4,6},{5,7},{6,4},{7,5},{8,10},{9,11},{10,... | collective-permute-start | bytes 147464 | tf_op jit(solution)/shard_map/ppermute | solution.py:959
  98.9 31.1 %collective-permute-start.22 = (bf16[320,512]{1,0:T(8,128)(2,1)S(1)}, bf16[320,512]{1,0:T(8,128)(2,1)S(1)}, u32[]{:S(2)}, u32[]{:S(2)}) collective-permute-start(bf16[320,512]{1,0:T(8,128)(2,1)S(1)} %add_body.12.refs_3_.refs_1_), channel_id=1, source_target_pairs={{0,8},{1,9},{2,10},{3,11},{4,12},{5,13},{6,14},{7,15},{8,0},{9,1},... | collective-permute-start | bytes 983048 | tf_op jit(solution)/shard_map/ppermute | solution.py:539
  104.5 26.3 %collective-permute-start.21 = (bf16[256,512]{1,0:T(8,128)(2,1)S(1)}, bf16[256,512]{1,0:T(8,128)(2,1)S(1)}, u32[]{:S(2)}, u32[]{:S(2)}) collective-permute-start(bf16[256,512]{1,0:T(8,128)(2,1)S(1)} %add_body.13.refs_6_.refs_1_), channel_id=1, source_target_pairs={{0,8},{1,9},{2,10},{3,11},{4,12},{5,13},{6,14},{7,15},{8,0},{9,1},... | collective-permute-start | bytes 786440 | tf_op jit(solution)/shard_map/ppermute | solution.py:539
  123.6 14.0 %collective-permute-start.19 = (bf16[384,512]{1,0:T(8,128)(2,1)S(1)}, bf16[384,512]{1,0:T(8,128)(2,1)S(1)}, u32[]{:S(2)}, u32[]{:S(2)}) collective-permute-start(bf16[384,512]{1,0:T(8,128)(2,1)S(1)} %get-tuple-element.120.refs_3_.refs_2_), channel_id=1, source_target_pairs={{0,8},{1,9},{2,10},{3,11},{4,12},{5,13},{6,14},{7,15},{8,0},{9,1},... | collective-permute-start | bytes 1179656 | tf_op jit(solution)/shard_map/ppermute | solution.py:539
  130.2 8.3 %collective-permute-start.26 = (bf16[320,512]{1,0:T(8,128)(2,1)S(1)}, bf16[320,512]{1,0:T(8,128)(2,1)S(1)}, u32[]{:S(2)}, u32[]{:S(2)}) collective-permute-start(bf16[320,512]{1,0:T(8,128)(2,1)S(1)} %add_body.15.refs_3_.refs_1_), channel_id=1, source_target_pairs={{0,2},{1,3},{2,0},{3,1},{4,6},{5,7},{6,4},{7,5},{8,10},{9,11},{10,... | collective-permute-start | bytes 983048 | tf_op jit(solution)/shard_map/ppermute | solution.py:539
  131.0 10.1 %collective-permute-start.25 = (bf16[256,512]{1,0:T(8,128)(2,1)S(1)}, bf16[256,512]{1,0:T(8,128)(2,1)S(1)}, u32[]{:S(2)}, u32[]{:S(2)}) collective-permute-start(bf16[256,512]{1,0:T(8,128)(2,1)S(1)} %add_body.16.refs_6_.refs_1_), channel_id=1, source_target_pairs={{0,2},{1,3},{2,0},{3,1},{4,6},{5,7},{6,4},{7,5},{8,10},{9,11},{10,... | collective-permute-start | bytes 786440 | tf_op jit(solution)/shard_map/ppermute | solution.py:539
  137.7 13.1 %collective-permute-start.23 = (bf16[384,512]{1,0:T(8,128)(2,1)S(1)}, bf16[384,512]{1,0:T(8,128)(2,1)S(1)}, u32[]{:S(2)}, u32[]{:S(2)}) collective-permute-start(bf16[384,512]{1,0:T(8,128)(2,1)S(1)} %get-tuple-element.122.refs_3_.refs_2_), channel_id=1, source_target_pairs={{0,2},{1,3},{2,0},{3,1},{4,6},{5,7},{6,4},{7,5},{8,10},{9,11},{10,... | collective-permute-start | bytes 1179656 | tf_op jit(solution)/shard_map/ppermute | solution.py:539
  139.4 12.5 %collective-permute-start.32 = (bf16[640,512]{1,0:T(8,128)(2,1)}, bf16[640,512]{1,0:T(8,128)(2,1)S(1)}, u32[]{:S(2)}, u32[]{:S(2)}) collective-permute-start(bf16[640,512]{1,0:T(8,128)(2,1)} %merge_body.3.refs_3_.p0), channel_id=1, source_target_pairs={{0,16},{16,0},{1,17},{17,1},{2,18},{18,2},{3,19},{19,3},{4,20},{20... | collective-permute-start | bytes 1966088 | tf_op jit(solution)/shard_map/ppermute | solution.py:514
  139.4 25.6 %collective-permute-start.29 = (bf16[640,512]{1,0:T(8,128)(2,1)}, bf16[640,512]{1,0:T(8,128)(2,1)}, u32[]{:S(2)}, u32[]{:S(2)}) collective-permute-start(bf16[640,512]{1,0:T(8,128)(2,1)} %merge_body.3.refs_3_.p0), channel_id=1, source_target_pairs={{0,1},{1,0},{2,3},{3,2},{4,5},{5,4},{6,7},{7,6},{8,9},{9,8},{10,11... | collective-permute-start | bytes 1966088 | tf_op jit(solution)/shard_map/ppermute | solution.py:539
  141.0 9.8 %collective-permute-start.24 = (bf16[144,512]{1,0:T(8,128)(2,1)S(1)}, bf16[144,512]{1,0:T(8,128)(2,1)S(1)}, u32[]{:S(2)}, u32[]{:S(2)}) collective-permute-start(bf16[144,512]{1,0:T(8,128)(2,1)S(1)} %get-tuple-element.123.refs_4_), channel_id=1, source_target_pairs={{0,8},{1,9},{2,10},{3,11},{4,12},{5,13},{6,14},{7,15},{8,0},{9,1},... | collective-permute-start | bytes 442376 | tf_op jit(solution)/shard_map/ppermute | solution.py:959
  150.8 9.9 %collective-permute-start.31 = (bf16[512,512]{1,0:T(8,128)(2,1)S(1)}, bf16[512,512]{1,0:T(8,128)(2,1)S(1)}, u32[]{:S(2)}, u32[]{:S(2)}) collective-permute-start(bf16[512,512]{1,0:T(8,128)(2,1)S(1)} %merge_body.4.refs_6_.p0), channel_id=1, source_target_pairs={{0,16},{16,0},{1,17},{17,1},{2,18},{18,2},{3,19},{19,3},{4,20},{20... | collective-permute-start | bytes 1572872 | tf_op jit(solution)/shard_map/ppermute | solution.py:514
  150.8 15.3 %collective-permute-start.28 = (bf16[512,512]{1,0:T(8,128)(2,1)S(1)}, bf16[512,512]{1,0:T(8,128)(2,1)S(1)}, u32[]{:S(2)}, u32[]{:S(2)}) collective-permute-start(bf16[512,512]{1,0:T(8,128)(2,1)S(1)} %merge_body.4.refs_6_.p0), channel_id=1, source_target_pairs={{0,1},{1,0},{2,3},{3,2},{4,5},{5,4},{6,7},{7,6},{8,9},{9,8},{10,11... | collective-permute-start | bytes 1572872 | tf_op jit(solution)/shard_map/ppermute | solution.py:539
  151.4 11.2 %collective-permute-start.30 = (bf16[768,512]{1,0:T(8,128)(2,1)S(1)}, bf16[768,512]{1,0:T(8,128)(2,1)S(1)}, u32[]{:S(2)}, u32[]{:S(2)}) collective-permute-start(bf16[768,512]{1,0:T(8,128)(2,1)S(1)} %get-tuple-element.125.after_ref.p0), channel_id=1, source_target_pairs={{0,16},{16,0},{1,17},{17,1},{2,18},{18,2},{3,19},{19,3},{4,20},{20... | collective-permute-start | bytes 2359304 | tf_op jit(solution)/shard_map/ppermute | solution.py:514
  151.8 16.6 %collective-permute-start.27 = (bf16[768,512]{1,0:T(8,128)(2,1)S(1)}, bf16[768,512]{1,0:T(8,128)(2,1)S(1)}, u32[]{:S(2)}, u32[]{:S(2)}) collective-permute-start(bf16[768,512]{1,0:T(8,128)(2,1)S(1)} %get-tuple-element.125.after_ref.p0), channel_id=1, source_target_pairs={{0,1},{1,0},{2,3},{3,2},{4,5},{5,4},{6,7},{7,6},{8,9},{9,8},{10,11... | collective-permute-start | bytes 2359304 | tf_op jit(solution)/shard_map/ppermute | solution.py:539
  168.4 7.4 %collective-permute-start.33 = (bf16[768,512]{1,0:T(8,128)(2,1)S(1)}, bf16[768,512]{1,0:T(8,128)(2,1)S(1)}, u32[]{:S(2)}, u32[]{:S(2)}) collective-permute-start(bf16[768,512]{1,0:T(8,128)(2,1)S(1)} %then.5.after_ref.p0), channel_id=1, source_target_pairs={{0,16},{16,0},{1,17},{17,1},{2,18},{18,2},{3,19},{19,3},{4,20},{20... | collective-permute-start | bytes 2359304 | tf_op jit(solution)/shard_map/ppermute | solution.py:514
  (21 other events, 85.4 us)

commit v4 on v3

--- a/solution.py
+++ b/solution.py
@@ -15,8 +15,8 @@
 F32 = jnp.float32
 BF16 = jnp.bfloat16
 VMEM = 56 * 1024 * 1024
-KB_VMEM = 48 * 1024 * 1024
-KC_VMEM = 48 * 1024 * 1024
+KB_VMEM = 56 * 1024 * 1024
+KC_VMEM = 32 * 1024 * 1024
 
 
 def nn(a, b):
@@ -459,6 +459,39 @@
     )(*[w[1] for w in works], *[x for w in works for x in w[2:4]], after)
 
 
+def first_kernel(bit_ref, held, got, after_ref, keep, give, bufs, sems):
+    rows = keep.shape[0]
+    bit = bit_ref[0]
+    copies = []
+    for i, half in enumerate((1 - bit, bit)):
+        for j, array in enumerate((held, got)):
+            copies.append(
+                pltpu.make_async_copy(
+                    array.at[at_bit(half, rows), :], bufs.at[2 * i + j], sems.at[2 * i + j]
+                )
+            )
+    for copy in copies:
+        copy.start()
+    for i, out in enumerate((give, keep)):
+        copies[2 * i].wait()
+        copies[2 * i + 1].wait()
+        out[...] = total(bufs[2 * i], bufs[2 * i + 1])
+
+
+def split_first(held, got, bit, after, cost):
+    rows, width = held.shape[0] // 2, held.shape[1]
+    return pl.pallas_call(
+        first_kernel,
+        in_specs=[IN_SMEM, IN_HBM, IN_HBM, ANYWHERE],
+        out_specs=[IN_VMEM] * 2,
+        out_shape=[struct(rows, width)] * 2,
+        scratch_shapes=[pltpu.VMEM((4, rows, width), BF16), pltpu.SemaphoreType.DMA((4,))],
+        compiler_params=pltpu.CompilerParams(vmem_limit_bytes=24 * 1024 * 1024),
+        cost_estimate=cost,
+        name="split_first",
+    )(bit, held, got, after)
+
+
 def then_kernel(x_ref, after_ref, out_ref):
     out_ref[...] = x_ref[...]
 
@@ -554,21 +587,23 @@
         self.step = 0
 
     def turn(self, after, more=(), cost=LARGE):
-        sums = self.sums
-        halved = sums.levels - 2
+        sums, last = self.sums, self.sums.levels - 1
         at = self.step
         self.step += 1
         rows, width = self.held.shape
-        if at < halved:
+        if at == 0:
+            self.held, give = split_first(self.held, self.got, sums.bit(0), after, cost)
+            self.got, rest = sums.send(give, 0), []
+        elif at < last:
             work = (split_body, sums.bit(at), self.held, self.got, [struct(rows // 2, width)] * 2)
             self.held, give, *rest = pair_call([work, *more], after, cost)
             self.got = sums.send(give, at)
-        elif at <= halved + 2:
+        elif at <= last + 1:
             work = (add_body, sums.bit(0), self.held, self.got, [struct(rows, width)])
             self.held, *rest = pair_call([work, *more], after, cost)
-            self.got = sums.send(self.held, at if at < halved + 2 else halved - 1)
+            self.got = sums.send(self.held, at if at == last else last - 1)
         else:
-            back = 2 * halved + 2 - at
+            back = 2 * last + 1 - at
             work = (merge_body, sums.bit(back), self.held, self.got, [struct(2 * rows, width)])
             self.held, *rest = pair_call([work, *more], after, cost)
             self.got = sums.send(self.held, back - 1)
@@ -576,7 +611,7 @@
 
     @property
     def turns(self):
-        return 2 * self.sums.levels - 2
+        return 2 * self.sums.levels - 1
 
     def early(self, shapes, spots, after, outs=()):
         return place(self.sums.runs(), (0, 2), (self.held, swap(self.held)), shapes, spots, after, outs)
@@ -861,16 +896,17 @@
     if len(other) > 3:
         other[-2], other[-1] = other[-1], other[-2]
     sums = Sum((bits, other))
-    unit = 16 * lax.axis_size("dp") // 4
-
-    def batch(keep, give):
+    far_first = Sum((bits[2:] + bits[:2], bits[:1:-1] + bits[1::-1]))
+    unit = 16 * lax.axis_size("dp") // 2
+
+    def batch(keep, give, sums):
         rows = keep.shape[0] * half
         rows = -(-rows // unit) * unit
         return Batch(
             sums, padded(keep.reshape(-1, width), rows), padded(give.reshape(-1, width), rows)
         )
 
-    batch_a, batch_c = batch(keep_a, give_a), batch(keep_c, give_c)
+    batch_a, batch_c = batch(keep_a, give_a, far_first), batch(keep_c, give_c, sums)
     block_got, skip_got, other_edge = swap(block_give), swap(skip_give), swap(edge)
     spec = pl.BlockSpec((2, half, width), lambda i, *_: (i, 0, 0))
     keep_b, give_b = pl.pallas_call(
@@ -887,10 +923,9 @@
         cost_estimate=LARGE,
         name="weights",
     )(sec, stack, d_pre)
-    batch_b = batch(keep_b, give_b)
+    batch_b = batch(keep_b, give_b, sums)
     (after,) = batch_a.turn(keep_b)
     (after,) = batch_c.turn(after)
-    (after,) = batch_b.turn(after)
 
     group = -(-(micro * slots + 2) // 16) * 16
     rows_last = own // EDGE - 1
@@ -937,16 +972,14 @@
     )
     in_got = swap(in_give)
 
+    (after,) = batch_b.turn(rows_now)
     block_out, skip_out, after = join(
-        sec, rows_now, (block_keep, block_got), (skip_keep, skip_got)
+        sec, after, (block_keep, block_got), (skip_keep, skip_got)
     )
     rows_got, rows_bit, gathered = swap(rows_now), sec, 0
     batches = {"a": batch_a, "b": batch_b, "c": batch_c}
-    first = True
-    for name in "ac-b" * (batch_a.turns - 1):
-        if name == "-":
-            first = False
-            continue
+    order = "acb" + "cab" * 2 + "acb" * (batch_a.turns - 5) + "cab"
+    for name in order:
         turner = batches[name]
         if name == "b" and gathered <= sums.levels:
             n = rows_now.shape[0]
@@ -955,12 +988,13 @@
                 work = (gather_body, rows_bit, rows_now, rows_got, [struct(2 * n - EDGE, width)])
             after, rows_now = turner.turn(after, [work])
             if gathered < sums.levels:
-                route = [(d, d ^ (1 << gathered)) for d in range(sums.chips)]
+                at = sums.levels - 1 - gathered
+                route = [(d, d ^ (1 << at)) for d in range(sums.chips)]
                 rows_got = lax.ppermute(rows_now, "dp", route)
-                rows_bit = ((sums.chip >> gathered) & 1).astype(jnp.int32).reshape(1)
+                rows_bit = ((sums.chip >> at) & 1).astype(jnp.int32).reshape(1)
             gathered += 1
         else:
-            (after,) = turner.turn(after, cost=SMALL if first else LARGE)
+            (after,) = turner.turn(after)
 
     line = struct(1, wide, F32)
     g_step, g_convb, g_resb, g_outb, levels, mark = pl.pallas_call(

time: 179 us -> 166 us (0.927)
  waiting for transfers between devices: 38.1 us -> 32.2 us
  starting transfers between devices: 42 us -> 36.4 us
  local copies, waits for them, and re-layouts: 7.79 us -> 4.15 us
    pallas_call x0 -> x3, Pallas kernels: none -> 4.69 us  [split_first(): pl.pallas_call(first_kernel, in_specs=[IN_SMEM, IN_HBM, IN_HBM, ANYWHERE]...]
    ppermute x4, waiting for transfers between devices: 11.3 us -> 7.33 us  [on_device(): rows_got = lax.ppermute(rows_now, 'dp', route)]
    ppermute x18 -> x21, starting transfers between devices: 32.9 us -> 29.2 us  [send(): return lax.ppermute(x, ('section', 'dp'), route)]
    unnamed x34 -> x26, local copies, waits for them, and re-layouts: 7.16 us -> 3.53 us
    ppermute x4, starting transfers between devices: 5.85 us -> 3.82 us  [on_device(): rows_got = lax.ppermute(rows_now, 'dp', route)]
    ppermute x18 -> x21, waiting for transfers between devices: 24.7 us -> 22.8 us  [send(): return lax.ppermute(x, ('section', 'dp'), route)]
    pallas_call x18, Pallas kernels: 10.1 us -> 8.32 us  [pair_call(): pl.pallas_call(functools.partial(pair_kernel, [w[0] for w in works], outs...]
  transfers between devices with their start and end apart: 36 -> 39, of which waited for: 10 -> 14; matrix products, arithmetic and copies ran while one was open for 0% -> 0% of each run, Pallas kernels for 27% -> 30%
where the time goes in v4:
time: 166 us; the launch traced here: 165 us
  Pallas kernels  91.2 us (55%)
  starting transfers between devices  36.4 us (22%)
  waiting for transfers between devices  32.2 us (19%)
  local copies, waits for them, and re-layouts  4.15 us (3%)
    pallas_call x1, Pallas kernels, on_device(): pl.pallas_call(functools.partial(forward_kernel, (tile, slots, nq, subs,...  38.7 us
    ppermute x21, starting transfers between devices, send(): return lax.ppermute(x, ('section', 'dp'), route)  29.2 us
    ppermute x21, waiting for transfers between devices, send(): return lax.ppermute(x, ('section', 'dp'), route)  22.8 us
    pallas_call x6, Pallas kernels, place(): pl.pallas_call(functools.partial(place_kernel, which, full, len(shapes)),...  14.1 us
    pallas_call x1, Pallas kernels, on_device(): pl.pallas_call(weight_kernel, grid_spec=pltpu.PrefetchScalarGridSpec(num_...  9.09 us
    pallas_call x18, Pallas kernels, pair_call(): pl.pallas_call(functools.partial(pair_kernel, [w[0] for w in works], outs...  8.32 us
    pallas_call x1, Pallas kernels, on_device(): pl.pallas_call(functools.partial(back_kernel, (tile, slots, subs, tiles,...  7.53 us
    ppermute x4, waiting for transfers between devices, on_device(): rows_got = lax.ppermute(rows_now, 'dp', route)  7.33 us
  transfers between devices with their start and end apart: 39, of which 14 were waited for; matrix products, arithmetic and copies ran while one was open for 0% of the time, Pallas kernels for 30%

profile of v4, /device:TPU:0, one launch (start us, length us, event | category | flops | bytes accessed | tf_op | source)
XLA Modules:
  0.0 165.4 jit_solution(15182714835670896160)
XLA Ops:
  0.7 38.7 %forward.1 = (bf16[1536,1536]{1,0:T(8,128)(2,1)}, bf16[1536,1024]{1,0:T(8,128)(2,1)}, bf16[32,1024]{1,0:T(8,128)(2,1)}, bf16[1536,512]{1,0:T(8,128)(2,1)}, bf16[...) custom-call(s32[1]{0:T(128)} %bitcast.sec_ref.refs_1_, ...), custom_call_target="tpu_custom_call" | custom-call | flops 68719476736 | bytes 1024 | tf_op jit(solution)/shard_map/forward/pallas_call | solution.py:829
  40.4 9.1 %weights.1 = (bf16[6,256,512]{2,1,0:T(8,128)(2,1)}, bf16[6,256,512]{2,1,0:T(8,128)(2,1)}) custom-call(s32[1]{0:T(128)} %bitcast.sec_ref.refs_1_, bf16[1536,1536]{1,0:T(8,128)(2,1)} %get-tuple-element.93.left_ref, bf16[1536,1024]{1,0:T(8,128)(2,1)} %get-tuple-element.94.dpre_ref.prev_ref.next_ref), custom_call_target="tpu_custom_call" | custom-call | flops 68719476736 | bytes 1024 | tf_op jit(solution)/shard_map/weights/pallas_call | solution.py:912
  53.0 1.8 %split_first.3 = (bf16[640,512]{1,0:T(8,128)(2,1)S(1)}, bf16[640,512]{1,0:T(8,128)(2,1)}) custom-call(s32[1]{0:T(128)} %bitcast.11.bit_ref.refs_0_, bf16[1280,512]{1,0:T(8,128)(2,1)S(1)} %bitcast.35, bf16[1280,512]{1,0:T(8,128)(2,1)S(1)} %collective-permute-done.5.got, bf16[6,256,512]{2,1,0:T(8,128)(2,1)S(1)} %copy-done.6), custom_call_target="tpu_custom_call" | custom-call | flops 68719476736 | bytes 1024 | tf_op jit(solution)/shard_map/split_first/pallas_call | solution.py:483
  54.9 3.1 %collective-permute-start.10 = (bf16[640,512]{1,0:T(8,128)(2,1)}, bf16[640,512]{1,0:T(8,128)(2,1)}, u32[]{:S(2)}, u32[]{:S(2)}) collective-permute-start(bf16[640,512]{1,0:T(8,128)(2,1)} %get-tuple-element.114), channel_id=1, source_target_pairs={{0,4},{1,5},{2,6},{3,7},{4,0},{5,1},{6,2},{7,3},{8,12},{9,13},{10,... | collective-permute-start | bytes 1966088 | tf_op jit(solution)/shard_map/ppermute | solution.py:572
  61.5 7.5 %back.1 = (bf16[1536,256]{1,0:T(8,128)(2,1)S(1)}, bf16[1536,256]{1,0:T(8,128)(2,1)}, bf16[32,512]{1,0:T(8,128)(2,1)}) custom-call(s32[1]{0:T(128)} %bitcast.sec_ref.refs_1_, s32[3]{0:T(128)S(1)} %copy-done.5, s32[3,4]{1,0:T(4,128)S(1)} %copy-done.3, bf16[1536,1024]{1,0:T(8,128)(2,1)S(1)} %copy-done.10, bf16[1536,1024]{1,0:T(8,128)(2,1)S(1)} %copy-done.10, ...), custom_call_target="tpu_custom_call" | custom-call | flops 68719476736 | bytes 1024 | tf_op jit(solution)/shard_map/back/pallas_call | solution.py:932
  69.9 1.7 %split_first.5 = (bf16[768,512]{1,0:T(8,128)(2,1)S(1)}, bf16[768,512]{1,0:T(8,128)(2,1)S(1)}) custom-call(s32[1]{0:T(128)} %bitcast.6.bit_ref.refs_0_, bf16[1536,512]{1,0:T(8,128)(2,1)S(1)} %bitcast.34, bf16[1536,512]{1,0:T(8,128)(2,1)} %collective-permute-done.2.got, bf16[32,512]{1,0:T(8,128)(2,1)} %get-tuple-element.106.after_ref.refs_4_), custom_call_target="tpu_custom_call" | custom-call | flops 68719476736 | bytes 1024 | tf_op jit(solution)/shard_map/split_first/pallas_call | solution.py:483
  73.3 3.1 %join.2 = (bf16[3072,256]{1,0:T(8,128)(2,1)}, bf16[3072,256]{1,0:T(8,128)(2,1)}, f32[8,128]{1,0:T(8,128)S(1)}) custom-call(s32[1]{0:T(128)} %bitcast.sec_ref.refs_1_, bf16[1536,256]{1,0:T(8,128)(2,1)S(1)} %copy-done, bf16[1536,256]{1,0:T(8,128)(2,1)} %collective-permute-done.refs_1_, bf16[1536,256]{1,0:T(8,128)(2,1)S(1)} %copy-done.1, ...), custom_call_target="tpu_custom_call" | custom-call | flops 1024 | bytes 1024 | tf_op jit(solution)/shard_map/join/pallas_call | solution.py:534
  80.4 2.2 %collective-permute-start.13 = (bf16[320,512]{1,0:T(8,128)(2,1)S(1)}, bf16[320,512]{1,0:T(8,128)(2,1)S(1)}, u32[]{:S(2)}, u32[]{:S(2)}) collective-permute-start(bf16[320,512]{1,0:T(8,128)(2,1)S(1)} %get-tuple-element.121), channel_id=1, source_target_pairs={{0,8},{1,9},{2,10},{3,11},{4,12},{5,13},{6,14},{7,15},{8,0},{9,1},... | collective-permute-start | bytes 983048 | tf_op jit(solution)/shard_map/ppermute | solution.py:572
  82.6 3.3 %collective-permute-done.7.refs_3_ = bf16[768,512]{1,0:T(8,128)(2,1)S(1)} collective-permute-done((bf16[768,512]{1,0:T(8,128)(2,1)S(1)}, bf16[768,512]{1,0:T(8,128)(2,1)S(1)}, u32[]{:S(2)}, u32[]{:S(2)}) %collective-permute-start.7) | collective-permute-done | bytes 786464 | tf_op jit(solution)/shard_map/ppermute | solution.py:572
  86.8 2.3 %collective-permute-start.11 = (bf16[384,512]{1,0:T(8,128)(2,1)S(1)}, bf16[384,512]{1,0:T(8,128)(2,1)S(1)}, u32[]{:S(2)}, u32[]{:S(2)}) collective-permute-start(bf16[384,512]{1,0:T(8,128)(2,1)S(1)} %get-tuple-element.119), channel_id=1, source_target_pairs={{0,2},{1,3},{2,0},{3,1},{4,6},{5,7},{6,4},{7,5},{8,10},{9,11},{10,... | collective-permute-start | bytes 1179656 | tf_op jit(solution)/shard_map/ppermute | solution.py:572
  89.1 2.2 %collective-permute-start.12 = (bf16[32,512]{1,0:T(8,128)(2,1)S(1)}, bf16[32,512]{1,0:T(8,128)(2,1)S(1)}, u32[]{:S(2)}, u32[]{:S(2)}) collective-permute-start(bf16[32,512]{1,0:T(8,128)(2,1)S(1)} %get-tuple-element.120.refs_4_), channel_id=1, source_target_pairs={{0,8},{1,9},{2,10},{3,11},{4,12},{5,13},{6,14},{7,15},{8,0},{9,1},... | collective-permute-start | bytes 98312 | tf_op jit(solution)/shard_map/ppermute | solution.py:993
  91.9 2.3 %collective-permute-done.13.refs_2_ = bf16[320,512]{1,0:T(8,128)(2,1)S(1)} collective-permute-done((bf16[320,512]{1,0:T(8,128)(2,1)S(1)}, bf16[320,512]{1,0:T(8,128)(2,1)S(1)}, u32[]{:S(2)}, u32[]{:S(2)}) %collective-permute-start.13) | collective-permute-done | bytes 327712 | tf_op jit(solution)/shard_map/ppermute | solution.py:572
  96.8 1.6 collective-permute-start.15
  99.5 2.3 %collective-permute-start.21 = (bf16[128,512]{1,0:T(8,128)(2,1)}, bf16[128,512]{1,0:T(8,128)(2,1)}, u32[]{:S(2)}, u32[]{:S(2)}) collective-permute-start(bf16[128,512]{1,0:T(8,128)(2,1)} %add_body.6.refs_3_.refs_1_), channel_id=1, source_target_pairs={{0,8},{1,9},{2,10},{3,11},{4,12},{5,13},{6,14},{7,15},{8,0},{9,1},... | collective-permute-start | bytes 393224 | tf_op jit(solution)/shard_map/ppermute | solution.py:572
  101.9 2.0 %collective-permute-start.22 = (bf16[160,512]{1,0:T(8,128)(2,1)S(1)}, bf16[160,512]{1,0:T(8,128)(2,1)S(1)}, u32[]{:S(2)}, u32[]{:S(2)}) collective-permute-start(bf16[160,512]{1,0:T(8,128)(2,1)S(1)} %add_body.7.refs_6_.refs_1_), channel_id=1, source_target_pairs={{0,2},{1,3},{2,0},{3,1},{4,6},{5,7},{6,4},{7,5},{8,10},{9,11},{10,... | collective-permute-start | bytes 491528 | tf_op jit(solution)/shard_map/ppermute | solution.py:572
  103.9 4.3 %collective-permute-done.16.refs_5_ = bf16[48,512]{1,0:T(8,128)(2,1)S(1)} collective-permute-done((bf16[48,512]{1,0:T(8,128)(2,1)S(1)}, bf16[48,512]{1,0:T(8,128)(2,1)S(1)}, u32[]{:S(2)}, u32[]{:S(2)}) %collective-permute-start.16) | collective-permute-done | bytes 49184 | tf_op jit(solution)/shard_map/ppermute | solution.py:993
  112.9 7.4 %collective-permute-done.19.refs_3_ = bf16[192,512]{1,0:T(8,128)(2,1)S(1)} collective-permute-done((bf16[192,512]{1,0:T(8,128)(2,1)S(1)}, bf16[192,512]{1,0:T(8,128)(2,1)S(1)}, u32[]{:S(2)}, u32[]{:S(2)}) %collective-permute-start.19) | collective-permute-done | bytes 196640 | tf_op jit(solution)/shard_map/ppermute | solution.py:572
  121.3 2.7 %collective-permute-start.28 = (bf16[320,512]{1,0:T(8,128)(2,1)}, bf16[320,512]{1,0:T(8,128)(2,1)}, u32[]{:S(2)}, u32[]{:S(2)}) collective-permute-start(bf16[320,512]{1,0:T(8,128)(2,1)} %merge_body.6.refs_3_.refs_1_), channel_id=1, source_target_pairs={{0,8},{1,9},{2,10},{3,11},{4,12},{5,13},{6,14},{7,15},{8,0},{9,1},... | collective-permute-start | bytes 983048 | tf_op jit(solution)/shard_map/ppermute | solution.py:572
  125.0 2.2 %collective-permute-done.24.refs_5_ = bf16[144,512]{1,0:T(8,128)(2,1)S(1)} collective-permute-done((bf16[144,512]{1,0:T(8,128)(2,1)S(1)}, bf16[144,512]{1,0:T(8,128)(2,1)S(1)}, u32[]{:S(2)}, u32[]{:S(2)}) %collective-permute-start.24) | collective-permute-done | bytes 147488 | tf_op jit(solution)/shard_map/ppermute | solution.py:993
  128.1 2.4 %collective-permute-done.29.refs_2_ = bf16[256,512]{1,0:T(8,128)(2,1)S(1)} collective-permute-done((bf16[256,512]{1,0:T(8,128)(2,1)S(1)}, bf16[256,512]{1,0:T(8,128)(2,1)S(1)}, u32[]{:S(2)}, u32[]{:S(2)}) %collective-permute-start.29) | collective-permute-done | bytes 262176 | tf_op jit(solution)/shard_map/ppermute | solution.py:572
  134.3 1.8 %collective-permute-done.27.refs_2_ = bf16[384,512]{1,0:T(8,128)(2,1)S(1)} collective-permute-done((bf16[384,512]{1,0:T(8,128)(2,1)S(1)}, bf16[384,512]{1,0:T(8,128)(2,1)S(1)}, u32[]{:S(2)}, u32[]{:S(2)}) %collective-permute-start.27) | collective-permute-done | bytes 393248 | tf_op jit(solution)/shard_map/ppermute | solution.py:572
  136.4 2.0 %collective-permute-start.30 = (bf16[768,512]{1,0:T(8,128)(2,1)S(1)}, bf16[768,512]{1,0:T(8,128)(2,1)S(1)}, u32[]{:S(2)}, u32[]{:S(2)}) collective-permute-start(bf16[768,512]{1,0:T(8,128)(2,1)S(1)} %merge_body.11.after_ref.p0), channel_id=1, source_target_pairs={{0,1},{1,0},{2,3},{3,2},{4,5},{5,4},{6,7},{7,6},{8,9},{9,8},{10,11... | collective-permute-start | bytes 2359304 | tf_op jit(solution)/shard_map/ppermute | solution.py:572
  138.4 2.3 %step_grad.1 = (f32[512,512]{1,0:T(8,128)}, f32[1,1024]{1,0:T(1,128)}, f32[1,1024]{1,0:T(1,128)}, f32[1,1024]{1,0:T(1,128)}, f32[3,128]{1,0:T(4,128)S(1)}, /*index=5*/f32[8,128]{1,0:T(8,128)S(1)}) custom-call(bf16[272,512]{1,0:T(8,128)(2,1)S(1)} %get-tuple-element.134.rows_ref, bf16[768,512]{1,0:T(8,128)(2,1)S(1)} %merge_body.11.after_ref.p0), custom_call_target="tpu_custom_call" | custom-call | flops 68719476736 | bytes 1024 | tf_op jit(solution)/shard_map/step_grad/pallas_call | solution.py:1000
  140.6 2.3 %join.3 = (bf16[3072,256]{1,0:T(8,128)(2,1)}, f32[8,128]{1,0:T(8,128)S(1)}) custom-call(s32[1]{0:T(128)} %bitcast.sec_ref.refs_1_, bf16[1536,256]{1,0:T(8,128)(2,1)S(1)} %get-tuple-element.110.refs_0_, bf16[1536,256]{1,0:T(8,128)(2,1)} %collective-permute-done.6.refs_1_, f32[8,128]{1,0:T(8,128)S(1)} %get-tuple-element.136.refs_2_), custom_call_target="tpu_custom_call" | custom-call | flops 1024 | bytes 1024 | tf_op jit(solution)/shard_map/join/pallas_call | solution.py:534
  142.9 2.1 %place.6 = (f32[512,1024]{1,0:T(8,128)}, f32[512,512]{1,0:T(8,128)}, f32[512,512]{1,0:T(8,128)}, f32[512,512]{1,0:T(8,128)}, f32[8,128]{1,0:T(8,128)S(1)}) custom-call(s32[4]{0:T(128)S(1)} %pad_add_fusion.1.runs, bf16[640,512]{1,0:T(8,128)(2,1)S(1)} %merge_body.10.refs_3_.p0, bf16[640,512]{1,0:T(8,128)(2,1)S(1)} %collective-permute-done.35.p1, ...), custom_call_target="tpu_custom_call" | custom-call | flops 1024 | bytes 1024 | tf_op jit(solution)/shard_map/place/pallas_call | solution.py:679
  145.1 2.6 %place.7 = (f32[512,1024]{1,0:T(8,128)}, f32[512,1024]{1,0:T(8,128)}, f32[8,128]{1,0:T(8,128)S(1)}) custom-call(s32[4]{0:T(128)S(1)} %pad_add_fusion.runs, bf16[512,512]{1,0:T(8,128)(2,1)} %merge_body.9.refs_3_.p0, bf16[512,512]{1,0:T(8,128)(2,1)} %collective-permute-done.34.p1, f32[8,128]{1,0:T(8,128)S(1)} %get-tuple-element.140.after_ref), custom_call_target="tpu_custom_call" | custom-call | flops 1024 | bytes 1024 | tf_op jit(solution)/shard_map/place/pallas_call | solution.py:679
  147.7 2.3 %place.8 = (f32[1536,1024]{1,0:T(8,128)}, f32[8,128]{1,0:T(8,128)S(1)}) custom-call(s32[4]{0:T(128)S(1)} %pad_add_fusion.runs, bf16[768,512]{1,0:T(8,128)(2,1)S(1)} %merge_body.11.after_ref.p0, bf16[768,512]{1,0:T(8,128)(2,1)S(1)} %collective-permute-done.33.p1, f32[8,128]{1,0:T(8,128)S(1)} %get-tuple-element.141.after_ref), custom_call_target="tpu_custom_call" | custom-call | flops 1024 | bytes 1024 | tf_op jit(solution)/shard_map/place/pallas_call | solution.py:679
  150.0 3.6 %collective-permute-done.32.x_ref = bf16[640,512]{1,0:T(8,128)(2,1)S(1)} collective-permute-done((bf16[640,512]{1,0:T(8,128)(2,1)S(1)}, bf16[640,512]{1,0:T(8,128)(2,1)S(1)}, u32[]{:S(2)}, u32[]{:S(2)}) %collective-permute-start.32) | collective-permute-done | bytes 655392 | tf_op jit(solution)/shard_map/ppermute | solution.py:572
  156.2 2.0 %collective-permute-done.38.p1 = bf16[640,512]{1,0:T(8,128)(2,1)S(1)} collective-permute-done((bf16[640,512]{1,0:T(8,128)(2,1)S(1)}, bf16[640,512]{1,0:T(8,128)(2,1)S(1)}, u32[]{:S(2)}, u32[]{:S(2)}) %collective-permute-start.38) | collective-permute-done | bytes 655392 | tf_op jit(solution)/shard_map/ppermute | solution.py:547
  158.2 2.1 %place.9 = (f32[512,1024]{1,0:T(8,128)}, f32[512,512]{1,0:T(8,128)}, f32[512,512]{1,0:T(8,128)}, f32[512,512]{1,0:T(8,128)}, f32[8,128]{1,0:T(8,128)S(1)}) custom-call(s32[4]{0:T(128)S(1)} %pad_add_fusion.1.runs, bf16[640,512]{1,0:T(8,128)(2,1)S(1)} %then.3.after_ref.p0, ...), custom_call_target="tpu_custom_call", output_to_operand_aliasing={{0}: (4, {}), {1}: (5, {}), {2}: (6, {}), {3}: (7, {})} | custom-call | flops 1024 | bytes 1024 | tf_op jit(solution)/shard_map/place/pallas_call | solution.py:679
  160.3 2.0 %place.10 = (f32[512,1024]{1,0:T(8,128)}, f32[512,1024]{1,0:T(8,128)}, f32[8,128]{1,0:T(8,128)S(1)}) custom-call(s32[4]{0:T(128)S(1)} %pad_add_fusion.runs, bf16[512,512]{1,0:T(8,128)(2,1)S(1)} %then.4.after_ref.p0, bf16[512,512]{1,0:T(8,128)(2,1)S(1)} %collective-permute-done.37.p1, ...), custom_call_target="tpu_custom_call", output_to_operand_aliasing={{0}: (4, {}), {1}: (5, {})} | custom-call | flops 1024 | bytes 1024 | tf_op jit(solution)/shard_map/place/pallas_call | solution.py:679
  162.3 2.9 %place.11 = (f32[1536,1024]{1,0:T(8,128)}, f32[8,128]{1,0:T(8,128)}) custom-call(s32[4]{0:T(128)S(1)} %pad_add_fusion.runs, bf16[768,512]{1,0:T(8,128)(2,1)S(1)} %then.5.after_ref.p0, bf16[768,512]{1,0:T(8,128)(2,1)S(1)} %collective-permute-done.36.p1, f32[8,128]{1,0:T(8,128)S(1)} %get-tuple-element.150.after_ref, ...), custom_call_target="tpu_custom_call", output_to_operand_aliasing={{0}: (4, {})} | custom-call | flops 1024 | bytes 1024 | tf_op jit(solution)/shard_map/place/pallas_call | solution.py:679
  (111 shorter events, 33.8 us)
Async XLA Ops:
  39.4 10.8 %collective-permute-start.5 = (bf16[1280,512]{1,0:T(8,128)(2,1)}, bf16[1280,512]{1,0:T(8,128)(2,1)S(1)}, u32[]{:S(2)}, u32[]{:S(2)}) collective-permute-start(bf16[1280,512]{1,0:T(8,128)(2,1)} %bitcast.39), channel_id=1, source_target_pairs={{0,16},{16,0},{1,17},{17,1},{2,18},{18,2},{3,19},{19,3},{4,20},{20... | collective-permute-start | bytes 3932168 | tf_op jit(solution)/shard_map/ppermute | solution.py:547
  39.9 14.9 %collective-permute-start.4 = (bf16[1024,512]{1,0:T(8,128)(2,1)}, bf16[1024,512]{1,0:T(8,128)(2,1)S(1)}, u32[]{:S(2)}, u32[]{:S(2)}) collective-permute-start(bf16[1024,512]{1,0:T(8,128)(2,1)} %bitcast.40), channel_id=1, source_target_pairs={{0,16},{16,0},{1,17},{17,1},{2,18},{18,2},{3,19},{19,3},{4,20},{20... | collective-permute-start | bytes 3145736 | tf_op jit(solution)/shard_map/ppermute | solution.py:547
  40.0 19.1 %collective-permute-start.3 = (bf16[32,1024]{1,0:T(8,128)(2,1)}, bf16[32,1024]{1,0:T(8,128)(2,1)}, u32[]{:S(2)}, u32[]{:S(2)}) collective-permute-start(bf16[32,1024]{1,0:T(8,128)(2,1)} %get-tuple-element.97), channel_id=1, source_target_pairs={{0,16},{16,0},{1,17},{17,1},{2,18},{18,2},{3,19},{19,3},{4,20},{20... | collective-permute-start | bytes 196616 | tf_op jit(solution)/shard_map/ppermute | solution.py:547
  49.5 19.5 %collective-permute-start.2 = (bf16[1536,512]{1,0:T(8,128)(2,1)}, bf16[1536,512]{1,0:T(8,128)(2,1)}, u32[]{:S(2)}, u32[]{:S(2)}) collective-permute-start(bf16[1536,512]{1,0:T(8,128)(2,1)} %bitcast.38), channel_id=1, source_target_pairs={{0,16},{16,0},{1,17},{17,1},{2,18},{18,2},{3,19},{19,3},{4,20},{20... | collective-permute-start | bytes 4718600 | tf_op jit(solution)/shard_map/ppermute | solution.py:547
  49.6 22.0 %collective-permute-start = (bf16[1536,256]{1,0:T(8,128)(2,1)}, bf16[1536,256]{1,0:T(8,128)(2,1)}, u32[]{:S(2)}, u32[]{:S(2)}) collective-permute-start(bf16[1536,256]{1,0:T(8,128)(2,1)} %get-tuple-element.90), channel_id=1, source_target_pairs={{0,16},{16,0},{1,17},{17,1},{2,18},{18,2},{3,19},{19,3},{4,20},{20... | collective-permute-start | bytes 2359304 | tf_op jit(solution)/shard_map/ppermute | solution.py:547
  50.2 21.6 %collective-permute-start.1 = (bf16[1536,256]{1,0:T(8,128)(2,1)}, bf16[1536,256]{1,0:T(8,128)(2,1)}, u32[]{:S(2)}, u32[]{:S(2)}) collective-permute-start(bf16[1536,256]{1,0:T(8,128)(2,1)} %get-tuple-element.92), channel_id=1, source_target_pairs={{0,16},{16,0},{1,17},{17,1},{2,18},{18,2},{3,19},{19,3},{4,20},{20... | collective-permute-start | bytes 2359304 | tf_op jit(solution)/shard_map/ppermute | solution.py:547
  54.9 21.5 %collective-permute-start.10 = (bf16[640,512]{1,0:T(8,128)(2,1)}, bf16[640,512]{1,0:T(8,128)(2,1)}, u32[]{:S(2)}, u32[]{:S(2)}) collective-permute-start(bf16[640,512]{1,0:T(8,128)(2,1)} %get-tuple-element.114), channel_id=1, source_target_pairs={{0,4},{1,5},{2,6},{3,7},{4,0},{5,1},{6,2},{7,3},{8,12},{9,13},{10,... | collective-permute-start | bytes 1966088 | tf_op jit(solution)/shard_map/ppermute | solution.py:572
  59.1 18.5 %collective-permute-start.9 = (bf16[512,512]{1,0:T(8,128)(2,1)}, bf16[512,512]{1,0:T(8,128)(2,1)}, u32[]{:S(2)}, u32[]{:S(2)}) collective-permute-start(bf16[512,512]{1,0:T(8,128)(2,1)} %get-tuple-element.113), channel_id=1, source_target_pairs={{0,1},{1,0},{2,3},{3,2},{4,5},{5,4},{6,7},{7,6},{8,9},{9,8},{10,11... | collective-permute-start | bytes 1572872 | tf_op jit(solution)/shard_map/ppermute | solution.py:572
  69.0 13.6 %collective-permute-start.8 = (bf16[32,512]{1,0:T(8,128)(2,1)}, bf16[32,512]{1,0:T(8,128)(2,1)}, u32[]{:S(2)}, u32[]{:S(2)}) collective-permute-start(bf16[32,512]{1,0:T(8,128)(2,1)} %get-tuple-element.106.after_ref.refs_4_), channel_id=1, source_target_pairs={{0,16},{16,0},{1,17},{17,1},{2,18},{18,2},{3,19},{19,3},{4,20},{20... | collective-permute-start | bytes 98312 | tf_op jit(solution)/shard_map/ppermute | solution.py:547
  71.6 64.7 %collective-permute-start.6 = (bf16[1536,256]{1,0:T(8,128)(2,1)}, bf16[1536,256]{1,0:T(8,128)(2,1)}, u32[]{:S(2)}, u32[]{:S(2)}) collective-permute-start(bf16[1536,256]{1,0:T(8,128)(2,1)} %get-tuple-element.111), channel_id=1, source_target_pairs={{0,16},{16,0},{1,17},{17,1},{2,18},{18,2},{3,19},{19,3},{4,20},{20... | collective-permute-start | bytes 2359304 | tf_op jit(solution)/shard_map/ppermute | solution.py:547
  71.7 14.1 %collective-permute-start.7 = (bf16[768,512]{1,0:T(8,128)(2,1)S(1)}, bf16[768,512]{1,0:T(8,128)(2,1)S(1)}, u32[]{:S(2)}, u32[]{:S(2)}) collective-permute-start(bf16[768,512]{1,0:T(8,128)(2,1)S(1)} %get-tuple-element.112), channel_id=1, source_target_pairs={{0,1},{1,0},{2,3},{3,2},{4,5},{5,4},{6,7},{7,6},{8,9},{9,8},{10,11... | collective-permute-start | bytes 2359304 | tf_op jit(solution)/shard_map/ppermute | solution.py:572
  78.8 12.5 %collective-permute-start.14 = (bf16[256,512]{1,0:T(8,128)(2,1)S(1)}, bf16[256,512]{1,0:T(8,128)(2,1)S(1)}, u32[]{:S(2)}, u32[]{:S(2)}) collective-permute-start(bf16[256,512]{1,0:T(8,128)(2,1)S(1)} %get-tuple-element.122), channel_id=1, source_target_pairs={{0,2},{1,3},{2,0},{3,1},{4,6},{5,7},{6,4},{7,5},{8,10},{9,11},{10,... | collective-permute-start | bytes 786440 | tf_op jit(solution)/shard_map/ppermute | solution.py:572
  80.4 13.9 %collective-permute-start.13 = (bf16[320,512]{1,0:T(8,128)(2,1)S(1)}, bf16[320,512]{1,0:T(8,128)(2,1)S(1)}, u32[]{:S(2)}, u32[]{:S(2)}) collective-permute-start(bf16[320,512]{1,0:T(8,128)(2,1)S(1)} %get-tuple-element.121), channel_id=1, source_target_pairs={{0,8},{1,9},{2,10},{3,11},{4,12},{5,13},{6,14},{7,15},{8,0},{9,1},... | collective-permute-start | bytes 983048 | tf_op jit(solution)/shard_map/ppermute | solution.py:572
  86.8 9.8 %collective-permute-start.11 = (bf16[384,512]{1,0:T(8,128)(2,1)S(1)}, bf16[384,512]{1,0:T(8,128)(2,1)S(1)}, u32[]{:S(2)}, u32[]{:S(2)}) collective-permute-start(bf16[384,512]{1,0:T(8,128)(2,1)S(1)} %get-tuple-element.119), channel_id=1, source_target_pairs={{0,2},{1,3},{2,0},{3,1},{4,6},{5,7},{6,4},{7,5},{8,10},{9,11},{10,... | collective-permute-start | bytes 1179656 | tf_op jit(solution)/shard_map/ppermute | solution.py:572
  91.4 7.5 %collective-permute-start.18 = (bf16[128,512]{1,0:T(8,128)(2,1)S(1)}, bf16[128,512]{1,0:T(8,128)(2,1)S(1)}, u32[]{:S(2)}, u32[]{:S(2)}) collective-permute-start(bf16[128,512]{1,0:T(8,128)(2,1)S(1)} %get-tuple-element.129), channel_id=1, source_target_pairs={{0,4},{1,5},{2,6},{3,7},{4,0},{5,1},{6,2},{7,3},{8,12},{9,13},{10,... | collective-permute-start | bytes 393224 | tf_op jit(solution)/shard_map/ppermute | solution.py:572
  94.3 7.5 %collective-permute-start.17 = (bf16[160,512]{1,0:T(8,128)(2,1)S(1)}, bf16[160,512]{1,0:T(8,128)(2,1)S(1)}, u32[]{:S(2)}, u32[]{:S(2)}) collective-permute-start(bf16[160,512]{1,0:T(8,128)(2,1)S(1)} %get-tuple-element.128), channel_id=1, source_target_pairs={{0,1},{1,0},{2,3},{3,2},{4,5},{5,4},{6,7},{7,6},{8,9},{9,8},{10,11... | collective-permute-start | bytes 491528 | tf_op jit(solution)/shard_map/ppermute | solution.py:572
  96.8 11.5 %collective-permute-start.15 = (bf16[192,512]{1,0:T(8,128)(2,1)S(1)}, bf16[192,512]{1,0:T(8,128)(2,1)S(1)}, u32[]{:S(2)}, u32[]{:S(2)}) collective-permute-start(bf16[192,512]{1,0:T(8,128)(2,1)S(1)} %get-tuple-element.126), channel_id=1, source_target_pairs={{0,4},{1,5},{2,6},{3,7},{4,0},{5,1},{6,2},{7,3},{8,12},{9,13},{10,... | collective-permute-start | bytes 589832 | tf_op jit(solution)/shard_map/ppermute | solution.py:572
  98.4 9.8 %collective-permute-start.16 = (bf16[48,512]{1,0:T(8,128)(2,1)S(1)}, bf16[48,512]{1,0:T(8,128)(2,1)S(1)}, u32[]{:S(2)}, u32[]{:S(2)}) collective-permute-start(bf16[48,512]{1,0:T(8,128)(2,1)S(1)} %get-tuple-element.127.refs_4_), channel_id=1, source_target_pairs={{0,4},{1,5},{2,6},{3,7},{4,0},{5,1},{6,2},{7,3},{8,12},{9,13},{10,... | collective-permute-start | bytes 147464 | tf_op jit(solution)/shard_map/ppermute | solution.py:993
  99.5 10.6 %collective-permute-start.21 = (bf16[128,512]{1,0:T(8,128)(2,1)}, bf16[128,512]{1,0:T(8,128)(2,1)}, u32[]{:S(2)}, u32[]{:S(2)}) collective-permute-start(bf16[128,512]{1,0:T(8,128)(2,1)} %add_body.6.refs_3_.refs_1_), channel_id=1, source_target_pairs={{0,8},{1,9},{2,10},{3,11},{4,12},{5,13},{6,14},{7,15},{8,0},{9,1},... | collective-permute-start | bytes 393224 | tf_op jit(solution)/shard_map/ppermute | solution.py:572
  101.9 7.6 %collective-permute-start.22 = (bf16[160,512]{1,0:T(8,128)(2,1)S(1)}, bf16[160,512]{1,0:T(8,128)(2,1)S(1)}, u32[]{:S(2)}, u32[]{:S(2)}) collective-permute-start(bf16[160,512]{1,0:T(8,128)(2,1)S(1)} %add_body.7.refs_6_.refs_1_), channel_id=1, source_target_pairs={{0,2},{1,3},{2,0},{3,1},{4,6},{5,7},{6,4},{7,5},{8,10},{9,11},{10,... | collective-permute-start | bytes 491528 | tf_op jit(solution)/shard_map/ppermute | solution.py:572
  108.3 12.0 %collective-permute-start.19 = (bf16[192,512]{1,0:T(8,128)(2,1)S(1)}, bf16[192,512]{1,0:T(8,128)(2,1)S(1)}, u32[]{:S(2)}, u32[]{:S(2)}) collective-permute-start(bf16[192,512]{1,0:T(8,128)(2,1)S(1)} %get-tuple-element.130.refs_3_.refs_2_), channel_id=1, source_target_pairs={{0,8},{1,9},{2,10},{3,11},{4,12},{5,13},{6,14},{7,15},{8,0},{9,1},... | collective-permute-start | bytes 589832 | tf_op jit(solution)/shard_map/ppermute | solution.py:572
  109.5 11.0 %collective-permute-start.26 = (bf16[160,512]{1,0:T(8,128)(2,1)S(1)}, bf16[160,512]{1,0:T(8,128)(2,1)S(1)}, u32[]{:S(2)}, u32[]{:S(2)}) collective-permute-start(bf16[160,512]{1,0:T(8,128)(2,1)S(1)} %add_body.9.refs_3_.refs_1_), channel_id=1, source_target_pairs={{0,1},{1,0},{2,3},{3,2},{4,5},{5,4},{6,7},{7,6},{8,9},{9,8},{10,11... | collective-permute-start | bytes 491528 | tf_op jit(solution)/shard_map/ppermute | solution.py:572
  111.1 12.9 %collective-permute-start.25 = (bf16[128,512]{1,0:T(8,128)(2,1)S(1)}, bf16[128,512]{1,0:T(8,128)(2,1)S(1)}, u32[]{:S(2)}, u32[]{:S(2)}) collective-permute-start(bf16[128,512]{1,0:T(8,128)(2,1)S(1)} %add_body.10.refs_6_.refs_1_), channel_id=1, source_target_pairs={{0,4},{1,5},{2,6},{3,7},{4,0},{5,1},{6,2},{7,3},{8,12},{9,13},{10,... | collective-permute-start | bytes 393224 | tf_op jit(solution)/shard_map/ppermute | solution.py:572
  120.4 7.2 %collective-permute-start.23 = (bf16[192,512]{1,0:T(8,128)(2,1)S(1)}, bf16[192,512]{1,0:T(8,128)(2,1)S(1)}, u32[]{:S(2)}, u32[]{:S(2)}) collective-permute-start(bf16[192,512]{1,0:T(8,128)(2,1)S(1)} %get-tuple-element.132.refs_3_.refs_2_), channel_id=1, source_target_pairs={{0,4},{1,5},{2,6},{3,7},{4,0},{5,1},{6,2},{7,3},{8,12},{9,13},{10,... | collective-permute-start | bytes 589832 | tf_op jit(solution)/shard_map/ppermute | solution.py:572
  121.3 11.8 %collective-permute-start.28 = (bf16[320,512]{1,0:T(8,128)(2,1)}, bf16[320,512]{1,0:T(8,128)(2,1)}, u32[]{:S(2)}, u32[]{:S(2)}) collective-permute-start(bf16[320,512]{1,0:T(8,128)(2,1)} %merge_body.6.refs_3_.refs_1_), channel_id=1, source_target_pairs={{0,8},{1,9},{2,10},{3,11},{4,12},{5,13},{6,14},{7,15},{8,0},{9,1},... | collective-permute-start | bytes 983048 | tf_op jit(solution)/shard_map/ppermute | solution.py:572
  127.6 8.6 %collective-permute-start.27 = (bf16[384,512]{1,0:T(8,128)(2,1)S(1)}, bf16[384,512]{1,0:T(8,128)(2,1)S(1)}, u32[]{:S(2)}, u32[]{:S(2)}) collective-permute-start(bf16[384,512]{1,0:T(8,128)(2,1)S(1)} %get-tuple-element.135.refs_3_.refs_1_), channel_id=1, source_target_pairs={{0,2},{1,3},{2,0},{3,1},{4,6},{5,7},{6,4},{7,5},{8,10},{9,11},{10,... | collective-permute-start | bytes 1179656 | tf_op jit(solution)/shard_map/ppermute | solution.py:572
  131.3 13.8 %collective-permute-start.34 = (bf16[512,512]{1,0:T(8,128)(2,1)}, bf16[512,512]{1,0:T(8,128)(2,1)}, u32[]{:S(2)}, u32[]{:S(2)}) collective-permute-start(bf16[512,512]{1,0:T(8,128)(2,1)} %merge_body.9.refs_3_.p0), channel_id=1, source_target_pairs={{0,16},{16,0},{1,17},{17,1},{2,18},{18,2},{3,19},{19,3},{4,20},{20... | collective-permute-start | bytes 1572872 | tf_op jit(solution)/shard_map/ppermute | solution.py:547
  131.3 22.4 %collective-permute-start.31 = (bf16[512,512]{1,0:T(8,128)(2,1)}, bf16[512,512]{1,0:T(8,128)(2,1)}, u32[]{:S(2)}, u32[]{:S(2)}) collective-permute-start(bf16[512,512]{1,0:T(8,128)(2,1)} %merge_body.9.refs_3_.p0), channel_id=1, source_target_pairs={{0,1},{1,0},{2,3},{3,2},{4,5},{5,4},{6,7},{7,6},{8,9},{9,8},{10,11... | collective-permute-start | bytes 1572872 | tf_op jit(solution)/shard_map/ppermute | solution.py:572
  136.2 17.5 %collective-permute-start.32 = (bf16[640,512]{1,0:T(8,128)(2,1)S(1)}, bf16[640,512]{1,0:T(8,128)(2,1)S(1)}, u32[]{:S(2)}, u32[]{:S(2)}) collective-permute-start(bf16[640,512]{1,0:T(8,128)(2,1)S(1)} %merge_body.10.refs_3_.p0), channel_id=1, source_target_pairs={{0,4},{1,5},{2,6},{3,7},{4,0},{5,1},{6,2},{7,3},{8,12},{9,13},{10,... | collective-permute-start | bytes 1966088 | tf_op jit(solution)/shard_map/ppermute | solution.py:572
  136.3 11.4 %collective-permute-start.33 = (bf16[768,512]{1,0:T(8,128)(2,1)S(1)}, bf16[768,512]{1,0:T(8,128)(2,1)S(1)}, u32[]{:S(2)}, u32[]{:S(2)}) collective-permute-start(bf16[768,512]{1,0:T(8,128)(2,1)S(1)} %merge_body.11.after_ref.p0), channel_id=1, source_target_pairs={{0,16},{16,0},{1,17},{17,1},{2,18},{18,2},{3,19},{19,3},{4,20},{20... | collective-permute-start | bytes 2359304 | tf_op jit(solution)/shard_map/ppermute | solution.py:547
  136.4 18.4 %collective-permute-start.30 = (bf16[768,512]{1,0:T(8,128)(2,1)S(1)}, bf16[768,512]{1,0:T(8,128)(2,1)S(1)}, u32[]{:S(2)}, u32[]{:S(2)}) collective-permute-start(bf16[768,512]{1,0:T(8,128)(2,1)S(1)} %merge_body.11.after_ref.p0), channel_id=1, source_target_pairs={{0,1},{1,0},{2,3},{3,2},{4,5},{5,4},{6,7},{7,6},{8,9},{9,8},{10,11... | collective-permute-start | bytes 2359304 | tf_op jit(solution)/shard_map/ppermute | solution.py:572
  154.9 7.4 %collective-permute-start.36 = (bf16[768,512]{1,0:T(8,128)(2,1)S(1)}, bf16[768,512]{1,0:T(8,128)(2,1)S(1)}, u32[]{:S(2)}, u32[]{:S(2)}) collective-permute-start(bf16[768,512]{1,0:T(8,128)(2,1)S(1)} %then.5.after_ref.p0), channel_id=1, source_target_pairs={{0,16},{16,0},{1,17},{17,1},{2,18},{18,2},{3,19},{19,3},{4,20},{20... | collective-permute-start | bytes 2359304 | tf_op jit(solution)/shard_map/ppermute | solution.py:547
  (20 other events, 78.1 us)

commit v5 on v4

--- a/solution.py
+++ b/solution.py
@@ -482,7 +482,7 @@
     rows, width = held.shape[0] // 2, held.shape[1]
     return pl.pallas_call(
         first_kernel,
-        in_specs=[IN_SMEM, IN_HBM, IN_HBM, ANYWHERE],
+        in_specs=[IN_SMEM, ANYWHERE, ANYWHERE, ANYWHERE],
         out_specs=[IN_VMEM] * 2,
         out_shape=[struct(rows, width)] * 2,
         scratch_shapes=[pltpu.VMEM((4, rows, width), BF16), pltpu.SemaphoreType.DMA((4,))],
@@ -811,7 +811,7 @@
         return const((n, half, width)), shape(n, half, width)
 
     film_spec, film_shape = blocks_of(5)
-    side_spec, side_shape = blocks_of(4)
+    side_spec, side_shape = blocks_of(4)[0], shape(6, half, width)
     (
         stack,
         d_pre,
@@ -906,26 +906,33 @@
             sums, padded(keep.reshape(-1, width), rows), padded(give.reshape(-1, width), rows)
         )
 
-    batch_a, batch_c = batch(keep_a, give_a, far_first), batch(keep_c, give_c, sums)
+    def tap_grads(first, end, blocks, at, after, outs=()):
+        spec = pl.BlockSpec((2, half, width), lambda i, *_: (at + i, 0, 0))
+        return pl.pallas_call(
+            weight_kernel,
+            grid_spec=pltpu.PrefetchScalarGridSpec(
+                num_scalar_prefetch=1,
+                grid=(end - first,),
+                in_specs=[pl.BlockSpec((own, width), lambda i, *_: (0, first + i)), whole(d_pre)]
+                + [ANYWHERE] * (1 + len(outs)),
+                out_specs=[spec, spec],
+                scratch_shapes=[pltpu.VMEM((width, wide), F32)],
+            ),
+            out_shape=[shape(blocks, half, width)] * 2,
+            input_output_aliases={4 + k: k for k in range(len(outs))},
+            compiler_params=pltpu.CompilerParams(vmem_limit_bytes=KB_VMEM),
+            cost_estimate=LARGE,
+            name="weights",
+        )(sec, stack, d_pre, after, *outs)
+
+    batch_a = batch(keep_a, give_a, far_first)
     block_got, skip_got, other_edge = swap(block_give), swap(skip_give), swap(edge)
-    spec = pl.BlockSpec((2, half, width), lambda i, *_: (i, 0, 0))
-    keep_b, give_b = pl.pallas_call(
-        weight_kernel,
-        grid_spec=pltpu.PrefetchScalarGridSpec(
-            num_scalar_prefetch=1,
-            grid=(taps,),
-            in_specs=[pl.BlockSpec((own, width), lambda i, *_: (0, i)), whole(d_pre)],
-            out_specs=[spec, spec],
-            scratch_shapes=[pltpu.VMEM((width, wide), F32)],
-        ),
-        out_shape=[shape(2 * taps, half, width)] * 2,
-        compiler_params=pltpu.CompilerParams(vmem_limit_bytes=KB_VMEM),
-        cost_estimate=LARGE,
-        name="weights",
-    )(sec, stack, d_pre)
+    keep_c, give_c = tap_grads(0, 1, 6, 2, vec, (keep_c, give_c))
+    batch_c = batch(keep_c, give_c, sums)
+    (after,) = batch_a.turn(keep_c)
+    (after,) = batch_c.turn(after)
+    keep_b, give_b = tap_grads(1, taps, 2 * (taps - 1), 0, after)
     batch_b = batch(keep_b, give_b, sums)
-    (after,) = batch_a.turn(keep_b)
-    (after,) = batch_c.turn(after)
 
     group = -(-(micro * slots + 2) // 16) * 16
     rows_last = own // EDGE - 1
@@ -954,7 +961,7 @@
         ),
         out_shape=[shape(own, half), shape(own, half), shape(group + EDGE, width)],
         compiler_params=pltpu.CompilerParams(vmem_limit_bytes=KC_VMEM),
-        cost_estimate=LARGE,
+        cost_estimate=SMALL,
         name="back",
     )(
         sec,
@@ -968,20 +975,19 @@
         conv_flat,
         step_index,
         vec,
-        after,
+        keep_b,
     )
     in_got = swap(in_give)
 
-    (after,) = batch_b.turn(rows_now)
     block_out, skip_out, after = join(
-        sec, after, (block_keep, block_got), (skip_keep, skip_got)
+        sec, rows_now, (block_keep, block_got), (skip_keep, skip_got)
     )
     rows_got, rows_bit, gathered = swap(rows_now), sec, 0
     batches = {"a": batch_a, "b": batch_b, "c": batch_c}
-    order = "acb" + "cab" * 2 + "acb" * (batch_a.turns - 5) + "cab"
+    order = "cab" * (batch_a.turns - 1) + "b"
     for name in order:
         turner = batches[name]
-        if name == "b" and gathered <= sums.levels:
+        if name == "b" and turner.step and gathered <= sums.levels:
             n = rows_now.shape[0]
             work = (add_body, rows_bit, rows_now, rows_got, [struct(n, width)])
             if gathered:
@@ -1015,18 +1021,21 @@
     square, tall = struct(width, width, F32), struct(width, wide, F32)
     shapes_a = [tall, square, square, square]
     spots_a = spots_of(pairs(0, 1) + [(k, 0, 0) for k in (1, 2, 3)], width)
-    shapes_b, spots_b = [struct(taps * width, wide, F32)], spots_of(pairs(0, taps), width)
-    shapes_c, spots_c = [tall, tall], spots_of(pairs(0, 1) + pairs(1, 1), width)
+    conv = struct(taps * width, wide, F32)
+    shapes_c, spots_c = [tall, tall, conv], spots_of(pairs(0, 1) + pairs(1, 1) + pairs(2, 1), width)
+    shapes_b, spots_b = [conv], spots_of(pairs(0, taps - 1, width), width)
     *outs_a, mark = batch_a.early(shapes_a, spots_a, mark)
     *outs_c, mark = batch_c.early(shapes_c, spots_c, mark)
-    *outs_b, mark = batch_b.early(shapes_b, spots_b, mark)
-    mark = batch_b.arrive(batch_c.arrive(batch_a.arrive(mark)))
+    outs_c[2], mark = batch_b.early(shapes_b, spots_b, mark, outs_c[2:])
+    mark = batch_a.arrive(mark)
+    mark = batch_c.arrive(mark)
+    mark = batch_b.arrive(mark)
     *outs_a, mark = batch_a.late(shapes_a, spots_a, mark, outs_a)
     *outs_c, mark = batch_c.late(shapes_c, spots_c, mark, outs_c)
-    *outs_b, mark = batch_b.late(shapes_b, spots_b, mark, outs_b)
+    outs_c[2], mark = batch_b.late(shapes_b, spots_b, mark, outs_c[2:])
     g_out, g_query, g_key, g_value = outs_a
-    g_conv = outs_b[0].reshape(conv_w.shape)
-    g_res, g_cond = outs_c
+    g_res, g_cond, g_conv = outs_c
+    g_conv = g_conv.reshape(conv_w.shape)
     g_convb, g_resb, g_outb = (x.reshape(wide) for x in (g_convb, g_resb, g_outb))
     levels = levels[:, 0]
     return (

time: 166 us -> 170 us (1.024)
  waiting for transfers between devices: 32.2 us -> 43 us
  starting transfers between devices: 36.4 us -> 32.5 us
  Pallas kernels: 91.2 us -> 87.4 us
    ppermute x21, waiting for transfers between devices: 22.8 us -> 37.5 us  [send(): return lax.ppermute(x, ('section', 'dp'), route)]
    pallas_call x18, Pallas kernels: 8.32 us -> 4.25 us  [pair_call(): pl.pallas_call(functools.partial(pair_kernel, [w[0] for w in works], outs...]
    ppermute x21, starting transfers between devices: 29.2 us -> 25.4 us  [send(): return lax.ppermute(x, ('section', 'dp'), route)]
    pallas_call x4 -> x5, Pallas kernels: 13.8 us -> 16.3 us  [the longest x2 12.7 us: tap_grads(): pl.pallas_call(weight_kernel, grid_spec=pltpu.PrefetchScalarGridSpec(num_...]
    ppermute x14, waiting for transfers between devices: 2.06 us -> 0.04 us  [swap(): return lax.ppermute(x, 'section', [(0, 1), (1, 0)])]
    ppermute x4, waiting for transfers between devices: 7.33 us -> 5.42 us  [on_device(): rows_got = lax.ppermute(rows_now, 'dp', route)]
    unnamed x26 -> x42, local copies, waits for them, and re-layouts: 3.53 us -> 4.89 us
  transfers between devices with their start and end apart: 39 -> 39, of which waited for: 14 -> 12; matrix products, arithmetic and copies ran while one was open for 0% -> 0% of each run, Pallas kernels for 30% -> 27%
where the time goes in v5:
time: 170 us
  Pallas kernels  87.4 us (51%)
  waiting for transfers between devices  43 us (25%)
  starting transfers between devices  32.5 us (19%)
  local copies, waits for them, and re-layouts  5.52 us (3%)
    pallas_call x1, Pallas kernels, on_device(): pl.pallas_call(functools.partial(forward_kernel, (tile, slots, nq, subs,...  38.7 us
    ppermute x21, waiting for transfers between devices, send(): return lax.ppermute(x, ('section', 'dp'), route)  37.5 us
    ppermute x21, starting transfers between devices, send(): return lax.ppermute(x, ('section', 'dp'), route)  25.4 us
    pallas_call x6, Pallas kernels, place(): pl.pallas_call(functools.partial(place_kernel, which, full, len(shapes)),...  13.5 us
    pallas_call x2, Pallas kernels, tap_grads(): pl.pallas_call(weight_kernel, grid_spec=pltpu.PrefetchScalarGridSpec(num_...  12.7 us
    pallas_call x1, Pallas kernels, on_device(): pl.pallas_call(functools.partial(back_kernel, (tile, slots, subs, tiles,...  7.39 us
    ppermute x4, waiting for transfers between devices, on_device(): rows_got = lax.ppermute(rows_now, 'dp', route)  5.42 us
    unnamed x42, local copies, waits for them, and re-layouts  4.89 us
  transfers between devices with their start and end apart: 39, of which 12 were waited for; matrix products, arithmetic and copies ran while one was open for 0% of the time, Pallas kernels for 27%

profile of v5, /device:TPU:0, one launch (start us, length us, event | category | flops | bytes accessed | tf_op | source)
XLA Modules:
  0.0 169.8 jit_solution(8635408474604802159)
XLA Ops:
  0.7 38.7 %forward.1 = (bf16[1536,1536]{1,0:T(8,128)(2,1)}, bf16[1536,1024]{1,0:T(8,128)(2,1)}, bf16[32,1024]{1,0:T(8,128)(2,1)}, bf16[1536,512]{1,0:T(8,128)(2,1)}, bf16[...) custom-call(s32[1]{0:T(128)} %bitcast.sec_ref.refs_1_, ...), custom_call_target="tpu_custom_call" | custom-call | flops 68719476736 | bytes 1024 | tf_op jit(solution)/shard_map/forward/pallas_call | solution.py:829
  39.9 5.2 %weights.2 = (bf16[6,256,512]{2,1,0:T(8,128)(2,1)}, bf16[6,256,512]{2,1,0:T(8,128)(2,1)}) custom-call(s32[1]{0:T(128)} %bitcast.sec_ref.refs_1_, bf16[1536,1536]{1,0:T(8,128)(2,1)} %get-tuple-element.101.left_ref, bf16[1536,1024]{1,0:T(8,128)(2,1)} %get-tuple-element.97.dpre_ref.prev_ref.next_ref, ...), custom_call_target="tpu_custom_call", output_to_operand_aliasing={{0}: (4, {}), {1}: (5, {})} | custom-call | flops 68719476736 | bytes 1024 | tf_op jit(solution)/shard_map/weights/pallas_call | solution.py:911
  48.9 1.9 %split_first.3 = (bf16[640,512]{1,0:T(8,128)(2,1)S(1)}, bf16[640,512]{1,0:T(8,128)(2,1)}) custom-call(s32[1]{0:T(128)} %bitcast.9.bit_ref.refs_0_, bf16[1280,512]{1,0:T(8,128)(2,1)S(1)} %bitcast.36, bf16[1280,512]{1,0:T(8,128)(2,1)S(1)} %collective-permute-done.4.got, bf16[6,256,512]{2,1,0:T(8,128)(2,1)S(1)} %copy-done.14), custom_call_target="tpu_custom_call" | custom-call | flops 68719476736 | bytes 1024 | tf_op jit(solution)/shard_map/split_first/pallas_call | solution.py:483
  50.8 2.7 %collective-permute-start.7 = (bf16[640,512]{1,0:T(8,128)(2,1)}, bf16[640,512]{1,0:T(8,128)(2,1)}, u32[]{:S(2)}, u32[]{:S(2)}) collective-permute-start(bf16[640,512]{1,0:T(8,128)(2,1)} %get-tuple-element.117), channel_id=1, source_target_pairs={{0,4},{1,5},{2,6},{3,7},{4,0},{5,1},{6,2},{7,3},{8,12},{9,13},{10,... | collective-permute-start | bytes 1966088 | tf_op jit(solution)/shard_map/ppermute | solution.py:572
  55.6 1.5 collective-permute-start.8
  57.2 7.5 %weights.3 = (bf16[4,256,512]{2,1,0:T(8,128)(2,1)}, bf16[4,256,512]{2,1,0:T(8,128)(2,1)}) custom-call(s32[1]{0:T(128)} %bitcast.sec_ref.refs_1_, bf16[1536,1536]{1,0:T(8,128)(2,1)} %get-tuple-element.101.left_ref, bf16[1536,1024]{1,0:T(8,128)(2,1)} %get-tuple-element.97.dpre_ref.prev_ref.next_ref, bf16[768,512]{1,0:T(8,128)(2,1)} %copy-done.17), custom_call_target="tpu_custom_call" | custom-call | flops 68719476736 | bytes 1024 | tf_op jit(solution)/shard_map/weights/pallas_call | solution.py:911
  66.9 7.4 %back.1 = (bf16[1536,256]{1,0:T(8,128)(2,1)S(1)}, bf16[1536,256]{1,0:T(8,128)(2,1)S(1)}, bf16[32,512]{1,0:T(8,128)(2,1)}) custom-call(s32[1]{0:T(128)} %bitcast.sec_ref.refs_1_, s32[3]{0:T(128)S(1)} %copy-done.11, s32[3,4]{1,0:T(4,128)S(1)} %copy-done.9, bf16[1536,1024]{1,0:T(8,128)(2,1)S(1)} %copy-done, bf16[1536,1024]{1,0:T(8,128)(2,1)S(1)} %copy-done, ...), custom_call_target="tpu_custom_call" | custom-call | flops 1024 | bytes 1024 | tf_op jit(solution)/shard_map/back/pallas_call | solution.py:939
  74.4 3.7 %join.2 = (bf16[3072,256]{1,0:T(8,128)(2,1)}, bf16[3072,256]{1,0:T(8,128)(2,1)}, f32[8,128]{1,0:T(8,128)S(1)}) custom-call(s32[1]{0:T(128)} %bitcast.sec_ref.refs_1_, bf16[1536,256]{1,0:T(8,128)(2,1)S(1)} %copy-done.6, bf16[1536,256]{1,0:T(8,128)(2,1)} %collective-permute-done.refs_1_, bf16[1536,256]{1,0:T(8,128)(2,1)S(1)} %copy-done.7, ...), custom_call_target="tpu_custom_call" | custom-call | flops 1024 | bytes 1024 | tf_op jit(solution)/shard_map/join/pallas_call | solution.py:534
  81.5 2.7 %collective-permute-start.11 = (bf16[320,512]{1,0:T(8,128)(2,1)S(1)}, bf16[320,512]{1,0:T(8,128)(2,1)S(1)}, u32[]{:S(2)}, u32[]{:S(2)}) collective-permute-start(bf16[320,512]{1,0:T(8,128)(2,1)S(1)} %get-tuple-element.124), channel_id=1, source_target_pairs={{0,8},{1,9},{2,10},{3,11},{4,12},{5,13},{6,14},{7,15},{8,0},{9,1},... | collective-permute-start | bytes 983048 | tf_op jit(solution)/shard_map/ppermute | solution.py:572
  85.2 2.9 %collective-permute-done.12.refs_2_ = bf16[384,512]{1,0:T(8,128)(2,1)S(1)} collective-permute-done((bf16[384,512]{1,0:T(8,128)(2,1)S(1)}, bf16[384,512]{1,0:T(8,128)(2,1)S(1)}, u32[]{:S(2)}, u32[]{:S(2)}) %collective-permute-start.12) | collective-permute-done | bytes 393248 | tf_op jit(solution)/shard_map/ppermute | solution.py:572
  88.2 2.7 %collective-permute-start.16 = (bf16[192,512]{1,0:T(8,128)(2,1)S(1)}, bf16[192,512]{1,0:T(8,128)(2,1)S(1)}, u32[]{:S(2)}, u32[]{:S(2)}) collective-permute-start(bf16[192,512]{1,0:T(8,128)(2,1)S(1)} %get-tuple-element.132), channel_id=1, source_target_pairs={{0,4},{1,5},{2,6},{3,7},{4,0},{5,1},{6,2},{7,3},{8,12},{9,13},{10,... | collective-permute-start | bytes 589832 | tf_op jit(solution)/shard_map/ppermute | solution.py:572
  91.0 5.2 %collective-permute-done.11.refs_2_ = bf16[320,512]{1,0:T(8,128)(2,1)S(1)} collective-permute-done((bf16[320,512]{1,0:T(8,128)(2,1)S(1)}, bf16[320,512]{1,0:T(8,128)(2,1)S(1)}, u32[]{:S(2)}, u32[]{:S(2)}) %collective-permute-start.11) | collective-permute-done | bytes 327712 | tf_op jit(solution)/shard_map/ppermute | solution.py:572
  98.3 2.2 %collective-permute-start.13 = (bf16[256,512]{1,0:T(8,128)(2,1)S(1)}, bf16[256,512]{1,0:T(8,128)(2,1)S(1)}, u32[]{:S(2)}, u32[]{:S(2)}) collective-permute-start(bf16[256,512]{1,0:T(8,128)(2,1)S(1)} %get-tuple-element.129), channel_id=1, source_target_pairs={{0,2},{1,3},{2,0},{3,1},{4,6},{5,7},{6,4},{7,5},{8,10},{9,11},{10,... | collective-permute-start | bytes 786440 | tf_op jit(solution)/shard_map/ppermute | solution.py:572
  100.5 3.0 %collective-permute-start.20 = (bf16[192,512]{1,0:T(8,128)(2,1)S(1)}, bf16[192,512]{1,0:T(8,128)(2,1)S(1)}, u32[]{:S(2)}, u32[]{:S(2)}) collective-permute-start(bf16[192,512]{1,0:T(8,128)(2,1)S(1)} %add_body.6.refs_3_.refs_1_), channel_id=1, source_target_pairs={{0,8},{1,9},{2,10},{3,11},{4,12},{5,13},{6,14},{7,15},{8,0},{9,1},... | collective-permute-start | bytes 589832 | tf_op jit(solution)/shard_map/ppermute | solution.py:572
  104.9 2.8 %collective-permute-done.14.refs_5_ = bf16[32,512]{1,0:T(8,128)(2,1)S(1)} collective-permute-done((bf16[32,512]{1,0:T(8,128)(2,1)S(1)}, bf16[32,512]{1,0:T(8,128)(2,1)S(1)}, u32[]{:S(2)}, u32[]{:S(2)}) %collective-permute-start.14) | collective-permute-done | bytes 32800 | tf_op jit(solution)/shard_map/ppermute | solution.py:999
  107.9 2.0 %collective-permute-start.18 = (bf16[48,512]{1,0:T(8,128)(2,1)S(1)}, bf16[48,512]{1,0:T(8,128)(2,1)S(1)}, u32[]{:S(2)}, u32[]{:S(2)}) collective-permute-start(bf16[48,512]{1,0:T(8,128)(2,1)S(1)} %get-tuple-element.135.refs_4_), channel_id=1, source_target_pairs={{0,4},{1,5},{2,6},{3,7},{4,0},{5,1},{6,2},{7,3},{8,12},{9,13},{10,... | collective-permute-start | bytes 147464 | tf_op jit(solution)/shard_map/ppermute | solution.py:999
  109.9 5.7 %collective-permute-done.20.refs_2_ = bf16[192,512]{1,0:T(8,128)(2,1)S(1)} collective-permute-done((bf16[192,512]{1,0:T(8,128)(2,1)S(1)}, bf16[192,512]{1,0:T(8,128)(2,1)S(1)}, u32[]{:S(2)}, u32[]{:S(2)}) %collective-permute-start.20) | collective-permute-done | bytes 196640 | tf_op jit(solution)/shard_map/ppermute | solution.py:572
  116.0 2.6 %collective-permute-done.18.refs_5_ = bf16[48,512]{1,0:T(8,128)(2,1)S(1)} collective-permute-done((bf16[48,512]{1,0:T(8,128)(2,1)S(1)}, bf16[48,512]{1,0:T(8,128)(2,1)S(1)}, u32[]{:S(2)}, u32[]{:S(2)}) %collective-permute-start.18) | collective-permute-done | bytes 49184 | tf_op jit(solution)/shard_map/ppermute | solution.py:999
  119.9 5.1 %collective-permute-done.24.refs_2_ = bf16[192,512]{1,0:T(8,128)(2,1)S(1)} collective-permute-done((bf16[192,512]{1,0:T(8,128)(2,1)S(1)}, bf16[192,512]{1,0:T(8,128)(2,1)S(1)}, u32[]{:S(2)}, u32[]{:S(2)}) %collective-permute-start.24) | collective-permute-done | bytes 196640 | tf_op jit(solution)/shard_map/ppermute | solution.py:572
  126.4 1.6 collective-permute-done.21.refs_3_
  129.3 3.6 %collective-permute-done.28.refs_2_ = bf16[384,512]{1,0:T(8,128)(2,1)S(1)} collective-permute-done((bf16[384,512]{1,0:T(8,128)(2,1)S(1)}, bf16[384,512]{1,0:T(8,128)(2,1)S(1)}, u32[]{:S(2)}, u32[]{:S(2)}) %collective-permute-start.28) | collective-permute-done | bytes 393248 | tf_op jit(solution)/shard_map/ppermute | solution.py:572
  132.9 3.8 %collective-permute-done.27.refs_2_ = bf16[320,512]{1,0:T(8,128)(2,1)S(1)} collective-permute-done((bf16[320,512]{1,0:T(8,128)(2,1)S(1)}, bf16[320,512]{1,0:T(8,128)(2,1)S(1)}, u32[]{:S(2)}, u32[]{:S(2)}) %collective-permute-start.27) | collective-permute-done | bytes 327712 | tf_op jit(solution)/shard_map/ppermute | solution.py:572
  136.8 1.7 %collective-permute-start.29 = (bf16[256,512]{1,0:T(8,128)(2,1)S(1)}, bf16[256,512]{1,0:T(8,128)(2,1)S(1)}, u32[]{:S(2)}, u32[]{:S(2)}) collective-permute-start(bf16[256,512]{1,0:T(8,128)(2,1)S(1)} %get-tuple-element.141.refs_1_.refs_3_), channel_id=1, source_target_pairs={{0,2},{1,3},{2,0},{3,1},{4,6},{5,7},{6,4},{7,5},{8,10},{9,11},{10,... | collective-permute-start | bytes 786440 | tf_op jit(solution)/shard_map/ppermute | solution.py:572
  139.3 4.9 %collective-permute-done.29.refs_2_ = bf16[256,512]{1,0:T(8,128)(2,1)S(1)} collective-permute-done((bf16[256,512]{1,0:T(8,128)(2,1)S(1)}, bf16[256,512]{1,0:T(8,128)(2,1)S(1)}, u32[]{:S(2)}, u32[]{:S(2)}) %collective-permute-start.29) | collective-permute-done | bytes 262176 | tf_op jit(solution)/shard_map/ppermute | solution.py:572
  146.4 2.3 %step_grad.1 = (f32[512,512]{1,0:T(8,128)}, f32[1,1024]{1,0:T(1,128)}, f32[1,1024]{1,0:T(1,128)}, f32[1,1024]{1,0:T(1,128)}, f32[3,128]{1,0:T(4,128)S(1)}, /*index=5*/f32[8,128]{1,0:T(8,128)S(1)}) custom-call(bf16[272,512]{1,0:T(8,128)(2,1)S(1)} %get-tuple-element.140.rows_ref, bf16[512,512]{1,0:T(8,128)(2,1)S(1)} %merge_body.11.after_ref.p0), custom_call_target="tpu_custom_call" | custom-call | flops 68719476736 | bytes 1024 | tf_op jit(solution)/shard_map/step_grad/pallas_call | solution.py:1006
  149.9 2.1 %place.6 = (f32[512,1024]{1,0:T(8,128)}, f32[512,512]{1,0:T(8,128)}, f32[512,512]{1,0:T(8,128)}, f32[512,512]{1,0:T(8,128)}, f32[8,128]{1,0:T(8,128)S(1)}) custom-call(s32[4]{0:T(128)S(1)} %pad_add_fusion.1.runs, bf16[640,512]{1,0:T(8,128)(2,1)S(1)} %merge_body.9.refs_6_.p0, bf16[640,512]{1,0:T(8,128)(2,1)S(1)} %collective-permute-done.35.p1, ...), custom_call_target="tpu_custom_call" | custom-call | flops 1024 | bytes 1024 | tf_op jit(solution)/shard_map/place/pallas_call | solution.py:679
  152.0 2.3 %place.7 = (f32[512,1024]{1,0:T(8,128)}, f32[512,1024]{1,0:T(8,128)}, f32[1536,1024]{1,0:T(8,128)}, f32[8,128]{1,0:T(8,128)S(1)}) custom-call(s32[4]{0:T(128)S(1)} %pad_add_fusion.runs, bf16[768,512]{1,0:T(8,128)(2,1)S(1)} %merge_body.8.refs_3_.p0, bf16[768,512]{1,0:T(8,128)(2,1)S(1)} %collective-permute-done.34.p1, f32[8,128]{1,0:T(8,128)S(1)} %get-tuple-element.146.after_ref), custom_call_target="tpu_custom_call" | custom-call | flops 1024 | bytes 1024 | tf_op jit(solution)/shard_map/place/pallas_call | solution.py:679
  154.4 2.0 %place.8 = (f32[1536,1024]{1,0:T(8,128)}, f32[8,128]{1,0:T(8,128)S(1)}) custom-call(s32[4]{0:T(128)S(1)} %pad_add_fusion.runs, bf16[512,512]{1,0:T(8,128)(2,1)S(1)} %merge_body.11.after_ref.p0, bf16[512,512]{1,0:T(8,128)(2,1)S(1)} %collective-permute-done.33.p1, f32[8,128]{1,0:T(8,128)S(1)} %get-tuple-element.147.after_ref, ...), custom_call_target="tpu_custom_call", output_to_operand_aliasing={{0}: (4, {})} | custom-call | flops 1024 | bytes 1024 | tf_op jit(solution)/shard_map/place/pallas_call | solution.py:679
  157.2 4.6 %collective-permute-done.30.x_ref = bf16[512,512]{1,0:T(8,128)(2,1)S(1)} collective-permute-done((bf16[512,512]{1,0:T(8,128)(2,1)S(1)}, bf16[512,512]{1,0:T(8,128)(2,1)S(1)}, u32[]{:S(2)}, u32[]{:S(2)}) %collective-permute-start.30) | collective-permute-done | bytes 524320 | tf_op jit(solution)/shard_map/ppermute | solution.py:572
  162.6 2.1 %place.9 = (f32[512,1024]{1,0:T(8,128)}, f32[512,512]{1,0:T(8,128)}, f32[512,512]{1,0:T(8,128)}, f32[512,512]{1,0:T(8,128)}, f32[8,128]{1,0:T(8,128)S(1)}) custom-call(s32[4]{0:T(128)S(1)} %pad_add_fusion.1.runs, bf16[640,512]{1,0:T(8,128)(2,1)S(1)} %then.3.after_ref.p0, ...), custom_call_target="tpu_custom_call", output_to_operand_aliasing={{0}: (4, {}), {1}: (5, {}), {2}: (6, {}), {3}: (7, {})} | custom-call | flops 1024 | bytes 1024 | tf_op jit(solution)/shard_map/place/pallas_call | solution.py:679
  164.7 2.3 %place.10 = (f32[512,1024]{1,0:T(8,128)}, f32[512,1024]{1,0:T(8,128)}, f32[1536,1024]{1,0:T(8,128)}, f32[8,128]{1,0:T(8,128)S(1)}) custom-call(s32[4]{0:T(128)S(1)} %pad_add_fusion.runs, bf16[768,512]{1,0:T(8,128)(2,1)S(1)} %then.4.after_ref.p0, ...), custom_call_target="tpu_custom_call", output_to_operand_aliasing={{0}: (4, {}), {1}: (5, {}), {2}: (6, {})} | custom-call | flops 1024 | bytes 1024 | tf_op jit(solution)/shard_map/place/pallas_call | solution.py:679
  167.1 2.6 %place.11 = (f32[1536,1024]{1,0:T(8,128)}, f32[8,128]{1,0:T(8,128)}) custom-call(s32[4]{0:T(128)S(1)} %pad_add_fusion.runs, bf16[512,512]{1,0:T(8,128)(2,1)S(1)} %then.5.after_ref.p0, bf16[512,512]{1,0:T(8,128)(2,1)S(1)} %collective-permute-done.36.p1, f32[8,128]{1,0:T(8,128)S(1)} %get-tuple-element.158.after_ref, ...), custom_call_target="tpu_custom_call", output_to_operand_aliasing={{0}: (4, {})} | custom-call | flops 1024 | bytes 1024 | tf_op jit(solution)/shard_map/place/pallas_call | solution.py:679
  (128 shorter events, 27.2 us)
Async XLA Ops:
  45.1 8.3 %collective-permute-start.3 = (bf16[1536,512]{1,0:T(8,128)(2,1)}, bf16[1536,512]{1,0:T(8,128)(2,1)S(1)}, u32[]{:S(2)}, u32[]{:S(2)}) collective-permute-start(bf16[1536,512]{1,0:T(8,128)(2,1)} %bitcast.38), channel_id=1, source_target_pairs={{0,16},{16,0},{1,17},{17,1},{2,18},{18,2},{3,19},{19,3},{4,20},{20... | collective-permute-start | bytes 4718600 | tf_op jit(solution)/shard_map/ppermute | solution.py:547
  45.2 19.5 %collective-permute-start.2 = (bf16[32,1024]{1,0:T(8,128)(2,1)}, bf16[32,1024]{1,0:T(8,128)(2,1)}, u32[]{:S(2)}, u32[]{:S(2)}) collective-permute-start(bf16[32,1024]{1,0:T(8,128)(2,1)} %get-tuple-element.98), channel_id=1, source_target_pairs={{0,16},{16,0},{1,17},{17,1},{2,18},{18,2},{3,19},{19,3},{4,20},{20... | collective-permute-start | bytes 196616 | tf_op jit(solution)/shard_map/ppermute | solution.py:547
  45.6 28.7 %collective-permute-start = (bf16[1536,256]{1,0:T(8,128)(2,1)}, bf16[1536,256]{1,0:T(8,128)(2,1)}, u32[]{:S(2)}, u32[]{:S(2)}) collective-permute-start(bf16[1536,256]{1,0:T(8,128)(2,1)} %get-tuple-element.94), channel_id=1, source_target_pairs={{0,16},{16,0},{1,17},{17,1},{2,18},{18,2},{3,19},{19,3},{4,20},{20... | collective-permute-start | bytes 2359304 | tf_op jit(solution)/shard_map/ppermute | solution.py:547
  45.7 28.7 %collective-permute-start.1 = (bf16[1536,256]{1,0:T(8,128)(2,1)}, bf16[1536,256]{1,0:T(8,128)(2,1)}, u32[]{:S(2)}, u32[]{:S(2)}) collective-permute-start(bf16[1536,256]{1,0:T(8,128)(2,1)} %get-tuple-element.96), channel_id=1, source_target_pairs={{0,16},{16,0},{1,17},{17,1},{2,18},{18,2},{3,19},{19,3},{4,20},{20... | collective-permute-start | bytes 2359304 | tf_op jit(solution)/shard_map/ppermute | solution.py:547
  50.8 29.5 %collective-permute-start.7 = (bf16[640,512]{1,0:T(8,128)(2,1)}, bf16[640,512]{1,0:T(8,128)(2,1)}, u32[]{:S(2)}, u32[]{:S(2)}) collective-permute-start(bf16[640,512]{1,0:T(8,128)(2,1)} %get-tuple-element.117), channel_id=1, source_target_pairs={{0,4},{1,5},{2,6},{3,7},{4,0},{5,1},{6,2},{7,3},{8,12},{9,13},{10,... | collective-permute-start | bytes 1966088 | tf_op jit(solution)/shard_map/ppermute | solution.py:572
  55.6 22.5 %collective-permute-start.8 = (bf16[768,512]{1,0:T(8,128)(2,1)}, bf16[768,512]{1,0:T(8,128)(2,1)}, u32[]{:S(2)}, u32[]{:S(2)}) collective-permute-start(bf16[768,512]{1,0:T(8,128)(2,1)} %get-tuple-element.118), channel_id=1, source_target_pairs={{0,1},{1,0},{2,3},{3,2},{4,5},{5,4},{6,7},{7,6},{8,9},{9,8},{10,11... | collective-permute-start | bytes 2359304 | tf_op jit(solution)/shard_map/ppermute | solution.py:572
  64.7 19.5 %collective-permute-start.6 = (bf16[1024,512]{1,0:T(8,128)(2,1)}, bf16[1024,512]{1,0:T(8,128)(2,1)S(1)}, u32[]{:S(2)}, u32[]{:S(2)}) collective-permute-start(bf16[1024,512]{1,0:T(8,128)(2,1)} %bitcast.40), channel_id=1, source_target_pairs={{0,16},{16,0},{1,17},{17,1},{2,18},{18,2},{3,19},{19,3},{4,20},{20... | collective-permute-start | bytes 3145736 | tf_op jit(solution)/shard_map/ppermute | solution.py:547
  74.3 23.1 %collective-permute-start.10 = (bf16[32,512]{1,0:T(8,128)(2,1)}, bf16[32,512]{1,0:T(8,128)(2,1)}, u32[]{:S(2)}, u32[]{:S(2)}) collective-permute-start(bf16[32,512]{1,0:T(8,128)(2,1)} %get-tuple-element.111.refs_4_), channel_id=1, source_target_pairs={{0,16},{16,0},{1,17},{17,1},{2,18},{18,2},{3,19},{19,3},{4,20},{20... | collective-permute-start | bytes 98312 | tf_op jit(solution)/shard_map/ppermute | solution.py:547
  79.6 8.6 %collective-permute-start.12 = (bf16[384,512]{1,0:T(8,128)(2,1)S(1)}, bf16[384,512]{1,0:T(8,128)(2,1)S(1)}, u32[]{:S(2)}, u32[]{:S(2)}) collective-permute-start(bf16[384,512]{1,0:T(8,128)(2,1)S(1)} %get-tuple-element.125), channel_id=1, source_target_pairs={{0,2},{1,3},{2,0},{3,1},{4,6},{5,7},{6,4},{7,5},{8,10},{9,11},{10,... | collective-permute-start | bytes 1179656 | tf_op jit(solution)/shard_map/ppermute | solution.py:572
  81.5 14.6 %collective-permute-start.11 = (bf16[320,512]{1,0:T(8,128)(2,1)S(1)}, bf16[320,512]{1,0:T(8,128)(2,1)S(1)}, u32[]{:S(2)}, u32[]{:S(2)}) collective-permute-start(bf16[320,512]{1,0:T(8,128)(2,1)S(1)} %get-tuple-element.124), channel_id=1, source_target_pairs={{0,8},{1,9},{2,10},{3,11},{4,12},{5,13},{6,14},{7,15},{8,0},{9,1},... | collective-permute-start | bytes 983048 | tf_op jit(solution)/shard_map/ppermute | solution.py:572
  84.6 12.8 %collective-permute-start.9 = (bf16[512,512]{1,0:T(8,128)(2,1)S(1)}, bf16[512,512]{1,0:T(8,128)(2,1)S(1)}, u32[]{:S(2)}, u32[]{:S(2)}) collective-permute-start(bf16[512,512]{1,0:T(8,128)(2,1)S(1)} %get-tuple-element.123), channel_id=1, source_target_pairs={{0,1},{1,0},{2,3},{3,2},{4,5},{5,4},{6,7},{7,6},{8,9},{9,8},{10,11... | collective-permute-start | bytes 1572872 | tf_op jit(solution)/shard_map/ppermute | solution.py:572
  88.2 12.3 %collective-permute-start.16 = (bf16[192,512]{1,0:T(8,128)(2,1)S(1)}, bf16[192,512]{1,0:T(8,128)(2,1)S(1)}, u32[]{:S(2)}, u32[]{:S(2)}) collective-permute-start(bf16[192,512]{1,0:T(8,128)(2,1)S(1)} %get-tuple-element.132), channel_id=1, source_target_pairs={{0,4},{1,5},{2,6},{3,7},{4,0},{5,1},{6,2},{7,3},{8,12},{9,13},{10,... | collective-permute-start | bytes 589832 | tf_op jit(solution)/shard_map/ppermute | solution.py:572
  98.3 9.4 %collective-permute-start.13 = (bf16[256,512]{1,0:T(8,128)(2,1)S(1)}, bf16[256,512]{1,0:T(8,128)(2,1)S(1)}, u32[]{:S(2)}, u32[]{:S(2)}) collective-permute-start(bf16[256,512]{1,0:T(8,128)(2,1)S(1)} %get-tuple-element.129), channel_id=1, source_target_pairs={{0,2},{1,3},{2,0},{3,1},{4,6},{5,7},{6,4},{7,5},{8,10},{9,11},{10,... | collective-permute-start | bytes 786440 | tf_op jit(solution)/shard_map/ppermute | solution.py:572
  100.5 15.0 %collective-permute-start.20 = (bf16[192,512]{1,0:T(8,128)(2,1)S(1)}, bf16[192,512]{1,0:T(8,128)(2,1)S(1)}, u32[]{:S(2)}, u32[]{:S(2)}) collective-permute-start(bf16[192,512]{1,0:T(8,128)(2,1)S(1)} %add_body.6.refs_3_.refs_1_), channel_id=1, source_target_pairs={{0,8},{1,9},{2,10},{3,11},{4,12},{5,13},{6,14},{7,15},{8,0},{9,1},... | collective-permute-start | bytes 589832 | tf_op jit(solution)/shard_map/ppermute | solution.py:572
  103.6 12.1 %collective-permute-start.19 = (bf16[160,512]{1,0:T(8,128)(2,1)S(1)}, bf16[160,512]{1,0:T(8,128)(2,1)S(1)}, u32[]{:S(2)}, u32[]{:S(2)}) collective-permute-start(bf16[160,512]{1,0:T(8,128)(2,1)S(1)} %add_body.7.refs_6_.refs_1_), channel_id=1, source_target_pairs={{0,2},{1,3},{2,0},{3,1},{4,6},{5,7},{6,4},{7,5},{8,10},{9,11},{10,... | collective-permute-start | bytes 491528 | tf_op jit(solution)/shard_map/ppermute | solution.py:572
  107.8 10.9 %collective-permute-start.17 = (bf16[128,512]{1,0:T(8,128)(2,1)S(1)}, bf16[128,512]{1,0:T(8,128)(2,1)S(1)}, u32[]{:S(2)}, u32[]{:S(2)}) collective-permute-start(bf16[128,512]{1,0:T(8,128)(2,1)S(1)} %get-tuple-element.134), channel_id=1, source_target_pairs={{0,4},{1,5},{2,6},{3,7},{4,0},{5,1},{6,2},{7,3},{8,12},{9,13},{10,... | collective-permute-start | bytes 393224 | tf_op jit(solution)/shard_map/ppermute | solution.py:572
  107.9 10.8 %collective-permute-start.18 = (bf16[48,512]{1,0:T(8,128)(2,1)S(1)}, bf16[48,512]{1,0:T(8,128)(2,1)S(1)}, u32[]{:S(2)}, u32[]{:S(2)}) collective-permute-start(bf16[48,512]{1,0:T(8,128)(2,1)S(1)} %get-tuple-element.135.refs_4_), channel_id=1, source_target_pairs={{0,4},{1,5},{2,6},{3,7},{4,0},{5,1},{6,2},{7,3},{8,12},{9,13},{10,... | collective-permute-start | bytes 147464 | tf_op jit(solution)/shard_map/ppermute | solution.py:999
  115.6 9.4 %collective-permute-start.24 = (bf16[192,512]{1,0:T(8,128)(2,1)S(1)}, bf16[192,512]{1,0:T(8,128)(2,1)S(1)}, u32[]{:S(2)}, u32[]{:S(2)}) collective-permute-start(bf16[192,512]{1,0:T(8,128)(2,1)S(1)} %add_body.8.refs_3_.refs_1_), channel_id=1, source_target_pairs={{0,4},{1,5},{2,6},{3,7},{4,0},{5,1},{6,2},{7,3},{8,12},{9,13},{10,... | collective-permute-start | bytes 589832 | tf_op jit(solution)/shard_map/ppermute | solution.py:572
  115.8 10.5 %collective-permute-start.23 = (bf16[160,512]{1,0:T(8,128)(2,1)S(1)}, bf16[160,512]{1,0:T(8,128)(2,1)S(1)}, u32[]{:S(2)}, u32[]{:S(2)}) collective-permute-start(bf16[160,512]{1,0:T(8,128)(2,1)S(1)} %add_body.9.refs_6_.refs_1_), channel_id=1, source_target_pairs={{0,1},{1,0},{2,3},{3,2},{4,5},{5,4},{6,7},{7,6},{8,9},{9,8},{10,11... | collective-permute-start | bytes 491528 | tf_op jit(solution)/shard_map/ppermute | solution.py:572
  118.7 9.3 %collective-permute-start.21 = (bf16[128,512]{1,0:T(8,128)(2,1)S(1)}, bf16[128,512]{1,0:T(8,128)(2,1)S(1)}, u32[]{:S(2)}, u32[]{:S(2)}) collective-permute-start(bf16[128,512]{1,0:T(8,128)(2,1)S(1)} %get-tuple-element.136.refs_3_.refs_2_), channel_id=1, source_target_pairs={{0,8},{1,9},{2,10},{3,11},{4,12},{5,13},{6,14},{7,15},{8,0},{9,1},... | collective-permute-start | bytes 393224 | tf_op jit(solution)/shard_map/ppermute | solution.py:572
  118.8 7.6 %collective-permute-start.22 = (bf16[80,512]{1,0:T(8,128)(2,1)S(1)}, bf16[80,512]{1,0:T(8,128)(2,1)S(1)}, u32[]{:S(2)}, u32[]{:S(2)}) collective-permute-start(bf16[80,512]{1,0:T(8,128)(2,1)S(1)} %get-tuple-element.137.refs_4_), channel_id=1, source_target_pairs={{0,2},{1,3},{2,0},{3,1},{4,6},{5,7},{6,4},{7,5},{8,10},{9,11},{10,... | collective-permute-start | bytes 245768 | tf_op jit(solution)/shard_map/ppermute | solution.py:999
  125.0 7.8 %collective-permute-start.28 = (bf16[384,512]{1,0:T(8,128)(2,1)S(1)}, bf16[384,512]{1,0:T(8,128)(2,1)S(1)}, u32[]{:S(2)}, u32[]{:S(2)}) collective-permute-start(bf16[384,512]{1,0:T(8,128)(2,1)S(1)} %merge_body.6.refs_3_.refs_1_), channel_id=1, source_target_pairs={{0,2},{1,3},{2,0},{3,1},{4,6},{5,7},{6,4},{7,5},{8,10},{9,11},{10,... | collective-permute-start | bytes 1179656 | tf_op jit(solution)/shard_map/ppermute | solution.py:572
  126.3 10.4 %collective-permute-start.27 = (bf16[320,512]{1,0:T(8,128)(2,1)S(1)}, bf16[320,512]{1,0:T(8,128)(2,1)S(1)}, u32[]{:S(2)}, u32[]{:S(2)}) collective-permute-start(bf16[320,512]{1,0:T(8,128)(2,1)S(1)} %merge_body.7.refs_6_.refs_1_), channel_id=1, source_target_pairs={{0,8},{1,9},{2,10},{3,11},{4,12},{5,13},{6,14},{7,15},{8,0},{9,1},... | collective-permute-start | bytes 983048 | tf_op jit(solution)/shard_map/ppermute | solution.py:572
  128.0 8.7 %collective-permute-start.26 = (bf16[144,512]{1,0:T(8,128)(2,1)S(1)}, bf16[144,512]{1,0:T(8,128)(2,1)S(1)}, u32[]{:S(2)}, u32[]{:S(2)}) collective-permute-start(bf16[144,512]{1,0:T(8,128)(2,1)S(1)} %get-tuple-element.139.refs_4_), channel_id=1, source_target_pairs={{0,1},{1,0},{2,3},{3,2},{4,5},{5,4},{6,7},{7,6},{8,9},{9,8},{10,11... | collective-permute-start | bytes 442376 | tf_op jit(solution)/shard_map/ppermute | solution.py:999
  128.1 8.7 %collective-permute-start.25 = (bf16[128,512]{1,0:T(8,128)(2,1)S(1)}, bf16[128,512]{1,0:T(8,128)(2,1)S(1)}, u32[]{:S(2)}, u32[]{:S(2)}) collective-permute-start(bf16[128,512]{1,0:T(8,128)(2,1)S(1)} %get-tuple-element.138.refs_3_.refs_2_), channel_id=1, source_target_pairs={{0,4},{1,5},{2,6},{3,7},{4,0},{5,1},{6,2},{7,3},{8,12},{9,13},{10,... | collective-permute-start | bytes 393224 | tf_op jit(solution)/shard_map/ppermute | solution.py:572
  136.8 7.4 %collective-permute-start.29 = (bf16[256,512]{1,0:T(8,128)(2,1)S(1)}, bf16[256,512]{1,0:T(8,128)(2,1)S(1)}, u32[]{:S(2)}, u32[]{:S(2)}) collective-permute-start(bf16[256,512]{1,0:T(8,128)(2,1)S(1)} %get-tuple-element.141.refs_1_.refs_3_), channel_id=1, source_target_pairs={{0,2},{1,3},{2,0},{3,1},{4,6},{5,7},{6,4},{7,5},{8,10},{9,11},{10,... | collective-permute-start | bytes 786440 | tf_op jit(solution)/shard_map/ppermute | solution.py:572
  139.3 12.8 %collective-permute-start.34 = (bf16[768,512]{1,0:T(8,128)(2,1)S(1)}, bf16[768,512]{1,0:T(8,128)(2,1)S(1)}, u32[]{:S(2)}, u32[]{:S(2)}) collective-permute-start(bf16[768,512]{1,0:T(8,128)(2,1)S(1)} %merge_body.8.refs_3_.p0), channel_id=1, source_target_pairs={{0,16},{16,0},{1,17},{17,1},{2,18},{18,2},{3,19},{19,3},{4,20},{20... | collective-permute-start | bytes 2359304 | tf_op jit(solution)/shard_map/ppermute | solution.py:547
  139.3 17.2 %collective-permute-start.32 = (bf16[640,512]{1,0:T(8,128)(2,1)S(1)}, bf16[640,512]{1,0:T(8,128)(2,1)S(1)}, u32[]{:S(2)}, u32[]{:S(2)}) collective-permute-start(bf16[640,512]{1,0:T(8,128)(2,1)S(1)} %merge_body.9.refs_6_.p0), channel_id=1, source_target_pairs={{0,4},{1,5},{2,6},{3,7},{4,0},{5,1},{6,2},{7,3},{8,12},{9,13},{10,... | collective-permute-start | bytes 1966088 | tf_op jit(solution)/shard_map/ppermute | solution.py:572
  144.2 12.4 %collective-permute-start.31 = (bf16[768,512]{1,0:T(8,128)(2,1)S(1)}, bf16[768,512]{1,0:T(8,128)(2,1)S(1)}, u32[]{:S(2)}, u32[]{:S(2)}) collective-permute-start(bf16[768,512]{1,0:T(8,128)(2,1)S(1)} %merge_body.8.refs_3_.p0), channel_id=1, source_target_pairs={{0,1},{1,0},{2,3},{3,2},{4,5},{5,4},{6,7},{7,6},{8,9},{9,8},{10,11... | collective-permute-start | bytes 2359304 | tf_op jit(solution)/shard_map/ppermute | solution.py:572
  145.6 8.8 %collective-permute-start.33 = (bf16[512,512]{1,0:T(8,128)(2,1)S(1)}, bf16[512,512]{1,0:T(8,128)(2,1)S(1)}, u32[]{:S(2)}, u32[]{:S(2)}) collective-permute-start(bf16[512,512]{1,0:T(8,128)(2,1)S(1)} %merge_body.11.after_ref.p0), channel_id=1, source_target_pairs={{0,16},{16,0},{1,17},{17,1},{2,18},{18,2},{3,19},{19,3},{4,20},{20... | collective-permute-start | bytes 1572872 | tf_op jit(solution)/shard_map/ppermute | solution.py:547
  145.7 16.1 %collective-permute-start.30 = (bf16[512,512]{1,0:T(8,128)(2,1)S(1)}, bf16[512,512]{1,0:T(8,128)(2,1)S(1)}, u32[]{:S(2)}, u32[]{:S(2)}) collective-permute-start(bf16[512,512]{1,0:T(8,128)(2,1)S(1)} %merge_body.11.after_ref.p0), channel_id=1, source_target_pairs={{0,1},{1,0},{2,3},{3,2},{4,5},{5,4},{6,7},{7,6},{8,9},{9,8},{10,11... | collective-permute-start | bytes 1572872 | tf_op jit(solution)/shard_map/ppermute | solution.py:572
  156.6 8.1 %collective-permute-start.37 = (bf16[768,512]{1,0:T(8,128)(2,1)S(1)}, bf16[768,512]{1,0:T(8,128)(2,1)S(1)}, u32[]{:S(2)}, u32[]{:S(2)}) collective-permute-start(bf16[768,512]{1,0:T(8,128)(2,1)S(1)} %then.4.after_ref.p0), channel_id=1, source_target_pairs={{0,16},{16,0},{1,17},{17,1},{2,18},{18,2},{3,19},{19,3},{4,20},{20... | collective-permute-start | bytes 2359304 | tf_op jit(solution)/shard_map/ppermute | solution.py:547
  (28 other events, 154.3 us)

commit v6 on v4

--- a/solution.py
+++ b/solution.py
@@ -300,8 +300,8 @@
         o_vec[9:16, :] = jnp.where(lane < 8, digits, 0).astype(F32)
 
 
-def weight_kernel(sec_ref, left_ref, dpre_ref, *refs):
-    o_keep, o_give, acc = refs[-3:]
+def weight_kernel(sec_ref, left_ref, dpre_ref, o_keep, o_give, mark, acc):
+    mark[...] = jnp.zeros_like(mark)
     section = sec_ref[0]
     width = acc.shape[0]
     half = width // 2
@@ -459,7 +459,8 @@
     )(*[w[1] for w in works], *[x for w in works for x in w[2:4]], after)
 
 
-def first_kernel(bit_ref, held, got, after_ref, keep, give, bufs, sems):
+def first_kernel(bit_ref, held, got, after_ref, keep, give, mark, same, bufs, sems):
+    mark[...] = jnp.zeros_like(mark)
     rows = keep.shape[0]
     bit = bit_ref[0]
     copies = []
@@ -482,14 +483,15 @@
     rows, width = held.shape[0] // 2, held.shape[1]
     return pl.pallas_call(
         first_kernel,
-        in_specs=[IN_SMEM, IN_HBM, IN_HBM, ANYWHERE],
-        out_specs=[IN_VMEM] * 2,
-        out_shape=[struct(rows, width)] * 2,
+        in_specs=[IN_SMEM, ANYWHERE, ANYWHERE, ANYWHERE],
+        out_specs=[IN_VMEM] * 3 + [ANYWHERE],
+        out_shape=[struct(rows, width)] * 2 + [struct(8, 128, F32), struct(2 * rows, width)],
+        input_output_aliases={1: 3},
         scratch_shapes=[pltpu.VMEM((4, rows, width), BF16), pltpu.SemaphoreType.DMA((4,))],
         compiler_params=pltpu.CompilerParams(vmem_limit_bytes=24 * 1024 * 1024),
         cost_estimate=cost,
         name="split_first",
-    )(bit, held, got, after)
+    )(bit, held, got, after)[:3]
 
 
 def then_kernel(x_ref, after_ref, out_ref):
@@ -592,8 +594,9 @@
         self.step += 1
         rows, width = self.held.shape
         if at == 0:
-            self.held, give = split_first(self.held, self.got, sums.bit(0), after, cost)
-            self.got, rest = sums.send(give, 0), []
+            self.held, give, mark = split_first(self.held, self.got, sums.bit(0), after, cost)
+            self.got = sums.send(give, 0)
+            return (mark,)
         elif at < last:
             work = (split_body, sums.bit(at), self.held, self.got, [struct(rows // 2, width)] * 2)
             self.held, give, *rest = pair_call([work, *more], after, cost)
@@ -909,22 +912,22 @@
     batch_a, batch_c = batch(keep_a, give_a, far_first), batch(keep_c, give_c, sums)
     block_got, skip_got, other_edge = swap(block_give), swap(skip_give), swap(edge)
     spec = pl.BlockSpec((2, half, width), lambda i, *_: (i, 0, 0))
-    keep_b, give_b = pl.pallas_call(
+    keep_b, give_b, after = pl.pallas_call(
         weight_kernel,
         grid_spec=pltpu.PrefetchScalarGridSpec(
             num_scalar_prefetch=1,
             grid=(taps,),
             in_specs=[pl.BlockSpec((own, width), lambda i, *_: (0, i)), whole(d_pre)],
-            out_specs=[spec, spec],
+            out_specs=[spec, spec, const((8, 128))],
             scratch_shapes=[pltpu.VMEM((width, wide), F32)],
         ),
-        out_shape=[shape(2 * taps, half, width)] * 2,
+        out_shape=[shape(2 * taps, half, width)] * 2 + [shape(8, 128, dtype=F32)],
         compiler_params=pltpu.CompilerParams(vmem_limit_bytes=KB_VMEM),
         cost_estimate=LARGE,
         name="weights",
     )(sec, stack, d_pre)
     batch_b = batch(keep_b, give_b, sums)
-    (after,) = batch_a.turn(keep_b)
+    (after,) = batch_a.turn(after)
     (after,) = batch_c.turn(after)
 
     group = -(-(micro * slots + 2) // 16) * 16
@@ -978,7 +981,7 @@
     )
     rows_got, rows_bit, gathered = swap(rows_now), sec, 0
     batches = {"a": batch_a, "b": batch_b, "c": batch_c}
-    order = "acb" + "cab" * 2 + "acb" * (batch_a.turns - 5) + "cab"
+    order = "acb" * (batch_a.turns - 1)
     for name in order:
         turner = batches[name]
         if name == "b" and gathered <= sums.levels:
@@ -1020,9 +1023,11 @@
     *outs_a, mark = batch_a.early(shapes_a, spots_a, mark)
     *outs_c, mark = batch_c.early(shapes_c, spots_c, mark)
     *outs_b, mark = batch_b.early(shapes_b, spots_b, mark)
-    mark = batch_b.arrive(batch_c.arrive(batch_a.arrive(mark)))
+    mark = batch_a.arrive(mark)
+    mark = batch_c.arrive(mark)
     *outs_a, mark = batch_a.late(shapes_a, spots_a, mark, outs_a)
     *outs_c, mark = batch_c.late(shapes_c, spots_c, mark, outs_c)
+    mark = batch_b.arrive(mark)
     *outs_b, mark = batch_b.late(shapes_b, spots_b, mark, outs_b)
     g_out, g_query, g_key, g_value = outs_a
     g_conv = outs_b[0].reshape(conv_w.shape)

time: 166 us -> 163 us (0.982)
  Pallas kernels: 91.2 us -> 87.9 us
  starting transfers between devices: 36.4 us -> 38.9 us
    pallas_call x18, Pallas kernels: 8.32 us -> 4.98 us  [pair_call(): pl.pallas_call(functools.partial(pair_kernel, [w[0] for w in works], outs...]
    ppermute x4, starting transfers between devices: 3.82 us -> 6.79 us  [on_device(): rows_got = lax.ppermute(rows_now, 'dp', route)]
    ppermute x21, waiting for transfers between devices: 22.8 us -> 20.9 us  [send(): return lax.ppermute(x, ('section', 'dp'), route)]
  transfers between devices with their start and end apart: 39 -> 39, of which waited for: 14 -> 13; matrix products, arithmetic and copies ran while one was open for 0% -> 0% of each run, Pallas kernels for 30% -> 28%
where the time goes in v6:
time: 163 us; the launch traced here: 162 us
  Pallas kernels  87.9 us (54%)
  starting transfers between devices  38.9 us (24%)
  waiting for transfers between devices  30.7 us (19%)
  local copies, waits for them, and re-layouts  3.43 us (2%)
    pallas_call x1, Pallas kernels, on_device(): pl.pallas_call(functools.partial(forward_kernel, (tile, slots, nq, subs,...  38.7 us
    ppermute x21, starting transfers between devices, send(): return lax.ppermute(x, ('section', 'dp'), route)  27.9 us
    ppermute x21, waiting for transfers between devices, send(): return lax.ppermute(x, ('section', 'dp'), route)  20.9 us
    pallas_call x6, Pallas kernels, place(): pl.pallas_call(functools.partial(place_kernel, which, full, len(shapes)),...  14 us
    pallas_call x1, Pallas kernels, on_device(): pl.pallas_call(weight_kernel, grid_spec=pltpu.PrefetchScalarGridSpec(num_...  9.1 us
    pallas_call x1, Pallas kernels, on_device(): pl.pallas_call(functools.partial(back_kernel, (tile, slots, subs, tiles,...  7.54 us
    ppermute x4, waiting for transfers between devices, on_device(): rows_got = lax.ppermute(rows_now, 'dp', route)  6.9 us
    ppermute x4, starting transfers between devices, on_device(): rows_got = lax.ppermute(rows_now, 'dp', route)  6.79 us
  transfers between devices with their start and end apart: 39, of which 13 were waited for; matrix products, arithmetic and copies ran while one was open for 0% of the time, Pallas kernels for 28%

profile of v6, /device:TPU:0, one launch (start us, length us, event | category | flops | bytes accessed | tf_op | source)
XLA Modules:
  0.0 162.3 jit_solution(6375639836437851506)
XLA Ops:
  0.7 38.7 %forward.1 = (bf16[1536,1536]{1,0:T(8,128)(2,1)}, bf16[1536,1024]{1,0:T(8,128)(2,1)}, bf16[32,1024]{1,0:T(8,128)(2,1)}, bf16[1536,512]{1,0:T(8,128)(2,1)}, bf16[...) custom-call(s32[1]{0:T(128)} %bitcast.sec_ref.refs_1_, ...), custom_call_target="tpu_custom_call" | custom-call | flops 68719476736 | bytes 1024 | tf_op jit(solution)/shard_map/forward/pallas_call | solution.py:832
  40.4 9.1 %weights.1 = (bf16[6,256,512]{2,1,0:T(8,128)(2,1)}, bf16[6,256,512]{2,1,0:T(8,128)(2,1)}, f32[8,128]{1,0:T(8,128)}) custom-call(s32[1]{0:T(128)} %bitcast.sec_ref.refs_1_, bf16[1536,1536]{1,0:T(8,128)(2,1)} %get-tuple-element.97.left_ref, bf16[1536,1024]{1,0:T(8,128)(2,1)} %get-tuple-element.98.dpre_ref.prev_ref.next_ref), custom_call_target="tpu_custom_call" | custom-call | flops 68719476736 | bytes 1024 | tf_op jit(solution)/shard_map/weights/pallas_call | solution.py:915
  52.3 1.8 %split_first.3 = (bf16[640,512]{1,0:T(8,128)(2,1)S(1)}, bf16[640,512]{1,0:T(8,128)(2,1)}, f32[8,128]{1,0:T(8,128)S(1)}, bf16[1280,512]{1,0:T(8,128)(2,1)S(1)}) custom-call(s32[1]{0:T(128)} %bitcast.11.bit_ref.refs_0_, bf16[1280,512]{1,0:T(8,128)(2,1)S(1)} %bitcast.35, ...), custom_call_target="tpu_custom_call", output_to_operand_aliasing={{3}: (1, {})} | custom-call | flops 68719476736 | bytes 1024 | tf_op jit(solution)/shard_map/split_first/pallas_call | solution.py:484
  54.1 3.1 %collective-permute-start.10 = (bf16[640,512]{1,0:T(8,128)(2,1)}, bf16[640,512]{1,0:T(8,128)(2,1)}, u32[]{:S(2)}, u32[]{:S(2)}) collective-permute-start(bf16[640,512]{1,0:T(8,128)(2,1)} %get-tuple-element.122), channel_id=1, source_target_pairs={{0,4},{1,5},{2,6},{3,7},{4,0},{5,1},{6,2},{7,3},{8,12},{9,13},{10,... | collective-permute-start | bytes 1966088 | tf_op jit(solution)/shard_map/ppermute | solution.py:574
  58.4 1.6 collective-permute-start.9
  60.7 7.5 %back.1 = (bf16[1536,256]{1,0:T(8,128)(2,1)S(1)}, bf16[1536,256]{1,0:T(8,128)(2,1)}, bf16[32,512]{1,0:T(8,128)(2,1)}) custom-call(s32[1]{0:T(128)} %bitcast.sec_ref.refs_1_, s32[3]{0:T(128)S(1)} %copy-done.5, s32[3,4]{1,0:T(4,128)S(1)} %copy-done.3, bf16[1536,1024]{1,0:T(8,128)(2,1)S(1)} %copy-done.9, bf16[1536,1024]{1,0:T(8,128)(2,1)S(1)} %copy-done.9, ...), custom_call_target="tpu_custom_call" | custom-call | flops 68719476736 | bytes 1024 | tf_op jit(solution)/shard_map/back/pallas_call | solution.py:935
  69.2 1.7 %split_first.5 = (bf16[768,512]{1,0:T(8,128)(2,1)S(1)}, bf16[768,512]{1,0:T(8,128)(2,1)S(1)}, f32[8,128]{1,0:T(8,128)S(1)}, bf16[1536,512]{1,0:T(8,128)(2,1)S(1)}) custom-call(s32[1]{0:T(128)} %bitcast.6.bit_ref.refs_0_, bf16[1536,512]{1,0:T(8,128)(2,1)S(1)} %bitcast.34, ...), custom_call_target="tpu_custom_call", output_to_operand_aliasing={{3}: (1, {})} | custom-call | flops 68719476736 | bytes 1024 | tf_op jit(solution)/shard_map/split_first/pallas_call | solution.py:484
  72.6 3.1 %join.2 = (bf16[3072,256]{1,0:T(8,128)(2,1)}, bf16[3072,256]{1,0:T(8,128)(2,1)}, f32[8,128]{1,0:T(8,128)S(1)}) custom-call(s32[1]{0:T(128)} %bitcast.sec_ref.refs_1_, bf16[1536,256]{1,0:T(8,128)(2,1)S(1)} %copy-done, bf16[1536,256]{1,0:T(8,128)(2,1)} %collective-permute-done.refs_1_, bf16[1536,256]{1,0:T(8,128)(2,1)S(1)} %copy-done.1, ...), custom_call_target="tpu_custom_call" | custom-call | flops 1024 | bytes 1024 | tf_op jit(solution)/shard_map/join/pallas_call | solution.py:536
  76.9 2.3 %collective-permute-start.14 = (bf16[320,512]{1,0:T(8,128)(2,1)S(1)}, bf16[320,512]{1,0:T(8,128)(2,1)S(1)}, u32[]{:S(2)}, u32[]{:S(2)}) collective-permute-start(bf16[320,512]{1,0:T(8,128)(2,1)S(1)} %get-tuple-element.130), channel_id=1, source_target_pairs={{0,8},{1,9},{2,10},{3,11},{4,12},{5,13},{6,14},{7,15},{8,0},{9,1},... | collective-permute-start | bytes 983048 | tf_op jit(solution)/shard_map/ppermute | solution.py:574
  80.4 1.6 collective-permute-start.13
  82.0 1.8 %collective-permute-done.7.refs_3_ = bf16[768,512]{1,0:T(8,128)(2,1)S(1)} collective-permute-done((bf16[768,512]{1,0:T(8,128)(2,1)S(1)}, bf16[768,512]{1,0:T(8,128)(2,1)S(1)}, u32[]{:S(2)}, u32[]{:S(2)}) %collective-permute-start.7) | collective-permute-done | bytes 786464 | tf_op jit(solution)/shard_map/ppermute | solution.py:574
  84.7 2.6 %collective-permute-start.11 = (bf16[384,512]{1,0:T(8,128)(2,1)S(1)}, bf16[384,512]{1,0:T(8,128)(2,1)S(1)}, u32[]{:S(2)}, u32[]{:S(2)}) collective-permute-start(bf16[384,512]{1,0:T(8,128)(2,1)S(1)} %get-tuple-element.127), channel_id=1, source_target_pairs={{0,2},{1,3},{2,0},{3,1},{4,6},{5,7},{6,4},{7,5},{8,10},{9,11},{10,... | collective-permute-start | bytes 1179656 | tf_op jit(solution)/shard_map/ppermute | solution.py:574
  87.4 3.3 %collective-permute-start.12 = (bf16[32,512]{1,0:T(8,128)(2,1)S(1)}, bf16[32,512]{1,0:T(8,128)(2,1)S(1)}, u32[]{:S(2)}, u32[]{:S(2)}) collective-permute-start(bf16[32,512]{1,0:T(8,128)(2,1)S(1)} %get-tuple-element.128.refs_4_), channel_id=1, source_target_pairs={{0,8},{1,9},{2,10},{3,11},{4,12},{5,13},{6,14},{7,15},{8,0},{9,1},... | collective-permute-start | bytes 98312 | tf_op jit(solution)/shard_map/ppermute | solution.py:996
  97.1 2.1 %collective-permute-start.22 = (bf16[160,512]{1,0:T(8,128)(2,1)S(1)}, bf16[160,512]{1,0:T(8,128)(2,1)S(1)}, u32[]{:S(2)}, u32[]{:S(2)}) collective-permute-start(bf16[160,512]{1,0:T(8,128)(2,1)S(1)} %add_body.6.refs_3_.refs_1_), channel_id=1, source_target_pairs={{0,2},{1,3},{2,0},{3,1},{4,6},{5,7},{6,4},{7,5},{8,10},{9,11},{10,... | collective-permute-start | bytes 491528 | tf_op jit(solution)/shard_map/ppermute | solution.py:574
  100.8 3.4 %collective-permute-done.16.refs_5_ = bf16[48,512]{1,0:T(8,128)(2,1)S(1)} collective-permute-done((bf16[48,512]{1,0:T(8,128)(2,1)S(1)}, bf16[48,512]{1,0:T(8,128)(2,1)S(1)}, u32[]{:S(2)}, u32[]{:S(2)}) %collective-permute-start.16) | collective-permute-done | bytes 49184 | tf_op jit(solution)/shard_map/ppermute | solution.py:996
  106.2 1.7 %collective-permute-start.26 = (bf16[160,512]{1,0:T(8,128)(2,1)S(1)}, bf16[160,512]{1,0:T(8,128)(2,1)S(1)}, u32[]{:S(2)}, u32[]{:S(2)}) collective-permute-start(bf16[160,512]{1,0:T(8,128)(2,1)S(1)} %add_body.9.refs_3_.refs_1_), channel_id=1, source_target_pairs={{0,1},{1,0},{2,3},{3,2},{4,5},{5,4},{6,7},{7,6},{8,9},{9,8},{10,11... | collective-permute-start | bytes 491528 | tf_op jit(solution)/shard_map/ppermute | solution.py:574
  108.0 5.5 %collective-permute-done.21.refs_2_ = bf16[128,512]{1,0:T(8,128)(2,1)S(1)} collective-permute-done((bf16[128,512]{1,0:T(8,128)(2,1)S(1)}, bf16[128,512]{1,0:T(8,128)(2,1)S(1)}, u32[]{:S(2)}, u32[]{:S(2)}) %collective-permute-start.21) | collective-permute-done | bytes 131104 | tf_op jit(solution)/shard_map/ppermute | solution.py:574
  113.6 4.1 %collective-permute-done.19.refs_3_ = bf16[192,512]{1,0:T(8,128)(2,1)S(1)} collective-permute-done((bf16[192,512]{1,0:T(8,128)(2,1)S(1)}, bf16[192,512]{1,0:T(8,128)(2,1)S(1)}, u32[]{:S(2)}, u32[]{:S(2)}) %collective-permute-start.19) | collective-permute-done | bytes 196640 | tf_op jit(solution)/shard_map/ppermute | solution.py:574
  119.4 2.5 %collective-permute-start.29 = (bf16[320,512]{1,0:T(8,128)(2,1)S(1)}, bf16[320,512]{1,0:T(8,128)(2,1)S(1)}, u32[]{:S(2)}, u32[]{:S(2)}) collective-permute-start(bf16[320,512]{1,0:T(8,128)(2,1)S(1)} %merge_body.6.refs_3_.refs_1_), channel_id=1, source_target_pairs={{0,8},{1,9},{2,10},{3,11},{4,12},{5,13},{6,14},{7,15},{8,0},{9,1},... | collective-permute-start | bytes 983048 | tf_op jit(solution)/shard_map/ppermute | solution.py:574
  122.2 2.4 %collective-permute-done.24.refs_5_ = bf16[144,512]{1,0:T(8,128)(2,1)S(1)} collective-permute-done((bf16[144,512]{1,0:T(8,128)(2,1)S(1)}, bf16[144,512]{1,0:T(8,128)(2,1)S(1)}, u32[]{:S(2)}, u32[]{:S(2)}) %collective-permute-start.24) | collective-permute-done | bytes 147488 | tf_op jit(solution)/shard_map/ppermute | solution.py:996
  124.7 1.6 collective-permute-start.27
  126.3 4.7 %collective-permute-done.29.refs_2_ = bf16[320,512]{1,0:T(8,128)(2,1)S(1)} collective-permute-done((bf16[320,512]{1,0:T(8,128)(2,1)S(1)}, bf16[320,512]{1,0:T(8,128)(2,1)S(1)}, u32[]{:S(2)}, u32[]{:S(2)}) %collective-permute-start.29) | collective-permute-done | bytes 327712 | tf_op jit(solution)/shard_map/ppermute | solution.py:574
  132.6 1.7 %collective-permute-start.31 = (bf16[512,512]{1,0:T(8,128)(2,1)S(1)}, bf16[512,512]{1,0:T(8,128)(2,1)S(1)}, u32[]{:S(2)}, u32[]{:S(2)}) collective-permute-start(bf16[512,512]{1,0:T(8,128)(2,1)S(1)} %merge_body.10.refs_3_.p0), channel_id=1, source_target_pairs={{0,1},{1,0},{2,3},{3,2},{4,5},{5,4},{6,7},{7,6},{8,9},{9,8},{10,11... | collective-permute-start | bytes 1572872 | tf_op jit(solution)/shard_map/ppermute | solution.py:574
  134.9 2.3 %step_grad.1 = (f32[512,512]{1,0:T(8,128)}, f32[1,1024]{1,0:T(1,128)}, f32[1,1024]{1,0:T(1,128)}, f32[1,1024]{1,0:T(1,128)}, f32[3,128]{1,0:T(4,128)S(1)}, /*index=5*/f32[8,128]{1,0:T(8,128)S(1)}) custom-call(bf16[272,512]{1,0:T(8,128)(2,1)S(1)} %get-tuple-element.142.rows_ref, bf16[768,512]{1,0:T(8,128)(2,1)S(1)} %merge_body.11.after_ref.p0), custom_call_target="tpu_custom_call" | custom-call | flops 68719476736 | bytes 1024 | tf_op jit(solution)/shard_map/step_grad/pallas_call | solution.py:1003
  137.1 2.3 %join.3 = (bf16[3072,256]{1,0:T(8,128)(2,1)}, f32[8,128]{1,0:T(8,128)S(1)}) custom-call(s32[1]{0:T(128)} %bitcast.sec_ref.refs_1_, bf16[1536,256]{1,0:T(8,128)(2,1)S(1)} %get-tuple-element.115.refs_0_, bf16[1536,256]{1,0:T(8,128)(2,1)} %collective-permute-done.6.refs_1_, f32[8,128]{1,0:T(8,128)S(1)} %get-tuple-element.144.refs_2_), custom_call_target="tpu_custom_call" | custom-call | flops 1024 | bytes 1024 | tf_op jit(solution)/shard_map/join/pallas_call | solution.py:536
  139.4 2.7 %place.6 = (f32[512,1024]{1,0:T(8,128)}, f32[512,512]{1,0:T(8,128)}, f32[512,512]{1,0:T(8,128)}, f32[512,512]{1,0:T(8,128)}, f32[8,128]{1,0:T(8,128)S(1)}) custom-call(s32[4]{0:T(128)S(1)} %pad_add_fusion.1.runs, bf16[640,512]{1,0:T(8,128)(2,1)} %merge_body.9.refs_3_.p0, bf16[640,512]{1,0:T(8,128)(2,1)S(1)} %collective-permute-done.35.p1, ...), custom_call_target="tpu_custom_call" | custom-call | flops 1024 | bytes 1024 | tf_op jit(solution)/shard_map/place/pallas_call | solution.py:682
  142.1 1.9 %place.7 = (f32[512,1024]{1,0:T(8,128)}, f32[512,1024]{1,0:T(8,128)}, f32[8,128]{1,0:T(8,128)S(1)}) custom-call(s32[4]{0:T(128)S(1)} %pad_add_fusion.runs, bf16[512,512]{1,0:T(8,128)(2,1)S(1)} %merge_body.10.refs_3_.p0, bf16[512,512]{1,0:T(8,128)(2,1)S(1)} %collective-permute-done.34.p1, f32[8,128]{1,0:T(8,128)S(1)} %get-tuple-element.148.after_ref), custom_call_target="tpu_custom_call" | custom-call | flops 1024 | bytes 1024 | tf_op jit(solution)/shard_map/place/pallas_call | solution.py:682
  144.1 2.3 %place.8 = (f32[1536,1024]{1,0:T(8,128)}, f32[8,128]{1,0:T(8,128)S(1)}) custom-call(s32[4]{0:T(128)S(1)} %pad_add_fusion.runs, bf16[768,512]{1,0:T(8,128)(2,1)S(1)} %merge_body.11.after_ref.p0, bf16[768,512]{1,0:T(8,128)(2,1)S(1)} %collective-permute-done.33.p1, f32[8,128]{1,0:T(8,128)S(1)} %get-tuple-element.149.after_ref), custom_call_target="tpu_custom_call" | custom-call | flops 1024 | bytes 1024 | tf_op jit(solution)/shard_map/place/pallas_call | solution.py:682
  146.4 2.9 %collective-permute-done.32.x_ref = bf16[640,512]{1,0:T(8,128)(2,1)} collective-permute-done((bf16[640,512]{1,0:T(8,128)(2,1)}, bf16[640,512]{1,0:T(8,128)(2,1)}, u32[]{:S(2)}, u32[]{:S(2)}) %collective-permute-start.32) | collective-permute-done | bytes 655392 | tf_op jit(solution)/shard_map/ppermute | solution.py:574
  152.6 2.1 %place.9 = (f32[512,1024]{1,0:T(8,128)}, f32[512,512]{1,0:T(8,128)}, f32[512,512]{1,0:T(8,128)}, f32[512,512]{1,0:T(8,128)}, f32[8,128]{1,0:T(8,128)S(1)}) custom-call(s32[4]{0:T(128)S(1)} %pad_add_fusion.1.runs, bf16[640,512]{1,0:T(8,128)(2,1)S(1)} %then.3.after_ref.p0, ...), custom_call_target="tpu_custom_call", output_to_operand_aliasing={{0}: (4, {}), {1}: (5, {}), {2}: (6, {}), {3}: (7, {})} | custom-call | flops 1024 | bytes 1024 | tf_op jit(solution)/shard_map/place/pallas_call | solution.py:682
  154.8 2.0 %place.10 = (f32[512,1024]{1,0:T(8,128)}, f32[512,1024]{1,0:T(8,128)}, f32[8,128]{1,0:T(8,128)S(1)}) custom-call(s32[4]{0:T(128)S(1)} %pad_add_fusion.runs, bf16[512,512]{1,0:T(8,128)(2,1)S(1)} %then.4.after_ref.p0, bf16[512,512]{1,0:T(8,128)(2,1)S(1)} %collective-permute-done.36.p1, ...), custom_call_target="tpu_custom_call", output_to_operand_aliasing={{0}: (4, {}), {1}: (5, {})} | custom-call | flops 1024 | bytes 1024 | tf_op jit(solution)/shard_map/place/pallas_call | solution.py:682
  159.2 2.9 %place.11 = (f32[1536,1024]{1,0:T(8,128)}, f32[8,128]{1,0:T(8,128)}) custom-call(s32[4]{0:T(128)S(1)} %pad_add_fusion.runs, bf16[768,512]{1,0:T(8,128)(2,1)S(1)} %then.5.p0.after_ref, bf16[768,512]{1,0:T(8,128)(2,1)S(1)} %collective-permute-done.38.p1, bf16[768,512]{1,0:T(8,128)(2,1)S(1)} %then.5.p0.after_ref, ...), custom_call_target="tpu_custom_call", output_to_operand_aliasing={{0}: (4, {})} | custom-call | flops 1024 | bytes 1024 | tf_op jit(solution)/shard_map/place/pallas_call | solution.py:682
  (111 shorter events, 31.7 us)
Async XLA Ops:
  39.4 10.8 %collective-permute-start.5 = (bf16[1280,512]{1,0:T(8,128)(2,1)}, bf16[1280,512]{1,0:T(8,128)(2,1)S(1)}, u32[]{:S(2)}, u32[]{:S(2)}) collective-permute-start(bf16[1280,512]{1,0:T(8,128)(2,1)} %bitcast.39), channel_id=1, source_target_pairs={{0,16},{16,0},{1,17},{17,1},{2,18},{18,2},{3,19},{19,3},{4,20},{20... | collective-permute-start | bytes 3932168 | tf_op jit(solution)/shard_map/ppermute | solution.py:549
  39.9 14.2 %collective-permute-start.4 = (bf16[1024,512]{1,0:T(8,128)(2,1)}, bf16[1024,512]{1,0:T(8,128)(2,1)S(1)}, u32[]{:S(2)}, u32[]{:S(2)}) collective-permute-start(bf16[1024,512]{1,0:T(8,128)(2,1)} %bitcast.40), channel_id=1, source_target_pairs={{0,16},{16,0},{1,17},{17,1},{2,18},{18,2},{3,19},{19,3},{4,20},{20... | collective-permute-start | bytes 3145736 | tf_op jit(solution)/shard_map/ppermute | solution.py:549
  40.0 18.4 %collective-permute-start.3 = (bf16[32,1024]{1,0:T(8,128)(2,1)}, bf16[32,1024]{1,0:T(8,128)(2,1)}, u32[]{:S(2)}, u32[]{:S(2)}) collective-permute-start(bf16[32,1024]{1,0:T(8,128)(2,1)} %get-tuple-element.101), channel_id=1, source_target_pairs={{0,16},{16,0},{1,17},{17,1},{2,18},{18,2},{3,19},{19,3},{4,20},{20... | collective-permute-start | bytes 196616 | tf_op jit(solution)/shard_map/ppermute | solution.py:549
  49.5 18.8 %collective-permute-start.2 = (bf16[1536,512]{1,0:T(8,128)(2,1)}, bf16[1536,512]{1,0:T(8,128)(2,1)}, u32[]{:S(2)}, u32[]{:S(2)}) collective-permute-start(bf16[1536,512]{1,0:T(8,128)(2,1)} %bitcast.38), channel_id=1, source_target_pairs={{0,16},{16,0},{1,17},{17,1},{2,18},{18,2},{3,19},{19,3},{4,20},{20... | collective-permute-start | bytes 4718600 | tf_op jit(solution)/shard_map/ppermute | solution.py:549
  49.6 21.3 %collective-permute-start = (bf16[1536,256]{1,0:T(8,128)(2,1)}, bf16[1536,256]{1,0:T(8,128)(2,1)}, u32[]{:S(2)}, u32[]{:S(2)}) collective-permute-start(bf16[1536,256]{1,0:T(8,128)(2,1)} %get-tuple-element.94), channel_id=1, source_target_pairs={{0,16},{16,0},{1,17},{17,1},{2,18},{18,2},{3,19},{19,3},{4,20},{20... | collective-permute-start | bytes 2359304 | tf_op jit(solution)/shard_map/ppermute | solution.py:549
  50.2 20.8 %collective-permute-start.1 = (bf16[1536,256]{1,0:T(8,128)(2,1)}, bf16[1536,256]{1,0:T(8,128)(2,1)}, u32[]{:S(2)}, u32[]{:S(2)}) collective-permute-start(bf16[1536,256]{1,0:T(8,128)(2,1)} %get-tuple-element.96), channel_id=1, source_target_pairs={{0,16},{16,0},{1,17},{17,1},{2,18},{18,2},{3,19},{19,3},{4,20},{20... | collective-permute-start | bytes 2359304 | tf_op jit(solution)/shard_map/ppermute | solution.py:549
  54.1 21.5 %collective-permute-start.10 = (bf16[640,512]{1,0:T(8,128)(2,1)}, bf16[640,512]{1,0:T(8,128)(2,1)}, u32[]{:S(2)}, u32[]{:S(2)}) collective-permute-start(bf16[640,512]{1,0:T(8,128)(2,1)} %get-tuple-element.122), channel_id=1, source_target_pairs={{0,4},{1,5},{2,6},{3,7},{4,0},{5,1},{6,2},{7,3},{8,12},{9,13},{10,... | collective-permute-start | bytes 1966088 | tf_op jit(solution)/shard_map/ppermute | solution.py:574
  58.4 20.8 %collective-permute-start.9 = (bf16[512,512]{1,0:T(8,128)(2,1)}, bf16[512,512]{1,0:T(8,128)(2,1)}, u32[]{:S(2)}, u32[]{:S(2)}) collective-permute-start(bf16[512,512]{1,0:T(8,128)(2,1)} %get-tuple-element.120), channel_id=1, source_target_pairs={{0,1},{1,0},{2,3},{3,2},{4,5},{5,4},{6,7},{7,6},{8,9},{9,8},{10,11... | collective-permute-start | bytes 1572872 | tf_op jit(solution)/shard_map/ppermute | solution.py:574
  68.3 13.7 %collective-permute-start.8 = (bf16[32,512]{1,0:T(8,128)(2,1)}, bf16[32,512]{1,0:T(8,128)(2,1)}, u32[]{:S(2)}, u32[]{:S(2)}) collective-permute-start(bf16[32,512]{1,0:T(8,128)(2,1)} %get-tuple-element.111.after_ref.refs_4_), channel_id=1, source_target_pairs={{0,16},{16,0},{1,17},{17,1},{2,18},{18,2},{3,19},{19,3},{4,20},{20... | collective-permute-start | bytes 98312 | tf_op jit(solution)/shard_map/ppermute | solution.py:549
  70.9 63.4 %collective-permute-start.6 = (bf16[1536,256]{1,0:T(8,128)(2,1)}, bf16[1536,256]{1,0:T(8,128)(2,1)}, u32[]{:S(2)}, u32[]{:S(2)}) collective-permute-start(bf16[1536,256]{1,0:T(8,128)(2,1)} %get-tuple-element.116), channel_id=1, source_target_pairs={{0,16},{16,0},{1,17},{17,1},{2,18},{18,2},{3,19},{19,3},{4,20},{20... | collective-permute-start | bytes 2359304 | tf_op jit(solution)/shard_map/ppermute | solution.py:549
  71.0 12.7 %collective-permute-start.7 = (bf16[768,512]{1,0:T(8,128)(2,1)S(1)}, bf16[768,512]{1,0:T(8,128)(2,1)S(1)}, u32[]{:S(2)}, u32[]{:S(2)}) collective-permute-start(bf16[768,512]{1,0:T(8,128)(2,1)S(1)} %get-tuple-element.118), channel_id=1, source_target_pairs={{0,1},{1,0},{2,3},{3,2},{4,5},{5,4},{6,7},{7,6},{8,9},{9,8},{10,11... | collective-permute-start | bytes 2359304 | tf_op jit(solution)/shard_map/ppermute | solution.py:574
  76.9 13.7 %collective-permute-start.14 = (bf16[320,512]{1,0:T(8,128)(2,1)S(1)}, bf16[320,512]{1,0:T(8,128)(2,1)S(1)}, u32[]{:S(2)}, u32[]{:S(2)}) collective-permute-start(bf16[320,512]{1,0:T(8,128)(2,1)S(1)} %get-tuple-element.130), channel_id=1, source_target_pairs={{0,8},{1,9},{2,10},{3,11},{4,12},{5,13},{6,14},{7,15},{8,0},{9,1},... | collective-permute-start | bytes 983048 | tf_op jit(solution)/shard_map/ppermute | solution.py:574
  80.4 11.9 %collective-permute-start.13 = (bf16[256,512]{1,0:T(8,128)(2,1)S(1)}, bf16[256,512]{1,0:T(8,128)(2,1)S(1)}, u32[]{:S(2)}, u32[]{:S(2)}) collective-permute-start(bf16[256,512]{1,0:T(8,128)(2,1)S(1)} %get-tuple-element.129), channel_id=1, source_target_pairs={{0,2},{1,3},{2,0},{3,1},{4,6},{5,7},{6,4},{7,5},{8,10},{9,11},{10,... | collective-permute-start | bytes 786440 | tf_op jit(solution)/shard_map/ppermute | solution.py:574
  84.7 10.1 %collective-permute-start.11 = (bf16[384,512]{1,0:T(8,128)(2,1)S(1)}, bf16[384,512]{1,0:T(8,128)(2,1)S(1)}, u32[]{:S(2)}, u32[]{:S(2)}) collective-permute-start(bf16[384,512]{1,0:T(8,128)(2,1)S(1)} %get-tuple-element.127), channel_id=1, source_target_pairs={{0,2},{1,3},{2,0},{3,1},{4,6},{5,7},{6,4},{7,5},{8,10},{9,11},{10,... | collective-permute-start | bytes 1179656 | tf_op jit(solution)/shard_map/ppermute | solution.py:574
  92.3 7.2 %collective-permute-start.17 = (bf16[128,512]{1,0:T(8,128)(2,1)S(1)}, bf16[128,512]{1,0:T(8,128)(2,1)S(1)}, u32[]{:S(2)}, u32[]{:S(2)}) collective-permute-start(bf16[128,512]{1,0:T(8,128)(2,1)S(1)} %get-tuple-element.136), channel_id=1, source_target_pairs={{0,4},{1,5},{2,6},{3,7},{4,0},{5,1},{6,2},{7,3},{8,12},{9,13},{10,... | collective-permute-start | bytes 393224 | tf_op jit(solution)/shard_map/ppermute | solution.py:574
  95.0 9.2 %collective-permute-start.15 = (bf16[192,512]{1,0:T(8,128)(2,1)S(1)}, bf16[192,512]{1,0:T(8,128)(2,1)S(1)}, u32[]{:S(2)}, u32[]{:S(2)}) collective-permute-start(bf16[192,512]{1,0:T(8,128)(2,1)S(1)} %get-tuple-element.134), channel_id=1, source_target_pairs={{0,4},{1,5},{2,6},{3,7},{4,0},{5,1},{6,2},{7,3},{8,12},{9,13},{10,... | collective-permute-start | bytes 589832 | tf_op jit(solution)/shard_map/ppermute | solution.py:574
  95.9 8.3 %collective-permute-start.16 = (bf16[48,512]{1,0:T(8,128)(2,1)S(1)}, bf16[48,512]{1,0:T(8,128)(2,1)S(1)}, u32[]{:S(2)}, u32[]{:S(2)}) collective-permute-start(bf16[48,512]{1,0:T(8,128)(2,1)S(1)} %get-tuple-element.135.refs_4_), channel_id=1, source_target_pairs={{0,4},{1,5},{2,6},{3,7},{4,0},{5,1},{6,2},{7,3},{8,12},{9,13},{10,... | collective-permute-start | bytes 147464 | tf_op jit(solution)/shard_map/ppermute | solution.py:996
  97.1 9.1 %collective-permute-start.22 = (bf16[160,512]{1,0:T(8,128)(2,1)S(1)}, bf16[160,512]{1,0:T(8,128)(2,1)S(1)}, u32[]{:S(2)}, u32[]{:S(2)}) collective-permute-start(bf16[160,512]{1,0:T(8,128)(2,1)S(1)} %add_body.6.refs_3_.refs_1_), channel_id=1, source_target_pairs={{0,2},{1,3},{2,0},{3,1},{4,6},{5,7},{6,4},{7,5},{8,10},{9,11},{10,... | collective-permute-start | bytes 491528 | tf_op jit(solution)/shard_map/ppermute | solution.py:574
  99.6 13.9 %collective-permute-start.21 = (bf16[128,512]{1,0:T(8,128)(2,1)S(1)}, bf16[128,512]{1,0:T(8,128)(2,1)S(1)}, u32[]{:S(2)}, u32[]{:S(2)}) collective-permute-start(bf16[128,512]{1,0:T(8,128)(2,1)S(1)} %add_body.7.refs_6_.refs_1_), channel_id=1, source_target_pairs={{0,8},{1,9},{2,10},{3,11},{4,12},{5,13},{6,14},{7,15},{8,0},{9,1},... | collective-permute-start | bytes 393224 | tf_op jit(solution)/shard_map/ppermute | solution.py:574
  104.3 13.5 %collective-permute-start.19 = (bf16[192,512]{1,0:T(8,128)(2,1)S(1)}, bf16[192,512]{1,0:T(8,128)(2,1)S(1)}, u32[]{:S(2)}, u32[]{:S(2)}) collective-permute-start(bf16[192,512]{1,0:T(8,128)(2,1)S(1)} %get-tuple-element.138.refs_3_.refs_2_), channel_id=1, source_target_pairs={{0,8},{1,9},{2,10},{3,11},{4,12},{5,13},{6,14},{7,15},{8,0},{9,1},... | collective-permute-start | bytes 589832 | tf_op jit(solution)/shard_map/ppermute | solution.py:574
  105.3 8.3 %collective-permute-start.20 = (bf16[80,512]{1,0:T(8,128)(2,1)S(1)}, bf16[80,512]{1,0:T(8,128)(2,1)S(1)}, u32[]{:S(2)}, u32[]{:S(2)}) collective-permute-start(bf16[80,512]{1,0:T(8,128)(2,1)S(1)} %get-tuple-element.139.refs_4_), channel_id=1, source_target_pairs={{0,2},{1,3},{2,0},{3,1},{4,6},{5,7},{6,4},{7,5},{8,10},{9,11},{10,... | collective-permute-start | bytes 245768 | tf_op jit(solution)/shard_map/ppermute | solution.py:996
  106.2 13.1 %collective-permute-start.26 = (bf16[160,512]{1,0:T(8,128)(2,1)S(1)}, bf16[160,512]{1,0:T(8,128)(2,1)S(1)}, u32[]{:S(2)}, u32[]{:S(2)}) collective-permute-start(bf16[160,512]{1,0:T(8,128)(2,1)S(1)} %add_body.9.refs_3_.refs_1_), channel_id=1, source_target_pairs={{0,1},{1,0},{2,3},{3,2},{4,5},{5,4},{6,7},{7,6},{8,9},{9,8},{10,11... | collective-permute-start | bytes 491528 | tf_op jit(solution)/shard_map/ppermute | solution.py:574
  113.6 8.4 %collective-permute-start.25 = (bf16[128,512]{1,0:T(8,128)(2,1)S(1)}, bf16[128,512]{1,0:T(8,128)(2,1)S(1)}, u32[]{:S(2)}, u32[]{:S(2)}) collective-permute-start(bf16[128,512]{1,0:T(8,128)(2,1)S(1)} %add_body.10.refs_6_.refs_1_), channel_id=1, source_target_pairs={{0,4},{1,5},{2,6},{3,7},{4,0},{5,1},{6,2},{7,3},{8,12},{9,13},{10,... | collective-permute-start | bytes 393224 | tf_op jit(solution)/shard_map/ppermute | solution.py:574
  117.8 6.8 %collective-permute-start.23 = (bf16[192,512]{1,0:T(8,128)(2,1)S(1)}, bf16[192,512]{1,0:T(8,128)(2,1)S(1)}, u32[]{:S(2)}, u32[]{:S(2)}) collective-permute-start(bf16[192,512]{1,0:T(8,128)(2,1)S(1)} %get-tuple-element.140.refs_3_.refs_2_), channel_id=1, source_target_pairs={{0,4},{1,5},{2,6},{3,7},{4,0},{5,1},{6,2},{7,3},{8,12},{9,13},{10,... | collective-permute-start | bytes 589832 | tf_op jit(solution)/shard_map/ppermute | solution.py:574
  119.4 11.6 %collective-permute-start.29 = (bf16[320,512]{1,0:T(8,128)(2,1)S(1)}, bf16[320,512]{1,0:T(8,128)(2,1)S(1)}, u32[]{:S(2)}, u32[]{:S(2)}) collective-permute-start(bf16[320,512]{1,0:T(8,128)(2,1)S(1)} %merge_body.6.refs_3_.refs_1_), channel_id=1, source_target_pairs={{0,8},{1,9},{2,10},{3,11},{4,12},{5,13},{6,14},{7,15},{8,0},{9,1},... | collective-permute-start | bytes 983048 | tf_op jit(solution)/shard_map/ppermute | solution.py:574
  122.0 9.9 %collective-permute-start.28 = (bf16[256,512]{1,0:T(8,128)(2,1)S(1)}, bf16[256,512]{1,0:T(8,128)(2,1)S(1)}, u32[]{:S(2)}, u32[]{:S(2)}) collective-permute-start(bf16[256,512]{1,0:T(8,128)(2,1)S(1)} %merge_body.7.refs_6_.refs_1_), channel_id=1, source_target_pairs={{0,2},{1,3},{2,0},{3,1},{4,6},{5,7},{6,4},{7,5},{8,10},{9,11},{10,... | collective-permute-start | bytes 786440 | tf_op jit(solution)/shard_map/ppermute | solution.py:574
  124.7 7.9 %collective-permute-start.27 = (bf16[384,512]{1,0:T(8,128)(2,1)S(1)}, bf16[384,512]{1,0:T(8,128)(2,1)S(1)}, u32[]{:S(2)}, u32[]{:S(2)}) collective-permute-start(bf16[384,512]{1,0:T(8,128)(2,1)S(1)} %get-tuple-element.143.refs_3_.refs_1_), channel_id=1, source_target_pairs={{0,2},{1,3},{2,0},{3,1},{4,6},{5,7},{6,4},{7,5},{8,10},{9,11},{10,... | collective-permute-start | bytes 1179656 | tf_op jit(solution)/shard_map/ppermute | solution.py:574
  131.8 17.5 %collective-permute-start.32 = (bf16[640,512]{1,0:T(8,128)(2,1)}, bf16[640,512]{1,0:T(8,128)(2,1)}, u32[]{:S(2)}, u32[]{:S(2)}) collective-permute-start(bf16[640,512]{1,0:T(8,128)(2,1)} %merge_body.9.refs_3_.p0), channel_id=1, source_target_pairs={{0,4},{1,5},{2,6},{3,7},{4,0},{5,1},{6,2},{7,3},{8,12},{9,13},{10,... | collective-permute-start | bytes 1966088 | tf_op jit(solution)/shard_map/ppermute | solution.py:574
  131.9 10.2 %collective-permute-start.34 = (bf16[512,512]{1,0:T(8,128)(2,1)S(1)}, bf16[512,512]{1,0:T(8,128)(2,1)S(1)}, u32[]{:S(2)}, u32[]{:S(2)}) collective-permute-start(bf16[512,512]{1,0:T(8,128)(2,1)S(1)} %merge_body.10.refs_3_.p0), channel_id=1, source_target_pairs={{0,16},{16,0},{1,17},{17,1},{2,18},{18,2},{3,19},{19,3},{4,20},{20... | collective-permute-start | bytes 1572872 | tf_op jit(solution)/shard_map/ppermute | solution.py:549
  132.6 18.2 %collective-permute-start.31 = (bf16[512,512]{1,0:T(8,128)(2,1)S(1)}, bf16[512,512]{1,0:T(8,128)(2,1)S(1)}, u32[]{:S(2)}, u32[]{:S(2)}) collective-permute-start(bf16[512,512]{1,0:T(8,128)(2,1)S(1)} %merge_body.10.refs_3_.p0), channel_id=1, source_target_pairs={{0,1},{1,0},{2,3},{3,2},{4,5},{5,4},{6,7},{7,6},{8,9},{9,8},{10,11... | collective-permute-start | bytes 1572872 | tf_op jit(solution)/shard_map/ppermute | solution.py:574
  134.4 9.7 %collective-permute-start.33 = (bf16[768,512]{1,0:T(8,128)(2,1)S(1)}, bf16[768,512]{1,0:T(8,128)(2,1)S(1)}, u32[]{:S(2)}, u32[]{:S(2)}) collective-permute-start(bf16[768,512]{1,0:T(8,128)(2,1)S(1)} %merge_body.11.after_ref.p0), channel_id=1, source_target_pairs={{0,16},{16,0},{1,17},{17,1},{2,18},{18,2},{3,19},{19,3},{4,20},{20... | collective-permute-start | bytes 2359304 | tf_op jit(solution)/shard_map/ppermute | solution.py:549
  134.5 22.3 %collective-permute-start.30 = (bf16[768,512]{1,0:T(8,128)(2,1)S(1)}, bf16[768,512]{1,0:T(8,128)(2,1)S(1)}, u32[]{:S(2)}, u32[]{:S(2)}) collective-permute-start(bf16[768,512]{1,0:T(8,128)(2,1)S(1)} %merge_body.11.after_ref.p0), channel_id=1, source_target_pairs={{0,1},{1,0},{2,3},{3,2},{4,5},{5,4},{6,7},{7,6},{8,9},{9,8},{10,11... | collective-permute-start | bytes 2359304 | tf_op jit(solution)/shard_map/ppermute | solution.py:574
  (20 other events, 73.4 us)

commit v7 on v6

--- a/solution.py
+++ b/solution.py
@@ -15,7 +15,7 @@
 F32 = jnp.float32
 BF16 = jnp.bfloat16
 VMEM = 56 * 1024 * 1024
-KB_VMEM = 56 * 1024 * 1024
+KB_VMEM = 52 * 1024 * 1024
 KC_VMEM = 32 * 1024 * 1024
 
 
@@ -278,17 +278,15 @@
             keep[i] = ref[pl.ds(mine, half), pl.ds(left, width)].astype(BF16)
             give[i] = ref[pl.ds(theirs, half), pl.ds(left, width)].astype(BF16)
 
-        put(0, g_out, 0)
-        put(1, g_out, width)
+        put(0, g_query, 0)
+        g_query[...] = tn(here, (d_keys[...] * factor).astype(BF16))
+        put(1, g_query, 0)
+        g_query[...] = tn(here, d_values[...].astype(BF16))
         put(2, g_query, 0)
-        g_query[...] = tn(here, (d_keys[...] * factor).astype(BF16))
-        put(3, g_query, 0)
-        g_query[...] = tn(here, d_values[...].astype(BF16))
-        put(4, g_query, 0)
-        put(0, g_res, 0, o_keep_c, o_give_c)
-        put(1, g_res, width, o_keep_c, o_give_c)
-        put(2, g_cond, 0, o_keep_c, o_give_c)
-        put(3, g_cond, width, o_keep_c, o_give_c)
+        put(3, g_out, 0)
+        put(4, g_out, width)
+        for i, (ref, left) in enumerate(((g_res, 0), (g_res, width), (g_cond, 0), (g_cond, width))):
+            put(i, ref, left, o_keep_c, o_give_c)
         for i in range(3):
             line = jnp.sum(sums[i], axis=0, keepdims=True)
             o_vec[2 * i : 2 * i + 1, :] = line[:, :width]
@@ -383,7 +381,6 @@
         index = jnp.zeros((1, width), jnp.int32)
         for i in range(items):
             index = jnp.where(lane == i, steps[i // slots, i % slots], index)
-        index = jnp.where(section == 0, index, 0)
         d_step[items : items + 1, :] = (index >> 5).astype(F32)
         d_step[items + 1 : items + 2, :] = (index & 31).astype(F32)
         o_rows[:group, :] = d_step[...].astype(BF16)
@@ -429,11 +426,44 @@
     out[at_bit(1 - bit, rows), :] = got[...]
 
 
-def gather_body(bit, cur, got, out):
-    rows = cur.shape[0] - EDGE
-    out[at_bit(bit, rows), :] = cur[:rows, :]
-    out[at_bit(1 - bit, rows), :] = got[:rows, :]
-    out[2 * rows :, :] = total(cur[rows:, :], got[rows:, :])
+def ride(bit, sent, got, out, before, place):
+    rows = sent.shape[0] - before - EDGE
+    end = before + rows
+    out[pl.ds(pl.multiple_of(place + bit * rows, 16), rows), :] = sent[before:end, :]
+    out[pl.ds(pl.multiple_of(place + rows - bit * rows, 16), rows), :] = got[before:end, :]
+    out[place + 2 * rows :, :] = total(sent[end:, :], got[end:, :])
+
+
+def split_ride_kernel(bit_ref, last_ref, held, got, sent, after_ref, keep, give):
+    rows = keep.shape[0]
+    bit = bit_ref[0]
+    keep[...] = total(held[at_bit(bit, rows), :], got[at_bit(bit, rows), :])
+    give[:rows, :] = total(held[at_bit(1 - bit, rows), :], got[at_bit(1 - bit, rows), :])
+    ride(last_ref[0], sent, got, give, 2 * rows, rows)
+
+
+def add_ride_kernel(last_ref, held, got, sent, after_ref, out):
+    rows = held.shape[0]
+    out[:rows, :] = total(held[...], got[:rows, :])
+    ride(last_ref[0], sent, got, out, rows, rows)
+
+
+def end_ride_kernel(last_ref, sent, got, after_ref, out, rows_out):
+    rows = out.shape[0]
+    out[...] = total(sent[:rows, :], got[:rows, :])
+    ride(last_ref[0], sent, got, rows_out, rows, 0)
+
+
+def ride_call(kernel, bits, arrays, after, shapes):
+    return pl.pallas_call(
+        kernel,
+        in_specs=[IN_SMEM] * len(bits) + [IN_VMEM] * len(arrays) + [ANYWHERE],
+        out_specs=[IN_VMEM] * len(shapes),
+        out_shape=shapes,
+        compiler_params=pltpu.CompilerParams(vmem_limit_bytes=24 * 1024 * 1024),
+        cost_estimate=LARGE,
+        name="ride",
+    )(*bits, *arrays, after)
 
 
 def pair_kernel(bodies, outs, *refs):
@@ -459,7 +489,8 @@
     )(*[w[1] for w in works], *[x for w in works for x in w[2:4]], after)
 
 
-def first_kernel(bit_ref, held, got, after_ref, keep, give, mark, same, bufs, sems):
+def first_kernel(bit_ref, held, got, after_ref, *refs):
+    behind, (keep, give, mark, same, bufs, sems) = refs[:-6], refs[-6:]
     mark[...] = jnp.zeros_like(mark)
     rows = keep.shape[0]
     bit = bit_ref[0]
@@ -476,22 +507,26 @@
     for i, out in enumerate((give, keep)):
         copies[2 * i].wait()
         copies[2 * i + 1].wait()
-        out[...] = total(bufs[2 * i], bufs[2 * i + 1])
-
-
-def split_first(held, got, bit, after, cost):
+        out[:rows, :] = total(bufs[2 * i], bufs[2 * i + 1])
+    if behind:
+        give[rows:, :] = behind[0][...]
+
+
+def split_first(held, got, bit, after, cost, behind=()):
     rows, width = held.shape[0] // 2, held.shape[1]
+    more = sum(x.shape[0] for x in behind)
     return pl.pallas_call(
         first_kernel,
-        in_specs=[IN_SMEM, ANYWHERE, ANYWHERE, ANYWHERE],
+        in_specs=[IN_SMEM, ANYWHERE, ANYWHERE, ANYWHERE] + [IN_VMEM] * len(behind),
         out_specs=[IN_VMEM] * 3 + [ANYWHERE],
-        out_shape=[struct(rows, width)] * 2 + [struct(8, 128, F32), struct(2 * rows, width)],
+        out_shape=[struct(rows, width), struct(rows + more, width)]
+        + [struct(8, 128, F32), struct(2 * rows, width)],
         input_output_aliases={1: 3},
         scratch_shapes=[pltpu.VMEM((4, rows, width), BF16), pltpu.SemaphoreType.DMA((4,))],
         compiler_params=pltpu.CompilerParams(vmem_limit_bytes=24 * 1024 * 1024),
         cost_estimate=cost,
         name="split_first",
-    )(bit, held, got, after)[:3]
+    )(bit, held, got, after, *behind)[:3]
 
 
 def then_kernel(x_ref, after_ref, out_ref):
@@ -588,77 +623,114 @@
         self.got = swap(give)
         self.step = 0
 
-    def turn(self, after, more=(), cost=LARGE):
+    def turn(self, after, cost=LARGE, behind=None):
         sums, last = self.sums, self.sums.levels - 1
         at = self.step
         self.step += 1
         rows, width = self.held.shape
         if at == 0:
-            self.held, give, mark = split_first(self.held, self.got, sums.bit(0), after, cost)
+            more = () if behind is None else (behind,)
+            self.held, give, mark = split_first(
+                self.held, self.got, sums.bit(0), after, cost, more
+            )
+            self.riders = 0 if behind is None else behind.shape[0]
+            self.sent = give
             self.got = sums.send(give, 0)
-            return (mark,)
-        elif at < last:
+            return mark
+        if self.riders and at <= last + 1:
+            return self.ride(at, after)
+        if at < last:
             work = (split_body, sums.bit(at), self.held, self.got, [struct(rows // 2, width)] * 2)
-            self.held, give, *rest = pair_call([work, *more], after, cost)
+            self.held, give = pair_call([work], after, cost)
             self.got = sums.send(give, at)
         elif at <= last + 1:
             work = (add_body, sums.bit(0), self.held, self.got, [struct(rows, width)])
-            self.held, *rest = pair_call([work, *more], after, cost)
+            (self.held,) = pair_call([work], after, cost)
             self.got = sums.send(self.held, at if at == last else last - 1)
         else:
             back = 2 * last + 1 - at
             work = (merge_body, sums.bit(back), self.held, self.got, [struct(2 * rows, width)])
-            self.held, *rest = pair_call([work, *more], after, cost)
+            (self.held,) = pair_call([work], after, cost)
             self.got = sums.send(self.held, back - 1)
-        return (self.held, *rest)
+        return self.held
+
+    def ride(self, at, after):
+        sums, last = self.sums, self.sums.levels - 1
+        rows, width = self.held.shape
+        before = sums.bit(at - 1)
+        more = 2 * self.riders - EDGE
+        self.riders = more
+        if at < last:
+            shapes = [struct(rows // 2, width), struct(rows // 2 + more, width)]
+            arrays = (self.held, self.got, self.sent)
+            bits = (sums.bit(at), before)
+            self.held, self.sent = ride_call(split_ride_kernel, bits, arrays, after, shapes)
+            self.got = sums.send(self.sent, at)
+            return self.held
+        if at == last:
+            shapes = [struct(rows + more, width)]
+            arrays = (self.held, self.got, self.sent)
+            (self.sent,) = ride_call(add_ride_kernel, (before,), arrays, after, shapes)
+            self.got = sums.send(self.sent, at)
+            return self.sent
+        shapes = [struct(rows, width), struct(more, width)]
+        arrays = (self.sent, self.got)
+        self.held, self.rows = ride_call(end_ride_kernel, (before,), arrays, after, shapes)
+        self.got = sums.send(self.held, last - 1)
+        return self.held
 
     @property
     def turns(self):
         return 2 * self.sums.levels - 1
 
-    def early(self, shapes, spots, after, outs=()):
-        return place(self.sums.runs(), (0, 2), (self.held, swap(self.held)), shapes, spots, after, outs)
+    def early(self):
+        return self.sums.runs(), (0, 2), (self.held, swap(self.held)), self.spots
 
     def arrive(self, after):
         self.got = then(self.got, after)
         self.last = swap(self.got)
         return self.got
 
-    def late(self, shapes, spots, after, outs):
-        return place(self.sums.runs(), (1, 3), (self.got, self.last), shapes, spots, after, outs)
-
-
-def place_kernel(which, spots, count, runs, p0, p1, after_ref, *refs):
-    outs, (mark, buf, sems) = refs[-3 - count : -3], refs[-3:]
+    def late(self):
+        return self.sums.runs(), (1, 3), (self.got, self.last), self.spots
+
+
+def place_kernel(groups, count, *refs):
+    n = len(groups)
+    runs, pieces = refs[:n], refs[n : 3 * n]
+    outs, mark = refs[-count - 1 - 2 * n : -1 - 2 * n], refs[-1 - 2 * n]
+    bufs, sems = refs[-2 * n : -n], refs[-n:]
     mark[...] = jnp.zeros_like(mark)
-    rows = buf.shape[1]
-    per_run = p0.shape[0] // rows
     for wait in (False, True):
-        for run in range(4):
-            mine, theirs = runs[which[0]] == run, runs[which[1]] == run
-            base = run * per_run
-
-            @pl.when(mine | theirs)
-            def _(run=run, mine=mine):
-                slot = jnp.where(mine, 0, 1)
-                for w in range(run * per_run, (run + 1) * per_run):
-                    spot = spots[w]
-                    if spot is None:
-                        continue
-                    j = w - base
-                    k, row, col = spot
-                    copy = pltpu.make_async_copy(
-                        buf.at[slot * per_run + j],
-                        outs[k].at[pl.ds(row, rows), pl.ds(col, buf.shape[2])],
-                        sems.at[slot * per_run + j],
-                    )
-                    if wait:
-                        copy.wait()
-                    else:
-                        part = slice(j * rows, (j + 1) * rows)
-                        value = jnp.where(mine, p0[part, :], p1[part, :])
-                        buf[slot * per_run + j] = value.astype(F32)
-                        copy.start()
+        for g, (which, spots) in enumerate(groups):
+            rows, width = bufs[g].shape[1:]
+            per_run = pieces[2 * g].shape[0] // rows
+            for run in range(4):
+                mine = runs[g][which[0]] == run
+                theirs = runs[g][which[1]] == run
+
+                @pl.when(mine | theirs)
+                def _(g=g, run=run, mine=mine, spots=spots, rows=rows, per_run=per_run):
+                    slot = jnp.where(mine, 0, 1) * per_run
+                    for j in range(per_run):
+                        spot = spots[run * per_run + j]
+                        if spot is None:
+                            continue
+                        k, row, col = spot
+                        copy = pltpu.make_async_copy(
+                            bufs[g].at[slot + j],
+                            outs[k].at[pl.ds(row, rows), pl.ds(col, width)],
+                            sems[g].at[slot + j],
+                        )
+                        if wait:
+                            copy.wait()
+                        else:
+                            part = slice(j * rows, (j + 1) * rows)
+                            value = jnp.where(
+                                mine, pieces[2 * g][part, :], pieces[2 * g + 1][part, :]
+                            )
+                            bufs[g][slot + j] = value.astype(F32)
+                            copy.start()
 
 
 def spots_of(targets, width):
@@ -671,49 +743,59 @@
     return spots
 
 
-def place(runs, which, pieces, shapes, spots, after, outs=()):
-    length, width = pieces[0].shape
-    quarter = width // 4
-    per_run = length // quarter
-    half = len(spots) // 2
-    full = [None] * (4 * per_run)
-    full[:half] = spots[:half]
-    full[2 * per_run : 2 * per_run + half] = spots[half:]
+def place(parts, shapes, after, outs=()):
+    groups, scratch, sems = [], [], []
+    for _, which, pieces, spots in parts:
+        length, width = pieces[0].shape
+        quarter = width // 4
+        per_run = length // quarter
+        half = len(spots) // 2
+        full = [None] * (4 * per_run)
+        full[:half] = spots[:half]
+        full[2 * per_run : 2 * per_run + half] = spots[half:]
+        groups.append((which, full))
+        scratch.append(pltpu.VMEM((2 * per_run, quarter, width), F32))
+        sems.append(pltpu.SemaphoreType.DMA((2 * per_run,)))
+    n = len(parts)
     return pl.pallas_call(
-        functools.partial(place_kernel, which, full, len(shapes)),
-        in_specs=[IN_SMEM] + [IN_VMEM] * 2 + [ANYWHERE] + [IN_HBM] * len(outs),
+        functools.partial(place_kernel, groups, len(shapes)),
+        in_specs=[IN_SMEM] * n + [IN_VMEM] * (2 * n) + [ANYWHERE] + [IN_HBM] * len(outs),
         out_specs=[IN_HBM] * len(shapes) + [IN_VMEM],
         out_shape=list(shapes) + [struct(8, 128, F32)],
-        input_output_aliases={4 + k: k for k in range(len(outs))},
-        scratch_shapes=[
-            pltpu.VMEM((2 * per_run, quarter, width), F32),
-            pltpu.SemaphoreType.DMA((2 * per_run,)),
-        ],
-        compiler_params=pltpu.CompilerParams(vmem_limit_bytes=24 * 1024 * 1024),
+        input_output_aliases={3 * n + 1 + k: k for k in range(len(outs))},
+        scratch_shapes=scratch + sems,
+        compiler_params=pltpu.CompilerParams(vmem_limit_bytes=40 * 1024 * 1024),
         cost_estimate=SMALL,
         name="place",
-    )(runs, *pieces, after, *outs)
-
-
-def step_kernel(items, group, rows_ref, after_ref, out_ref, o_low, o_res, o_out, o_levels, mark):
+    )(*[p[0] for p in parts], *[x for p in parts for x in p[2]], after, *outs)
+
+
+def step_kernel(
+    items, group, own_ref, other_ref, after_ref, out_ref, o_low, o_res, o_out, o_levels, mark
+):
     mark[...] = jnp.zeros_like(mark)
-    width = rows_ref.shape[1]
+    width = own_ref.shape[1]
     half = width // 2
-    rows = rows_ref[: rows_ref.shape[0] - EDGE, :].astype(F32).reshape(-1, group, width)
-    lanes = (rows.shape[0], group, 128)
-    index = 32.0 * rows[:, items : items + 1, :128] + rows[:, items + 1 : items + 2, :128]
-    diagonal = lax.broadcasted_iota(jnp.int32, lanes, 1) == lax.broadcasted_iota(
-        jnp.int32, lanes, 2
-    )
-    index = jnp.sum(jnp.where(diagonal, index, 0.0), axis=2, keepdims=True)
-    index = index.reshape(-1, 1)
-    lane = lax.broadcasted_iota(jnp.int32, (index.shape[0], half), 1).astype(F32)
-    angle = index * jnp.exp(lane * F32(-math.log(10000.0) / half))
-    emb = jnp.concatenate([jnp.sin(angle), jnp.cos(angle)], axis=1)
-    used = lax.broadcasted_iota(jnp.int32, rows.shape, 1) < items
-    sums = jnp.where(used, rows, 0.0).reshape(-1, width)
-    out_ref[...] = tn(emb.astype(BF16), sums.astype(BF16))
-    vec = rows_ref[rows_ref.shape[0] - EDGE :, :].astype(F32)
+    count = own_ref.shape[0] - EDGE
+
+    def product(rows_ref):
+        rows = rows_ref[:count, :].astype(F32).reshape(-1, group, width)
+        lanes = (rows.shape[0], group, 128)
+        index = 32.0 * rows[:, items : items + 1, :128] + rows[:, items + 1 : items + 2, :128]
+        diagonal = lax.broadcasted_iota(jnp.int32, lanes, 1) == lax.broadcasted_iota(
+            jnp.int32, lanes, 2
+        )
+        index = jnp.sum(jnp.where(diagonal, index, 0.0), axis=2, keepdims=True)
+        index = index.reshape(-1, 1)
+        lane = lax.broadcasted_iota(jnp.int32, (index.shape[0], half), 1).astype(F32)
+        angle = index * jnp.exp(lane * F32(-math.log(10000.0) / half))
+        emb = jnp.concatenate([jnp.sin(angle), jnp.cos(angle)], axis=1)
+        used = lax.broadcasted_iota(jnp.int32, rows.shape, 1) < items
+        sums = jnp.where(used, rows, 0.0).reshape(-1, width)
+        return tn(emb.astype(BF16), sums.astype(BF16))
+
+    out_ref[...] = product(own_ref) + product(other_ref)
+    vec = own_ref[count:, :].astype(F32) + other_ref[count:, :].astype(F32)
     for i, out in enumerate((o_low, o_res, o_out)):
         out[:, :width] = vec[2 * i : 2 * i + 1, :]
         out[:, width:] = vec[2 * i + 1 : 2 * i + 2, :]
@@ -927,8 +1009,7 @@
         name="weights",
     )(sec, stack, d_pre)
     batch_b = batch(keep_b, give_b, sums)
-    (after,) = batch_a.turn(after)
-    (after,) = batch_c.turn(after)
+    after = batch_c.turn(batch_a.turn(after))
 
     group = -(-(micro * slots + 2) // 16) * 16
     rows_last = own // EDGE - 1
@@ -975,63 +1056,50 @@
     )
     in_got = swap(in_give)
 
-    (after,) = batch_b.turn(rows_now)
-    block_out, skip_out, after = join(
-        sec, after, (block_keep, block_got), (skip_keep, skip_got)
-    )
-    rows_got, rows_bit, gathered = swap(rows_now), sec, 0
+    after = batch_b.turn(rows_now, behind=rows_now)
     batches = {"a": batch_a, "b": batch_b, "c": batch_c}
-    order = "acb" * (batch_a.turns - 1)
+    order = "acb" * 2 + "J" + "acb" * (batch_a.turns - 3)
     for name in order:
+        if name == "J":
+            block_out, skip_out, after = join(
+                sec, after, (block_keep, block_got), (skip_keep, skip_got)
+            )
+            continue
         turner = batches[name]
-        if name == "b" and gathered <= sums.levels:
-            n = rows_now.shape[0]
-            work = (add_body, rows_bit, rows_now, rows_got, [struct(n, width)])
-            if gathered:
-                work = (gather_body, rows_bit, rows_now, rows_got, [struct(2 * n - EDGE, width)])
-            after, rows_now = turner.turn(after, [work])
-            if gathered < sums.levels:
-                at = sums.levels - 1 - gathered
-                route = [(d, d ^ (1 << at)) for d in range(sums.chips)]
-                rows_got = lax.ppermute(rows_now, "dp", route)
-                rows_bit = ((sums.chip >> at) & 1).astype(jnp.int32).reshape(1)
-            gathered += 1
-        else:
-            (after,) = turner.turn(after)
+        after = turner.turn(after)
 
     line = struct(1, wide, F32)
     g_step, g_convb, g_resb, g_outb, levels, mark = pl.pallas_call(
         functools.partial(step_kernel, micro * slots, group),
-        in_specs=[IN_VMEM, ANYWHERE],
+        in_specs=[IN_VMEM, IN_VMEM, ANYWHERE],
         out_specs=[IN_VMEM] * 6,
         out_shape=[struct(width, width, F32), line, line, line]
         + [struct(3, 128, F32), struct(8, 128, F32)],
         compiler_params=pltpu.CompilerParams(vmem_limit_bytes=24 * 1024 * 1024),
         cost_estimate=LARGE,
         name="step_grad",
-    )(rows_now, after)
+    )(batch_b.rows, swap(batch_b.rows), after)
     in_grad, mark = join(sec, mark, (in_keep, in_got))
 
     def pairs(k, count, base=0):
         return [(k, base + i * width, col) for i in range(count) for col in (0, width)]
 
     square, tall = struct(width, width, F32), struct(width, wide, F32)
-    shapes_a = [tall, square, square, square]
-    spots_a = spots_of(pairs(0, 1) + [(k, 0, 0) for k in (1, 2, 3)], width)
-    shapes_b, spots_b = [struct(taps * width, wide, F32)], spots_of(pairs(0, taps), width)
-    shapes_c, spots_c = [tall, tall], spots_of(pairs(0, 1) + pairs(1, 1), width)
-    *outs_a, mark = batch_a.early(shapes_a, spots_a, mark)
-    *outs_c, mark = batch_c.early(shapes_c, spots_c, mark)
-    *outs_b, mark = batch_b.early(shapes_b, spots_b, mark)
+    shapes = [tall, square, square, square, tall, tall, struct(taps * width, wide, F32)]
+    batch_a.spots = spots_of([(1, 0, 0), (2, 0, 0), (3, 0, 0)] + pairs(0, 1), width)
+    batch_c.spots = spots_of(pairs(4, 1) + pairs(5, 1), width)
+    batch_b.spots = spots_of(pairs(6, taps), width)
+    both = (batch_a, batch_c, batch_b)
+    *outs, mark = place([batch_a.early()], shapes, mark)
+    *outs, mark = place([batch_c.early()], shapes, mark, outs)
+    *outs, mark = place([batch_b.early()], shapes, mark, outs)
     mark = batch_a.arrive(mark)
     mark = batch_c.arrive(mark)
-    *outs_a, mark = batch_a.late(shapes_a, spots_a, mark, outs_a)
-    *outs_c, mark = batch_c.late(shapes_c, spots_c, mark, outs_c)
+    *outs, mark = place([batch_a.late(), batch_c.late()], shapes, mark, outs)
     mark = batch_b.arrive(mark)
-    *outs_b, mark = batch_b.late(shapes_b, spots_b, mark, outs_b)
-    g_out, g_query, g_key, g_value = outs_a
-    g_conv = outs_b[0].reshape(conv_w.shape)
-    g_res, g_cond = outs_c
+    *outs, mark = place([batch_b.late()], shapes, mark, outs)
+    g_out, g_query, g_key, g_value, g_res, g_cond, g_conv = outs
+    g_conv = g_conv.reshape(conv_w.shape)
     g_convb, g_resb, g_outb = (x.reshape(wide) for x in (g_convb, g_resb, g_outb))
     levels = levels[:, 0]
     return (

time: 163 us -> 176 us (1.080)
  starting transfers between devices: 38.9 us -> 45.2 us
  waiting for transfers between devices: 30.7 us -> 35.8 us
    ppermute x21, starting transfers between devices: 27.9 us -> 41.7 us  [send(): return lax.ppermute(x, ('section', 'dp'), route)]
    ppermute x21, waiting for transfers between devices: 20.9 us -> 32 us  [send(): return lax.ppermute(x, ('section', 'dp'), route)]
    ppermute x4 -> x0, waiting for transfers between devices: 6.9 us -> none  [on_device(): rows_got = lax.ppermute(rows_now, 'dp', route)]
    ppermute x4 -> x0, starting transfers between devices: 6.79 us -> none  [on_device(): rows_got = lax.ppermute(rows_now, 'dp', route)]
    pallas_call x1, Pallas kernels: 2.26 us -> 4.3 us  [on_device(): pl.pallas_call(functools.partial(step_kernel, micro * slots, group), in_s...]
    pallas_call x18 -> x14, Pallas kernels: 4.98 us -> 3.75 us  [pair_call(): pl.pallas_call(functools.partial(pair_kernel, [w[0] for w in works], outs...]
    pallas_call x6 -> x9, Pallas kernels: 14 us -> 13.9 us  [the longest x5 12.8 us: place(): pl.pallas_call(functools.partial(place_kernel, groups, len(shapes)), in_s...]
  transfers between devices with their start and end apart: 39 -> 35, of which waited for: 13 -> 11; matrix products, arithmetic and copies ran while one was open for 0% -> 0% of each run, Pallas kernels for 28% -> 27%
where the time goes in v7:
time: 176 us
  Pallas kernels  88.3 us (50%)
  starting transfers between devices  45.2 us (26%)
  waiting for transfers between devices  35.8 us (20%)
  local copies, waits for them, and re-layouts  5.03 us (3%)
    ppermute x21, starting transfers between devices, send(): return lax.ppermute(x, ('section', 'dp'), route)  41.7 us
    pallas_call x1, Pallas kernels, on_device(): pl.pallas_call(functools.partial(forward_kernel, (tile, slots, nq, subs,...  38.8 us
    ppermute x21, waiting for transfers between devices, send(): return lax.ppermute(x, ('section', 'dp'), route)  32 us
    pallas_call x5, Pallas kernels, place(): pl.pallas_call(functools.partial(place_kernel, groups, len(shapes)), in_s...  12.8 us
    pallas_call x1, Pallas kernels, on_device(): pl.pallas_call(weight_kernel, grid_spec=pltpu.PrefetchScalarGridSpec(num_...  8.97 us
    pallas_call x1, Pallas kernels, on_device(): pl.pallas_call(functools.partial(back_kernel, (tile, slots, subs, tiles,...  7.51 us
    pallas_call x2, Pallas kernels, join(): pl.pallas_call(functools.partial(join_kernel, count), in_specs=[IN_SMEM]...  5.35 us
    pallas_call x3, Pallas kernels, split_first(): pl.pallas_call(first_kernel, in_specs=[IN_SMEM, ANYWHERE, ANYWHERE, ANYWH...  4.6 us
  transfers between devices with their start and end apart: 35, of which 11 were waited for; matrix products, arithmetic and copies ran while one was open for 0% of the time, Pallas kernels for 27%

profile of v7, /device:TPU:0, one launch (start us, length us, event | category | flops | bytes accessed | tf_op | source)
XLA Modules:
  0.0 175.6 jit_solution(6760828223289473007)
XLA Ops:
  0.7 38.8 %forward.1 = (bf16[1536,1536]{1,0:T(8,128)(2,1)}, bf16[1536,1024]{1,0:T(8,128)(2,1)}, bf16[32,1024]{1,0:T(8,128)(2,1)}, bf16[1536,512]{1,0:T(8,128)(2,1)}, bf16[...) custom-call(s32[1]{0:T(128)} %bitcast.sec_ref, ...), custom_call_target="tpu_custom_call" | custom-call | flops 68719476736 | bytes 1024 | tf_op jit(solution)/shard_map/forward/pallas_call | solution.py:914
  40.4 9.0 %weights.1 = (bf16[6,256,512]{2,1,0:T(8,128)(2,1)S(1)}, bf16[6,256,512]{2,1,0:T(8,128)(2,1)}, f32[8,128]{1,0:T(8,128)S(1)}) custom-call(s32[1]{0:T(128)} %bitcast.sec_ref, bf16[1536,1536]{1,0:T(8,128)(2,1)} %get-tuple-element.111.left_ref, bf16[1536,1024]{1,0:T(8,128)(2,1)} %get-tuple-element.112.dpre_ref.prev_ref.next_ref), custom_call_target="tpu_custom_call" | custom-call | flops 68719476736 | bytes 1024 | tf_op jit(solution)/shard_map/weights/pallas_call | solution.py:997
  52.6 1.8 %split_first.3 = (bf16[640,512]{1,0:T(8,128)(2,1)S(1)}, bf16[640,512]{1,0:T(8,128)(2,1)}, f32[8,128]{1,0:T(8,128)S(1)}, bf16[1280,512]{1,0:T(8,128)(2,1)S(1)}) custom-call(s32[1]{0:T(128)} %bitcast.6.bit_ref.refs_0_.last_ref, bf16[1280,512]{1,0:T(8,128)(2,1)S(1)} %bitcast.31, ...), custom_call_target="tpu_custom_call", output_to_operand_aliasing={{3}: (1, {})} | custom-call | flops 68719476736 | bytes 1024 | tf_op jit(solution)/shard_map/split_first/pallas_call | solution.py:518
  54.5 3.1 %collective-permute-start.8 = (bf16[640,512]{1,0:T(8,128)(2,1)}, bf16[640,512]{1,0:T(8,128)(2,1)}, u32[]{:S(2)}, u32[]{:S(2)}) collective-permute-start(bf16[640,512]{1,0:T(8,128)(2,1)} %get-tuple-element.131), channel_id=1, source_target_pairs={{0,4},{1,5},{2,6},{3,7},{4,0},{5,1},{6,2},{7,3},{8,12},{9,13},{10,... | collective-permute-start | bytes 1966088 | tf_op jit(solution)/shard_map/ppermute | solution.py:609
  61.1 7.5 %back.1 = (bf16[1536,256]{1,0:T(8,128)(2,1)S(1)}, bf16[1536,256]{1,0:T(8,128)(2,1)}, bf16[32,512]{1,0:T(8,128)(2,1)S(1)}) custom-call(s32[1]{0:T(128)} %bitcast.sec_ref, s32[3]{0:T(128)S(1)} %copy-done.5, s32[3,4]{1,0:T(4,128)S(1)} %copy-done.3, bf16[1536,1024]{1,0:T(8,128)(2,1)S(1)} %copy-done.10, bf16[1536,1024]{1,0:T(8,128)(2,1)S(1)} %copy-done.10, ...), custom_call_target="tpu_custom_call" | custom-call | flops 68719476736 | bytes 1024 | tf_op jit(solution)/shard_map/back/pallas_call | solution.py:1016
  69.4 1.7 split_first.5
  71.1 2.1 %collective-permute-done.8.refs_2_ = bf16[640,512]{1,0:T(8,128)(2,1)} collective-permute-done((bf16[640,512]{1,0:T(8,128)(2,1)}, bf16[640,512]{1,0:T(8,128)(2,1)}, u32[]{:S(2)}, u32[]{:S(2)}) %collective-permute-start.8) | collective-permute-done | bytes 655392 | tf_op jit(solution)/shard_map/ppermute | solution.py:609
  73.1 2.3 %collective-permute-start.6 = (bf16[800,512]{1,0:T(8,128)(2,1)S(1)}, bf16[800,512]{1,0:T(8,128)(2,1)S(1)}, u32[]{:S(2)}, u32[]{:S(2)}) collective-permute-start(bf16[800,512]{1,0:T(8,128)(2,1)S(1)} %get-tuple-element.127.sent), channel_id=1, source_target_pairs={{0,1},{1,0},{2,3},{3,2},{4,5},{5,4},{6,7},{7,6},{8,9},{9,8},{10,11... | collective-permute-start | bytes 2457608 | tf_op jit(solution)/shard_map/ppermute | solution.py:609
  76.6 1.7 collective-permute-start.11
  79.5 6.2 %collective-permute-done.6.got = bf16[800,512]{1,0:T(8,128)(2,1)S(1)} collective-permute-done((bf16[800,512]{1,0:T(8,128)(2,1)S(1)}, bf16[800,512]{1,0:T(8,128)(2,1)S(1)}, u32[]{:S(2)}, u32[]{:S(2)}) %collective-permute-start.6) | collective-permute-done | bytes 819232 | tf_op jit(solution)/shard_map/ppermute | solution.py:609
  85.7 2.0 %collective-permute-start.10 = (bf16[256,512]{1,0:T(8,128)(2,1)S(1)}, bf16[256,512]{1,0:T(8,128)(2,1)S(1)}, u32[]{:S(2)}, u32[]{:S(2)}) collective-permute-start(bf16[256,512]{1,0:T(8,128)(2,1)S(1)} %get-tuple-element.137), channel_id=1, source_target_pairs={{0,2},{1,3},{2,0},{3,1},{4,6},{5,7},{6,4},{7,5},{8,10},{9,11},{10,... | collective-permute-start | bytes 786440 | tf_op jit(solution)/shard_map/ppermute | solution.py:609
  89.8 2.3 %collective-permute-done.10.refs_2_ = bf16[256,512]{1,0:T(8,128)(2,1)S(1)} collective-permute-done((bf16[256,512]{1,0:T(8,128)(2,1)S(1)}, bf16[256,512]{1,0:T(8,128)(2,1)S(1)}, u32[]{:S(2)}, u32[]{:S(2)}) %collective-permute-start.10) | collective-permute-done | bytes 262176 | tf_op jit(solution)/shard_map/ppermute | solution.py:609
  92.1 2.0 %collective-permute-start.15 = (bf16[160,512]{1,0:T(8,128)(2,1)S(1)}, bf16[160,512]{1,0:T(8,128)(2,1)S(1)}, u32[]{:S(2)}, u32[]{:S(2)}) collective-permute-start(bf16[160,512]{1,0:T(8,128)(2,1)S(1)} %get-tuple-element.148), channel_id=1, source_target_pairs={{0,1},{1,0},{2,3},{3,2},{4,5},{5,4},{6,7},{7,6},{8,9},{9,8},{10,11... | collective-permute-start | bytes 491528 | tf_op jit(solution)/shard_map/ppermute | solution.py:609
  94.2 4.4 %collective-permute-done.9.got = bf16[432,512]{1,0:T(8,128)(2,1)S(1)} collective-permute-done((bf16[432,512]{1,0:T(8,128)(2,1)S(1)}, bf16[432,512]{1,0:T(8,128)(2,1)S(1)}, u32[]{:S(2)}, u32[]{:S(2)}) %collective-permute-start.9) | collective-permute-done | bytes 442400 | tf_op jit(solution)/shard_map/ppermute | solution.py:609
  98.6 2.0 %collective-permute-start.14 = (bf16[128,512]{1,0:T(8,128)(2,1)S(1)}, bf16[128,512]{1,0:T(8,128)(2,1)S(1)}, u32[]{:S(2)}, u32[]{:S(2)}) collective-permute-start(bf16[128,512]{1,0:T(8,128)(2,1)S(1)} %get-tuple-element.147), channel_id=1, source_target_pairs={{0,4},{1,5},{2,6},{3,7},{4,0},{5,1},{6,2},{7,3},{8,12},{9,13},{10,... | collective-permute-start | bytes 393224 | tf_op jit(solution)/shard_map/ppermute | solution.py:609
  102.0 3.1 %join.2 = (bf16[3072,256]{1,0:T(8,128)(2,1)}, bf16[3072,256]{1,0:T(8,128)(2,1)}, f32[8,128]{1,0:T(8,128)S(1)}) custom-call(s32[1]{0:T(128)} %bitcast.sec_ref, bf16[1536,256]{1,0:T(8,128)(2,1)S(1)} %copy-done, bf16[1536,256]{1,0:T(8,128)(2,1)} %collective-permute-done.refs_1_, bf16[1536,256]{1,0:T(8,128)(2,1)S(1)} %copy-done.1, ...), custom_call_target="tpu_custom_call" | custom-call | flops 1024 | bytes 1024 | tf_op jit(solution)/shard_map/join/pallas_call | solution.py:571
  106.7 3.9 %collective-permute-start.17 = (bf16[128,512]{1,0:T(8,128)(2,1)S(1)}, bf16[128,512]{1,0:T(8,128)(2,1)S(1)}, u32[]{:S(2)}, u32[]{:S(2)}) collective-permute-start(bf16[128,512]{1,0:T(8,128)(2,1)S(1)} %add_body.5.after_ref.refs_1_), channel_id=1, source_target_pairs={{0,8},{1,9},{2,10},{3,11},{4,12},{5,13},{6,14},{7,15},{8,0},{9,1},... | collective-permute-start | bytes 393224 | tf_op jit(solution)/shard_map/ppermute | solution.py:609
  111.4 5.7 %collective-permute-start.16 = (bf16[336,512]{1,0:T(8,128)(2,1)S(1)}, bf16[336,512]{1,0:T(8,128)(2,1)S(1)}, u32[]{:S(2)}, u32[]{:S(2)}) collective-permute-start(bf16[336,512]{1,0:T(8,128)(2,1)S(1)} %ride.6.refs_3_.sent), channel_id=1, source_target_pairs={{0,8},{1,9},{2,10},{3,11},{4,12},{5,13},{6,14},{7,15},{8,0},{9,1},... | collective-permute-start | bytes 1032200 | tf_op jit(solution)/shard_map/ppermute | solution.py:609
  118.7 2.5 %collective-permute-start.21 = (bf16[128,512]{1,0:T(8,128)(2,1)S(1)}, bf16[128,512]{1,0:T(8,128)(2,1)S(1)}, u32[]{:S(2)}, u32[]{:S(2)}) collective-permute-start(bf16[128,512]{1,0:T(8,128)(2,1)S(1)} %add_body.7.after_ref.refs_1_), channel_id=1, source_target_pairs={{0,4},{1,5},{2,6},{3,7},{4,0},{5,1},{6,2},{7,3},{8,12},{9,13},{10,... | collective-permute-start | bytes 393224 | tf_op jit(solution)/shard_map/ppermute | solution.py:609
  121.2 8.8 %collective-permute-done.16.got = bf16[336,512]{1,0:T(8,128)(2,1)S(1)} collective-permute-done((bf16[336,512]{1,0:T(8,128)(2,1)S(1)}, bf16[336,512]{1,0:T(8,128)(2,1)S(1)}, u32[]{:S(2)}, u32[]{:S(2)}) %collective-permute-start.16) | collective-permute-done | bytes 344096 | tf_op jit(solution)/shard_map/ppermute | solution.py:609
  131.9 3.5 %collective-permute-start.25 = (bf16[320,512]{1,0:T(8,128)(2,1)S(1)}, bf16[320,512]{1,0:T(8,128)(2,1)S(1)}, u32[]{:S(2)}, u32[]{:S(2)}) collective-permute-start(bf16[320,512]{1,0:T(8,128)(2,1)S(1)} %merge_body.6.refs_3_.refs_1_), channel_id=1, source_target_pairs={{0,8},{1,9},{2,10},{3,11},{4,12},{5,13},{6,14},{7,15},{8,0},{9,1},... | collective-permute-start | bytes 983048 | tf_op jit(solution)/shard_map/ppermute | solution.py:609
  135.5 1.6 collective-permute-start.24
  138.0 6.0 %collective-permute-done.25.refs_2_ = bf16[320,512]{1,0:T(8,128)(2,1)S(1)} collective-permute-done((bf16[320,512]{1,0:T(8,128)(2,1)S(1)}, bf16[320,512]{1,0:T(8,128)(2,1)S(1)}, u32[]{:S(2)}, u32[]{:S(2)}) %collective-permute-start.25) | collective-permute-done | bytes 327712 | tf_op jit(solution)/shard_map/ppermute | solution.py:609
  146.2 1.6 collective-permute-start.32
  149.5 4.3 %step_grad.1 = (f32[512,512]{1,0:T(8,128)}, f32[1,1024]{1,0:T(1,128)}, f32[1,1024]{1,0:T(1,128)}, f32[1,1024]{1,0:T(1,128)}, f32[3,128]{1,0:T(4,128)S(1)}, /*index=5*/f32[8,128]{1,0:T(8,128)S(1)}) custom-call(bf16[272,512]{1,0:T(8,128)(2,1)} %get-tuple-element.150.own_ref, bf16[272,512]{1,0:T(8,128)(2,1)} %collective-permute-done.19.other_ref, ...), custom_call_target="tpu_custom_call" | custom-call | flops 68719476736 | bytes 1024 | tf_op jit(solution)/shard_map/step_grad/pallas_call | solution.py:1072
  153.8 2.3 %join.3 = (bf16[3072,256]{1,0:T(8,128)(2,1)}, f32[8,128]{1,0:T(8,128)S(1)}) custom-call(s32[1]{0:T(128)} %bitcast.sec_ref, bf16[1536,256]{1,0:T(8,128)(2,1)S(1)} %get-tuple-element.144.refs_0_, bf16[1536,256]{1,0:T(8,128)(2,1)} %collective-permute-done.12.refs_1_, f32[8,128]{1,0:T(8,128)S(1)} %get-tuple-element.152.refs_2_), custom_call_target="tpu_custom_call" | custom-call | flops 1024 | bytes 1024 | tf_op jit(solution)/shard_map/join/pallas_call | solution.py:571
  156.1 2.7 %place.5 = (f32[512,1024]{1,0:T(8,128)}, f32[512,512]{1,0:T(8,128)}, f32[512,512]{1,0:T(8,128)}, f32[512,512]{1,0:T(8,128)}, f32[512,1024]{1,0:T(8,128)}, /*inde...) custom-call(s32[4]{0:T(128)S(1)} %pad_add_fusion.1.refs_0_, ...), custom_call_target="tpu_custom_call" | custom-call | flops 1024 | bytes 1024 | tf_op jit(solution)/shard_map/place/pallas_call | solution.py:760
  158.8 2.0 %place.6 = (f32[512,1024]{1,0:T(8,128)}, f32[512,512]{1,0:T(8,128)}, f32[512,512]{1,0:T(8,128)}, f32[512,512]{1,0:T(8,128)}, f32[512,1024]{1,0:T(8,128)}, /*inde...) custom-call(s32[4]{0:T(128)S(1)} %pad_add_fusion.refs_0_.refs_1_, ...), custom_call_target="tpu_custom_call", output_to_operand_aliasing={{0}: (4, {}), {1}: (5, {}), {2}: (6, {}), {3}: (7, {}), {4}... | custom-call | flops 1024 | bytes 1024 | tf_op jit(solution)/shard_map/place/pallas_call | solution.py:760
  160.8 2.3 %place.7 = (f32[512,1024]{1,0:T(8,128)}, f32[512,512]{1,0:T(8,128)}, f32[512,512]{1,0:T(8,128)}, f32[512,512]{1,0:T(8,128)}, f32[512,1024]{1,0:T(8,128)}, /*inde...) custom-call(s32[4]{0:T(128)S(1)} %pad_add_fusion.refs_0_.refs_1_, ...), custom_call_target="tpu_custom_call", output_to_operand_aliasing={{0}: (4, {}), {1}: (5, {}), {2}: (6, {}), {3}: (7, {}), {4}... | custom-call | flops 1024 | bytes 1024 | tf_op jit(solution)/shard_map/place/pallas_call | solution.py:760
  165.0 2.2 %collective-permute-done.33.refs_5_ = bf16[512,512]{1,0:T(8,128)(2,1)S(1)} collective-permute-done((bf16[512,512]{1,0:T(8,128)(2,1)S(1)}, bf16[512,512]{1,0:T(8,128)(2,1)S(1)}, u32[]{:S(2)}, u32[]{:S(2)}) %collective-permute-start.33) | collective-permute-done | bytes 524320 | tf_op jit(solution)/shard_map/ppermute | solution.py:584
  167.2 2.9 %place.8 = (f32[512,1024]{1,0:T(8,128)}, f32[512,512]{1,0:T(8,128)}, f32[512,512]{1,0:T(8,128)}, f32[512,512]{1,0:T(8,128)}, f32[512,1024]{1,0:T(8,128)}, /*inde...) custom-call(s32[4]{0:T(128)S(1)} %pad_add_fusion.1.refs_0_, ...), custom_call_target="tpu_custom_call", output_to_operand_aliasing={{0}: (7, {}), {1}: (8, {}), {2}: (9, {}), {3}: (10, {}), {4... | custom-call | flops 1024 | bytes 1024 | tf_op jit(solution)/shard_map/place/pallas_call | solution.py:760
  172.5 2.9 %place.9 = (f32[512,1024]{1,0:T(8,128)}, f32[512,512]{1,0:T(8,128)}, f32[512,512]{1,0:T(8,128)}, f32[512,512]{1,0:T(8,128)}, f32[512,1024]{1,0:T(8,128)}, /*inde...) custom-call(s32[4]{0:T(128)S(1)} %pad_add_fusion.refs_0_.refs_1_, ...), custom_call_target="tpu_custom_call", output_to_operand_aliasing={{0}: (4, {}), {1}: (5, {}), {2}: (6, {}), {3}: (7, {}), {4}... | custom-call | flops 1024 | bytes 1024 | tf_op jit(solution)/shard_map/place/pallas_call | solution.py:760
  (102 shorter events, 29.5 us)
Async XLA Ops:
  39.4 11.8 %collective-permute-start.5 = (bf16[1280,512]{1,0:T(8,128)(2,1)}, bf16[1280,512]{1,0:T(8,128)(2,1)S(1)}, u32[]{:S(2)}, u32[]{:S(2)}) collective-permute-start(bf16[1280,512]{1,0:T(8,128)(2,1)} %bitcast.35), channel_id=1, source_target_pairs={{0,16},{16,0},{1,17},{17,1},{2,18},{18,2},{3,19},{19,3},{4,20},{20... | collective-permute-start | bytes 3932168 | tf_op jit(solution)/shard_map/ppermute | solution.py:584
  39.9 14.6 %collective-permute-start.4 = (bf16[1024,512]{1,0:T(8,128)(2,1)}, bf16[1024,512]{1,0:T(8,128)(2,1)S(1)}, u32[]{:S(2)}, u32[]{:S(2)}) collective-permute-start(bf16[1024,512]{1,0:T(8,128)(2,1)} %bitcast.36), channel_id=1, source_target_pairs={{0,16},{16,0},{1,17},{17,1},{2,18},{18,2},{3,19},{19,3},{4,20},{20... | collective-permute-start | bytes 3145736 | tf_op jit(solution)/shard_map/ppermute | solution.py:584
  40.0 18.7 %collective-permute-start.3 = (bf16[32,1024]{1,0:T(8,128)(2,1)}, bf16[32,1024]{1,0:T(8,128)(2,1)}, u32[]{:S(2)}, u32[]{:S(2)}) collective-permute-start(bf16[32,1024]{1,0:T(8,128)(2,1)} %get-tuple-element.115), channel_id=1, source_target_pairs={{0,16},{16,0},{1,17},{17,1},{2,18},{18,2},{3,19},{19,3},{4,20},{20... | collective-permute-start | bytes 196616 | tf_op jit(solution)/shard_map/ppermute | solution.py:584
  50.5 18.0 %collective-permute-start.2 = (bf16[1536,512]{1,0:T(8,128)(2,1)}, bf16[1536,512]{1,0:T(8,128)(2,1)}, u32[]{:S(2)}, u32[]{:S(2)}) collective-permute-start(bf16[1536,512]{1,0:T(8,128)(2,1)} %bitcast.34), channel_id=1, source_target_pairs={{0,16},{16,0},{1,17},{17,1},{2,18},{18,2},{3,19},{19,3},{4,20},{20... | collective-permute-start | bytes 4718600 | tf_op jit(solution)/shard_map/ppermute | solution.py:584
  50.6 50.1 %collective-permute-start = (bf16[1536,256]{1,0:T(8,128)(2,1)}, bf16[1536,256]{1,0:T(8,128)(2,1)}, u32[]{:S(2)}, u32[]{:S(2)}) collective-permute-start(bf16[1536,256]{1,0:T(8,128)(2,1)} %get-tuple-element.108), channel_id=1, source_target_pairs={{0,16},{16,0},{1,17},{17,1},{2,18},{18,2},{3,19},{19,3},{4,20},{20... | collective-permute-start | bytes 2359304 | tf_op jit(solution)/shard_map/ppermute | solution.py:584
  51.2 49.6 %collective-permute-start.1 = (bf16[1536,256]{1,0:T(8,128)(2,1)}, bf16[1536,256]{1,0:T(8,128)(2,1)}, u32[]{:S(2)}, u32[]{:S(2)}) collective-permute-start(bf16[1536,256]{1,0:T(8,128)(2,1)} %get-tuple-element.110), channel_id=1, source_target_pairs={{0,16},{16,0},{1,17},{17,1},{2,18},{18,2},{3,19},{19,3},{4,20},{20... | collective-permute-start | bytes 2359304 | tf_op jit(solution)/shard_map/ppermute | solution.py:584
  54.5 18.6 %collective-permute-start.8 = (bf16[640,512]{1,0:T(8,128)(2,1)}, bf16[640,512]{1,0:T(8,128)(2,1)}, u32[]{:S(2)}, u32[]{:S(2)}) collective-permute-start(bf16[640,512]{1,0:T(8,128)(2,1)} %get-tuple-element.131), channel_id=1, source_target_pairs={{0,4},{1,5},{2,6},{3,7},{4,0},{5,1},{6,2},{7,3},{8,12},{9,13},{10,... | collective-permute-start | bytes 1966088 | tf_op jit(solution)/shard_map/ppermute | solution.py:609
  58.8 17.9 %collective-permute-start.7 = (bf16[512,512]{1,0:T(8,128)(2,1)}, bf16[512,512]{1,0:T(8,128)(2,1)}, u32[]{:S(2)}, u32[]{:S(2)}) collective-permute-start(bf16[512,512]{1,0:T(8,128)(2,1)} %get-tuple-element.129), channel_id=1, source_target_pairs={{0,1},{1,0},{2,3},{3,2},{4,5},{5,4},{6,7},{7,6},{8,9},{9,8},{10,11... | collective-permute-start | bytes 1572872 | tf_op jit(solution)/shard_map/ppermute | solution.py:609
  68.6 77.6 %collective-permute-start.12 = (bf16[1536,256]{1,0:T(8,128)(2,1)}, bf16[1536,256]{1,0:T(8,128)(2,1)}, u32[]{:S(2)}, u32[]{:S(2)}) collective-permute-start(bf16[1536,256]{1,0:T(8,128)(2,1)} %get-tuple-element.145), channel_id=1, source_target_pairs={{0,16},{16,0},{1,17},{17,1},{2,18},{18,2},{3,19},{19,3},{4,20},{20... | collective-permute-start | bytes 2359304 | tf_op jit(solution)/shard_map/ppermute | solution.py:584
  73.1 12.6 %collective-permute-start.6 = (bf16[800,512]{1,0:T(8,128)(2,1)S(1)}, bf16[800,512]{1,0:T(8,128)(2,1)S(1)}, u32[]{:S(2)}, u32[]{:S(2)}) collective-permute-start(bf16[800,512]{1,0:T(8,128)(2,1)S(1)} %get-tuple-element.127.sent), channel_id=1, source_target_pairs={{0,1},{1,0},{2,3},{3,2},{4,5},{5,4},{6,7},{7,6},{8,9},{9,8},{10,11... | collective-permute-start | bytes 2457608 | tf_op jit(solution)/shard_map/ppermute | solution.py:609
  76.6 11.6 %collective-permute-start.11 = (bf16[320,512]{1,0:T(8,128)(2,1)S(1)}, bf16[320,512]{1,0:T(8,128)(2,1)S(1)}, u32[]{:S(2)}, u32[]{:S(2)}) collective-permute-start(bf16[320,512]{1,0:T(8,128)(2,1)S(1)} %get-tuple-element.138), channel_id=1, source_target_pairs={{0,8},{1,9},{2,10},{3,11},{4,12},{5,13},{6,14},{7,15},{8,0},{9,1},... | collective-permute-start | bytes 983048 | tf_op jit(solution)/shard_map/ppermute | solution.py:609
  85.7 6.4 %collective-permute-start.10 = (bf16[256,512]{1,0:T(8,128)(2,1)S(1)}, bf16[256,512]{1,0:T(8,128)(2,1)S(1)}, u32[]{:S(2)}, u32[]{:S(2)}) collective-permute-start(bf16[256,512]{1,0:T(8,128)(2,1)S(1)} %get-tuple-element.137), channel_id=1, source_target_pairs={{0,2},{1,3},{2,0},{3,1},{4,6},{5,7},{6,4},{7,5},{8,10},{9,11},{10,... | collective-permute-start | bytes 786440 | tf_op jit(solution)/shard_map/ppermute | solution.py:609
  88.2 10.4 %collective-permute-start.9 = (bf16[432,512]{1,0:T(8,128)(2,1)S(1)}, bf16[432,512]{1,0:T(8,128)(2,1)S(1)}, u32[]{:S(2)}, u32[]{:S(2)}) collective-permute-start(bf16[432,512]{1,0:T(8,128)(2,1)S(1)} %get-tuple-element.136.sent), channel_id=1, source_target_pairs={{0,2},{1,3},{2,0},{3,1},{4,6},{5,7},{6,4},{7,5},{8,10},{9,11},{10,... | collective-permute-start | bytes 1327112 | tf_op jit(solution)/shard_map/ppermute | solution.py:609
  92.1 12.9 %collective-permute-start.15 = (bf16[160,512]{1,0:T(8,128)(2,1)S(1)}, bf16[160,512]{1,0:T(8,128)(2,1)S(1)}, u32[]{:S(2)}, u32[]{:S(2)}) collective-permute-start(bf16[160,512]{1,0:T(8,128)(2,1)S(1)} %get-tuple-element.148), channel_id=1, source_target_pairs={{0,1},{1,0},{2,3},{3,2},{4,5},{5,4},{6,7},{7,6},{8,9},{9,8},{10,11... | collective-permute-start | bytes 491528 | tf_op jit(solution)/shard_map/ppermute | solution.py:609
  98.6 8.0 %collective-permute-start.14 = (bf16[128,512]{1,0:T(8,128)(2,1)S(1)}, bf16[128,512]{1,0:T(8,128)(2,1)S(1)}, u32[]{:S(2)}, u32[]{:S(2)}) collective-permute-start(bf16[128,512]{1,0:T(8,128)(2,1)S(1)} %get-tuple-element.147), channel_id=1, source_target_pairs={{0,4},{1,5},{2,6},{3,7},{4,0},{5,1},{6,2},{7,3},{8,12},{9,13},{10,... | collective-permute-start | bytes 393224 | tf_op jit(solution)/shard_map/ppermute | solution.py:609
  100.7 10.6 %collective-permute-start.13 = (bf16[272,512]{1,0:T(8,128)(2,1)S(1)}, bf16[272,512]{1,0:T(8,128)(2,1)S(1)}, u32[]{:S(2)}, u32[]{:S(2)}) collective-permute-start(bf16[272,512]{1,0:T(8,128)(2,1)S(1)} %get-tuple-element.146.sent), channel_id=1, source_target_pairs={{0,4},{1,5},{2,6},{3,7},{4,0},{5,1},{6,2},{7,3},{8,12},{9,13},{10,... | collective-permute-start | bytes 835592 | tf_op jit(solution)/shard_map/ppermute | solution.py:609
  105.1 11.9 %collective-permute-start.18 = (bf16[160,512]{1,0:T(8,128)(2,1)S(1)}, bf16[160,512]{1,0:T(8,128)(2,1)S(1)}, u32[]{:S(2)}, u32[]{:S(2)}) collective-permute-start(bf16[160,512]{1,0:T(8,128)(2,1)S(1)} %add_body.4.refs_3_.refs_1_), channel_id=1, source_target_pairs={{0,2},{1,3},{2,0},{3,1},{4,6},{5,7},{6,4},{7,5},{8,10},{9,11},{10,... | collective-permute-start | bytes 491528 | tf_op jit(solution)/shard_map/ppermute | solution.py:609
  106.7 11.9 %collective-permute-start.17 = (bf16[128,512]{1,0:T(8,128)(2,1)S(1)}, bf16[128,512]{1,0:T(8,128)(2,1)S(1)}, u32[]{:S(2)}, u32[]{:S(2)}) collective-permute-start(bf16[128,512]{1,0:T(8,128)(2,1)S(1)} %add_body.5.after_ref.refs_1_), channel_id=1, source_target_pairs={{0,8},{1,9},{2,10},{3,11},{4,12},{5,13},{6,14},{7,15},{8,0},{9,1},... | collective-permute-start | bytes 393224 | tf_op jit(solution)/shard_map/ppermute | solution.py:609
  111.4 18.6 %collective-permute-start.16 = (bf16[336,512]{1,0:T(8,128)(2,1)S(1)}, bf16[336,512]{1,0:T(8,128)(2,1)S(1)}, u32[]{:S(2)}, u32[]{:S(2)}) collective-permute-start(bf16[336,512]{1,0:T(8,128)(2,1)S(1)} %ride.6.refs_3_.sent), channel_id=1, source_target_pairs={{0,8},{1,9},{2,10},{3,11},{4,12},{5,13},{6,14},{7,15},{8,0},{9,1},... | collective-permute-start | bytes 1032200 | tf_op jit(solution)/shard_map/ppermute | solution.py:609
  117.1 14.8 %collective-permute-start.22 = (bf16[160,512]{1,0:T(8,128)(2,1)S(1)}, bf16[160,512]{1,0:T(8,128)(2,1)S(1)}, u32[]{:S(2)}, u32[]{:S(2)}) collective-permute-start(bf16[160,512]{1,0:T(8,128)(2,1)S(1)} %add_body.6.refs_3_.refs_1_), channel_id=1, source_target_pairs={{0,1},{1,0},{2,3},{3,2},{4,5},{5,4},{6,7},{7,6},{8,9},{9,8},{10,11... | collective-permute-start | bytes 491528 | tf_op jit(solution)/shard_map/ppermute | solution.py:609
  118.7 16.8 %collective-permute-start.21 = (bf16[128,512]{1,0:T(8,128)(2,1)S(1)}, bf16[128,512]{1,0:T(8,128)(2,1)S(1)}, u32[]{:S(2)}, u32[]{:S(2)}) collective-permute-start(bf16[128,512]{1,0:T(8,128)(2,1)S(1)} %add_body.7.after_ref.refs_1_), channel_id=1, source_target_pairs={{0,4},{1,5},{2,6},{3,7},{4,0},{5,1},{6,2},{7,3},{8,12},{9,13},{10,... | collective-permute-start | bytes 393224 | tf_op jit(solution)/shard_map/ppermute | solution.py:609
  130.7 6.3 %collective-permute-start.20 = (bf16[192,512]{1,0:T(8,128)(2,1)S(1)}, bf16[192,512]{1,0:T(8,128)(2,1)S(1)}, u32[]{:S(2)}, u32[]{:S(2)}) collective-permute-start(bf16[192,512]{1,0:T(8,128)(2,1)S(1)} %get-tuple-element.151.refs_3_.refs_1_), channel_id=1, source_target_pairs={{0,4},{1,5},{2,6},{3,7},{4,0},{5,1},{6,2},{7,3},{8,12},{9,13},{10,... | collective-permute-start | bytes 589832 | tf_op jit(solution)/shard_map/ppermute | solution.py:609
  131.9 12.1 %collective-permute-start.25 = (bf16[320,512]{1,0:T(8,128)(2,1)S(1)}, bf16[320,512]{1,0:T(8,128)(2,1)S(1)}, u32[]{:S(2)}, u32[]{:S(2)}) collective-permute-start(bf16[320,512]{1,0:T(8,128)(2,1)S(1)} %merge_body.6.refs_3_.refs_1_), channel_id=1, source_target_pairs={{0,8},{1,9},{2,10},{3,11},{4,12},{5,13},{6,14},{7,15},{8,0},{9,1},... | collective-permute-start | bytes 983048 | tf_op jit(solution)/shard_map/ppermute | solution.py:609
  135.5 9.4 %collective-permute-start.24 = (bf16[256,512]{1,0:T(8,128)(2,1)S(1)}, bf16[256,512]{1,0:T(8,128)(2,1)S(1)}, u32[]{:S(2)}, u32[]{:S(2)}) collective-permute-start(bf16[256,512]{1,0:T(8,128)(2,1)S(1)} %merge_body.7.refs_3_.refs_1_), channel_id=1, source_target_pairs={{0,2},{1,3},{2,0},{3,1},{4,6},{5,7},{6,4},{7,5},{8,10},{9,11},{10,... | collective-permute-start | bytes 786440 | tf_op jit(solution)/shard_map/ppermute | solution.py:609
  137.0 10.8 %collective-permute-start.19 = (bf16[272,512]{1,0:T(8,128)(2,1)}, bf16[272,512]{1,0:T(8,128)(2,1)}, u32[]{:S(2)}, u32[]{:S(2)}) collective-permute-start(bf16[272,512]{1,0:T(8,128)(2,1)} %get-tuple-element.150.own_ref), channel_id=1, source_target_pairs={{0,16},{16,0},{1,17},{17,1},{2,18},{18,2},{3,19},{19,3},{4,20},{20... | collective-permute-start | bytes 835592 | tf_op jit(solution)/shard_map/ppermute | solution.py:584
  137.1 9.0 %collective-permute-start.23 = (bf16[384,512]{1,0:T(8,128)(2,1)S(1)}, bf16[384,512]{1,0:T(8,128)(2,1)S(1)}, u32[]{:S(2)}, u32[]{:S(2)}) collective-permute-start(bf16[384,512]{1,0:T(8,128)(2,1)S(1)} %merge_body.8.refs_3_.refs_1_), channel_id=1, source_target_pairs={{0,2},{1,3},{2,0},{3,1},{4,6},{5,7},{6,4},{7,5},{8,10},{9,11},{10,... | collective-permute-start | bytes 1179656 | tf_op jit(solution)/shard_map/ppermute | solution.py:609
  144.9 3.1 %collective-permute-start.30 = (bf16[640,512]{1,0:T(8,128)(2,1)}, bf16[640,512]{1,0:T(8,128)(2,1)S(1)}, u32[]{:S(2)}, u32[]{:S(2)}) collective-permute-start(bf16[640,512]{1,0:T(8,128)(2,1)} %merge_body.9.refs_3_.refs_1_), channel_id=1, source_target_pairs={{0,16},{16,0},{1,17},{17,1},{2,18},{18,2},{3,19},{19,3},{4,20},{20... | collective-permute-start | bytes 1966088 | tf_op jit(solution)/shard_map/ppermute | solution.py:584
  144.9 18.3 %collective-permute-start.27 = (bf16[640,512]{1,0:T(8,128)(2,1)}, bf16[640,512]{1,0:T(8,128)(2,1)}, u32[]{:S(2)}, u32[]{:S(2)}) collective-permute-start(bf16[640,512]{1,0:T(8,128)(2,1)} %merge_body.9.refs_3_.refs_1_), channel_id=1, source_target_pairs={{0,4},{1,5},{2,6},{3,7},{4,0},{5,1},{6,2},{7,3},{8,12},{9,13},{10,... | collective-permute-start | bytes 1966088 | tf_op jit(solution)/shard_map/ppermute | solution.py:609
  146.1 12.7 %collective-permute-start.29 = (bf16[512,512]{1,0:T(8,128)(2,1)S(1)}, bf16[512,512]{1,0:T(8,128)(2,1)S(1)}, u32[]{:S(2)}, u32[]{:S(2)}) collective-permute-start(bf16[512,512]{1,0:T(8,128)(2,1)S(1)} %merge_body.10.refs_3_.refs_1_), channel_id=1, source_target_pairs={{0,16},{16,0},{1,17},{17,1},{2,18},{18,2},{3,19},{19,3},{4,20},{20... | collective-permute-start | bytes 1572872 | tf_op jit(solution)/shard_map/ppermute | solution.py:584
  146.2 18.2 %collective-permute-start.32 = (bf16[512,512]{1,0:T(8,128)(2,1)S(1)}, bf16[512,512]{1,0:T(8,128)(2,1)S(1)}, u32[]{:S(2)}, u32[]{:S(2)}) collective-permute-start(bf16[512,512]{1,0:T(8,128)(2,1)S(1)} %merge_body.10.refs_3_.refs_1_), channel_id=1, source_target_pairs={{0,1},{1,0},{2,3},{3,2},{4,5},{5,4},{6,7},{7,6},{8,9},{9,8},{10,11... | collective-permute-start | bytes 1572872 | tf_op jit(solution)/shard_map/ppermute | solution.py:609
  147.8 13.0 %collective-permute-start.28 = (bf16[768,512]{1,0:T(8,128)(2,1)S(1)}, bf16[768,512]{1,0:T(8,128)(2,1)S(1)}, u32[]{:S(2)}, u32[]{:S(2)}) collective-permute-start(bf16[768,512]{1,0:T(8,128)(2,1)S(1)} %merge_body.11.after_ref.refs_1_), channel_id=1, source_target_pairs={{0,16},{16,0},{1,17},{17,1},{2,18},{18,2},{3,19},{19,3},{4,20},{20... | collective-permute-start | bytes 2359304 | tf_op jit(solution)/shard_map/ppermute | solution.py:584
  148.0 22.1 %collective-permute-start.26 = (bf16[768,512]{1,0:T(8,128)(2,1)S(1)}, bf16[768,512]{1,0:T(8,128)(2,1)S(1)}, u32[]{:S(2)}, u32[]{:S(2)}) collective-permute-start(bf16[768,512]{1,0:T(8,128)(2,1)S(1)} %merge_body.11.after_ref.refs_1_), channel_id=1, source_target_pairs={{0,1},{1,0},{2,3},{3,2},{4,5},{5,4},{6,7},{7,6},{8,9},{9,8},{10,11... | collective-permute-start | bytes 2359304 | tf_op jit(solution)/shard_map/ppermute | solution.py:609
  (16 other events, 47.2 us)

commit v8 on v6

--- a/solution.py
+++ b/solution.py
@@ -278,17 +278,16 @@
             keep[i] = ref[pl.ds(mine, half), pl.ds(left, width)].astype(BF16)
             give[i] = ref[pl.ds(theirs, half), pl.ds(left, width)].astype(BF16)
 
-        put(0, g_out, 0)
-        put(1, g_out, width)
+        put(0, g_query, 0)
+        g_query[...] = tn(here, (d_keys[...] * factor).astype(BF16))
+        put(1, g_query, 0)
+        g_query[...] = tn(here, d_values[...].astype(BF16))
         put(2, g_query, 0)
-        g_query[...] = tn(here, (d_keys[...] * factor).astype(BF16))
-        put(3, g_query, 0)
-        g_query[...] = tn(here, d_values[...].astype(BF16))
-        put(4, g_query, 0)
-        put(0, g_res, 0, o_keep_c, o_give_c)
-        put(1, g_res, width, o_keep_c, o_give_c)
-        put(2, g_cond, 0, o_keep_c, o_give_c)
-        put(3, g_cond, width, o_keep_c, o_give_c)
+        put(3, g_res, width)
+        for i, (ref, left) in enumerate(
+            ((g_out, 0), (g_out, width), (g_cond, 0), (g_cond, width), (g_res, 0))
+        ):
+            put(i, ref, left, o_keep_c, o_give_c)
         for i in range(3):
             line = jnp.sum(sums[i], axis=0, keepdims=True)
             o_vec[2 * i : 2 * i + 1, :] = line[:, :width]
@@ -813,8 +812,8 @@
     def blocks_of(n):
         return const((n, half, width)), shape(n, half, width)
 
-    film_spec, film_shape = blocks_of(5)
-    side_spec, side_shape = blocks_of(4)
+    film_spec, film_shape = blocks_of(4)
+    side_spec, side_shape = blocks_of(5)
     (
         stack,
         d_pre,
@@ -1017,21 +1016,22 @@
 
     square, tall = struct(width, width, F32), struct(width, wide, F32)
     shapes_a = [tall, square, square, square]
-    spots_a = spots_of(pairs(0, 1) + [(k, 0, 0) for k in (1, 2, 3)], width)
+    spots_a = spots_of([(k, 0, 0) for k in (1, 2, 3)] + [(0, 0, width)], width)
     shapes_b, spots_b = [struct(taps * width, wide, F32)], spots_of(pairs(0, taps), width)
-    shapes_c, spots_c = [tall, tall], spots_of(pairs(0, 1) + pairs(1, 1), width)
-    *outs_a, mark = batch_a.early(shapes_a, spots_a, mark)
-    *outs_c, mark = batch_c.early(shapes_c, spots_c, mark)
+    shapes_c = [tall, tall, tall]
+    spots_c = spots_of(pairs(1, 1) + pairs(2, 1) + [(0, 0, 0)], width)
+    g_res, *outs_a, mark = batch_a.early(shapes_a, spots_a, mark)
+    g_res, *outs_c, mark = batch_c.early(shapes_c, spots_c, mark, [g_res])
     *outs_b, mark = batch_b.early(shapes_b, spots_b, mark)
+    mark = batch_c.arrive(mark)
     mark = batch_a.arrive(mark)
-    mark = batch_c.arrive(mark)
-    *outs_a, mark = batch_a.late(shapes_a, spots_a, mark, outs_a)
-    *outs_c, mark = batch_c.late(shapes_c, spots_c, mark, outs_c)
+    g_res, *outs_c, mark = batch_c.late(shapes_c, spots_c, mark, [g_res, *outs_c])
+    g_res, *outs_a, mark = batch_a.late(shapes_a, spots_a, mark, [g_res, *outs_a])
     mark = batch_b.arrive(mark)
     *outs_b, mark = batch_b.late(shapes_b, spots_b, mark, outs_b)
-    g_out, g_query, g_key, g_value = outs_a
+    g_query, g_key, g_value = outs_a
     g_conv = outs_b[0].reshape(conv_w.shape)
-    g_res, g_cond = outs_c
+    g_out, g_cond = outs_c
     g_convb, g_resb, g_outb = (x.reshape(wide) for x in (g_convb, g_resb, g_outb))
     levels = levels[:, 0]
     return (

time: 163 us -> 160 us (0.982)
  starting transfers between devices: 38.9 us -> 36.3 us
  waiting for transfers between devices: 30.7 us -> 32.8 us
  local copies, waits for them, and re-layouts: 3.43 us -> 1.41 us
    ppermute x21, starting transfers between devices: 27.9 us -> 24.6 us  [send(): return lax.ppermute(x, ('section', 'dp'), route)]
    ppermute x4, waiting for transfers between devices: 6.9 us -> 9.01 us  [on_device(): rows_got = lax.ppermute(rows_now, 'dp', route)]
    unnamed x26, local copies, waits for them, and re-layouts: 2.81 us -> 0.79 us
  transfers between devices with their start and end apart: 39 -> 39, of which waited for: 13 -> 12; matrix products, arithmetic and copies ran while one was open for 0% -> 0% of each run, Pallas kernels for 28% -> 29%
where the time goes in v8:
time: 160 us
  Pallas kernels  88 us (55%)
  starting transfers between devices  36.3 us (23%)
  waiting for transfers between devices  32.8 us (20%)
    pallas_call x1, Pallas kernels, on_device(): pl.pallas_call(functools.partial(forward_kernel, (tile, slots, nq, subs,...  38.8 us
    ppermute x21, starting transfers between devices, send(): return lax.ppermute(x, ('section', 'dp'), route)  24.6 us
    ppermute x21, waiting for transfers between devices, send(): return lax.ppermute(x, ('section', 'dp'), route)  21.8 us
    pallas_call x6, Pallas kernels, place(): pl.pallas_call(functools.partial(place_kernel, which, full, len(shapes)),...  14 us
    pallas_call x1, Pallas kernels, on_device(): pl.pallas_call(weight_kernel, grid_spec=pltpu.PrefetchScalarGridSpec(num_...  9.19 us
    ppermute x4, waiting for transfers between devices, on_device(): rows_got = lax.ppermute(rows_now, 'dp', route)  9.01 us
    pallas_call x1, Pallas kernels, on_device(): pl.pallas_call(functools.partial(back_kernel, (tile, slots, subs, tiles,...  7.63 us
    ppermute x4, starting transfers between devices, on_device(): rows_got = lax.ppermute(rows_now, 'dp', route)  7.59 us
  transfers between devices with their start and end apart: 39, of which 12 were waited for; matrix products, arithmetic and copies ran while one was open for 0% of the time, Pallas kernels for 29%

profile of v8, /device:TPU:0, one launch (start us, length us, event | category | flops | bytes accessed | tf_op | source)
XLA Modules:
  0.0 159.8 jit_solution(16285524556349323275)
XLA Ops:
  0.7 38.8 %forward.1 = (bf16[1536,1536]{1,0:T(8,128)(2,1)}, bf16[1536,1024]{1,0:T(8,128)(2,1)}, bf16[32,1024]{1,0:T(8,128)(2,1)}, bf16[1536,512]{1,0:T(8,128)(2,1)}, bf16[...) custom-call(s32[1]{0:T(128)} %bitcast.sec_ref.refs_1_, ...), custom_call_target="tpu_custom_call" | custom-call | flops 68719476736 | bytes 1024 | tf_op jit(solution)/shard_map/forward/pallas_call | solution.py:831
  40.5 9.2 %weights.1 = (bf16[6,256,512]{2,1,0:T(8,128)(2,1)}, bf16[6,256,512]{2,1,0:T(8,128)(2,1)}, f32[8,128]{1,0:T(8,128)}) custom-call(s32[1]{0:T(128)} %bitcast.sec_ref.refs_1_, bf16[1536,1536]{1,0:T(8,128)(2,1)} %get-tuple-element.99.left_ref, bf16[1536,1024]{1,0:T(8,128)(2,1)} %get-tuple-element.100.dpre_ref.prev_ref.next_ref), custom_call_target="tpu_custom_call" | custom-call | flops 68719476736 | bytes 1024 | tf_op jit(solution)/shard_map/weights/pallas_call | solution.py:914
  52.2 3.1 %collective-permute-start.10 = (bf16[512,512]{1,0:T(8,128)(2,1)}, bf16[512,512]{1,0:T(8,128)(2,1)}, u32[]{:S(2)}, u32[]{:S(2)}) collective-permute-start(bf16[512,512]{1,0:T(8,128)(2,1)} %get-tuple-element.124), channel_id=1, source_target_pairs={{0,4},{1,5},{2,6},{3,7},{4,0},{5,1},{6,2},{7,3},{8,12},{9,13},{10,... | collective-permute-start | bytes 1572872 | tf_op jit(solution)/shard_map/ppermute | solution.py:573
  55.4 1.9 %split_first.4 = (bf16[640,512]{1,0:T(8,128)(2,1)S(1)}, bf16[640,512]{1,0:T(8,128)(2,1)}, f32[8,128]{1,0:T(8,128)S(1)}, bf16[1280,512]{1,0:T(8,128)(2,1)S(1)}) custom-call(s32[1]{0:T(128)} %bitcast.6.bit_ref.refs_0_, bf16[1280,512]{1,0:T(8,128)(2,1)S(1)} %bitcast.35, ...), custom_call_target="tpu_custom_call", output_to_operand_aliasing={{3}: (1, {})} | custom-call | flops 68719476736 | bytes 1024 | tf_op jit(solution)/shard_map/split_first/pallas_call | solution.py:483
  58.9 7.6 %back.1 = (bf16[1536,256]{1,0:T(8,128)(2,1)S(1)}, bf16[1536,256]{1,0:T(8,128)(2,1)}, bf16[32,512]{1,0:T(8,128)(2,1)}) custom-call(s32[1]{0:T(128)} %bitcast.sec_ref.refs_1_, s32[3]{0:T(128)S(1)} %copy-done.5, s32[3,4]{1,0:T(4,128)S(1)} %copy-done.3, bf16[1536,1024]{1,0:T(8,128)(2,1)S(1)} %copy-done.9, bf16[1536,1024]{1,0:T(8,128)(2,1)S(1)} %copy-done.9, ...), custom_call_target="tpu_custom_call" | custom-call | flops 68719476736 | bytes 1024 | tf_op jit(solution)/shard_map/back/pallas_call | solution.py:934
  67.4 1.7 %split_first.5 = (bf16[768,512]{1,0:T(8,128)(2,1)S(1)}, bf16[768,512]{1,0:T(8,128)(2,1)S(1)}, f32[8,128]{1,0:T(8,128)S(1)}, bf16[1536,512]{1,0:T(8,128)(2,1)S(1)}) custom-call(s32[1]{0:T(128)} %bitcast.6.bit_ref.refs_0_, bf16[1536,512]{1,0:T(8,128)(2,1)S(1)} %bitcast.34, ...), custom_call_target="tpu_custom_call", output_to_operand_aliasing={{3}: (1, {})} | custom-call | flops 68719476736 | bytes 1024 | tf_op jit(solution)/shard_map/split_first/pallas_call | solution.py:483
  70.8 3.1 %join.2 = (bf16[3072,256]{1,0:T(8,128)(2,1)}, bf16[3072,256]{1,0:T(8,128)(2,1)}, f32[8,128]{1,0:T(8,128)S(1)}) custom-call(s32[1]{0:T(128)} %bitcast.sec_ref.refs_1_, bf16[1536,256]{1,0:T(8,128)(2,1)S(1)} %copy-done, bf16[1536,256]{1,0:T(8,128)(2,1)} %collective-permute-done.refs_1_, bf16[1536,256]{1,0:T(8,128)(2,1)S(1)} %copy-done.1, ...), custom_call_target="tpu_custom_call" | custom-call | flops 1024 | bytes 1024 | tf_op jit(solution)/shard_map/join/pallas_call | solution.py:535
  75.0 2.3 %collective-permute-start.14 = (bf16[256,512]{1,0:T(8,128)(2,1)S(1)}, bf16[256,512]{1,0:T(8,128)(2,1)S(1)}, u32[]{:S(2)}, u32[]{:S(2)}) collective-permute-start(bf16[256,512]{1,0:T(8,128)(2,1)S(1)} %get-tuple-element.132), channel_id=1, source_target_pairs={{0,8},{1,9},{2,10},{3,11},{4,12},{5,13},{6,14},{7,15},{8,0},{9,1},... | collective-permute-start | bytes 786440 | tf_op jit(solution)/shard_map/ppermute | solution.py:573
  78.6 1.6 collective-permute-start.13
  80.1 1.9 %collective-permute-done.7.refs_3_ = bf16[768,512]{1,0:T(8,128)(2,1)S(1)} collective-permute-done((bf16[768,512]{1,0:T(8,128)(2,1)S(1)}, bf16[768,512]{1,0:T(8,128)(2,1)S(1)}, u32[]{:S(2)}, u32[]{:S(2)}) %collective-permute-start.7) | collective-permute-done | bytes 786464 | tf_op jit(solution)/shard_map/ppermute | solution.py:573
  83.0 2.6 %collective-permute-start.11 = (bf16[384,512]{1,0:T(8,128)(2,1)S(1)}, bf16[384,512]{1,0:T(8,128)(2,1)S(1)}, u32[]{:S(2)}, u32[]{:S(2)}) collective-permute-start(bf16[384,512]{1,0:T(8,128)(2,1)S(1)} %get-tuple-element.129), channel_id=1, source_target_pairs={{0,2},{1,3},{2,0},{3,1},{4,6},{5,7},{6,4},{7,5},{8,10},{9,11},{10,... | collective-permute-start | bytes 1179656 | tf_op jit(solution)/shard_map/ppermute | solution.py:573
  85.6 3.7 %collective-permute-start.12 = (bf16[32,512]{1,0:T(8,128)(2,1)S(1)}, bf16[32,512]{1,0:T(8,128)(2,1)S(1)}, u32[]{:S(2)}, u32[]{:S(2)}) collective-permute-start(bf16[32,512]{1,0:T(8,128)(2,1)S(1)} %get-tuple-element.130.refs_4_), channel_id=1, source_target_pairs={{0,8},{1,9},{2,10},{3,11},{4,12},{5,13},{6,14},{7,15},{8,0},{9,1},... | collective-permute-start | bytes 98312 | tf_op jit(solution)/shard_map/ppermute | solution.py:995
  89.3 1.6 collective-permute-start.18
  95.0 2.1 %collective-permute-start.22 = (bf16[128,512]{1,0:T(8,128)(2,1)S(1)}, bf16[128,512]{1,0:T(8,128)(2,1)S(1)}, u32[]{:S(2)}, u32[]{:S(2)}) collective-permute-start(bf16[128,512]{1,0:T(8,128)(2,1)S(1)} %add_body.6.refs_3_.refs_1_), channel_id=1, source_target_pairs={{0,2},{1,3},{2,0},{3,1},{4,6},{5,7},{6,4},{7,5},{8,10},{9,11},{10,... | collective-permute-start | bytes 393224 | tf_op jit(solution)/shard_map/ppermute | solution.py:573
  97.1 1.9 %collective-permute-done.17.refs_2_ = bf16[160,512]{1,0:T(8,128)(2,1)S(1)} collective-permute-done((bf16[160,512]{1,0:T(8,128)(2,1)S(1)}, bf16[160,512]{1,0:T(8,128)(2,1)S(1)}, u32[]{:S(2)}, u32[]{:S(2)}) %collective-permute-start.17) | collective-permute-done | bytes 163872 | tf_op jit(solution)/shard_map/ppermute | solution.py:573
  99.4 5.5 %collective-permute-done.16.refs_5_ = bf16[48,512]{1,0:T(8,128)(2,1)S(1)} collective-permute-done((bf16[48,512]{1,0:T(8,128)(2,1)S(1)}, bf16[48,512]{1,0:T(8,128)(2,1)S(1)}, u32[]{:S(2)}, u32[]{:S(2)}) %collective-permute-start.16) | collective-permute-done | bytes 49184 | tf_op jit(solution)/shard_map/ppermute | solution.py:995
  107.1 6.8 %collective-permute-done.21.refs_2_ = bf16[160,512]{1,0:T(8,128)(2,1)S(1)} collective-permute-done((bf16[160,512]{1,0:T(8,128)(2,1)S(1)}, bf16[160,512]{1,0:T(8,128)(2,1)S(1)}, u32[]{:S(2)}, u32[]{:S(2)}) %collective-permute-start.21) | collective-permute-done | bytes 163872 | tf_op jit(solution)/shard_map/ppermute | solution.py:573
  114.1 4.1 %collective-permute-done.19.refs_3_ = bf16[192,512]{1,0:T(8,128)(2,1)S(1)} collective-permute-done((bf16[192,512]{1,0:T(8,128)(2,1)S(1)}, bf16[192,512]{1,0:T(8,128)(2,1)S(1)}, u32[]{:S(2)}, u32[]{:S(2)}) %collective-permute-start.19) | collective-permute-done | bytes 196640 | tf_op jit(solution)/shard_map/ppermute | solution.py:573
  118.4 2.0 %collective-permute-start.24 = (bf16[144,512]{1,0:T(8,128)(2,1)S(1)}, bf16[144,512]{1,0:T(8,128)(2,1)S(1)}, u32[]{:S(2)}, u32[]{:S(2)}) collective-permute-start(bf16[144,512]{1,0:T(8,128)(2,1)S(1)} %get-tuple-element.143.refs_4_), channel_id=1, source_target_pairs={{0,1},{1,0},{2,3},{3,2},{4,5},{5,4},{6,7},{7,6},{8,9},{9,8},{10,11... | collective-permute-start | bytes 442376 | tf_op jit(solution)/shard_map/ppermute | solution.py:995
  120.4 2.3 %collective-permute-start.29 = (bf16[256,512]{1,0:T(8,128)(2,1)S(1)}, bf16[256,512]{1,0:T(8,128)(2,1)S(1)}, u32[]{:S(2)}, u32[]{:S(2)}) collective-permute-start(bf16[256,512]{1,0:T(8,128)(2,1)S(1)} %merge_body.6.refs_3_.refs_1_), channel_id=1, source_target_pairs={{0,8},{1,9},{2,10},{3,11},{4,12},{5,13},{6,14},{7,15},{8,0},{9,1},... | collective-permute-start | bytes 786440 | tf_op jit(solution)/shard_map/ppermute | solution.py:573
  122.9 2.4 %collective-permute-done.24.refs_5_ = bf16[144,512]{1,0:T(8,128)(2,1)S(1)} collective-permute-done((bf16[144,512]{1,0:T(8,128)(2,1)S(1)}, bf16[144,512]{1,0:T(8,128)(2,1)S(1)}, u32[]{:S(2)}, u32[]{:S(2)}) %collective-permute-start.24) | collective-permute-done | bytes 147488 | tf_op jit(solution)/shard_map/ppermute | solution.py:995
  126.2 4.4 %collective-permute-done.29.refs_2_ = bf16[256,512]{1,0:T(8,128)(2,1)S(1)} collective-permute-done((bf16[256,512]{1,0:T(8,128)(2,1)S(1)}, bf16[256,512]{1,0:T(8,128)(2,1)S(1)}, u32[]{:S(2)}, u32[]{:S(2)}) %collective-permute-start.29) | collective-permute-done | bytes 262176 | tf_op jit(solution)/shard_map/ppermute | solution.py:573
  132.0 2.1 %collective-permute-done.27.refs_2_ = bf16[384,512]{1,0:T(8,128)(2,1)S(1)} collective-permute-done((bf16[384,512]{1,0:T(8,128)(2,1)S(1)}, bf16[384,512]{1,0:T(8,128)(2,1)S(1)}, u32[]{:S(2)}, u32[]{:S(2)}) %collective-permute-start.27) | collective-permute-done | bytes 393248 | tf_op jit(solution)/shard_map/ppermute | solution.py:573
  134.1 1.6 collective-permute-start.32
  136.4 2.3 %step_grad.1 = (f32[512,512]{1,0:T(8,128)}, f32[1,1024]{1,0:T(1,128)}, f32[1,1024]{1,0:T(1,128)}, f32[1,1024]{1,0:T(1,128)}, f32[3,128]{1,0:T(4,128)S(1)}, /*index=5*/f32[8,128]{1,0:T(8,128)S(1)}) custom-call(bf16[272,512]{1,0:T(8,128)(2,1)S(1)} %get-tuple-element.144.rows_ref, bf16[768,512]{1,0:T(8,128)(2,1)S(1)} %merge_body.11.after_ref.p0), custom_call_target="tpu_custom_call" | custom-call | flops 68719476736 | bytes 1024 | tf_op jit(solution)/shard_map/step_grad/pallas_call | solution.py:1002
  138.7 2.3 %join.3 = (bf16[3072,256]{1,0:T(8,128)(2,1)}, f32[8,128]{1,0:T(8,128)S(1)}) custom-call(s32[1]{0:T(128)} %bitcast.sec_ref.refs_1_, bf16[1536,256]{1,0:T(8,128)(2,1)S(1)} %get-tuple-element.117.refs_0_, bf16[1536,256]{1,0:T(8,128)(2,1)} %collective-permute-done.6.refs_1_, f32[8,128]{1,0:T(8,128)S(1)} %get-tuple-element.146.refs_2_), custom_call_target="tpu_custom_call" | custom-call | flops 1024 | bytes 1024 | tf_op jit(solution)/shard_map/join/pallas_call | solution.py:535
  140.9 2.5 %place.6 = (f32[512,1024]{1,0:T(8,128)}, f32[512,512]{1,0:T(8,128)}, f32[512,512]{1,0:T(8,128)}, f32[512,512]{1,0:T(8,128)}, f32[8,128]{1,0:T(8,128)S(1)}) custom-call(s32[4]{0:T(128)S(1)} %pad_add_fusion.1.runs, bf16[512,512]{1,0:T(8,128)(2,1)} %merge_body.9.refs_3_.p0, bf16[512,512]{1,0:T(8,128)(2,1)S(1)} %collective-permute-done.35.p1, ...), custom_call_target="tpu_custom_call" | custom-call | flops 1024 | bytes 1024 | tf_op jit(solution)/shard_map/place/pallas_call | solution.py:681
  143.4 2.1 %place.7 = (f32[512,1024]{1,0:T(8,128)}, f32[512,1024]{1,0:T(8,128)}, f32[512,1024]{1,0:T(8,128)}, f32[8,128]{1,0:T(8,128)S(1)}) custom-call(s32[4]{0:T(128)S(1)} %pad_add_fusion.runs, bf16[640,512]{1,0:T(8,128)(2,1)S(1)} %merge_body.10.refs_3_.p0, bf16[640,512]{1,0:T(8,128)(2,1)S(1)} %collective-permute-done.34.p1, ...), custom_call_target="tpu_custom_call", output_to_operand_aliasing={{0}: (4, {})} | custom-call | flops 1024 | bytes 1024 | tf_op jit(solution)/shard_map/place/pallas_call | solution.py:681
  145.6 2.3 %place.8 = (f32[1536,1024]{1,0:T(8,128)}, f32[8,128]{1,0:T(8,128)S(1)}) custom-call(s32[4]{0:T(128)S(1)} %pad_add_fusion.runs, bf16[768,512]{1,0:T(8,128)(2,1)S(1)} %merge_body.11.after_ref.p0, bf16[768,512]{1,0:T(8,128)(2,1)S(1)} %collective-permute-done.33.p1, f32[8,128]{1,0:T(8,128)S(1)} %get-tuple-element.152.after_ref), custom_call_target="tpu_custom_call" | custom-call | flops 1024 | bytes 1024 | tf_op jit(solution)/shard_map/place/pallas_call | solution.py:681
  150.2 2.1 %place.9 = (f32[512,1024]{1,0:T(8,128)}, f32[512,1024]{1,0:T(8,128)}, f32[512,1024]{1,0:T(8,128)}, f32[8,128]{1,0:T(8,128)S(1)}) custom-call(s32[4]{0:T(128)S(1)} %pad_add_fusion.runs, bf16[640,512]{1,0:T(8,128)(2,1)S(1)} %then.3.after_ref.p0, ...), custom_call_target="tpu_custom_call", output_to_operand_aliasing={{0}: (4, {}), {1}: (5, {}), {2}: (6, {})} | custom-call | flops 1024 | bytes 1024 | tf_op jit(solution)/shard_map/place/pallas_call | solution.py:681
  152.3 2.0 %place.10 = (f32[512,1024]{1,0:T(8,128)}, f32[512,512]{1,0:T(8,128)}, f32[512,512]{1,0:T(8,128)}, f32[512,512]{1,0:T(8,128)}, f32[8,128]{1,0:T(8,128)S(1)}) custom-call(s32[4]{0:T(128)S(1)} %pad_add_fusion.1.runs, bf16[512,512]{1,0:T(8,128)(2,1)S(1)} %then.4.after_ref.p0, ...), custom_call_target="tpu_custom_call", output_to_operand_aliasing={{0}: (4, {}), {1}: (5, {}), {2}: (6, {}), {3}: (7, {})} | custom-call | flops 1024 | bytes 1024 | tf_op jit(solution)/shard_map/place/pallas_call | solution.py:681
  156.7 2.9 %place.11 = (f32[1536,1024]{1,0:T(8,128)}, f32[8,128]{1,0:T(8,128)}) custom-call(s32[4]{0:T(128)S(1)} %pad_add_fusion.runs, bf16[768,512]{1,0:T(8,128)(2,1)S(1)} %then.5.p0.after_ref, bf16[768,512]{1,0:T(8,128)(2,1)S(1)} %collective-permute-done.38.p1, bf16[768,512]{1,0:T(8,128)(2,1)S(1)} %then.5.p0.after_ref, ...), custom_call_target="tpu_custom_call", output_to_operand_aliasing={{0}: (4, {})} | custom-call | flops 1024 | bytes 1024 | tf_op jit(solution)/shard_map/place/pallas_call | solution.py:681
  (111 shorter events, 26.0 us)
Async XLA Ops:
  39.4 10.9 %collective-permute-start.5 = (bf16[1024,512]{1,0:T(8,128)(2,1)}, bf16[1024,512]{1,0:T(8,128)(2,1)S(1)}, u32[]{:S(2)}, u32[]{:S(2)}) collective-permute-start(bf16[1024,512]{1,0:T(8,128)(2,1)} %bitcast.40), channel_id=1, source_target_pairs={{0,16},{16,0},{1,17},{17,1},{2,18},{18,2},{3,19},{19,3},{4,20},{20... | collective-permute-start | bytes 3145736 | tf_op jit(solution)/shard_map/ppermute | solution.py:548
  40.0 12.3 %collective-permute-start.4 = (bf16[1280,512]{1,0:T(8,128)(2,1)}, bf16[1280,512]{1,0:T(8,128)(2,1)S(1)}, u32[]{:S(2)}, u32[]{:S(2)}) collective-permute-start(bf16[1280,512]{1,0:T(8,128)(2,1)} %bitcast.39), channel_id=1, source_target_pairs={{0,16},{16,0},{1,17},{17,1},{2,18},{18,2},{3,19},{19,3},{4,20},{20... | collective-permute-start | bytes 3932168 | tf_op jit(solution)/shard_map/ppermute | solution.py:548
  40.0 17.2 %collective-permute-start.3 = (bf16[32,1024]{1,0:T(8,128)(2,1)}, bf16[32,1024]{1,0:T(8,128)(2,1)}, u32[]{:S(2)}, u32[]{:S(2)}) collective-permute-start(bf16[32,1024]{1,0:T(8,128)(2,1)} %get-tuple-element.103), channel_id=1, source_target_pairs={{0,16},{16,0},{1,17},{17,1},{2,18},{18,2},{3,19},{19,3},{4,20},{20... | collective-permute-start | bytes 196616 | tf_op jit(solution)/shard_map/ppermute | solution.py:548
  49.7 16.8 %collective-permute-start.2 = (bf16[1536,512]{1,0:T(8,128)(2,1)}, bf16[1536,512]{1,0:T(8,128)(2,1)}, u32[]{:S(2)}, u32[]{:S(2)}) collective-permute-start(bf16[1536,512]{1,0:T(8,128)(2,1)} %bitcast.38), channel_id=1, source_target_pairs={{0,16},{16,0},{1,17},{17,1},{2,18},{18,2},{3,19},{19,3},{4,20},{20... | collective-permute-start | bytes 4718600 | tf_op jit(solution)/shard_map/ppermute | solution.py:548
  49.7 19.4 %collective-permute-start = (bf16[1536,256]{1,0:T(8,128)(2,1)}, bf16[1536,256]{1,0:T(8,128)(2,1)}, u32[]{:S(2)}, u32[]{:S(2)}) collective-permute-start(bf16[1536,256]{1,0:T(8,128)(2,1)} %get-tuple-element.96), channel_id=1, source_target_pairs={{0,16},{16,0},{1,17},{17,1},{2,18},{18,2},{3,19},{19,3},{4,20},{20... | collective-permute-start | bytes 2359304 | tf_op jit(solution)/shard_map/ppermute | solution.py:548
  50.3 18.9 %collective-permute-start.1 = (bf16[1536,256]{1,0:T(8,128)(2,1)}, bf16[1536,256]{1,0:T(8,128)(2,1)}, u32[]{:S(2)}, u32[]{:S(2)}) collective-permute-start(bf16[1536,256]{1,0:T(8,128)(2,1)} %get-tuple-element.98), channel_id=1, source_target_pairs={{0,16},{16,0},{1,17},{17,1},{2,18},{18,2},{3,19},{19,3},{4,20},{20... | collective-permute-start | bytes 2359304 | tf_op jit(solution)/shard_map/ppermute | solution.py:548
  52.2 21.6 %collective-permute-start.10 = (bf16[512,512]{1,0:T(8,128)(2,1)}, bf16[512,512]{1,0:T(8,128)(2,1)}, u32[]{:S(2)}, u32[]{:S(2)}) collective-permute-start(bf16[512,512]{1,0:T(8,128)(2,1)} %get-tuple-element.124), channel_id=1, source_target_pairs={{0,4},{1,5},{2,6},{3,7},{4,0},{5,1},{6,2},{7,3},{8,12},{9,13},{10,... | collective-permute-start | bytes 1572872 | tf_op jit(solution)/shard_map/ppermute | solution.py:573
  57.2 20.1 %collective-permute-start.9 = (bf16[640,512]{1,0:T(8,128)(2,1)}, bf16[640,512]{1,0:T(8,128)(2,1)}, u32[]{:S(2)}, u32[]{:S(2)}) collective-permute-start(bf16[640,512]{1,0:T(8,128)(2,1)} %get-tuple-element.122), channel_id=1, source_target_pairs={{0,1},{1,0},{2,3},{3,2},{4,5},{5,4},{6,7},{7,6},{8,9},{9,8},{10,11... | collective-permute-start | bytes 1966088 | tf_op jit(solution)/shard_map/ppermute | solution.py:573
  66.5 13.6 %collective-permute-start.8 = (bf16[32,512]{1,0:T(8,128)(2,1)}, bf16[32,512]{1,0:T(8,128)(2,1)}, u32[]{:S(2)}, u32[]{:S(2)}) collective-permute-start(bf16[32,512]{1,0:T(8,128)(2,1)} %get-tuple-element.113.after_ref.refs_4_), channel_id=1, source_target_pairs={{0,16},{16,0},{1,17},{17,1},{2,18},{18,2},{3,19},{19,3},{4,20},{20... | collective-permute-start | bytes 98312 | tf_op jit(solution)/shard_map/ppermute | solution.py:548
  69.1 66.7 %collective-permute-start.6 = (bf16[1536,256]{1,0:T(8,128)(2,1)}, bf16[1536,256]{1,0:T(8,128)(2,1)}, u32[]{:S(2)}, u32[]{:S(2)}) collective-permute-start(bf16[1536,256]{1,0:T(8,128)(2,1)} %get-tuple-element.118), channel_id=1, source_target_pairs={{0,16},{16,0},{1,17},{17,1},{2,18},{18,2},{3,19},{19,3},{4,20},{20... | collective-permute-start | bytes 2359304 | tf_op jit(solution)/shard_map/ppermute | solution.py:548
  69.3 12.8 %collective-permute-start.7 = (bf16[768,512]{1,0:T(8,128)(2,1)S(1)}, bf16[768,512]{1,0:T(8,128)(2,1)S(1)}, u32[]{:S(2)}, u32[]{:S(2)}) collective-permute-start(bf16[768,512]{1,0:T(8,128)(2,1)S(1)} %get-tuple-element.120), channel_id=1, source_target_pairs={{0,1},{1,0},{2,3},{3,2},{4,5},{5,4},{6,7},{7,6},{8,9},{9,8},{10,11... | collective-permute-start | bytes 2359304 | tf_op jit(solution)/shard_map/ppermute | solution.py:573
  75.0 14.2 %collective-permute-start.14 = (bf16[256,512]{1,0:T(8,128)(2,1)S(1)}, bf16[256,512]{1,0:T(8,128)(2,1)S(1)}, u32[]{:S(2)}, u32[]{:S(2)}) collective-permute-start(bf16[256,512]{1,0:T(8,128)(2,1)S(1)} %get-tuple-element.132), channel_id=1, source_target_pairs={{0,8},{1,9},{2,10},{3,11},{4,12},{5,13},{6,14},{7,15},{8,0},{9,1},... | collective-permute-start | bytes 786440 | tf_op jit(solution)/shard_map/ppermute | solution.py:573
  78.6 12.3 %collective-permute-start.13 = (bf16[320,512]{1,0:T(8,128)(2,1)S(1)}, bf16[320,512]{1,0:T(8,128)(2,1)S(1)}, u32[]{:S(2)}, u32[]{:S(2)}) collective-permute-start(bf16[320,512]{1,0:T(8,128)(2,1)S(1)} %get-tuple-element.131), channel_id=1, source_target_pairs={{0,2},{1,3},{2,0},{3,1},{4,6},{5,7},{6,4},{7,5},{8,10},{9,11},{10,... | collective-permute-start | bytes 983048 | tf_op jit(solution)/shard_map/ppermute | solution.py:573
  83.0 9.8 %collective-permute-start.11 = (bf16[384,512]{1,0:T(8,128)(2,1)S(1)}, bf16[384,512]{1,0:T(8,128)(2,1)S(1)}, u32[]{:S(2)}, u32[]{:S(2)}) collective-permute-start(bf16[384,512]{1,0:T(8,128)(2,1)S(1)} %get-tuple-element.129), channel_id=1, source_target_pairs={{0,2},{1,3},{2,0},{3,1},{4,6},{5,7},{6,4},{7,5},{8,10},{9,11},{10,... | collective-permute-start | bytes 1179656 | tf_op jit(solution)/shard_map/ppermute | solution.py:573
  91.0 8.0 %collective-permute-start.17 = (bf16[160,512]{1,0:T(8,128)(2,1)S(1)}, bf16[160,512]{1,0:T(8,128)(2,1)S(1)}, u32[]{:S(2)}, u32[]{:S(2)}) collective-permute-start(bf16[160,512]{1,0:T(8,128)(2,1)S(1)} %get-tuple-element.138), channel_id=1, source_target_pairs={{0,4},{1,5},{2,6},{3,7},{4,0},{5,1},{6,2},{7,3},{8,12},{9,13},{10,... | collective-permute-start | bytes 491528 | tf_op jit(solution)/shard_map/ppermute | solution.py:573
  92.9 12.0 %collective-permute-start.15 = (bf16[192,512]{1,0:T(8,128)(2,1)S(1)}, bf16[192,512]{1,0:T(8,128)(2,1)S(1)}, u32[]{:S(2)}, u32[]{:S(2)}) collective-permute-start(bf16[192,512]{1,0:T(8,128)(2,1)S(1)} %get-tuple-element.136), channel_id=1, source_target_pairs={{0,4},{1,5},{2,6},{3,7},{4,0},{5,1},{6,2},{7,3},{8,12},{9,13},{10,... | collective-permute-start | bytes 589832 | tf_op jit(solution)/shard_map/ppermute | solution.py:573
  94.2 10.7 %collective-permute-start.16 = (bf16[48,512]{1,0:T(8,128)(2,1)S(1)}, bf16[48,512]{1,0:T(8,128)(2,1)S(1)}, u32[]{:S(2)}, u32[]{:S(2)}) collective-permute-start(bf16[48,512]{1,0:T(8,128)(2,1)S(1)} %get-tuple-element.137.refs_4_), channel_id=1, source_target_pairs={{0,4},{1,5},{2,6},{3,7},{4,0},{5,1},{6,2},{7,3},{8,12},{9,13},{10,... | collective-permute-start | bytes 147464 | tf_op jit(solution)/shard_map/ppermute | solution.py:995
  95.0 11.2 %collective-permute-start.22 = (bf16[128,512]{1,0:T(8,128)(2,1)S(1)}, bf16[128,512]{1,0:T(8,128)(2,1)S(1)}, u32[]{:S(2)}, u32[]{:S(2)}) collective-permute-start(bf16[128,512]{1,0:T(8,128)(2,1)S(1)} %add_body.6.refs_3_.refs_1_), channel_id=1, source_target_pairs={{0,2},{1,3},{2,0},{3,1},{4,6},{5,7},{6,4},{7,5},{8,10},{9,11},{10,... | collective-permute-start | bytes 393224 | tf_op jit(solution)/shard_map/ppermute | solution.py:573
  99.0 15.0 %collective-permute-start.21 = (bf16[160,512]{1,0:T(8,128)(2,1)S(1)}, bf16[160,512]{1,0:T(8,128)(2,1)S(1)}, u32[]{:S(2)}, u32[]{:S(2)}) collective-permute-start(bf16[160,512]{1,0:T(8,128)(2,1)S(1)} %add_body.7.refs_6_.refs_1_), channel_id=1, source_target_pairs={{0,8},{1,9},{2,10},{3,11},{4,12},{5,13},{6,14},{7,15},{8,0},{9,1},... | collective-permute-start | bytes 491528 | tf_op jit(solution)/shard_map/ppermute | solution.py:573
  105.0 13.3 %collective-permute-start.19 = (bf16[192,512]{1,0:T(8,128)(2,1)S(1)}, bf16[192,512]{1,0:T(8,128)(2,1)S(1)}, u32[]{:S(2)}, u32[]{:S(2)}) collective-permute-start(bf16[192,512]{1,0:T(8,128)(2,1)S(1)} %get-tuple-element.140.refs_3_.refs_2_), channel_id=1, source_target_pairs={{0,8},{1,9},{2,10},{3,11},{4,12},{5,13},{6,14},{7,15},{8,0},{9,1},... | collective-permute-start | bytes 589832 | tf_op jit(solution)/shard_map/ppermute | solution.py:573
  105.0 9.1 %collective-permute-start.20 = (bf16[80,512]{1,0:T(8,128)(2,1)S(1)}, bf16[80,512]{1,0:T(8,128)(2,1)S(1)}, u32[]{:S(2)}, u32[]{:S(2)}) collective-permute-start(bf16[80,512]{1,0:T(8,128)(2,1)S(1)} %get-tuple-element.141.refs_4_), channel_id=1, source_target_pairs={{0,2},{1,3},{2,0},{3,1},{4,6},{5,7},{6,4},{7,5},{8,10},{9,11},{10,... | collective-permute-start | bytes 245768 | tf_op jit(solution)/shard_map/ppermute | solution.py:995
  106.2 14.2 %collective-permute-start.26 = (bf16[128,512]{1,0:T(8,128)(2,1)S(1)}, bf16[128,512]{1,0:T(8,128)(2,1)S(1)}, u32[]{:S(2)}, u32[]{:S(2)}) collective-permute-start(bf16[128,512]{1,0:T(8,128)(2,1)S(1)} %add_body.9.refs_3_.refs_1_), channel_id=1, source_target_pairs={{0,1},{1,0},{2,3},{3,2},{4,5},{5,4},{6,7},{7,6},{8,9},{9,8},{10,11... | collective-permute-start | bytes 393224 | tf_op jit(solution)/shard_map/ppermute | solution.py:573
  114.0 8.7 %collective-permute-start.25 = (bf16[160,512]{1,0:T(8,128)(2,1)S(1)}, bf16[160,512]{1,0:T(8,128)(2,1)S(1)}, u32[]{:S(2)}, u32[]{:S(2)}) collective-permute-start(bf16[160,512]{1,0:T(8,128)(2,1)S(1)} %add_body.10.refs_6_.refs_1_), channel_id=1, source_target_pairs={{0,4},{1,5},{2,6},{3,7},{4,0},{5,1},{6,2},{7,3},{8,12},{9,13},{10,... | collective-permute-start | bytes 491528 | tf_op jit(solution)/shard_map/ppermute | solution.py:573
  118.3 6.9 %collective-permute-start.23 = (bf16[192,512]{1,0:T(8,128)(2,1)S(1)}, bf16[192,512]{1,0:T(8,128)(2,1)S(1)}, u32[]{:S(2)}, u32[]{:S(2)}) collective-permute-start(bf16[192,512]{1,0:T(8,128)(2,1)S(1)} %get-tuple-element.142.refs_3_.refs_2_), channel_id=1, source_target_pairs={{0,4},{1,5},{2,6},{3,7},{4,0},{5,1},{6,2},{7,3},{8,12},{9,13},{10,... | collective-permute-start | bytes 589832 | tf_op jit(solution)/shard_map/ppermute | solution.py:573
  120.4 10.1 %collective-permute-start.29 = (bf16[256,512]{1,0:T(8,128)(2,1)S(1)}, bf16[256,512]{1,0:T(8,128)(2,1)S(1)}, u32[]{:S(2)}, u32[]{:S(2)}) collective-permute-start(bf16[256,512]{1,0:T(8,128)(2,1)S(1)} %merge_body.6.refs_3_.refs_1_), channel_id=1, source_target_pairs={{0,8},{1,9},{2,10},{3,11},{4,12},{5,13},{6,14},{7,15},{8,0},{9,1},... | collective-permute-start | bytes 786440 | tf_op jit(solution)/shard_map/ppermute | solution.py:573
  122.8 8.6 %collective-permute-start.28 = (bf16[320,512]{1,0:T(8,128)(2,1)S(1)}, bf16[320,512]{1,0:T(8,128)(2,1)S(1)}, u32[]{:S(2)}, u32[]{:S(2)}) collective-permute-start(bf16[320,512]{1,0:T(8,128)(2,1)S(1)} %merge_body.7.refs_6_.refs_1_), channel_id=1, source_target_pairs={{0,2},{1,3},{2,0},{3,1},{4,6},{5,7},{6,4},{7,5},{8,10},{9,11},{10,... | collective-permute-start | bytes 983048 | tf_op jit(solution)/shard_map/ppermute | solution.py:573
  125.3 8.8 %collective-permute-start.27 = (bf16[384,512]{1,0:T(8,128)(2,1)S(1)}, bf16[384,512]{1,0:T(8,128)(2,1)S(1)}, u32[]{:S(2)}, u32[]{:S(2)}) collective-permute-start(bf16[384,512]{1,0:T(8,128)(2,1)S(1)} %get-tuple-element.145.refs_3_.refs_1_), channel_id=1, source_target_pairs={{0,2},{1,3},{2,0},{3,1},{4,6},{5,7},{6,4},{7,5},{8,10},{9,11},{10,... | collective-permute-start | bytes 1179656 | tf_op jit(solution)/shard_map/ppermute | solution.py:573
  131.4 16.7 %collective-permute-start.31 = (bf16[512,512]{1,0:T(8,128)(2,1)}, bf16[512,512]{1,0:T(8,128)(2,1)}, u32[]{:S(2)}, u32[]{:S(2)}) collective-permute-start(bf16[512,512]{1,0:T(8,128)(2,1)} %merge_body.9.refs_3_.p0), channel_id=1, source_target_pairs={{0,4},{1,5},{2,6},{3,7},{4,0},{5,1},{6,2},{7,3},{8,12},{9,13},{10,... | collective-permute-start | bytes 1572872 | tf_op jit(solution)/shard_map/ppermute | solution.py:573
  131.5 11.9 %collective-permute-start.34 = (bf16[640,512]{1,0:T(8,128)(2,1)S(1)}, bf16[640,512]{1,0:T(8,128)(2,1)S(1)}, u32[]{:S(2)}, u32[]{:S(2)}) collective-permute-start(bf16[640,512]{1,0:T(8,128)(2,1)S(1)} %merge_body.10.refs_3_.p0), channel_id=1, source_target_pairs={{0,16},{16,0},{1,17},{17,1},{2,18},{18,2},{3,19},{19,3},{4,20},{20... | collective-permute-start | bytes 1966088 | tf_op jit(solution)/shard_map/ppermute | solution.py:548
  134.1 13.8 %collective-permute-start.32 = (bf16[640,512]{1,0:T(8,128)(2,1)S(1)}, bf16[640,512]{1,0:T(8,128)(2,1)S(1)}, u32[]{:S(2)}, u32[]{:S(2)}) collective-permute-start(bf16[640,512]{1,0:T(8,128)(2,1)S(1)} %merge_body.10.refs_3_.p0), channel_id=1, source_target_pairs={{0,1},{1,0},{2,3},{3,2},{4,5},{5,4},{6,7},{7,6},{8,9},{9,8},{10,11... | collective-permute-start | bytes 1966088 | tf_op jit(solution)/shard_map/ppermute | solution.py:573
  135.8 9.8 %collective-permute-start.33 = (bf16[768,512]{1,0:T(8,128)(2,1)S(1)}, bf16[768,512]{1,0:T(8,128)(2,1)S(1)}, u32[]{:S(2)}, u32[]{:S(2)}) collective-permute-start(bf16[768,512]{1,0:T(8,128)(2,1)S(1)} %merge_body.11.after_ref.p0), channel_id=1, source_target_pairs={{0,16},{16,0},{1,17},{17,1},{2,18},{18,2},{3,19},{19,3},{4,20},{20... | collective-permute-start | bytes 2359304 | tf_op jit(solution)/shard_map/ppermute | solution.py:548
  135.9 18.4 %collective-permute-start.30 = (bf16[768,512]{1,0:T(8,128)(2,1)S(1)}, bf16[768,512]{1,0:T(8,128)(2,1)S(1)}, u32[]{:S(2)}, u32[]{:S(2)}) collective-permute-start(bf16[768,512]{1,0:T(8,128)(2,1)S(1)} %merge_body.11.after_ref.p0), channel_id=1, source_target_pairs={{0,1},{1,0},{2,3},{3,2},{4,5},{5,4},{6,7},{7,6},{8,9},{9,8},{10,11... | collective-permute-start | bytes 2359304 | tf_op jit(solution)/shard_map/ppermute | solution.py:573
  (20 other events, 85.8 us)

commit v9 on v8

--- a/solution.py
+++ b/solution.py
@@ -975,13 +975,18 @@
     in_got = swap(in_give)
 
     (after,) = batch_b.turn(rows_now)
-    block_out, skip_out, after = join(
-        sec, after, (block_keep, block_got), (skip_keep, skip_got)
-    )
     rows_got, rows_bit, gathered = swap(rows_now), sec, 0
     batches = {"a": batch_a, "b": batch_b, "c": batch_c}
-    order = "acb" * (batch_a.turns - 1)
+    order = "J" + "acb" * 3 + "K" + "acb" * (batch_a.turns - 4)
     for name in order:
+        if name == "J":
+            block_out, skip_out, after = join(
+                sec, after, (block_keep, block_got), (skip_keep, skip_got)
+            )
+            continue
+        if name == "K":
+            in_grad, after = join(sec, after, (in_keep, in_got))
+            continue
         turner = batches[name]
         if name == "b" and gathered <= sums.levels:
             n = rows_now.shape[0]
@@ -1009,7 +1014,6 @@
         cost_estimate=LARGE,
         name="step_grad",
     )(rows_now, after)
-    in_grad, mark = join(sec, mark, (in_keep, in_got))
 
     def pairs(k, count, base=0):
         return [(k, base + i * width, col) for i in range(count) for col in (0, width)]

time: 160 us -> 157 us (0.981)
  waiting for transfers between devices: 32.8 us -> 29.7 us
    ppermute x21, waiting for transfers between devices: 21.8 us -> 19.4 us  [send(): return lax.ppermute(x, ('section', 'dp'), route)]
where the time goes in v9:
time: 157 us
  Pallas kernels  88 us (56%)
  starting transfers between devices  36.3 us (23%)
  waiting for transfers between devices  29.7 us (19%)
    pallas_call x1, Pallas kernels, on_device(): pl.pallas_call(functools.partial(forward_kernel, (tile, slots, nq, subs,...  38.8 us
    ppermute x21, starting transfers between devices, send(): return lax.ppermute(x, ('section', 'dp'), route)  24.8 us
    ppermute x21, waiting for transfers between devices, send(): return lax.ppermute(x, ('section', 'dp'), route)  19.4 us
    pallas_call x6, Pallas kernels, place(): pl.pallas_call(functools.partial(place_kernel, which, full, len(shapes)),...  14 us
    pallas_call x1, Pallas kernels, on_device(): pl.pallas_call(weight_kernel, grid_spec=pltpu.PrefetchScalarGridSpec(num_...  9.19 us
    ppermute x4, waiting for transfers between devices, on_device(): rows_got = lax.ppermute(rows_now, 'dp', route)  9.03 us
    pallas_call x1, Pallas kernels, on_device(): pl.pallas_call(functools.partial(back_kernel, (tile, slots, subs, tiles,...  7.63 us
    ppermute x4, starting transfers between devices, on_device(): rows_got = lax.ppermute(rows_now, 'dp', route)  7.54 us
  transfers between devices with their start and end apart: 39, of which 12 were waited for; matrix products, arithmetic and copies ran while one was open for 0% of the time, Pallas kernels for 29%

profile of v9, /device:TPU:0, one launch (start us, length us, event | category | flops | bytes accessed | tf_op | source)
XLA Modules:
  0.0 156.8 jit_solution(9198829640921566218)
XLA Ops:
  0.7 38.8 %forward.1 = (bf16[1536,1536]{1,0:T(8,128)(2,1)}, bf16[1536,1024]{1,0:T(8,128)(2,1)}, bf16[32,1024]{1,0:T(8,128)(2,1)}, bf16[1536,512]{1,0:T(8,128)(2,1)}, bf16[...) custom-call(s32[1]{0:T(128)} %bitcast.sec_ref.refs_1_, ...), custom_call_target="tpu_custom_call" | custom-call | flops 68719476736 | bytes 1024 | tf_op jit(solution)/shard_map/forward/pallas_call | solution.py:831
  40.5 9.2 %weights.1 = (bf16[6,256,512]{2,1,0:T(8,128)(2,1)}, bf16[6,256,512]{2,1,0:T(8,128)(2,1)}, f32[8,128]{1,0:T(8,128)}) custom-call(s32[1]{0:T(128)} %bitcast.sec_ref.refs_1_, bf16[1536,1536]{1,0:T(8,128)(2,1)} %get-tuple-element.99.left_ref, bf16[1536,1024]{1,0:T(8,128)(2,1)} %get-tuple-element.100.dpre_ref.prev_ref.next_ref), custom_call_target="tpu_custom_call" | custom-call | flops 68719476736 | bytes 1024 | tf_op jit(solution)/shard_map/weights/pallas_call | solution.py:914
  52.2 3.1 %collective-permute-start.10 = (bf16[512,512]{1,0:T(8,128)(2,1)}, bf16[512,512]{1,0:T(8,128)(2,1)}, u32[]{:S(2)}, u32[]{:S(2)}) collective-permute-start(bf16[512,512]{1,0:T(8,128)(2,1)} %get-tuple-element.124), channel_id=1, source_target_pairs={{0,4},{1,5},{2,6},{3,7},{4,0},{5,1},{6,2},{7,3},{8,12},{9,13},{10,... | collective-permute-start | bytes 1572872 | tf_op jit(solution)/shard_map/ppermute | solution.py:573
  55.4 1.9 %split_first.4 = (bf16[640,512]{1,0:T(8,128)(2,1)S(1)}, bf16[640,512]{1,0:T(8,128)(2,1)}, f32[8,128]{1,0:T(8,128)S(1)}, bf16[1280,512]{1,0:T(8,128)(2,1)S(1)}) custom-call(s32[1]{0:T(128)} %bitcast.6.bit_ref.refs_0_, bf16[1280,512]{1,0:T(8,128)(2,1)S(1)} %bitcast.35, ...), custom_call_target="tpu_custom_call", output_to_operand_aliasing={{3}: (1, {})} | custom-call | flops 68719476736 | bytes 1024 | tf_op jit(solution)/shard_map/split_first/pallas_call | solution.py:483
  58.9 7.6 %back.1 = (bf16[1536,256]{1,0:T(8,128)(2,1)S(1)}, bf16[1536,256]{1,0:T(8,128)(2,1)}, bf16[32,512]{1,0:T(8,128)(2,1)}) custom-call(s32[1]{0:T(128)} %bitcast.sec_ref.refs_1_, s32[3]{0:T(128)S(1)} %copy-done.5, s32[3,4]{1,0:T(4,128)S(1)} %copy-done.3, bf16[1536,1024]{1,0:T(8,128)(2,1)S(1)} %copy-done.9, bf16[1536,1024]{1,0:T(8,128)(2,1)S(1)} %copy-done.9, ...), custom_call_target="tpu_custom_call" | custom-call | flops 68719476736 | bytes 1024 | tf_op jit(solution)/shard_map/back/pallas_call | solution.py:934
  67.4 1.7 %split_first.5 = (bf16[768,512]{1,0:T(8,128)(2,1)S(1)}, bf16[768,512]{1,0:T(8,128)(2,1)S(1)}, f32[8,128]{1,0:T(8,128)S(1)}, bf16[1536,512]{1,0:T(8,128)(2,1)S(1)}) custom-call(s32[1]{0:T(128)} %bitcast.6.bit_ref.refs_0_, bf16[1536,512]{1,0:T(8,128)(2,1)S(1)} %bitcast.34, ...), custom_call_target="tpu_custom_call", output_to_operand_aliasing={{3}: (1, {})} | custom-call | flops 68719476736 | bytes 1024 | tf_op jit(solution)/shard_map/split_first/pallas_call | solution.py:483
  70.8 3.1 %join.2 = (bf16[3072,256]{1,0:T(8,128)(2,1)}, bf16[3072,256]{1,0:T(8,128)(2,1)}, f32[8,128]{1,0:T(8,128)S(1)}) custom-call(s32[1]{0:T(128)} %bitcast.sec_ref.refs_1_, bf16[1536,256]{1,0:T(8,128)(2,1)S(1)} %copy-done, bf16[1536,256]{1,0:T(8,128)(2,1)} %collective-permute-done.refs_1_, bf16[1536,256]{1,0:T(8,128)(2,1)S(1)} %copy-done.1, ...), custom_call_target="tpu_custom_call" | custom-call | flops 1024 | bytes 1024 | tf_op jit(solution)/shard_map/join/pallas_call | solution.py:535
  75.0 2.3 %collective-permute-start.14 = (bf16[256,512]{1,0:T(8,128)(2,1)S(1)}, bf16[256,512]{1,0:T(8,128)(2,1)S(1)}, u32[]{:S(2)}, u32[]{:S(2)}) collective-permute-start(bf16[256,512]{1,0:T(8,128)(2,1)S(1)} %get-tuple-element.132), channel_id=1, source_target_pairs={{0,8},{1,9},{2,10},{3,11},{4,12},{5,13},{6,14},{7,15},{8,0},{9,1},... | collective-permute-start | bytes 786440 | tf_op jit(solution)/shard_map/ppermute | solution.py:573
  78.6 1.6 %collective-permute-start.13 = (bf16[320,512]{1,0:T(8,128)(2,1)S(1)}, bf16[320,512]{1,0:T(8,128)(2,1)S(1)}, u32[]{:S(2)}, u32[]{:S(2)}) collective-permute-start(bf16[320,512]{1,0:T(8,128)(2,1)S(1)} %get-tuple-element.131), channel_id=1, source_target_pairs={{0,2},{1,3},{2,0},{3,1},{4,6},{5,7},{6,4},{7,5},{8,10},{9,11},{10,... | collective-permute-start | bytes 983048 | tf_op jit(solution)/shard_map/ppermute | solution.py:573
  80.1 1.9 %collective-permute-done.7.refs_3_ = bf16[768,512]{1,0:T(8,128)(2,1)S(1)} collective-permute-done((bf16[768,512]{1,0:T(8,128)(2,1)S(1)}, bf16[768,512]{1,0:T(8,128)(2,1)S(1)}, u32[]{:S(2)}, u32[]{:S(2)}) %collective-permute-start.7) | collective-permute-done | bytes 786464 | tf_op jit(solution)/shard_map/ppermute | solution.py:573
  83.0 2.6 %collective-permute-start.11 = (bf16[384,512]{1,0:T(8,128)(2,1)S(1)}, bf16[384,512]{1,0:T(8,128)(2,1)S(1)}, u32[]{:S(2)}, u32[]{:S(2)}) collective-permute-start(bf16[384,512]{1,0:T(8,128)(2,1)S(1)} %get-tuple-element.129), channel_id=1, source_target_pairs={{0,2},{1,3},{2,0},{3,1},{4,6},{5,7},{6,4},{7,5},{8,10},{9,11},{10,... | collective-permute-start | bytes 1179656 | tf_op jit(solution)/shard_map/ppermute | solution.py:573
  85.6 3.7 %collective-permute-start.12 = (bf16[32,512]{1,0:T(8,128)(2,1)S(1)}, bf16[32,512]{1,0:T(8,128)(2,1)S(1)}, u32[]{:S(2)}, u32[]{:S(2)}) collective-permute-start(bf16[32,512]{1,0:T(8,128)(2,1)S(1)} %get-tuple-element.130.refs_4_), channel_id=1, source_target_pairs={{0,8},{1,9},{2,10},{3,11},{4,12},{5,13},{6,14},{7,15},{8,0},{9,1},... | collective-permute-start | bytes 98312 | tf_op jit(solution)/shard_map/ppermute | solution.py:1000
  89.3 1.6 collective-permute-start.18
  95.0 2.1 %collective-permute-start.22 = (bf16[128,512]{1,0:T(8,128)(2,1)S(1)}, bf16[128,512]{1,0:T(8,128)(2,1)S(1)}, u32[]{:S(2)}, u32[]{:S(2)}) collective-permute-start(bf16[128,512]{1,0:T(8,128)(2,1)S(1)} %add_body.6.refs_3_.refs_1_), channel_id=1, source_target_pairs={{0,2},{1,3},{2,0},{3,1},{4,6},{5,7},{6,4},{7,5},{8,10},{9,11},{10,... | collective-permute-start | bytes 393224 | tf_op jit(solution)/shard_map/ppermute | solution.py:573
  97.1 1.9 %collective-permute-done.17.refs_2_ = bf16[160,512]{1,0:T(8,128)(2,1)S(1)} collective-permute-done((bf16[160,512]{1,0:T(8,128)(2,1)S(1)}, bf16[160,512]{1,0:T(8,128)(2,1)S(1)}, u32[]{:S(2)}, u32[]{:S(2)}) %collective-permute-start.17) | collective-permute-done | bytes 163872 | tf_op jit(solution)/shard_map/ppermute | solution.py:573
  99.4 5.5 %collective-permute-done.16.refs_5_ = bf16[48,512]{1,0:T(8,128)(2,1)S(1)} collective-permute-done((bf16[48,512]{1,0:T(8,128)(2,1)S(1)}, bf16[48,512]{1,0:T(8,128)(2,1)S(1)}, u32[]{:S(2)}, u32[]{:S(2)}) %collective-permute-start.16) | collective-permute-done | bytes 49184 | tf_op jit(solution)/shard_map/ppermute | solution.py:1000
  106.2 2.3 %join.3 = (bf16[3072,256]{1,0:T(8,128)(2,1)}, f32[8,128]{1,0:T(8,128)S(1)}) custom-call(s32[1]{0:T(128)} %bitcast.sec_ref.refs_1_, bf16[1536,256]{1,0:T(8,128)(2,1)S(1)} %get-tuple-element.117.refs_0_, bf16[1536,256]{1,0:T(8,128)(2,1)} %collective-permute-done.6.refs_1_, bf16[192,512]{1,0:T(8,128)(2,1)S(1)} %get-tuple-element.140.refs_2_), custom_call_target="tpu_custom_call" | custom-call | flops 1024 | bytes 1024 | tf_op jit(solution)/shard_map/join/pallas_call | solution.py:535
  109.5 3.9 %collective-permute-done.21.refs_2_ = bf16[160,512]{1,0:T(8,128)(2,1)S(1)} collective-permute-done((bf16[160,512]{1,0:T(8,128)(2,1)S(1)}, bf16[160,512]{1,0:T(8,128)(2,1)S(1)}, u32[]{:S(2)}, u32[]{:S(2)}) %collective-permute-start.21) | collective-permute-done | bytes 163872 | tf_op jit(solution)/shard_map/ppermute | solution.py:573
  113.5 4.1 %collective-permute-done.19.refs_3_ = bf16[192,512]{1,0:T(8,128)(2,1)S(1)} collective-permute-done((bf16[192,512]{1,0:T(8,128)(2,1)S(1)}, bf16[192,512]{1,0:T(8,128)(2,1)S(1)}, u32[]{:S(2)}, u32[]{:S(2)}) %collective-permute-start.19) | collective-permute-done | bytes 196640 | tf_op jit(solution)/shard_map/ppermute | solution.py:573
  117.8 2.0 %collective-permute-start.24 = (bf16[144,512]{1,0:T(8,128)(2,1)S(1)}, bf16[144,512]{1,0:T(8,128)(2,1)S(1)}, u32[]{:S(2)}, u32[]{:S(2)}) collective-permute-start(bf16[144,512]{1,0:T(8,128)(2,1)S(1)} %get-tuple-element.145.refs_4_), channel_id=1, source_target_pairs={{0,1},{1,0},{2,3},{3,2},{4,5},{5,4},{6,7},{7,6},{8,9},{9,8},{10,11... | collective-permute-start | bytes 442376 | tf_op jit(solution)/shard_map/ppermute | solution.py:1000
  119.8 2.2 %collective-permute-start.29 = (bf16[256,512]{1,0:T(8,128)(2,1)S(1)}, bf16[256,512]{1,0:T(8,128)(2,1)S(1)}, u32[]{:S(2)}, u32[]{:S(2)}) collective-permute-start(bf16[256,512]{1,0:T(8,128)(2,1)S(1)} %merge_body.6.refs_3_.refs_1_), channel_id=1, source_target_pairs={{0,8},{1,9},{2,10},{3,11},{4,12},{5,13},{6,14},{7,15},{8,0},{9,1},... | collective-permute-start | bytes 786440 | tf_op jit(solution)/shard_map/ppermute | solution.py:573
  122.2 2.4 %collective-permute-done.24.refs_5_ = bf16[144,512]{1,0:T(8,128)(2,1)S(1)} collective-permute-done((bf16[144,512]{1,0:T(8,128)(2,1)S(1)}, bf16[144,512]{1,0:T(8,128)(2,1)S(1)}, u32[]{:S(2)}, u32[]{:S(2)}) %collective-permute-start.24) | collective-permute-done | bytes 147488 | tf_op jit(solution)/shard_map/ppermute | solution.py:1000
  126.0 4.0 %collective-permute-done.29.refs_2_ = bf16[256,512]{1,0:T(8,128)(2,1)S(1)} collective-permute-done((bf16[256,512]{1,0:T(8,128)(2,1)S(1)}, bf16[256,512]{1,0:T(8,128)(2,1)S(1)}, u32[]{:S(2)}, u32[]{:S(2)}) %collective-permute-start.29) | collective-permute-done | bytes 262176 | tf_op jit(solution)/shard_map/ppermute | solution.py:573
  131.6 1.8 %collective-permute-done.27.refs_2_ = bf16[384,512]{1,0:T(8,128)(2,1)S(1)} collective-permute-done((bf16[384,512]{1,0:T(8,128)(2,1)S(1)}, bf16[384,512]{1,0:T(8,128)(2,1)S(1)}, u32[]{:S(2)}, u32[]{:S(2)}) %collective-permute-start.27) | collective-permute-done | bytes 393248 | tf_op jit(solution)/shard_map/ppermute | solution.py:573
  133.5 1.7 %collective-permute-start.30 = (bf16[768,512]{1,0:T(8,128)(2,1)S(1)}, bf16[768,512]{1,0:T(8,128)(2,1)S(1)}, u32[]{:S(2)}, u32[]{:S(2)}) collective-permute-start(bf16[768,512]{1,0:T(8,128)(2,1)S(1)} %merge_body.11.after_ref.p0), channel_id=1, source_target_pairs={{0,1},{1,0},{2,3},{3,2},{4,5},{5,4},{6,7},{7,6},{8,9},{9,8},{10,11... | collective-permute-start | bytes 2359304 | tf_op jit(solution)/shard_map/ppermute | solution.py:573
  135.2 2.3 %step_grad.1 = (f32[512,512]{1,0:T(8,128)}, f32[1,1024]{1,0:T(1,128)}, f32[1,1024]{1,0:T(1,128)}, f32[1,1024]{1,0:T(1,128)}, f32[3,128]{1,0:T(4,128)S(1)}, /*index=5*/f32[8,128]{1,0:T(8,128)S(1)}) custom-call(bf16[272,512]{1,0:T(8,128)(2,1)S(1)} %get-tuple-element.146.rows_ref, bf16[768,512]{1,0:T(8,128)(2,1)S(1)} %merge_body.11.after_ref.p0), custom_call_target="tpu_custom_call" | custom-call | flops 68719476736 | bytes 1024 | tf_op jit(solution)/shard_map/step_grad/pallas_call | solution.py:1007
  137.5 2.5 %place.6 = (f32[512,1024]{1,0:T(8,128)}, f32[512,512]{1,0:T(8,128)}, f32[512,512]{1,0:T(8,128)}, f32[512,512]{1,0:T(8,128)}, f32[8,128]{1,0:T(8,128)S(1)}) custom-call(s32[4]{0:T(128)S(1)} %pad_add_fusion.1.runs, bf16[512,512]{1,0:T(8,128)(2,1)} %merge_body.9.refs_3_.p0, bf16[512,512]{1,0:T(8,128)(2,1)S(1)} %collective-permute-done.35.p1, ...), custom_call_target="tpu_custom_call" | custom-call | flops 1024 | bytes 1024 | tf_op jit(solution)/shard_map/place/pallas_call | solution.py:681
  140.0 2.1 %place.7 = (f32[512,1024]{1,0:T(8,128)}, f32[512,1024]{1,0:T(8,128)}, f32[512,1024]{1,0:T(8,128)}, f32[8,128]{1,0:T(8,128)S(1)}) custom-call(s32[4]{0:T(128)S(1)} %pad_add_fusion.runs, bf16[640,512]{1,0:T(8,128)(2,1)S(1)} %merge_body.10.refs_3_.p0, bf16[640,512]{1,0:T(8,128)(2,1)S(1)} %collective-permute-done.34.p1, ...), custom_call_target="tpu_custom_call", output_to_operand_aliasing={{0}: (4, {})} | custom-call | flops 1024 | bytes 1024 | tf_op jit(solution)/shard_map/place/pallas_call | solution.py:681
  142.1 2.3 %place.8 = (f32[1536,1024]{1,0:T(8,128)}, f32[8,128]{1,0:T(8,128)S(1)}) custom-call(s32[4]{0:T(128)S(1)} %pad_add_fusion.runs, bf16[768,512]{1,0:T(8,128)(2,1)S(1)} %merge_body.11.after_ref.p0, bf16[768,512]{1,0:T(8,128)(2,1)S(1)} %collective-permute-done.33.p1, f32[8,128]{1,0:T(8,128)S(1)} %get-tuple-element.152.after_ref), custom_call_target="tpu_custom_call" | custom-call | flops 1024 | bytes 1024 | tf_op jit(solution)/shard_map/place/pallas_call | solution.py:681
  147.1 2.1 %place.9 = (f32[512,1024]{1,0:T(8,128)}, f32[512,1024]{1,0:T(8,128)}, f32[512,1024]{1,0:T(8,128)}, f32[8,128]{1,0:T(8,128)S(1)}) custom-call(s32[4]{0:T(128)S(1)} %pad_add_fusion.runs, bf16[640,512]{1,0:T(8,128)(2,1)S(1)} %then.3.after_ref.p0, ...), custom_call_target="tpu_custom_call", output_to_operand_aliasing={{0}: (4, {}), {1}: (5, {}), {2}: (6, {})} | custom-call | flops 1024 | bytes 1024 | tf_op jit(solution)/shard_map/place/pallas_call | solution.py:681
  149.2 2.0 %place.10 = (f32[512,1024]{1,0:T(8,128)}, f32[512,512]{1,0:T(8,128)}, f32[512,512]{1,0:T(8,128)}, f32[512,512]{1,0:T(8,128)}, f32[8,128]{1,0:T(8,128)S(1)}) custom-call(s32[4]{0:T(128)S(1)} %pad_add_fusion.1.runs, bf16[512,512]{1,0:T(8,128)(2,1)S(1)} %then.4.after_ref.p0, ...), custom_call_target="tpu_custom_call", output_to_operand_aliasing={{0}: (4, {}), {1}: (5, {}), {2}: (6, {}), {3}: (7, {})} | custom-call | flops 1024 | bytes 1024 | tf_op jit(solution)/shard_map/place/pallas_call | solution.py:681
  153.7 2.9 %place.11 = (f32[1536,1024]{1,0:T(8,128)}, f32[8,128]{1,0:T(8,128)}) custom-call(s32[4]{0:T(128)S(1)} %pad_add_fusion.runs, bf16[768,512]{1,0:T(8,128)(2,1)S(1)} %then.5.p0.after_ref, bf16[768,512]{1,0:T(8,128)(2,1)S(1)} %collective-permute-done.38.p1, bf16[768,512]{1,0:T(8,128)(2,1)S(1)} %then.5.p0.after_ref, ...), custom_call_target="tpu_custom_call", output_to_operand_aliasing={{0}: (4, {})} | custom-call | flops 1024 | bytes 1024 | tf_op jit(solution)/shard_map/place/pallas_call | solution.py:681
  (111 shorter events, 26.7 us)
Async XLA Ops:
  39.4 10.9 %collective-permute-start.5 = (bf16[1024,512]{1,0:T(8,128)(2,1)}, bf16[1024,512]{1,0:T(8,128)(2,1)S(1)}, u32[]{:S(2)}, u32[]{:S(2)}) collective-permute-start(bf16[1024,512]{1,0:T(8,128)(2,1)} %bitcast.40), channel_id=1, source_target_pairs={{0,16},{16,0},{1,17},{17,1},{2,18},{18,2},{3,19},{19,3},{4,20},{20... | collective-permute-start | bytes 3145736 | tf_op jit(solution)/shard_map/ppermute | solution.py:548
  40.0 12.3 %collective-permute-start.4 = (bf16[1280,512]{1,0:T(8,128)(2,1)}, bf16[1280,512]{1,0:T(8,128)(2,1)S(1)}, u32[]{:S(2)}, u32[]{:S(2)}) collective-permute-start(bf16[1280,512]{1,0:T(8,128)(2,1)} %bitcast.39), channel_id=1, source_target_pairs={{0,16},{16,0},{1,17},{17,1},{2,18},{18,2},{3,19},{19,3},{4,20},{20... | collective-permute-start | bytes 3932168 | tf_op jit(solution)/shard_map/ppermute | solution.py:548
  40.0 17.2 %collective-permute-start.3 = (bf16[32,1024]{1,0:T(8,128)(2,1)}, bf16[32,1024]{1,0:T(8,128)(2,1)}, u32[]{:S(2)}, u32[]{:S(2)}) collective-permute-start(bf16[32,1024]{1,0:T(8,128)(2,1)} %get-tuple-element.103), channel_id=1, source_target_pairs={{0,16},{16,0},{1,17},{17,1},{2,18},{18,2},{3,19},{19,3},{4,20},{20... | collective-permute-start | bytes 196616 | tf_op jit(solution)/shard_map/ppermute | solution.py:548
  49.7 16.8 %collective-permute-start.2 = (bf16[1536,512]{1,0:T(8,128)(2,1)}, bf16[1536,512]{1,0:T(8,128)(2,1)}, u32[]{:S(2)}, u32[]{:S(2)}) collective-permute-start(bf16[1536,512]{1,0:T(8,128)(2,1)} %bitcast.38), channel_id=1, source_target_pairs={{0,16},{16,0},{1,17},{17,1},{2,18},{18,2},{3,19},{19,3},{4,20},{20... | collective-permute-start | bytes 4718600 | tf_op jit(solution)/shard_map/ppermute | solution.py:548
  49.7 19.4 %collective-permute-start = (bf16[1536,256]{1,0:T(8,128)(2,1)}, bf16[1536,256]{1,0:T(8,128)(2,1)}, u32[]{:S(2)}, u32[]{:S(2)}) collective-permute-start(bf16[1536,256]{1,0:T(8,128)(2,1)} %get-tuple-element.96), channel_id=1, source_target_pairs={{0,16},{16,0},{1,17},{17,1},{2,18},{18,2},{3,19},{19,3},{4,20},{20... | collective-permute-start | bytes 2359304 | tf_op jit(solution)/shard_map/ppermute | solution.py:548
  50.3 18.9 %collective-permute-start.1 = (bf16[1536,256]{1,0:T(8,128)(2,1)}, bf16[1536,256]{1,0:T(8,128)(2,1)}, u32[]{:S(2)}, u32[]{:S(2)}) collective-permute-start(bf16[1536,256]{1,0:T(8,128)(2,1)} %get-tuple-element.98), channel_id=1, source_target_pairs={{0,16},{16,0},{1,17},{17,1},{2,18},{18,2},{3,19},{19,3},{4,20},{20... | collective-permute-start | bytes 2359304 | tf_op jit(solution)/shard_map/ppermute | solution.py:548
  52.2 21.6 %collective-permute-start.10 = (bf16[512,512]{1,0:T(8,128)(2,1)}, bf16[512,512]{1,0:T(8,128)(2,1)}, u32[]{:S(2)}, u32[]{:S(2)}) collective-permute-start(bf16[512,512]{1,0:T(8,128)(2,1)} %get-tuple-element.124), channel_id=1, source_target_pairs={{0,4},{1,5},{2,6},{3,7},{4,0},{5,1},{6,2},{7,3},{8,12},{9,13},{10,... | collective-permute-start | bytes 1572872 | tf_op jit(solution)/shard_map/ppermute | solution.py:573
  57.2 20.1 %collective-permute-start.9 = (bf16[640,512]{1,0:T(8,128)(2,1)}, bf16[640,512]{1,0:T(8,128)(2,1)}, u32[]{:S(2)}, u32[]{:S(2)}) collective-permute-start(bf16[640,512]{1,0:T(8,128)(2,1)} %get-tuple-element.122), channel_id=1, source_target_pairs={{0,1},{1,0},{2,3},{3,2},{4,5},{5,4},{6,7},{7,6},{8,9},{9,8},{10,11... | collective-permute-start | bytes 1966088 | tf_op jit(solution)/shard_map/ppermute | solution.py:573
  66.5 13.6 %collective-permute-start.8 = (bf16[32,512]{1,0:T(8,128)(2,1)}, bf16[32,512]{1,0:T(8,128)(2,1)}, u32[]{:S(2)}, u32[]{:S(2)}) collective-permute-start(bf16[32,512]{1,0:T(8,128)(2,1)} %get-tuple-element.113.after_ref.refs_4_), channel_id=1, source_target_pairs={{0,16},{16,0},{1,17},{17,1},{2,18},{18,2},{3,19},{19,3},{4,20},{20... | collective-permute-start | bytes 98312 | tf_op jit(solution)/shard_map/ppermute | solution.py:548
  69.1 37.1 %collective-permute-start.6 = (bf16[1536,256]{1,0:T(8,128)(2,1)}, bf16[1536,256]{1,0:T(8,128)(2,1)}, u32[]{:S(2)}, u32[]{:S(2)}) collective-permute-start(bf16[1536,256]{1,0:T(8,128)(2,1)} %get-tuple-element.118), channel_id=1, source_target_pairs={{0,16},{16,0},{1,17},{17,1},{2,18},{18,2},{3,19},{19,3},{4,20},{20... | collective-permute-start | bytes 2359304 | tf_op jit(solution)/shard_map/ppermute | solution.py:548
  69.3 12.8 %collective-permute-start.7 = (bf16[768,512]{1,0:T(8,128)(2,1)S(1)}, bf16[768,512]{1,0:T(8,128)(2,1)S(1)}, u32[]{:S(2)}, u32[]{:S(2)}) collective-permute-start(bf16[768,512]{1,0:T(8,128)(2,1)S(1)} %get-tuple-element.120), channel_id=1, source_target_pairs={{0,1},{1,0},{2,3},{3,2},{4,5},{5,4},{6,7},{7,6},{8,9},{9,8},{10,11... | collective-permute-start | bytes 2359304 | tf_op jit(solution)/shard_map/ppermute | solution.py:573
  75.0 14.2 %collective-permute-start.14 = (bf16[256,512]{1,0:T(8,128)(2,1)S(1)}, bf16[256,512]{1,0:T(8,128)(2,1)S(1)}, u32[]{:S(2)}, u32[]{:S(2)}) collective-permute-start(bf16[256,512]{1,0:T(8,128)(2,1)S(1)} %get-tuple-element.132), channel_id=1, source_target_pairs={{0,8},{1,9},{2,10},{3,11},{4,12},{5,13},{6,14},{7,15},{8,0},{9,1},... | collective-permute-start | bytes 786440 | tf_op jit(solution)/shard_map/ppermute | solution.py:573
  78.6 12.3 %collective-permute-start.13 = (bf16[320,512]{1,0:T(8,128)(2,1)S(1)}, bf16[320,512]{1,0:T(8,128)(2,1)S(1)}, u32[]{:S(2)}, u32[]{:S(2)}) collective-permute-start(bf16[320,512]{1,0:T(8,128)(2,1)S(1)} %get-tuple-element.131), channel_id=1, source_target_pairs={{0,2},{1,3},{2,0},{3,1},{4,6},{5,7},{6,4},{7,5},{8,10},{9,11},{10,... | collective-permute-start | bytes 983048 | tf_op jit(solution)/shard_map/ppermute | solution.py:573
  83.0 9.8 %collective-permute-start.11 = (bf16[384,512]{1,0:T(8,128)(2,1)S(1)}, bf16[384,512]{1,0:T(8,128)(2,1)S(1)}, u32[]{:S(2)}, u32[]{:S(2)}) collective-permute-start(bf16[384,512]{1,0:T(8,128)(2,1)S(1)} %get-tuple-element.129), channel_id=1, source_target_pairs={{0,2},{1,3},{2,0},{3,1},{4,6},{5,7},{6,4},{7,5},{8,10},{9,11},{10,... | collective-permute-start | bytes 1179656 | tf_op jit(solution)/shard_map/ppermute | solution.py:573
  91.0 8.0 %collective-permute-start.17 = (bf16[160,512]{1,0:T(8,128)(2,1)S(1)}, bf16[160,512]{1,0:T(8,128)(2,1)S(1)}, u32[]{:S(2)}, u32[]{:S(2)}) collective-permute-start(bf16[160,512]{1,0:T(8,128)(2,1)S(1)} %get-tuple-element.138), channel_id=1, source_target_pairs={{0,4},{1,5},{2,6},{3,7},{4,0},{5,1},{6,2},{7,3},{8,12},{9,13},{10,... | collective-permute-start | bytes 491528 | tf_op jit(solution)/shard_map/ppermute | solution.py:573
  92.9 12.0 %collective-permute-start.15 = (bf16[192,512]{1,0:T(8,128)(2,1)S(1)}, bf16[192,512]{1,0:T(8,128)(2,1)S(1)}, u32[]{:S(2)}, u32[]{:S(2)}) collective-permute-start(bf16[192,512]{1,0:T(8,128)(2,1)S(1)} %get-tuple-element.136), channel_id=1, source_target_pairs={{0,4},{1,5},{2,6},{3,7},{4,0},{5,1},{6,2},{7,3},{8,12},{9,13},{10,... | collective-permute-start | bytes 589832 | tf_op jit(solution)/shard_map/ppermute | solution.py:573
  94.2 10.7 %collective-permute-start.16 = (bf16[48,512]{1,0:T(8,128)(2,1)S(1)}, bf16[48,512]{1,0:T(8,128)(2,1)S(1)}, u32[]{:S(2)}, u32[]{:S(2)}) collective-permute-start(bf16[48,512]{1,0:T(8,128)(2,1)S(1)} %get-tuple-element.137.refs_4_), channel_id=1, source_target_pairs={{0,4},{1,5},{2,6},{3,7},{4,0},{5,1},{6,2},{7,3},{8,12},{9,13},{10,... | collective-permute-start | bytes 147464 | tf_op jit(solution)/shard_map/ppermute | solution.py:1000
  95.0 13.5 %collective-permute-start.22 = (bf16[128,512]{1,0:T(8,128)(2,1)S(1)}, bf16[128,512]{1,0:T(8,128)(2,1)S(1)}, u32[]{:S(2)}, u32[]{:S(2)}) collective-permute-start(bf16[128,512]{1,0:T(8,128)(2,1)S(1)} %add_body.6.refs_3_.refs_1_), channel_id=1, source_target_pairs={{0,2},{1,3},{2,0},{3,1},{4,6},{5,7},{6,4},{7,5},{8,10},{9,11},{10,... | collective-permute-start | bytes 393224 | tf_op jit(solution)/shard_map/ppermute | solution.py:573
  99.0 14.4 %collective-permute-start.21 = (bf16[160,512]{1,0:T(8,128)(2,1)S(1)}, bf16[160,512]{1,0:T(8,128)(2,1)S(1)}, u32[]{:S(2)}, u32[]{:S(2)}) collective-permute-start(bf16[160,512]{1,0:T(8,128)(2,1)S(1)} %add_body.7.refs_6_.refs_1_), channel_id=1, source_target_pairs={{0,8},{1,9},{2,10},{3,11},{4,12},{5,13},{6,14},{7,15},{8,0},{9,1},... | collective-permute-start | bytes 491528 | tf_op jit(solution)/shard_map/ppermute | solution.py:573
  105.0 12.7 %collective-permute-start.19 = (bf16[192,512]{1,0:T(8,128)(2,1)S(1)}, bf16[192,512]{1,0:T(8,128)(2,1)S(1)}, u32[]{:S(2)}, u32[]{:S(2)}) collective-permute-start(bf16[192,512]{1,0:T(8,128)(2,1)S(1)} %get-tuple-element.140.refs_2_), channel_id=1, source_target_pairs={{0,8},{1,9},{2,10},{3,11},{4,12},{5,13},{6,14},{7,15},{8,0},{9,1},... | collective-permute-start | bytes 589832 | tf_op jit(solution)/shard_map/ppermute | solution.py:573
  105.0 8.5 %collective-permute-start.20 = (bf16[80,512]{1,0:T(8,128)(2,1)S(1)}, bf16[80,512]{1,0:T(8,128)(2,1)S(1)}, u32[]{:S(2)}, u32[]{:S(2)}) collective-permute-start(bf16[80,512]{1,0:T(8,128)(2,1)S(1)} %get-tuple-element.142.refs_4_), channel_id=1, source_target_pairs={{0,2},{1,3},{2,0},{3,1},{4,6},{5,7},{6,4},{7,5},{8,10},{9,11},{10,... | collective-permute-start | bytes 245768 | tf_op jit(solution)/shard_map/ppermute | solution.py:1000
  108.6 11.2 %collective-permute-start.26 = (bf16[128,512]{1,0:T(8,128)(2,1)S(1)}, bf16[128,512]{1,0:T(8,128)(2,1)S(1)}, u32[]{:S(2)}, u32[]{:S(2)}) collective-permute-start(bf16[128,512]{1,0:T(8,128)(2,1)S(1)} %add_body.9.refs_3_.refs_1_), channel_id=1, source_target_pairs={{0,1},{1,0},{2,3},{3,2},{4,5},{5,4},{6,7},{7,6},{8,9},{9,8},{10,11... | collective-permute-start | bytes 393224 | tf_op jit(solution)/shard_map/ppermute | solution.py:573
  113.4 8.6 %collective-permute-start.25 = (bf16[160,512]{1,0:T(8,128)(2,1)S(1)}, bf16[160,512]{1,0:T(8,128)(2,1)S(1)}, u32[]{:S(2)}, u32[]{:S(2)}) collective-permute-start(bf16[160,512]{1,0:T(8,128)(2,1)S(1)} %add_body.10.refs_6_.refs_1_), channel_id=1, source_target_pairs={{0,4},{1,5},{2,6},{3,7},{4,0},{5,1},{6,2},{7,3},{8,12},{9,13},{10,... | collective-permute-start | bytes 491528 | tf_op jit(solution)/shard_map/ppermute | solution.py:573
  117.7 6.9 %collective-permute-start.23 = (bf16[192,512]{1,0:T(8,128)(2,1)S(1)}, bf16[192,512]{1,0:T(8,128)(2,1)S(1)}, u32[]{:S(2)}, u32[]{:S(2)}) collective-permute-start(bf16[192,512]{1,0:T(8,128)(2,1)S(1)} %get-tuple-element.144.refs_3_.refs_2_), channel_id=1, source_target_pairs={{0,4},{1,5},{2,6},{3,7},{4,0},{5,1},{6,2},{7,3},{8,12},{9,13},{10,... | collective-permute-start | bytes 589832 | tf_op jit(solution)/shard_map/ppermute | solution.py:573
  119.8 10.1 %collective-permute-start.29 = (bf16[256,512]{1,0:T(8,128)(2,1)S(1)}, bf16[256,512]{1,0:T(8,128)(2,1)S(1)}, u32[]{:S(2)}, u32[]{:S(2)}) collective-permute-start(bf16[256,512]{1,0:T(8,128)(2,1)S(1)} %merge_body.6.refs_3_.refs_1_), channel_id=1, source_target_pairs={{0,8},{1,9},{2,10},{3,11},{4,12},{5,13},{6,14},{7,15},{8,0},{9,1},... | collective-permute-start | bytes 786440 | tf_op jit(solution)/shard_map/ppermute | solution.py:573
  122.0 8.8 %collective-permute-start.28 = (bf16[320,512]{1,0:T(8,128)(2,1)S(1)}, bf16[320,512]{1,0:T(8,128)(2,1)S(1)}, u32[]{:S(2)}, u32[]{:S(2)}) collective-permute-start(bf16[320,512]{1,0:T(8,128)(2,1)S(1)} %merge_body.7.refs_6_.refs_1_), channel_id=1, source_target_pairs={{0,2},{1,3},{2,0},{3,1},{4,6},{5,7},{6,4},{7,5},{8,10},{9,11},{10,... | collective-permute-start | bytes 983048 | tf_op jit(solution)/shard_map/ppermute | solution.py:573
  124.7 8.7 %collective-permute-start.27 = (bf16[384,512]{1,0:T(8,128)(2,1)S(1)}, bf16[384,512]{1,0:T(8,128)(2,1)S(1)}, u32[]{:S(2)}, u32[]{:S(2)}) collective-permute-start(bf16[384,512]{1,0:T(8,128)(2,1)S(1)} %get-tuple-element.147.refs_3_.refs_1_), channel_id=1, source_target_pairs={{0,2},{1,3},{2,0},{3,1},{4,6},{5,7},{6,4},{7,5},{8,10},{9,11},{10,... | collective-permute-start | bytes 1179656 | tf_op jit(solution)/shard_map/ppermute | solution.py:573
  130.8 15.1 %collective-permute-start.31 = (bf16[512,512]{1,0:T(8,128)(2,1)}, bf16[512,512]{1,0:T(8,128)(2,1)}, u32[]{:S(2)}, u32[]{:S(2)}) collective-permute-start(bf16[512,512]{1,0:T(8,128)(2,1)} %merge_body.9.refs_3_.p0), channel_id=1, source_target_pairs={{0,4},{1,5},{2,6},{3,7},{4,0},{5,1},{6,2},{7,3},{8,12},{9,13},{10,... | collective-permute-start | bytes 1572872 | tf_op jit(solution)/shard_map/ppermute | solution.py:573
  130.9 9.1 %collective-permute-start.34 = (bf16[640,512]{1,0:T(8,128)(2,1)S(1)}, bf16[640,512]{1,0:T(8,128)(2,1)S(1)}, u32[]{:S(2)}, u32[]{:S(2)}) collective-permute-start(bf16[640,512]{1,0:T(8,128)(2,1)S(1)} %merge_body.10.refs_3_.p0), channel_id=1, source_target_pairs={{0,16},{16,0},{1,17},{17,1},{2,18},{18,2},{3,19},{19,3},{4,20},{20... | collective-permute-start | bytes 1966088 | tf_op jit(solution)/shard_map/ppermute | solution.py:548
  131.4 13.1 %collective-permute-start.32 = (bf16[640,512]{1,0:T(8,128)(2,1)S(1)}, bf16[640,512]{1,0:T(8,128)(2,1)S(1)}, u32[]{:S(2)}, u32[]{:S(2)}) collective-permute-start(bf16[640,512]{1,0:T(8,128)(2,1)S(1)} %merge_body.10.refs_3_.p0), channel_id=1, source_target_pairs={{0,1},{1,0},{2,3},{3,2},{4,5},{5,4},{6,7},{7,6},{8,9},{9,8},{10,11... | collective-permute-start | bytes 1966088 | tf_op jit(solution)/shard_map/ppermute | solution.py:573
  133.5 8.7 %collective-permute-start.33 = (bf16[768,512]{1,0:T(8,128)(2,1)S(1)}, bf16[768,512]{1,0:T(8,128)(2,1)S(1)}, u32[]{:S(2)}, u32[]{:S(2)}) collective-permute-start(bf16[768,512]{1,0:T(8,128)(2,1)S(1)} %merge_body.11.after_ref.p0), channel_id=1, source_target_pairs={{0,16},{16,0},{1,17},{17,1},{2,18},{18,2},{3,19},{19,3},{4,20},{20... | collective-permute-start | bytes 2359304 | tf_op jit(solution)/shard_map/ppermute | solution.py:548
  133.5 17.7 %collective-permute-start.30 = (bf16[768,512]{1,0:T(8,128)(2,1)S(1)}, bf16[768,512]{1,0:T(8,128)(2,1)S(1)}, u32[]{:S(2)}, u32[]{:S(2)}) collective-permute-start(bf16[768,512]{1,0:T(8,128)(2,1)S(1)} %merge_body.11.after_ref.p0), channel_id=1, source_target_pairs={{0,1},{1,0},{2,3},{3,2},{4,5},{5,4},{6,7},{7,6},{8,9},{9,8},{10,11... | collective-permute-start | bytes 2359304 | tf_op jit(solution)/shard_map/ppermute | solution.py:573
  (20 other events, 83.7 us)
